TPU v7x, 32 devices: a whole 2x2x4 slice. The times are simulated.
32 devices in a mesh: py: 8 (over y, x, core), pz: 4 (over z).
Axes of the slice: x: 2, y: 2, z: 4, core: 2. Of those that a mesh axis runs over, the one named last changes fastest.
Arguments:
- solution: float32 [64, 64, 512], P('py', 'pz'), may hold values from -6 to 6
- right_side: float32 [64, 64, 512], P('py', 'pz'), may hold values from -6 to 6
- span_index: int32 [64, 64, 512], P('py', 'pz'), may hold values from 0 to 7
- coef_table: float32 [8], replicated, may hold values from 0.5 to 2
- xaxis_bands: float32 [2, 7, 512], replicated, may hold values from -0.5 to 0.5
- yaxis_bands: float32 [2, 7, 64], P(None, None, 'py'), may hold values from -0.5 to 0.5
- zaxis_bands: float32 [2, 7, 64], P(None, None, 'pz'), may hold values from -0.5 to 0.5
- xaxis_vectors: float32 [512, 512], replicated, may hold values from -0.25 to 0.25
- yaxis_vectors: float32 [64, 64], replicated, may hold values from -0.75 to 0.75
- zaxis_vectors: float32 [64, 64], replicated, may hold values from -0.75 to 0.75
- xaxis_values: float32 [512], replicated, may hold values from 0.25 to 2
- yaxis_values: float32 [64], replicated, may hold values from 0.25 to 2
- zaxis_values: float32 [64], replicated, may hold values from 0.25 to 2
Outputs:
- updated: float32 [64, 64, 512], P('py', 'pz')
- residual: float32 [64, 64, 512], P('py', 'pz')
All inputs are finite; a program needn't handle non-finite values.
Results may differ from a plain program's by a relative error of at most 0.0001.
Values sent between devices are 32-bit elements; how exact they have to be, the bound alone decides.
No kernel may reach another device: no remote copies, remote signals or barrier semaphores. Data moves between devices by JAX's collectives and lax.ppermute only.
A program may use at most 64 MiB of HBM per device.

v0:
```python
import jax
import jax.numpy as jnp
from jax import lax
from jax.sharding import PartitionSpec as P

ITERS = 2


HIGH = lax.Precision.HIGHEST


def with_halo(cells, sides, width):
    for axis, dim in sides:
        count = lax.axis_size(axis)
        ends = count - 1
        head = lax.slice_in_dim(cells, 0, width, axis=dim)
        tail = lax.slice_in_dim(cells, cells.shape[dim] - width, cells.shape[dim], axis=dim)
        cells = jnp.concatenate(
            [
                lax.ppermute(tail, axis, [(i, (i + 1) % count) for i in range(ends)]),
                cells,
                lax.ppermute(head, axis, [((i + 1) % count, i) for i in range(ends)]),
            ],
            axis=dim,
        )
    return cells


def band_padded(padded, bands, axis):
    length = padded.shape[axis] - 6
    layout = [1, 1, 1]
    layout[axis] = length
    summed = None
    for offset in range(7):
        contrib = bands[offset].reshape(layout) * lax.slice_in_dim(
            padded, offset, offset + length, axis=axis
        )
        summed = contrib if summed is None else summed + contrib
    return summed


def shards(
    solution,
    right_side,
    span_index,
    coef_table,
    xaxis_bands,
    yaxis_bands,
    zaxis_bands,
    xaxis_vectors,
    yaxis_vectors,
    zaxis_vectors,
    xaxis_values,
    yaxis_values,
    zaxis_values,
):
    yblock = lax.axis_index("py")
    zblock = lax.axis_index("pz")
    coefficient = jnp.zeros(span_index.shape, jnp.float32)
    for entry in range(coef_table.shape[0]):
        coefficient = jnp.where(span_index == entry, coef_table[entry], coefficient)
    updated = solution
    residual = right_side
    for iteration in range(ITERS):
        weighted = coefficient * updated
        padded = with_halo(weighted, (("py", 0), ("pz", 1)), 3)
        mass_part = band_padded(padded, zaxis_bands[1], 1)
        stiff_part = band_padded(padded, zaxis_bands[0], 1)
        mass_mass = band_padded(mass_part, yaxis_bands[1], 0)
        stiff_mass = band_padded(mass_part, yaxis_bands[0], 0)
        mass_stiff = band_padded(stiff_part, yaxis_bands[1], 0)
        xwidths = ((0, 0), (0, 0), (3, 3))
        applied = band_padded(jnp.pad(mass_mass, xwidths), xaxis_bands[0], 2) + band_padded(
            jnp.pad(stiff_mass + mass_stiff, xwidths), xaxis_bands[1], 2
        )
        residual = right_side - coefficient * applied
        spectral = jnp.einsum("yzi,ij->yzj", residual, xaxis_vectors, precision=HIGH)
        zlocal = jnp.einsum(
            "kix,ij->kjx",
            lax.all_to_all(spectral, "pz", split_axis=2, concat_axis=1, tiled=True),
            zaxis_vectors,
            precision=HIGH,
        )
        ylocal = lax.all_to_all(zlocal, "py", split_axis=1, concat_axis=0, tiled=True)
        zcount = ylocal.shape[1]
        xcount = ylocal.shape[2]
        zpart = lax.dynamic_slice_in_dim(zaxis_values, yblock * zcount, zcount)
        xpart = lax.dynamic_slice_in_dim(xaxis_values, zblock * xcount, xcount)
        modes = jnp.einsum("ikx,ij->jkx", ylocal, yaxis_vectors, precision=HIGH)
        modes = modes / (yaxis_values[:, None, None] + zpart[None, :, None] + xpart[None, None, :])
        restored = jnp.einsum("jkx,ij->ikx", modes, yaxis_vectors, precision=HIGH)
        zback = jnp.einsum(
            "yjk,ij->yik",
            lax.all_to_all(restored, "py", split_axis=0, concat_axis=1, tiled=True),
            zaxis_vectors,
            precision=HIGH,
        )
        update = jnp.einsum(
            "ykj,ij->yki",
            lax.all_to_all(zback, "pz", split_axis=1, concat_axis=2, tiled=True),
            xaxis_vectors,
            precision=HIGH,
        )
        updated = updated + update
    return (updated, residual)


def solution(mesh):
    return jax.shard_map(
        shards,
        mesh=mesh,
        in_specs=(
            P("py", "pz", None),
            P("py", "pz", None),
            P("py", "pz", None),
            P(),
            P(),
            P(None, None, "py"),
            P(None, None, "pz"),
            P(),
            P(),
            P(),
            P(),
            P(),
            P(),
        ),
        out_specs=(P("py", "pz", None), P("py", "pz", None)),
        check_vma=False,
    )
```

profile of v0, /device:TPU:0, one launch (start us, length us, event | category | flops | bytes accessed | tf_op | source)
XLA Modules:
  0.0 179.6 jit_solution(14247935883780223303)
XLA Ops:
  0.7 1.6 fusion.126
  2.3 6.2 %fusion.120 = f32[8,16,512]{2,1,0:T(8,128)S(1)} fusion(f32[8,16,512]{2,1,0:T(8,128)} %param.13, f32[]{:T(128)} %bitcast.7, s32[8,16,512]{2,1,0:T(8,128)} %param.15, f32[]{:T(128)} %bitcast.6, f32[]{:T(128)} %bitcast.5, f32[]{:T(128)} %bitcast.4, f32[]{:T(128)} %bitcast.3, f32[]{:T(128)} %bitcast.2, f32[]{:T(128)} %bitcast.1, f32[]{:T(128)} %bitcast), kind=kLoop, calls=%fused_computation.200 | loop fusion | flops 1114112 | bytes 786464 | tf_op jit(solution)/shard_map/mul | solution.py:65
  8.5 2.4 %collective-permute-start = (f32[3,16,512]{2,1,0:T(8,128)S(1)}, f32[3,16,512]{2,1,0:T(8,128)S(1)}, u32[]{:S(2)}, u32[]{:S(2)}) collective-permute-start(f32[3,16,512]{2,1,0:T(8,128)S(1)} %get-tuple-element.12), channel_id=1, source_target_pairs={{0,4},{4,8},{8,12},{12,16},{16,20},{20,24},{24,28},{1,5},{5,9},{9,... | collective-permute-start | bytes 294920 | tf_op jit(solution)/shard_map/ppermute | solution.py:20
  14.0 2.2 %collective-permute-done.1 = f32[3,16,512]{2,1,0:T(8,128)S(1)} collective-permute-done((f32[3,16,512]{2,1,0:T(8,128)S(1)}, f32[3,16,512]{2,1,0:T(8,128)S(1)}, u32[]{:S(2)}, u32[]{:S(2)}) %collective-permute-start.1) | collective-permute-done | bytes 98336 | tf_op jit(solution)/shard_map/ppermute | solution.py:22
  16.3 3.5 %collective-permute-start.2 = (f32[14,3,512]{2,1,0:T(4,128)S(1)}, f32[14,3,512]{2,1,0:T(4,128)S(1)}, u32[]{:S(2)}, u32[]{:S(2)}) collective-permute-start(f32[14,3,512]{2,1,0:T(4,128)S(1)} %get-tuple-element.8), channel_id=1, source_target_pairs={{0,1},{1,2},{2,3},{4,5},{5,6},{6,7},{8,9},{9,10},{10,11},{12,13},{... | collective-permute-start | bytes 258056 | tf_op jit(solution)/shard_map/ppermute | solution.py:20
  22.1 4.3 %collective-permute-done.3 = f32[14,3,512]{2,1,0:T(4,128)S(1)} collective-permute-done((f32[14,3,512]{2,1,0:T(4,128)S(1)}, f32[14,3,512]{2,1,0:T(4,128)S(1)}, u32[]{:S(2)}, u32[]{:S(2)}) %collective-permute-start.3) | collective-permute-done | bytes 86048 | tf_op jit(solution)/shard_map/ppermute | solution.py:22
  28.8 7.2 %fusion.6 = f32[8,16,512]{2,1,0:T(8,128)} fusion(f32[512,512]{1,0:T(8,128)S(1)} %copy-done, f32[8,16,512]{2,1,0:T(8,128)S(1)} %copy-done.6, f32[8,16,512]{2,1,0:T(8,128)S(1)} %multiply_add_fusion.5, f32[8,16,512]{2,1,0:T(8,128)S(1)} %fusion.82, f32[512]{0:T(512)S(1)} %bitcast.218, f32[512]{0:T(512)S(1)} %bitcast.220, f32[512]{0:T(512)S(1)} %bitcast.196, ...), kind=kOutput, calls=%fused_computation.16 | convolution fusion | flops 405602304 | bytes 2388000 | tf_op jit(solution)/shard_map/yzi,ij->yzj/dot_general | solution.py:77
  36.1 1.7 copy.53
  37.8 1.5 reshape.156
  39.2 13.7 %all_to_all.144 = f32[4,1,16384]{2,1,0:T(1,128)S(1)} all-to-all(f32[4,1,16384]{2,1,0:T(1,128)} %reshape.156), channel_id=1, replica_groups=mesh['py'=8,'pz'=4] {'pz'}, dimensions={0} | all-to-all | bytes 524288 | tf_op jit(solution)/shard_map/all_to_all | solution.py:80
  53.5 2.0 %reduce = f32[4,16384]{1,0:T(4,128)} reduce(f32[4,1,16384]{2,1,0:T(1,128)S(1)} %all_to_all.144, f32[]{:T(128)} %broadcast.32), dimensions={1}, to_apply=%all_to_all.104.reduce_sub_computation | reduce | bytes 524292 | tf_op jit(solution)/shard_map/all_to_all | solution.py:80
  55.5 1.6 reshape.157
  57.2 1.4 copy.54
  58.5 1.4 convolution_bitcast_fusion.7
  60.8 5.0 %all-to-all-start.1 = ((f32[8,64,128]{2,0,1:T(8,128)}), f32[8,64,128]{2,0,1:T(8,128)S(1)}, u32[]{:S(2)}, u32[]{:S(2)}) async-start(f32[8,64,128]{2,0,1:T(8,128)} %copy.56), calls=%async_computation.1 | async-start | bytes 524288 | tf_op jit(solution)/shard_map/all_to_all | solution.py:84
  68.0 4.7 %all-to-all-done.1 = f32[8,64,128]{2,0,1:T(8,128)S(1)} async-done(((f32[8,64,128]{2,0,1:T(8,128)}), f32[8,64,128]{2,0,1:T(8,128)S(1)}, u32[]{:S(2)}, u32[]{:S(2)}) %all-to-all-start.1) | async-done | bytes 262176 | tf_op jit(solution)/shard_map/all_to_all | solution.py:84
  73.7 9.3 %all_to_all.145 = f32[64,8,128]{2,1,0:T(8,128)S(1)} all-to-all(f32[64,8,128]{2,1,0:T(8,128)S(1)} %copy.61), channel_id=1, replica_groups=mesh['py'=8,'pz'=4] {'py'}, dimensions={0} | all-to-all | bytes 524288 | tf_op jit(solution)/shard_map/all_to_all | solution.py:94
  83.6 10.9 %all_to_all.146 = f32[8,64,128]{2,0,1:T(8,128)S(1)} all-to-all(f32[8,64,128]{2,0,1:T(8,128)S(1)} %copy.63), channel_id=1, replica_groups=mesh['py'=8,'pz'=4] {'pz'}, dimensions={1} | all-to-all | bytes 524288 | tf_op jit(solution)/shard_map/all_to_all | solution.py:100
  94.8 6.9 %fusion.119 = (f32[8,16,512]{2,1,0:T(8,128)S(1)}, f32[8,16,512]{2,1,0:T(8,128)}) fusion(f32[]{:T(128)} %bitcast.7, s32[8,16,512]{2,1,0:T(8,128)S(1)} %copy-done.1, f32[]{:T(128)} %bitcast.6, f32[]{:T(128)} %bitcast.5, f32[]{:T(128)} %bitcast.4, f32[]{:T(128)} %bitcast.3, f32[]{:T(128)} %bitcast.2, f32[]{:T(128)} %bitcast.1, f32[]{:T(128)} %bitcast, ...), kind=kOutput, calls=%fused_computation.199 | convolution fusion | flops 403832832 | bytes 2359328 | tf_op jit(solution)/shard_map/ykj,ij->yki/dot_general | solution.py:98
  101.8 1.3 collective-permute-start.4
  103.1 1.3 collective-permute-start.5
  104.5 3.4 %collective-permute-done.5 = f32[3,16,512]{2,1,0:T(8,128)S(1)} collective-permute-done((f32[3,16,512]{2,1,0:T(8,128)S(1)}, f32[3,16,512]{2,1,0:T(8,128)S(1)}, u32[]{:S(2)}, u32[]{:S(2)}) %collective-permute-start.5) | collective-permute-done | bytes 98336 | tf_op jit(solution)/shard_map/ppermute | solution.py:22
  108.0 2.1 %collective-permute-start.6 = (f32[14,3,512]{2,1,0:T(4,128)S(1)}, f32[14,3,512]{2,1,0:T(4,128)S(1)}, u32[]{:S(2)}, u32[]{:S(2)}) collective-permute-start(f32[14,3,512]{2,1,0:T(4,128)S(1)} %get-tuple-element.4), channel_id=1, source_target_pairs={{0,1},{1,2},{2,3},{4,5},{5,6},{6,7},{8,9},{9,10},{10,11},{12,13},{... | collective-permute-start | bytes 258056 | tf_op jit(solution)/shard_map/ppermute | solution.py:20
  110.1 1.5 collective-permute-start.7
  112.4 4.3 %collective-permute-done.7 = f32[14,3,512]{2,1,0:T(4,128)S(1)} collective-permute-done((f32[14,3,512]{2,1,0:T(4,128)S(1)}, f32[14,3,512]{2,1,0:T(4,128)S(1)}, u32[]{:S(2)}, u32[]{:S(2)}) %collective-permute-start.7) | collective-permute-done | bytes 86048 | tf_op jit(solution)/shard_map/ppermute | solution.py:22
  119.5 5.9 %fusion.56 = f32[8,16,512]{2,1,0:T(8,128)S(1)} fusion(f32[8,16,512]{2,1,0:T(8,128)S(1)} %copy-done.7, f32[8,16,512]{2,1,0:T(8,128)S(1)} %multiply_add_fusion.4, f32[8,16,512]{2,1,0:T(8,128)S(1)} %fusion.75, f32[512]{0:T(512)S(1)} %bitcast.219, f32[512]{0:T(512)S(1)} %bitcast.221, f32[512]{0:T(512)S(1)} %bitcast.197, f32[512]{0:T(512)S(1)} %bitcast.199, ...), kind=kLoop, calls=%fused_computation.88 | loop fusion | flops 2949120 | bytes 1339424 | tf_op jit(solution)/shard_map/sub | solution.py:76
  128.3 12.7 %all_to_all.147 = f32[4,1,16384]{2,1,0:T(1,128)S(1)} all-to-all(f32[4,1,16384]{2,1,0:T(1,128)S(1)} %reshape.158), channel_id=1, replica_groups=mesh['py'=8,'pz'=4] {'pz'}, dimensions={0} | all-to-all | bytes 524288 | tf_op jit(solution)/shard_map/all_to_all | solution.py:80
  141.0 1.3 reduce.1
  144.3 11.3 %all_to_all.148 = f32[8,64,128]{2,0,1:T(8,128)S(1)} all-to-all(f32[8,64,128]{2,0,1:T(8,128)S(1)} %copy.68), channel_id=1, replica_groups=mesh['py'=8,'pz'=4] {'py'}, dimensions={1} | all-to-all | bytes 524288 | tf_op jit(solution)/shard_map/all_to_all | solution.py:84
  156.7 9.3 %all_to_all.149 = f32[64,8,128]{2,1,0:T(8,128)S(1)} all-to-all(f32[64,8,128]{2,1,0:T(8,128)S(1)} %copy.73), channel_id=1, replica_groups=mesh['py'=8,'pz'=4] {'py'}, dimensions={0} | all-to-all | bytes 524288 | tf_op jit(solution)/shard_map/all_to_all | solution.py:94
  166.6 10.9 %all_to_all.150 = f32[8,64,128]{2,0,1:T(8,128)S(1)} all-to-all(f32[8,64,128]{2,0,1:T(8,128)S(1)} %copy.75), channel_id=1, replica_groups=mesh['py'=8,'pz'=4] {'pz'}, dimensions={1} | all-to-all | bytes 524288 | tf_op jit(solution)/shard_map/all_to_all | solution.py:100
  177.8 1.9 %convolution_add_fusion = f32[8,16,512]{2,1,0:T(8,128)} fusion(f32[8,16,512]{2,1,0:T(8,128)S(1)} %copy-done.3, f32[8,16,512]{2,1,0:T(8,128)S(1)} %all_to_all.135, f32[512,512]{1,0:T(8,128)S(1)} %copy-done), kind=kOutput, calls=%fused_computation.10 | convolution fusion | flops 402718720 | bytes 1835008 | tf_op jit(solution)/shard_map/ykj,ij->yki/dot_general | solution.py:98
  (169 shorter events, 23.0 us)
Async XLA Ops:
  0.6 27.7 %copy-start = (f32[512,512]{1,0:T(8,128)S(1)}, f32[512,512]{1,0:T(8,128)}, u32[]{:S(2)}) copy-start(f32[512,512]{1,0:T(8,128)} %param.20) | copy-start | bytes 3145732
  0.6 20.4 %copy-start.11 = (f32[2,7,16]{2,0,1:T(2,128)S(1)}, f32[2,7,16]{2,0,1:T(2,128)}, u32[]{:S(2)}) copy-start(f32[2,7,16]{2,0,1:T(2,128)} %param.19) | copy-start | bytes 2692
  8.5 5.5 %collective-permute-start = (f32[3,16,512]{2,1,0:T(8,128)S(1)}, f32[3,16,512]{2,1,0:T(8,128)S(1)}, u32[]{:S(2)}, u32[]{:S(2)}) collective-permute-start(f32[3,16,512]{2,1,0:T(8,128)S(1)} %get-tuple-element.12), channel_id=1, source_target_pairs={{0,4},{4,8},{8,12},{12,16},{16,20},{20,24},{24,28},{1,5},{5,9},{9,... | collective-permute-start | bytes 294920 | tf_op jit(solution)/shard_map/ppermute | solution.py:20
  10.9 5.3 %collective-permute-start.1 = (f32[3,16,512]{2,1,0:T(8,128)S(1)}, f32[3,16,512]{2,1,0:T(8,128)S(1)}, u32[]{:S(2)}, u32[]{:S(2)}) collective-permute-start(f32[3,16,512]{2,1,0:T(8,128)S(1)} %get-tuple-element.13), channel_id=1, source_target_pairs={{4,0},{8,4},{12,8},{16,12},{20,16},{24,20},{28,24},{5,1},{9,5},{13... | collective-permute-start | bytes 294920 | tf_op jit(solution)/shard_map/ppermute | solution.py:22
  13.0 15.2 %copy-start.9 = (f32[1,1,512]{2,0,1:T(1,128)}, f32[1,1,512]{2,0,1:T(1,128)S(1)}, u32[]{:S(2)}) copy-start(f32[1,1,512]{2,0,1:T(1,128)S(1)} %get-tuple-element.27) | copy-start | bytes 6148
  13.9 13.9 %copy-start.12 = (f32[8]{0:T(128)}, f32[8]{0:T(128)S(1)}, u32[]{:S(2)}) copy-start(f32[8]{0:T(128)S(1)} %get-tuple-element.28) | copy-start | bytes 100
  13.9 13.9 %copy-start.14 = (f32[8]{0:T(128)}, f32[8]{0:T(128)S(1)}, u32[]{:S(2)}) copy-start(f32[8]{0:T(128)S(1)} %get-tuple-element.29) | copy-start | bytes 100
  13.9 13.9 %copy-start.16 = (f32[8]{0:T(128)}, f32[8]{0:T(128)S(1)}, u32[]{:S(2)}) copy-start(f32[8]{0:T(128)S(1)} %get-tuple-element.30) | copy-start | bytes 100
  13.9 13.9 %copy-start.18 = (f32[8]{0:T(128)}, f32[8]{0:T(128)S(1)}, u32[]{:S(2)}) copy-start(f32[8]{0:T(128)S(1)} %get-tuple-element.31) | copy-start | bytes 100
  13.9 13.9 %copy-start.20 = (f32[8]{0:T(128)}, f32[8]{0:T(128)S(1)}, u32[]{:S(2)}) copy-start(f32[8]{0:T(128)S(1)} %get-tuple-element.32) | copy-start | bytes 100
  13.9 13.9 %copy-start.22 = (f32[8]{0:T(128)}, f32[8]{0:T(128)S(1)}, u32[]{:S(2)}) copy-start(f32[8]{0:T(128)S(1)} %get-tuple-element.40) | copy-start | bytes 100
  14.0 13.9 %copy-start.24 = (f32[8]{0:T(128)}, f32[8]{0:T(128)S(1)}, u32[]{:S(2)}) copy-start(f32[8]{0:T(128)S(1)} %get-tuple-element.41) | copy-start | bytes 100
  16.3 5.8 %collective-permute-start.2 = (f32[14,3,512]{2,1,0:T(4,128)S(1)}, f32[14,3,512]{2,1,0:T(4,128)S(1)}, u32[]{:S(2)}, u32[]{:S(2)}) collective-permute-start(f32[14,3,512]{2,1,0:T(4,128)S(1)} %get-tuple-element.8), channel_id=1, source_target_pairs={{0,1},{1,2},{2,3},{4,5},{5,6},{6,7},{8,9},{9,10},{10,11},{12,13},{... | collective-permute-start | bytes 258056 | tf_op jit(solution)/shard_map/ppermute | solution.py:20
  19.7 6.7 %collective-permute-start.3 = (f32[14,3,512]{2,1,0:T(4,128)S(1)}, f32[14,3,512]{2,1,0:T(4,128)S(1)}, u32[]{:S(2)}, u32[]{:S(2)}) collective-permute-start(f32[14,3,512]{2,1,0:T(4,128)S(1)} %get-tuple-element.9), channel_id=1, source_target_pairs={{1,0},{2,1},{3,2},{5,4},{6,5},{7,6},{9,8},{10,9},{11,10},{13,12},{... | collective-permute-start | bytes 258056 | tf_op jit(solution)/shard_map/ppermute | solution.py:22
  57.1 15.6 %copy-start.8 = (f32[64,64]{1,0:T(8,128)S(1)}, f32[64,64]{1,0:T(8,128)}, u32[]{:S(2)}) copy-start(f32[64,64]{1,0:T(8,128)} %param.21) | copy-start | bytes 49156
  60.8 11.9 %all-to-all-start.1 = ((f32[8,64,128]{2,0,1:T(8,128)}), f32[8,64,128]{2,0,1:T(8,128)S(1)}, u32[]{:S(2)}, u32[]{:S(2)}) async-start(f32[8,64,128]{2,0,1:T(8,128)} %copy.56), calls=%async_computation.1 | async-start | bytes 524288 | tf_op jit(solution)/shard_map/all_to_all | solution.py:84
  67.2 16.4 %copy-start.56 = (f32[128]{0:T(128)}, f32[128]{0:T(128)S(1)}, u32[]{:S(2)}) copy-start(f32[128]{0:T(128)S(1)} %dynamic_slice.9) | copy-start | bytes 1540
  68.0 15.7 %copy-start.54 = (f32[64,8]{0,1:T(8,128)}, f32[64,8]{0,1:T(8,128)S(1)}, u32[]{:S(2)}) copy-start(f32[64,8]{0,1:T(8,128)S(1)} %broadcast_add_fusion) | copy-start | bytes 6148
  73.2 21.6 %copy-start.2 = (f32[8,16,512]{2,1,0:T(8,128)S(1)}, f32[8,16,512]{2,1,0:T(8,128)}, u32[]{:S(2)}) copy-start(f32[8,16,512]{2,1,0:T(8,128)} %param.13) | copy-start | bytes 786436
  101.8 15.2 %copy-start.41 = (f32[16]{0:T(128)S(1)}, f32[16]{0:T(128)}, u32[]{:S(2)}) copy-start(f32[16]{0:T(128)} %copy-done.40) | copy-start | bytes 196
  101.8 15.2 %copy-start.43 = (f32[16]{0:T(128)S(1)}, f32[16]{0:T(128)}, u32[]{:S(2)}) copy-start(f32[16]{0:T(128)} %copy-done.42) | copy-start | bytes 196
  101.8 15.2 %copy-start.45 = (f32[16]{0:T(128)S(1)}, f32[16]{0:T(128)}, u32[]{:S(2)}) copy-start(f32[16]{0:T(128)} %copy-done.44) | copy-start | bytes 196
  101.8 15.2 %copy-start.47 = (f32[16]{0:T(128)S(1)}, f32[16]{0:T(128)}, u32[]{:S(2)}) copy-start(f32[16]{0:T(128)} %copy-done.46) | copy-start | bytes 196
  101.8 15.2 %copy-start.49 = (f32[16]{0:T(128)S(1)}, f32[16]{0:T(128)}, u32[]{:S(2)}) copy-start(f32[16]{0:T(128)} %copy-done.48) | copy-start | bytes 196
  101.8 15.2 %copy-start.51 = (f32[16]{0:T(128)S(1)}, f32[16]{0:T(128)}, u32[]{:S(2)}) copy-start(f32[16]{0:T(128)} %copy-done.50) | copy-start | bytes 196
  101.8 15.2 %copy-start.53 = (f32[16]{0:T(128)S(1)}, f32[16]{0:T(128)}, u32[]{:S(2)}) copy-start(f32[16]{0:T(128)} %copy-done.52) | copy-start | bytes 196
  101.8 2.6 %collective-permute-start.4 = (f32[3,16,512]{2,1,0:T(8,128)S(1)}, f32[3,16,512]{2,1,0:T(8,128)S(1)}, u32[]{:S(2)}, u32[]{:S(2)}) collective-permute-start(f32[3,16,512]{2,1,0:T(8,128)S(1)} %get-tuple-element.10), channel_id=1, source_target_pairs={{0,4},{4,8},{8,12},{12,16},{16,20},{20,24},{24,28},{1,5},{5,9},{9,... | collective-permute-start | bytes 294920 | tf_op jit(solution)/shard_map/ppermute | solution.py:20
  103.1 4.7 %collective-permute-start.5 = (f32[3,16,512]{2,1,0:T(8,128)S(1)}, f32[3,16,512]{2,1,0:T(8,128)S(1)}, u32[]{:S(2)}, u32[]{:S(2)}) collective-permute-start(f32[3,16,512]{2,1,0:T(8,128)S(1)} %get-tuple-element.11), channel_id=1, source_target_pairs={{4,0},{8,4},{12,8},{16,12},{20,16},{24,20},{28,24},{5,1},{9,5},{13... | collective-permute-start | bytes 294920 | tf_op jit(solution)/shard_map/ppermute | solution.py:22
  108.0 4.5 %collective-permute-start.6 = (f32[14,3,512]{2,1,0:T(4,128)S(1)}, f32[14,3,512]{2,1,0:T(4,128)S(1)}, u32[]{:S(2)}, u32[]{:S(2)}) collective-permute-start(f32[14,3,512]{2,1,0:T(4,128)S(1)} %get-tuple-element.4), channel_id=1, source_target_pairs={{0,1},{1,2},{2,3},{4,5},{5,6},{6,7},{8,9},{9,10},{10,11},{12,13},{... | collective-permute-start | bytes 258056 | tf_op jit(solution)/shard_map/ppermute | solution.py:20
  110.1 6.7 %collective-permute-start.7 = (f32[14,3,512]{2,1,0:T(4,128)S(1)}, f32[14,3,512]{2,1,0:T(4,128)S(1)}, u32[]{:S(2)}, u32[]{:S(2)}) collective-permute-start(f32[14,3,512]{2,1,0:T(4,128)S(1)} %get-tuple-element.5), channel_id=1, source_target_pairs={{1,0},{2,1},{3,2},{5,4},{6,5},{7,6},{9,8},{10,9},{11,10},{13,12},{... | collective-permute-start | bytes 258056 | tf_op jit(solution)/shard_map/ppermute | solution.py:22
  143.0 12.7 %copy-start.55 = (f32[64,8]{0,1:T(8,128)S(1)}, f32[64,8]{0,1:T(8,128)}, u32[]{:S(2)}) copy-start(f32[64,8]{0,1:T(8,128)} %copy-done.54) | copy-start | bytes 6148
  156.1 21.6 %copy-start.3 = (f32[8,16,512]{2,1,0:T(8,128)S(1)}, f32[8,16,512]{2,1,0:T(8,128)}, u32[]{:S(2)}) copy-start(f32[8,16,512]{2,1,0:T(8,128)} %get-tuple-element.65) | copy-start | bytes 786436
  (35 other events, 114.7 us)
where the time goes:
time: 181 us; the launch traced here: 180 us
  blocking collectives  78.1 us (43%)
  matrix products  20.8 us (11%)
  waiting for transfers between devices  20.7 us (11%)
  starting transfers between devices  19.6 us (11%)
  other arithmetic  19.4 us (11%)
  local copies, waits for them, and re-layouts  19.1 us (11%)
    all_to_all x2, blocking collectives, shards(): lax.all_to_all(spectral, 'pz', split_axis=2, concat_axis=1, tiled=True)  26.3 us
    all_to_all x2, blocking collectives, shards(): lax.all_to_all(zback, 'pz', split_axis=1, concat_axis=2, tiled=True)  21.8 us
    all_to_all x2, blocking collectives, shards(): lax.all_to_all(restored, 'py', split_axis=0, concat_axis=1, tiled=True)  18.7 us
    ppermute x4, waiting for transfers between devices, with_halo(): lax.ppermute(head, axis, [((i + 1) % count, i) for i in range(ends)])  14.3 us
    all_to_all x1, blocking collectives, shards(): lax.all_to_all(zlocal, 'py', split_axis=1, concat_axis=0, tiled=True)  11.3 us
    ppermute x4, starting transfers between devices, with_halo(): lax.ppermute(tail, axis, [(i, (i + 1) % count) for i in range(ends)])  9.27 us
    dot_general x2, matrix products, shards(): jnp.einsum('ykj,ij->yki', lax.all_to_all(zback, 'pz', split_axis=1, conca...  8.83 us
    dot_general x2, matrix products, shards(): jnp.einsum('yzi,ij->yzj', residual, xaxis_vectors, precision=HIGH)  7.93 us
  transfers between devices with their start and end apart: 9, of which 7 were waited for; matrix products, arithmetic and copies ran while one was open for 2% of the time, Pallas kernels for 0%

commit v1 on v0

v1 whole, which is shorter than its diff:
```python
import jax
import jax.numpy as jnp
import numpy as np
from jax import lax
from jax.experimental import pallas as pl
from jax.experimental.pallas import tpu as pltpu
from jax.sharding import PartitionSpec as P

ITERS = 2
REACH = 3
HIGH = lax.Precision.HIGHEST
BOTH = ("py", "pz")
F32 = jnp.float32
BF16 = jnp.bfloat16
VMEM = pl.BlockSpec(memory_space=pltpu.VMEM)
SMEM = pl.BlockSpec(memory_space=pltpu.SMEM)


def up8(count):
    return -(-count // 8) * 8


def split(value):
    high = value.astype(BF16)
    return high, (value - high.astype(F32)).astype(BF16)


def mul(left, right):
    return lax.dot_general(left, right, (((1,), (0,)), ((), ())), preferred_element_type=F32)


def mul_t(left, right):
    return lax.dot_general(left, right, (((1,), (1,)), ((), ())), preferred_element_type=F32)


def call(kernel, outs, specs, flops, cost_bytes, scratch=()):
    return pl.pallas_call(
        kernel,
        out_shape=[jax.ShapeDtypeStruct(shape, dtype) for shape, dtype in outs],
        in_specs=specs,
        out_specs=[VMEM] * len(outs),
        scratch_shapes=list(scratch),
        compiler_params=pltpu.CompilerParams(vmem_limit_bytes=32 * 1024 * 1024),
        cost_estimate=pl.CostEstimate(flops=flops, bytes_accessed=cost_bytes, transcendentals=0),
    )


def store_z_rims(ly, lz, weighted, low_ref, high_ref):
    for y in range(ly):
        low_ref[y * REACH : (y + 1) * REACH, :] = weighted[y * lz : y * lz + REACH, :]
        high_ref[y * REACH : (y + 1) * REACH, :] = weighted[(y + 1) * lz - REACH : (y + 1) * lz, :]


def coefficient_kernel(ly, lz, table_ref, span_ref, field_ref, coef_ref, weighted_ref, low_ref, high_ref):
    span = span_ref[...]
    coef = jnp.full(span.shape, table_ref[0], F32)
    for entry in range(1, table_ref.shape[0]):
        coef = jnp.where(span == entry, table_ref[entry], coef)
    coef_ref[...] = coef
    weighted = coef * field_ref[...]
    weighted_ref[...] = weighted
    store_z_rims(ly, lz, weighted, low_ref, high_ref)


def y_rims_kernel(ly, lz, weighted_ref, zlow_ref, zhigh_ref, low_ref, high_ref):
    own, side = REACH * lz, REACH * REACH
    for ref, start, zstart in ((low_ref, 0, 0), (high_ref, (ly - REACH) * lz, (ly - REACH) * REACH)):
        ref[own:, :] = jnp.zeros((ref.shape[0] - own, ref.shape[1]), F32)
        ref[0:own, :] = weighted_ref[start : start + own, :]
        ref[own : own + side, :] = zlow_ref[zstart : zstart + side, :]
        ref[own + side : own + 2 * side, :] = zhigh_ref[zstart : zstart + side, :]


def point_columns(ly, lz):
    own = [(y, z) for y in range(ly) for z in range(lz)]
    below, above = range(-REACH, 0), range(REACH)
    zlow = [(y, z) for y in range(ly) for z in below]
    zhigh = [(y, lz + z) for y in range(ly) for z in above]
    sides = []
    for ys in (below, [ly + y for y in above]):
        rim = [(y, z) for y in ys for z in range(lz)]
        rim += [(y, z) for y in ys for z in below]
        rim += [(y, lz + z) for y in ys for z in above]
        sides += rim + [(1 << 20, 1 << 20)] * (up8(len(rim)) - len(rim))
    points = own + zlow + zhigh + sides
    points += [(1 << 20, 1 << 20)] * (-len(points) % 128)
    return np.array(points, np.int32).T.copy()


def stencil_kernel(ly, lz, ny, nz, place_ref, points_ref, ybands_ref, zbands_ref, high_ref, low_ref):
    count = ly * lz
    rows = lax.broadcasted_iota(jnp.int32, (count, 1), 0)
    yrow, zrow = lax.div(rows, lz), lax.rem(rows, lz)
    factors = []
    for bands_ref, length, row, column, first, whole in (
        (ybands_ref, ly, yrow, points_ref[0:1, :], place_ref[0] * ly, ny),
        (zbands_ref, lz, zrow, points_ref[1:2, :], place_ref[1] * lz, nz),
    ):
        pick = (lax.broadcasted_iota(jnp.int32, (count, length), 1) == row).astype(F32)
        spot = column + first
        inside = (spot >= 0) & (spot < whole)
        distance = jnp.where(inside, column, 1 << 20) - row
        for matrix in range(2):
            taps = lax.dot_general(
                pick, bands_ref[matrix], (((1,), (1,)), ((), ())), precision=HIGH, preferred_element_type=F32
            )
            dense = jnp.zeros(distance.shape, F32)
            for offset in range(2 * REACH + 1):
                dense = jnp.where(distance == offset - REACH, taps[:, offset : offset + 1], dense)
            factors.append(dense)
    ystiff, ymass, zstiff, zmass = factors
    for part, value in enumerate((ymass * zmass, ystiff * zmass + ymass * zstiff)):
        high, low = split(value)
        high_ref[part * count : (part + 1) * count, :] = high
        low_ref[part * count : (part + 1) * count, :] = low


def xvectors_kernel(vectors_ref, high_ref, low_ref):
    high, low = split(vectors_ref[...].T)
    high_ref[...] = high
    low_ref[...] = low


def yz_vectors_kernel(
    npy, npz, ly, lz, yvec_ref, yvec_t_ref, zvec_ref, zhigh_ref, zlow_ref, ydown_ref, yup_ref
):
    ny, nz = npy * ly, npz * lz
    twice = (lax.broadcasted_iota(jnp.int32, (nz, 2 * nz), 0)
             == lax.rem(lax.broadcasted_iota(jnp.int32, (nz, 2 * nz), 1), nz)).astype(F32)
    pair = lax.dot_general(zvec_ref[...], twice, (((1,), (0,)), ((), ())), precision=HIGH, preferred_element_type=F32)
    half = lax.broadcasted_iota(jnp.int32, pair.shape, 1) >= nz
    zhigh_ref[...] = jnp.zeros(zhigh_ref.shape, BF16)
    zlow_ref[...] = jnp.zeros(zlow_ref.shape, BF16)
    for parity in range(2):
        high, low = split(jnp.where(half == (parity == 1), pair, 0.0))
        for yl in range(parity, ly, 2):
            for block in range(npz):
                to = (pl.ds((block * ly + yl) * lz, lz), pl.ds(yl // 2 * 2 * nz, 2 * nz))
                zhigh_ref[to] = high[block * lz : (block + 1) * lz, :]
                zlow_ref[to] = low[block * lz : (block + 1) * lz, :]
    def y_of(p):
        spot = lax.div(p, npy)
        return lax.rem(p, npy) * ly + 2 * lax.rem(spot, ly // 2) + lax.div(spot, ly // 2)

    def four(array):
        high, low = split(array)
        late = lax.broadcasted_iota(jnp.int32, array.shape, 1) >= 2 * ny
        return jnp.where(late, low.astype(F32), high.astype(F32)).astype(BF16)

    lane = lax.broadcasted_iota(jnp.int32, (ny, 4 * ny), 1)
    row = lax.broadcasted_iota(jnp.int32, (ny, 4 * ny), 0)
    moved = (row == y_of(lax.rem(lane, ny))).astype(F32)
    down = lax.dot_general(yvec_t_ref[...], moved, (((1,), (0,)), ((), ())), precision=HIGH, preferred_element_type=F32)
    ydown_ref[...] = four(down)
    order = (lax.broadcasted_iota(jnp.int32, (ny, ny), 1)
             == y_of(lax.broadcasted_iota(jnp.int32, (ny, ny), 0))).astype(F32)
    sorted_rows = lax.dot_general(order, yvec_ref[...], (((1,), (0,)), ((), ())), precision=HIGH, preferred_element_type=F32)
    copies = (row == lax.rem(lane, ny)).astype(F32)
    up = lax.dot_general(sorted_rows, copies, (((1,), (0,)), ((), ())), precision=HIGH, preferred_element_type=F32)
    yup_ref[...] = four(up)


def residual_kernel(
    weighted_ref, zlow_ref, zhigh_ref, ylow_ref, yhigh_ref, high_ref, low_ref, coef_ref, right_ref, xbands_ref,
    vhigh_ref, vlow_ref, residual_ref, spectral_ref,
):
    count, nx = weighted_ref.shape
    pieces = [ref[...] for ref in (weighted_ref, zlow_ref, zhigh_ref, ylow_ref, yhigh_ref)]
    missing = high_ref.shape[1] - sum(piece.shape[0] for piece in pieces)
    if missing:
        pieces.append(jnp.zeros((missing, nx), F32))
    point_high, point_low = split(jnp.concatenate(pieces, axis=0))
    stencil = high_ref[...]
    both = mul(stencil, point_high) + mul(stencil, point_low) + mul(low_ref[...], point_high)
    mass, stiff = both[:count], both[count:]
    spot = lax.broadcasted_iota(jnp.int32, (1, nx), 1)
    applied = None
    for offset in range(2 * REACH + 1):
        move = offset - REACH
        inside = (spot - move >= 0) & (spot - move < nx)
        taps = []
        for matrix in range(2):
            band = xbands_ref[matrix, offset : offset + 1, :]
            band = pltpu.roll(band, move % nx, 1) if move else band
            taps.append(jnp.where(inside, band, 0.0))
        term = taps[0] * mass + taps[1] * stiff
        term = pltpu.roll(term, -move % nx, 1) if move else term
        applied = term if applied is None else applied + term
    residual = right_ref[...] - coef_ref[...] * applied
    residual_ref[...] = residual
    high, low = split(residual)
    vhigh = vhigh_ref[...]
    spectral_ref[...] = mul_t(vhigh, high) + mul_t(vhigh, low) + mul_t(vlow_ref[...], high)


def modes_kernel(
    npy, npz, part_ref, xvalues_ref, yvalues_ref, zvalues_ref, zhigh_ref, zlow_ref, ydown_ref, yup_ref, in_ref, out_ref
):
    count = in_ref.shape[0] // (npy * npz)
    lanes = in_ref.shape[1]
    nz = zvalues_ref.shape[1] // 2
    ny = yvalues_ref.shape[1]
    chunks = zhigh_ref.shape[1] // (2 * nz)
    rows = [
        jnp.concatenate([in_ref[pl.ds(b * count + j, npy, stride=npz * count), :] for b in range(npz)], axis=1)
        for j in range(count)
    ]
    high, low = split(jnp.concatenate(rows, axis=0))
    zhigh, zlow = zhigh_ref[...], zlow_ref[...]
    part = mul(high, zhigh) + mul(low, zhigh) + mul(high, zlow)
    late = lax.broadcasted_iota(jnp.int32, (npy, 2 * nz), 1) >= nz

    def swap(value):
        return pltpu.roll(value, nz, 1)

    def tile(array, j, c):
        return array[j * npy : (j + 1) * npy, c * 2 * nz : (c + 1) * 2 * nz]

    pairs = []
    for j in range(0, count, 2):
        first = [tile(part, j, c) for c in range(chunks)]
        second = [tile(part, j + 1, c) for c in range(chunks)]
        even = [jnp.where(late, swap(second[c]), first[c]) for c in range(chunks)]
        odd = [jnp.where(late, second[c], swap(first[c])) for c in range(chunks)]
        pairs.append(jnp.concatenate(even + odd, axis=0))
    stacked = jnp.concatenate(pairs, axis=1)

    def four(value):
        high, low = split(value)
        return jnp.concatenate([high, low, high, low], axis=0)

    modes = mul(ydown_ref[...], four(stacked))
    diagonal = lax.broadcasted_iota(jnp.int32, (ny, ny), 0) == lax.broadcasted_iota(jnp.int32, (ny, ny), 1)
    ycolumn = jnp.sum(jnp.where(diagonal, yvalues_ref[...], 0.0), axis=1, keepdims=True)
    yz = ycolumn + zvalues_ref[...]
    lane = lax.broadcasted_iota(jnp.int32, (1, 2 * nz), 1)
    first_mode = part_ref[0] * count
    parts = []
    for pair in range(count // 2):
        x = jnp.where(lane >= nz, xvalues_ref[first_mode + 2 * pair + 1], xvalues_ref[first_mode + 2 * pair])
        parts.append(modes[:, pair * 2 * nz : (pair + 1) * 2 * nz] / (yz + x))
    restored = mul(yup_ref[...], four(jnp.concatenate(parts, axis=1)))
    half = npy * chunks
    rows = []
    for pair in range(count // 2):
        block = restored[:, pair * 2 * nz : (pair + 1) * 2 * nz]
        even = [block[c * npy : (c + 1) * npy] for c in range(chunks)]
        odd = [block[half + c * npy : half + (c + 1) * npy] for c in range(chunks)]
        rows.append(jnp.concatenate([jnp.where(late, swap(odd[c]), even[c]) for c in range(chunks)], axis=1))
        rows.append(jnp.concatenate([jnp.where(late, odd[c], swap(even[c])) for c in range(chunks)], axis=1))
    high, low = split(jnp.concatenate(rows, axis=0))
    back = mul_t(high, zhigh) + mul_t(low, zhigh) + mul_t(high, zlow)
    for j in range(count):
        for b in range(npz):
            out_ref[pl.ds(b * count + j, npy, stride=npz * count), :] = back[
                j * npy : (j + 1) * npy, b * lanes : (b + 1) * lanes
            ]


def from_modes(spectral_ref, vhigh_ref, vlow_ref):
    high, low = split(spectral_ref[...].T)
    vhigh = vhigh_ref[...]
    return mul(high, vhigh) + mul(low, vhigh) + mul(high, vlow_ref[...])


def update_kernel(
    ly, lz, spectral_ref, vhigh_ref, vlow_ref, field_ref, coef_ref, updated_ref, weighted_ref, low_ref, high_ref
):
    updated = field_ref[...] + from_modes(spectral_ref, vhigh_ref, vlow_ref)
    updated_ref[...] = updated
    weighted = coef_ref[...] * updated
    weighted_ref[...] = weighted
    store_z_rims(ly, lz, weighted, low_ref, high_ref)


def last_update_kernel(spectral_ref, vhigh_ref, vlow_ref, field_ref, updated_ref):
    updated_ref[...] = field_ref[...] + from_modes(spectral_ref, vhigh_ref, vlow_ref)


def around(value, axis, step):
    count = lax.axis_size(axis)
    return lax.ppermute(value, axis, [(i, (i + step) % count) for i in range(count)])


def plain_modes(received, npy, npz, ly, lz, xvalues, yvalues, zvalues, yvectors, zvectors):
    count = received.shape[0] // (npy * npz)
    field = received.reshape(npy, npz, count, ly, lz).transpose(2, 0, 3, 1, 4).reshape(count, npy * ly, npz * lz)
    field = jnp.einsum("xyz,yj->xjz", field, yvectors, precision=HIGH)
    field = jnp.einsum("xyz,zk->xyk", field, zvectors, precision=HIGH)
    field = field / (yvalues[None, :, None] + zvalues[None, None, :] + xvalues[:, None, None])
    field = jnp.einsum("xjz,yj->xyz", field, yvectors, precision=HIGH)
    field = jnp.einsum("xyk,zk->xyz", field, zvectors, precision=HIGH)
    field = field.reshape(count, npy, ly, npz, lz).transpose(1, 3, 0, 2, 4)
    return field.reshape(npy * npz * count, ly * lz)


def shards(
    solution,
    right_side,
    span_index,
    coef_table,
    xaxis_bands,
    yaxis_bands,
    zaxis_bands,
    xaxis_vectors,
    yaxis_vectors,
    zaxis_vectors,
    xaxis_values,
    yaxis_values,
    zaxis_values,
):
    npy, npz = lax.axis_size("py"), lax.axis_size("pz")
    ly, lz, nx = solution.shape
    ny, nz = npy * ly, npz * lz
    count, devices = ly * lz, npy * npz
    modes = nx // devices
    place = jnp.stack([lax.axis_index("py"), lax.axis_index("pz")])
    part = lax.axis_index(BOTH)
    field = solution.reshape(count, nx)
    right = right_side.reshape(count, nx)
    block, zrim, yrim = (count, nx), (ly * REACH, nx), (up8(REACH * lz + 2 * REACH * REACH), nx)
    cell = count * nx * 4

    coef, weighted, zlow, zhigh = call(
        lambda *refs: coefficient_kernel(ly, lz, *refs),
        [(block, F32), (block, F32), (zrim, F32), (zrim, F32)],
        [SMEM, VMEM, VMEM], count * nx * 16, 4 * cell,
    )(coef_table, span_index.reshape(count, nx), field)

    points = point_columns(ly, lz)
    width = points.shape[1]
    shigh, slow = call(
        lambda *refs: stencil_kernel(ly, lz, ny, nz, *refs),
        [((2 * count, width), BF16)] * 2,
        [SMEM, VMEM, VMEM, VMEM], count * width * 60, 8 * count * width,
    )(place, jnp.asarray(points), yaxis_bands, zaxis_bands)
    vhigh, vlow = call(
        xvectors_kernel, [((nx, nx), BF16)] * 2, [VMEM], nx * nx * 40, 8 * nx * nx
    )(xaxis_vectors)

    fast = modes % 2 == 0 and npy % 8 == 0 and lz % 16 == 0 and ly % 2 == 0 and nz == 64 and ny % 8 == 0 and 4 * ny <= 256 and count == 128
    if fast:
        zmat, ymat = (npz * count, ly * nz), (ny, 4 * ny)
        tables = call(
            lambda *refs: yz_vectors_kernel(npy, npz, ly, lz, *refs),
            [(zmat, BF16), (zmat, BF16), (ymat, BF16), (ymat, BF16)],
            [VMEM] * 3, npz * count * ly * nz * 8, npz * count * ly * nz * 4,
        )(yaxis_vectors, yaxis_vectors.T, zaxis_vectors)
        yrow = yaxis_values.reshape(1, ny)
        zrow = jnp.concatenate([zaxis_values, zaxis_values]).reshape(1, 2 * nz)

        def precondition(received):
            return call(
                lambda *refs: modes_kernel(npy, npz, *refs),
                [((nx, count), F32)],
                [SMEM, SMEM] + [VMEM] * 7, 6 * 2 * count * nx * ly * nz, 2 * cell,
            )(part.reshape(1), xaxis_values, yrow, zrow, *tables, received)[0]
    else:
        xpart = lax.dynamic_slice_in_dim(xaxis_values, part * modes, modes)

        def precondition(received):
            return plain_modes(
                received, npy, npz, ly, lz, xpart, yaxis_values, zaxis_values, yaxis_vectors, zaxis_vectors
            )

    for iteration in range(ITERS):
        from_low, from_high = around(zhigh, "pz", 1), around(zlow, "pz", -1)
        ylow, yhigh = call(
            lambda *refs: y_rims_kernel(ly, lz, *refs),
            [(yrim, F32)] * 2, [VMEM] * 3, nx, 4 * nx * 4 * yrim[0],
        )(weighted, from_low, from_high)
        below, above = around(yhigh, "py", 1), around(ylow, "py", -1)
        residual, spectral = call(
            residual_kernel,
            [(block, F32), ((nx, count), F32)],
            [VMEM] * 12, 6 * count * nx * (nx + 2 * width), 5 * cell + 4 * nx * nx,
        )(weighted, from_low, from_high, below, above, shigh, slow, coef, right, xaxis_bands, vhigh, vlow)
        spectral = lax.all_to_all(spectral, BOTH, split_axis=0, concat_axis=0, tiled=True)
        spectral = precondition(spectral)
        spectral = lax.all_to_all(spectral, BOTH, split_axis=0, concat_axis=0, tiled=True)
        cost = (6 * count * nx * nx, 4 * cell + 4 * nx * nx)
        if iteration + 1 < ITERS:
            field, weighted, zlow, zhigh = call(
                lambda *refs: update_kernel(ly, lz, *refs),
                [(block, F32), (block, F32), (zrim, F32), (zrim, F32)], [VMEM] * 5, *cost,
            )(spectral, vhigh, vlow, field, coef)
        else:
            field = call(last_update_kernel, [(block, F32)], [VMEM] * 4, *cost)(spectral, vhigh, vlow, field)[0]
    return (field.reshape(solution.shape), residual.reshape(solution.shape))


def solution(mesh):
    return jax.shard_map(
        shards,
        mesh=mesh,
        in_specs=(
            P("py", "pz", None),
            P("py", "pz", None),
            P("py", "pz", None),
            P(),
            P(),
            P(None, None, "py"),
            P(None, None, "pz"),
            P(),
            P(),
            P(),
            P(),
            P(),
            P(),
        ),
        out_specs=(P("py", "pz", None), P("py", "pz", None)),
        check_vma=False,
    )
```

time: 181 us -> 98.7 us (0.55)
  blocking collectives: 78.1 us -> 40 us
  matrix products: 20.8 us -> 0 us
  other arithmetic: 19.4 us -> 0.15 us
  Pallas kernels: 0 us -> 13.3 us
  local copies, waits for them, and re-layouts: 19.1 us -> 6.67 us
  waiting for transfers between devices: 20.7 us -> 17.8 us
    all_to_all x7 -> x3, blocking collectives: 78.1 us -> 40 us  [shards(): lax.all_to_all(spectral, BOTH, split_axis=0, concat_axis=0, tiled=True)]
    dot_general x12 -> x0, matrix products: 20.8 us -> none  [the longest x2 8.83 us: shards(): jnp.einsum('ykj,ij->yki', lax.all_to_all(zback, 'pz', split_axis=1, conca...]
    pallas_call x0 -> x12, Pallas kernels: none -> 13.3 us  [the longest x2 4.42 us: precondition(): call(lambda *refs: modes_kernel(npy, npz, *refs), [((nx, count), F32)], [...]
    ppermute x8, waiting for transfers between devices: 16 us -> 9.16 us  [around(): lax.ppermute(value, axis, [(i, (i + step) % count) for i in range(count)])]
    mul x1 -> x0, other arithmetic: 6.18 us -> none  [shards(): weighted = coefficient * updated]
    sub x1 -> x0, other arithmetic: 5.89 us -> none  [shards(): residual = right_side - coefficient * applied]
    all_to_all x1, waiting for transfers between devices: 4.72 us -> 8.69 us  [shards(): lax.all_to_all(spectral, BOTH, split_axis=0, concat_axis=0, tiled=True)]
    add x9 -> x0, other arithmetic: 3.52 us -> none  [the longest x6 2.05 us: band_padded(): summed = contrib if summed is None else summed + contrib]
  transfers between devices with their start and end apart: 9 -> 9, of which waited for: 7 -> 5; matrix products, arithmetic and copies ran while one was open for 2% -> 0% of each run, Pallas kernels for 0% -> 2%
where the time goes in v1:
time: 98.7 us; the launch traced here: 98.1 us
  blocking collectives  40 us (41%)
  starting transfers between devices  19.3 us (20%)
  waiting for transfers between devices  17.8 us (18%)
  Pallas kernels  13.3 us (13%)
  local copies, waits for them, and re-layouts  6.67 us (7%)
    all_to_all x3, blocking collectives, shards(): lax.all_to_all(spectral, BOTH, split_axis=0, concat_axis=0, tiled=True)  40 us
    ppermute x8, starting transfers between devices, around(): lax.ppermute(value, axis, [(i, (i + step) % count) for i in range(count)])  14.5 us
    ppermute x8, waiting for transfers between devices, around(): lax.ppermute(value, axis, [(i, (i + step) % count) for i in range(count)])  9.16 us
    all_to_all x1, waiting for transfers between devices, shards(): lax.all_to_all(spectral, BOTH, split_axis=0, concat_axis=0, tiled=True)  8.69 us
    unnamed x34, local copies, waits for them, and re-layouts  6.67 us
    all_to_all x1, starting transfers between devices, shards(): lax.all_to_all(spectral, BOTH, split_axis=0, concat_axis=0, tiled=True)  4.86 us
    pallas_call x2, Pallas kernels, precondition(): call(lambda *refs: modes_kernel(npy, npz, *refs), [((nx, count), F32)], [...  4.42 us
    pallas_call x2, Pallas kernels, shards(): call(residual_kernel, [(block, F32), ((nx, count), F32)], [VMEM] * 12, 6...  4.18 us
  transfers between devices with their start and end apart: 9, of which 5 were waited for; matrix products, arithmetic and copies ran while one was open for 0% of the time, Pallas kernels for 2%

profile of v1, /device:TPU:0, one launch (start us, length us, event | category | flops | bytes accessed | tf_op | source)
XLA Modules:
  0.0 98.1 jit_solution(4050412051713587425)
XLA Ops:
  0.6 0.6 copy-done.10
  1.3 0.9 copy-done
  2.2 0.9 copy-done.4
  3.2 0.7 shard_map.150
  3.9 3.1 %collective-permute-start = (f32[24,512]{1,0:T(8,128)S(1)}, f32[24,512]{1,0:T(8,128)S(1)}, u32[]{:S(2)}, u32[]{:S(2)}) collective-permute-start(f32[24,512]{1,0:T(8,128)S(1)} %get-tuple-element.30), channel_id=1, source_target_pairs={{0,1},{1,2},{2,3},{3,0},{4,5},{5,6},{6,7},{7,4},{8,9},{9,10},{10,1... | collective-permute-start | bytes 147464 | tf_op jit(solution)/shard_map/ppermute | solution.py:282
  7.0 2.1 %collective-permute-start.1 = (f32[24,512]{1,0:T(8,128)S(1)}, f32[24,512]{1,0:T(8,128)S(1)}, u32[]{:S(2)}, u32[]{:S(2)}) collective-permute-start(f32[24,512]{1,0:T(8,128)S(1)} %get-tuple-element.31), channel_id=1, source_target_pairs={{0,3},{1,0},{2,1},{3,2},{4,7},{5,4},{6,5},{7,6},{8,11},{9,8},{10,9... | collective-permute-start | bytes 147464 | tf_op jit(solution)/shard_map/ppermute | solution.py:282
  9.1 2.1 %collective-permute-done.refs_1_.zlow_ref = f32[24,512]{1,0:T(8,128)S(1)} collective-permute-done((f32[24,512]{1,0:T(8,128)S(1)}, f32[24,512]{1,0:T(8,128)S(1)}, u32[]{:S(2)}, u32[]{:S(2)}) %collective-permute-start) | collective-permute-done | bytes 49184 | tf_op jit(solution)/shard_map/ppermute | solution.py:282
  11.2 0.4 collective-permute-done.1.refs_2_.zhigh_ref
  11.7 2.6 %collective-permute-start.3 = (f32[72,512]{1,0:T(8,128)S(1)}, f32[72,512]{1,0:T(8,128)S(1)}, u32[]{:S(2)}, u32[]{:S(2)}) collective-permute-start(f32[72,512]{1,0:T(8,128)S(1)} %get-tuple-element.33), channel_id=1, source_target_pairs={{0,28},{4,0},{8,4},{12,8},{16,12},{20,16},{24,20},{28,24},{1,29},{... | collective-permute-start | bytes 442376 | tf_op jit(solution)/shard_map/ppermute | solution.py:282
  14.5 0.6 copy-done.8
  15.1 1.7 %shard_map.152 = (bf16[256,384]{1,0:T(8,128)(2,1)S(1)}, bf16[256,384]{1,0:T(8,128)(2,1)S(1)}) custom-call(s32[2]{0:T(128)S(1)} %pad_add_fusion.refs_0_, s32[2,384]{1,0:T(2,128)S(1)} %copy-done.8, f32[2,7,8]{2,1,0:T(8,128)S(1)} %copy.17.refs_2_, f32[2,7,16]{2,1,0:T(8,128)S(1)} %copy.18.refs_3_), custom_call_target="tpu_custom_call" | custom-call | flops 2949120 | bytes 393216 | tf_op jit(solution)/shard_map/pallas_call | solution.py:332
  16.7 1.2 %copy-done.2 = f32[512,512]{1,0:T(8,128)S(1)} copy-done((f32[512,512]{1,0:T(8,128)S(1)}, f32[512,512]{1,0:T(8,128)}, u32[]{:S(2)}) %copy-start.2) | copy-done | bytes 1048600
  18.3 0.6 copy-done.3
  18.9 2.4 %shard_map.154 = (f32[128,512]{1,0:T(8,128)}, f32[512,128]{1,0:T(8,128)}) custom-call(f32[128,512]{1,0:T(8,128)S(1)} %get-tuple-element.29.refs_0_.weighted_ref, f32[24,512]{1,0:T(8,128)S(1)} %collective-permute-done.refs_1_.zlow_ref, f32[24,512]{1,0:T(8,128)S(1)} %collective-permute-done.1.refs_2_.zhigh_ref, f32[72,512]{1,0:T(8,128)S(1)} %collective-permute-done.2.ylow_ref, ...), custom_call_target="tpu_custom_call" | custom-call | flops 503316480 | bytes 2359296 | tf_op jit(solution)/shard_map/pallas_call | solution.py:373
  21.3 4.9 %all-to-all-start = ((f32[32,16,128]{2,1,0:T(8,128)}), f32[32,16,128]{2,1,0:T(8,128)S(1)}, u32[]{:S(2)}, u32[]{:S(2)}) async-start(f32[32,16,128]{2,1,0:T(8,128)} %bitcast.9), calls=%async_computation | async-start | bytes 524288 | tf_op jit(solution)/shard_map/all_to_all | solution.py:378
  26.2 0.7 copy-done.6
  26.9 0.4 shard_map.149
  27.6 8.7 %all-to-all-done = f32[32,16,128]{2,1,0:T(8,128)S(1)} async-done(((f32[32,16,128]{2,1,0:T(8,128)}), f32[32,16,128]{2,1,0:T(8,128)S(1)}, u32[]{:S(2)}, u32[]{:S(2)}) %all-to-all-start) | async-done | bytes 262176 | tf_op jit(solution)/shard_map/all_to_all | solution.py:378
  36.3 0.7 copy-done.7
  37.0 2.2 %shard_map.155 = f32[512,128]{1,0:T(8,128)S(1)} custom-call(s32[1]{0:T(128)} %bitcast.refs_0_, f32[512]{0:T(512)S(1)} %copy-done.7, f32[1,64]{1,0:T(1,128)S(1)} %bitcast.33, f32[1,128]{1,0:T(1,128)S(1)} %maximum_bitcast_fusion.refs_3_, bf16[512,512]{1,0:T(8,128)(2,1)S(1)} %get-tuple-element.25.refs_4_, bf16[512,512]{1,0:T(8,128)(2,1)S(1)} %get-tuple-element.26.refs_5_, ...), custom_call_target="tpu_custom_call" | custom-call | flops 402653184 | bytes 524288 | tf_op jit(solution)/shard_map/pallas_call | solution.py:353
  39.2 12.7 %all_to_all.44 = f32[32,16,128]{2,1,0:T(8,128)S(1)} all-to-all(f32[32,16,128]{2,1,0:T(8,128)S(1)} %bitcast.27), channel_id=1, replica_groups=mesh['py'=8,'pz'=4] {'py','pz'}, dimensions={0} | all-to-all | bytes 524288 | tf_op jit(solution)/shard_map/all_to_all | solution.py:380
  52.0 0.4 shard_map.156
  52.4 1.1 %collective-permute-start.4 = (f32[24,512]{1,0:T(8,128)S(1)}, f32[24,512]{1,0:T(8,128)S(1)}, u32[]{:S(2)}, u32[]{:S(2)}) collective-permute-start(f32[24,512]{1,0:T(8,128)S(1)} %get-tuple-element.41), channel_id=1, source_target_pairs={{0,1},{1,2},{2,3},{3,0},{4,5},{5,6},{6,7},{7,4},{8,9},{9,10},{10,1... | collective-permute-start | bytes 147464 | tf_op jit(solution)/shard_map/ppermute | solution.py:282
  53.6 2.8 %collective-permute-start.5 = (f32[24,512]{1,0:T(8,128)S(1)}, f32[24,512]{1,0:T(8,128)S(1)}, u32[]{:S(2)}, u32[]{:S(2)}) collective-permute-start(f32[24,512]{1,0:T(8,128)S(1)} %get-tuple-element.42), channel_id=1, source_target_pairs={{0,3},{1,0},{2,1},{3,2},{4,7},{5,4},{6,5},{7,6},{8,11},{9,8},{10,9... | collective-permute-start | bytes 147464 | tf_op jit(solution)/shard_map/ppermute | solution.py:282
  56.3 2.5 %collective-permute-done.4.refs_1_.zlow_ref = f32[24,512]{1,0:T(8,128)S(1)} collective-permute-done((f32[24,512]{1,0:T(8,128)S(1)}, f32[24,512]{1,0:T(8,128)S(1)}, u32[]{:S(2)}, u32[]{:S(2)}) %collective-permute-start.4) | collective-permute-done | bytes 49184 | tf_op jit(solution)/shard_map/ppermute | solution.py:282
  58.9 2.6 %collective-permute-start.7 = (f32[72,512]{1,0:T(8,128)S(1)}, f32[72,512]{1,0:T(8,128)S(1)}, u32[]{:S(2)}, u32[]{:S(2)}) collective-permute-start(f32[72,512]{1,0:T(8,128)S(1)} %get-tuple-element.44), channel_id=1, source_target_pairs={{0,28},{4,0},{8,4},{12,8},{16,12},{20,16},{24,20},{28,24},{1,29},{... | collective-permute-start | bytes 442376 | tf_op jit(solution)/shard_map/ppermute | solution.py:282
  61.6 4.1 %collective-permute-done.6.ylow_ref = f32[72,512]{1,0:T(8,128)S(1)} collective-permute-done((f32[72,512]{1,0:T(8,128)S(1)}, f32[72,512]{1,0:T(8,128)S(1)}, u32[]{:S(2)}, u32[]{:S(2)}) %collective-permute-start.6) | collective-permute-done | bytes 147488 | tf_op jit(solution)/shard_map/ppermute | solution.py:282
  65.7 1.8 %shard_map.158 = (f32[128,512]{1,0:T(8,128)}, f32[512,128]{1,0:T(8,128)S(1)}) custom-call(f32[128,512]{1,0:T(8,128)S(1)} %get-tuple-element.40.refs_0_.weighted_ref, f32[24,512]{1,0:T(8,128)S(1)} %collective-permute-done.4.refs_1_.zlow_ref, f32[24,512]{1,0:T(8,128)S(1)} %collective-permute-done.5.refs_2_.zhigh_ref, ...), custom_call_target="tpu_custom_call" | custom-call | flops 503316480 | bytes 2359296 | tf_op jit(solution)/shard_map/pallas_call | solution.py:373
  67.5 14.5 %all_to_all.45 = f32[32,16,128]{2,1,0:T(8,128)S(1)} all-to-all(f32[32,16,128]{2,1,0:T(8,128)S(1)} %bitcast.31), channel_id=1, replica_groups=mesh['py'=8,'pz'=4] {'py','pz'}, dimensions={0} | all-to-all | bytes 524288 | tf_op jit(solution)/shard_map/all_to_all | solution.py:378
  82.0 2.2 %shard_map.159 = f32[512,128]{1,0:T(8,128)S(1)} custom-call(s32[1]{0:T(128)} %bitcast.refs_0_, f32[512]{0:T(512)S(1)} %copy-done.7, f32[1,64]{1,0:T(1,128)S(1)} %bitcast.34, f32[1,128]{1,0:T(1,128)S(1)} %maximum_bitcast_fusion.refs_3_, bf16[512,512]{1,0:T(8,128)(2,1)S(1)} %get-tuple-element.25.refs_4_, bf16[512,512]{1,0:T(8,128)(2,1)S(1)} %get-tuple-element.26.refs_5_, ...), custom_call_target="tpu_custom_call" | custom-call | flops 402653184 | bytes 524288 | tf_op jit(solution)/shard_map/pallas_call | solution.py:353
  84.2 12.7 %all_to_all.46 = f32[32,16,128]{2,1,0:T(8,128)S(1)} all-to-all(f32[32,16,128]{2,1,0:T(8,128)S(1)} %bitcast.26), channel_id=1, replica_groups=mesh['py'=8,'pz'=4] {'py','pz'}, dimensions={0} | all-to-all | bytes 524288 | tf_op jit(solution)/shard_map/all_to_all | solution.py:380
  97.0 1.1 %shard_map.160 = f32[128,512]{1,0:T(8,128)} custom-call(f32[512,128]{1,0:T(8,128)S(1)} %bitcast.23, bf16[512,512]{1,0:T(8,128)(2,1)S(1)} %get-tuple-element.37.vhigh_ref.refs_1_, bf16[512,512]{1,0:T(8,128)(2,1)S(1)} %get-tuple-element.38.vlow_ref.refs_2_, f32[128,512]{1,0:T(8,128)S(1)} %get-tuple-element.46.field_ref), custom_call_target="tpu_custom_call" | custom-call | flops 201326592 | bytes 2097152 | tf_op jit(solution)/shard_map/pallas_call | solution.py:388
  (37 shorter events, 1.0 us)
Async XLA Ops:
  0.6 0.7 copy-start.10
  1.3 0.9 copy-start
  2.2 0.9 copy-start.4
  3.9 7.3 %collective-permute-start = (f32[24,512]{1,0:T(8,128)S(1)}, f32[24,512]{1,0:T(8,128)S(1)}, u32[]{:S(2)}, u32[]{:S(2)}) collective-permute-start(f32[24,512]{1,0:T(8,128)S(1)} %get-tuple-element.30), channel_id=1, source_target_pairs={{0,1},{1,2},{2,3},{3,0},{4,5},{5,6},{6,7},{7,4},{8,9},{9,10},{10,1... | collective-permute-start | bytes 147464 | tf_op jit(solution)/shard_map/ppermute | solution.py:282
  7.0 4.6 %collective-permute-start.1 = (f32[24,512]{1,0:T(8,128)S(1)}, f32[24,512]{1,0:T(8,128)S(1)}, u32[]{:S(2)}, u32[]{:S(2)}) collective-permute-start(f32[24,512]{1,0:T(8,128)S(1)} %get-tuple-element.31), channel_id=1, source_target_pairs={{0,3},{1,0},{2,1},{3,2},{4,7},{5,4},{6,5},{7,6},{8,11},{9,8},{10,9... | collective-permute-start | bytes 147464 | tf_op jit(solution)/shard_map/ppermute | solution.py:282
  11.6 2.7 %copy-start.12 = (f32[2,7,8]{2,0,1:T(2,128)S(1)}, f32[2,7,8]{2,0,1:T(2,128)}, u32[]{:S(2)}) copy-start(f32[2,7,8]{2,0,1:T(2,128)} %param.19) | copy-start | bytes 1348
  11.6 2.7 %copy-start.13 = (f32[2,7,16]{2,0,1:T(2,128)S(1)}, f32[2,7,16]{2,0,1:T(2,128)}, u32[]{:S(2)}) copy-start(f32[2,7,16]{2,0,1:T(2,128)} %param.20) | copy-start | bytes 2692
  11.6 2.7 %copy-start.11 = (f32[2,7,512]{2,0,1:T(2,128)S(1)}, f32[2,7,512]{2,0,1:T(2,128)}, u32[]{:S(2)}) copy-start(f32[2,7,512]{2,0,1:T(2,128)} %param.18) | copy-start | bytes 86020
  11.6 6.7 %collective-permute-start.2 = (f32[72,512]{1,0:T(8,128)S(1)}, f32[72,512]{1,0:T(8,128)S(1)}, u32[]{:S(2)}, u32[]{:S(2)}) collective-permute-start(f32[72,512]{1,0:T(8,128)S(1)} %get-tuple-element.32), channel_id=1, source_target_pairs={{0,4},{4,8},{8,12},{12,16},{16,20},{20,24},{24,28},{28,0},{1,5},{5... | collective-permute-start | bytes 442376 | tf_op jit(solution)/shard_map/ppermute | solution.py:282
  11.7 6.6 %collective-permute-start.3 = (f32[72,512]{1,0:T(8,128)S(1)}, f32[72,512]{1,0:T(8,128)S(1)}, u32[]{:S(2)}, u32[]{:S(2)}) collective-permute-start(f32[72,512]{1,0:T(8,128)S(1)} %get-tuple-element.33), channel_id=1, source_target_pairs={{0,28},{4,0},{8,4},{12,8},{16,12},{20,16},{24,20},{28,24},{1,29},{... | collective-permute-start | bytes 442376 | tf_op jit(solution)/shard_map/ppermute | solution.py:282
  14.4 0.7 copy-start.8
  16.7 1.2 %copy-start.2 = (f32[512,512]{1,0:T(8,128)S(1)}, f32[512,512]{1,0:T(8,128)}, u32[]{:S(2)}) copy-start(f32[512,512]{1,0:T(8,128)} %vectors_ref.1) | copy-start | bytes 3145732
  17.9 0.9 copy-start.3
  21.3 4.9 %copy-start.5 = (f32[64,64]{1,0:T(8,128)S(1)}, f32[64,64]{1,0:T(8,128)}, u32[]{:S(2)}) copy-start(f32[64,64]{1,0:T(8,128)} %refs_0_.2) | copy-start | bytes 49156
  21.3 15.1 %all-to-all-start = ((f32[32,16,128]{2,1,0:T(8,128)}), f32[32,16,128]{2,1,0:T(8,128)S(1)}, u32[]{:S(2)}, u32[]{:S(2)}) async-start(f32[32,16,128]{2,1,0:T(8,128)} %bitcast.9), calls=%async_computation | async-start | bytes 524288 | tf_op jit(solution)/shard_map/all_to_all | solution.py:378
  26.1 0.8 copy-start.6
  26.9 0.7 copy-start.14
  36.3 0.7 copy-start.7
  36.3 0.7 copy-start.9
  39.2 12.7 %copy-start.1 = (f32[8,16,512]{2,1,0:T(8,128)S(1)}, f32[8,16,512]{2,1,0:T(8,128)}, u32[]{:S(2)}) copy-start(f32[8,16,512]{2,1,0:T(8,128)} %param.14) | copy-start | bytes 786436
  52.4 6.4 %collective-permute-start.4 = (f32[24,512]{1,0:T(8,128)S(1)}, f32[24,512]{1,0:T(8,128)S(1)}, u32[]{:S(2)}, u32[]{:S(2)}) collective-permute-start(f32[24,512]{1,0:T(8,128)S(1)} %get-tuple-element.41), channel_id=1, source_target_pairs={{0,1},{1,2},{2,3},{3,0},{4,5},{5,6},{6,7},{7,4},{8,9},{9,10},{10,1... | collective-permute-start | bytes 147464 | tf_op jit(solution)/shard_map/ppermute | solution.py:282
  53.6 5.3 %collective-permute-start.5 = (f32[24,512]{1,0:T(8,128)S(1)}, f32[24,512]{1,0:T(8,128)S(1)}, u32[]{:S(2)}, u32[]{:S(2)}) collective-permute-start(f32[24,512]{1,0:T(8,128)S(1)} %get-tuple-element.42), channel_id=1, source_target_pairs={{0,3},{1,0},{2,1},{3,2},{4,7},{5,4},{6,5},{7,6},{8,11},{9,8},{10,9... | collective-permute-start | bytes 147464 | tf_op jit(solution)/shard_map/ppermute | solution.py:282
  58.9 6.8 %collective-permute-start.6 = (f32[72,512]{1,0:T(8,128)S(1)}, f32[72,512]{1,0:T(8,128)S(1)}, u32[]{:S(2)}, u32[]{:S(2)}) collective-permute-start(f32[72,512]{1,0:T(8,128)S(1)} %get-tuple-element.43), channel_id=1, source_target_pairs={{0,4},{4,8},{8,12},{12,16},{16,20},{20,24},{24,28},{28,0},{1,5},{5... | collective-permute-start | bytes 442376 | tf_op jit(solution)/shard_map/ppermute | solution.py:282
  58.9 6.8 %collective-permute-start.7 = (f32[72,512]{1,0:T(8,128)S(1)}, f32[72,512]{1,0:T(8,128)S(1)}, u32[]{:S(2)}, u32[]{:S(2)}) collective-permute-start(f32[72,512]{1,0:T(8,128)S(1)} %get-tuple-element.44), channel_id=1, source_target_pairs={{0,28},{4,0},{8,4},{12,8},{16,12},{20,16},{24,20},{28,24},{1,29},{... | collective-permute-start | bytes 442376 | tf_op jit(solution)/shard_map/ppermute | solution.py:282

commit v2 on v1

v2 whole, which is shorter than its diff:
```python
import jax
import jax.numpy as jnp
import numpy as np
from jax import lax
from jax.experimental import pallas as pl
from jax.experimental.pallas import tpu as pltpu
from jax.sharding import PartitionSpec as P

ITERS = 2
REACH = 3
LANES = 128
HIGH = lax.Precision.HIGHEST
BOTH = ("py", "pz")
F32 = jnp.float32
BF16 = jnp.bfloat16
VMEM = pl.BlockSpec(memory_space=pltpu.VMEM)
HBM = pl.BlockSpec(memory_space=pltpu.HBM)
ANY = pl.BlockSpec(memory_space=pl.ANY)


def up8(count):
    return -(-count // 8) * 8


def split(value):
    high = value.astype(BF16)
    return high, (value - high.astype(F32)).astype(BF16)


def exact(left, right, sides=(1, 0)):
    return lax.dot_general(
        left, right, (((sides[0],), (sides[1],)), ((), ())), precision=HIGH, preferred_element_type=F32
    )


def fetch(pairs, sem):
    copies = [pltpu.make_async_copy(source, target, sem.at[i]) for i, (source, target) in enumerate(pairs)]
    for copy in copies:
        copy.start()
    for copy in copies:
        copy.wait()


def mul(left, right):
    return lax.dot_general(left, right, (((1,), (0,)), ((), ())), preferred_element_type=F32)


def mul_t(left, right):
    return lax.dot_general(left, right, (((1,), (1,)), ((), ())), preferred_element_type=F32)


def call(kernel, outs, specs, flops, cost_bytes, scratch=(), out_specs=None):
    return pl.pallas_call(
        kernel,
        out_shape=[jax.ShapeDtypeStruct(shape, dtype) for shape, dtype in outs],
        in_specs=specs,
        out_specs=out_specs or [VMEM] * len(outs),
        scratch_shapes=list(scratch),
        compiler_params=pltpu.CompilerParams(vmem_limit_bytes=32 * 1024 * 1024),
        cost_estimate=pl.CostEstimate(flops=flops, bytes_accessed=cost_bytes, transcendentals=0),
    )


def store_z_rims(ly, lz, weighted, low_ref, high_ref):
    for y in range(ly):
        low_ref[y * REACH : (y + 1) * REACH, :] = weighted[y * lz : y * lz + REACH, :]
        high_ref[y * REACH : (y + 1) * REACH, :] = weighted[(y + 1) * lz - REACH : (y + 1) * lz, :]


def coefficient_kernel(
    ly, lz, table_ref, span_ref, field_ref, coef_ref, weighted_ref, low_ref, high_ref, table, span, field, sem
):
    fetch(((table_ref, table), (span_ref, span), (field_ref, field)), sem)
    entries = [table[entry] for entry in range(table_ref.shape[0])]
    for start in range(0, span.shape[0], lz):
        rows = pl.ds(start, lz)
        index = span[rows, :]
        coef = jnp.full(index.shape, entries[0], F32)
        for entry in range(1, len(entries)):
            coef = jnp.where(index == entry, entries[entry], coef)
        coef_ref[rows, :] = coef
        weighted = coef * field[rows, :]
        weighted_ref[rows, :] = weighted
        rim = pl.ds(start // lz * REACH, REACH)
        low_ref[rim, :] = weighted[:REACH]
        high_ref[rim, :] = weighted[lz - REACH :]


def y_rims_kernel(ly, lz, weighted_ref, zlow_ref, zhigh_ref, _, low_ref, high_ref):
    own, side = REACH * lz, REACH * REACH
    for ref, start, zstart in ((low_ref, 0, 0), (high_ref, (ly - REACH) * lz, (ly - REACH) * REACH)):
        ref[own:, :] = jnp.zeros((ref.shape[0] - own, ref.shape[1]), F32)
        ref[0:own, :] = weighted_ref[start : start + own, :]
        ref[own : own + side, :] = zlow_ref[zstart : zstart + side, :]
        ref[own + side : own + 2 * side, :] = zhigh_ref[zstart : zstart + side, :]


def point_columns(ly, lz):
    own = [(y, z) for y in range(ly) for z in range(lz)]
    below, above = range(-REACH, 0), range(REACH)
    zlow = [(y, z) for y in range(ly) for z in below]
    zhigh = [(y, lz + z) for y in range(ly) for z in above]
    sides = []
    for ys in (below, [ly + y for y in above]):
        rim = [(y, z) for y in ys for z in range(lz)]
        rim += [(y, z) for y in ys for z in below]
        rim += [(y, lz + z) for y in ys for z in above]
        sides += rim + [(1 << 20, 1 << 20)] * (up8(len(rim)) - len(rim))
    points = own + zlow + zhigh + sides
    points += [(1 << 20, 1 << 20)] * (-len(points) % 128)
    return np.array(points, np.int32).T.copy()


def stencil_kernel(
    ly, lz, ny, nz, points_hbm, ybands_hbm, zbands_hbm, xbands_hbm, _, out_ref, taps_ref,
    points_ref, ybands_ref, zbands_ref, xbands_ref, sem,
):
    fetch(
        (
            (points_hbm, points_ref), (ybands_hbm, ybands_ref), (zbands_hbm, zbands_ref), (xbands_hbm, xbands_ref),
        ),
        sem,
    )
    count = ly * lz
    rows = lax.broadcasted_iota(jnp.int32, (count, 1), 0)
    yrow, zrow = lax.div(rows, lz), lax.rem(rows, lz)
    factors = []
    for bands_ref, length, row, column, first, whole in (
        (ybands_ref, ly, yrow, points_ref[0:1, :], lax.axis_index("py") * ly, ny),
        (zbands_ref, lz, zrow, points_ref[1:2, :], lax.axis_index("pz") * lz, nz),
    ):
        pick = (lax.broadcasted_iota(jnp.int32, (count, length), 1) == row).astype(F32)
        spot = column + first
        inside = (spot >= 0) & (spot < whole)
        distance = jnp.where(inside, column, 1 << 20) - row
        here = [distance == offset - REACH for offset in range(2 * REACH + 1)]
        for matrix in range(2):
            taps = exact(pick, bands_ref[:, matrix, :], (1, 1))
            dense = jnp.zeros(distance.shape, F32)
            for offset in range(2 * REACH + 1):
                dense = jnp.where(here[offset], taps[:, offset : offset + 1], dense)
            factors.append(dense)
    ystiff, ymass, zstiff, zmass = factors
    for part, value in enumerate((ymass * zmass, ystiff * zmass + ymass * zstiff)):
        high, low = split(value)
        out_ref[part * count : (part + 1) * count, :] = high
        out_ref[(part + 2) * count : (part + 3) * count, :] = low
    nx = xbands_ref.shape[2]
    lane = lax.broadcasted_iota(jnp.int32, (1, nx), 1)
    for offset in range(2 * REACH + 1):
        move = offset - REACH
        inside = (lane - move >= 0) & (lane - move < nx)
        for matrix in range(2):
            band = xbands_ref[offset, matrix : matrix + 1, :]
            band = pltpu.roll(band, move % nx, 1) if move else band
            taps_ref[2 * offset + matrix] = jnp.broadcast_to(jnp.where(inside, band, 0.0), (8, nx))


def xvectors_kernel(source, out_ref, held, sem):
    fetch(((source, held),), sem)
    high, low = split(held[...].T)
    out_ref[: high.shape[0], :] = high
    out_ref[high.shape[0] :, :] = low


def tables_kernel(
    npy, npz, ly, lz, xvec_hbm, yvec_hbm, zvec_hbm, xval_hbm, yval_hbm, zval_hbm, _,
    xout_ref, zhigh_ref, zlow_ref, ydown_ref, yup_ref, sums_ref,
    xvec_ref, yvec_ref, zvec_ref, xval_ref, yval_ref, zval_ref, sem,
):
    fetch(
        (
            (xvec_hbm, xvec_ref), (yvec_hbm, yvec_ref), (zvec_hbm, zvec_ref),
            (xval_hbm, xval_ref), (yval_hbm, yval_ref), (zval_hbm, zval_ref),
        ),
        sem,
    )
    ny, nz = npy * ly, npz * lz
    nx = xvec_ref.shape[0]
    high, low = split(xvec_ref[...].T)
    xout_ref[:nx, :] = high
    xout_ref[nx:, :] = low
    twice = (
        lax.broadcasted_iota(jnp.int32, (nz, 2 * nz), 0)
        == lax.rem(lax.broadcasted_iota(jnp.int32, (nz, 2 * nz), 1), nz)
    ).astype(F32)
    pair = exact(zvec_ref[...], twice)
    half = lax.broadcasted_iota(jnp.int32, pair.shape, 1) >= nz
    zhigh_ref[...] = jnp.zeros(zhigh_ref.shape, BF16)
    zlow_ref[...] = jnp.zeros(zlow_ref.shape, BF16)
    for parity in range(2):
        high, low = split(jnp.where(half == (parity == 1), pair, 0.0))
        for yl in range(parity, ly, 2):
            for block in range(npz):
                to = (pl.ds((block * ly + yl) * lz, lz), pl.ds(yl // 2 * 2 * nz, 2 * nz))
                zhigh_ref[to] = high[block * lz : (block + 1) * lz, :]
                zlow_ref[to] = low[block * lz : (block + 1) * lz, :]

    def y_of(p):
        spot = lax.div(p, npy)
        return lax.rem(p, npy) * ly + 2 * lax.rem(spot, ly // 2) + lax.div(spot, ly // 2)

    def four(array):
        high, low = split(array)
        late = lax.broadcasted_iota(jnp.int32, array.shape, 1) >= 2 * ny
        return jnp.where(late, low.astype(F32), high.astype(F32)).astype(BF16)

    lane = lax.broadcasted_iota(jnp.int32, (ny, 4 * ny), 1)
    row = lax.broadcasted_iota(jnp.int32, (ny, 4 * ny), 0)
    moved = (row == y_of(lax.rem(lane, ny))).astype(F32)
    ydown_ref[...] = four(exact(yvec_ref[...].T, moved))
    order = (
        lax.broadcasted_iota(jnp.int32, (ny, ny), 1) == y_of(lax.broadcasted_iota(jnp.int32, (ny, ny), 0))
    ).astype(F32)
    copies = (row == lax.rem(lane, ny)).astype(F32)
    yup_ref[...] = four(exact(exact(order, yvec_ref[...]), copies))
    square = (ny, ny)
    diagonal = lax.broadcasted_iota(jnp.int32, square, 0) == lax.broadcasted_iota(jnp.int32, square, 1)
    ycolumn = jnp.sum(jnp.where(diagonal, yval_ref[...], 0.0), axis=1, keepdims=True)
    yz = ycolumn + exact(jnp.broadcast_to(zval_ref[...], (8, nz)), twice)[0:1]
    late = lax.broadcasted_iota(jnp.int32, (1, 2 * nz), 1) >= nz
    modes = nx // (npy * npz)
    first = (lax.axis_index("py") * npz + lax.axis_index("pz")) * modes
    for mode in range(0, modes, 2):
        x = jnp.where(late, xval_ref[first + mode + 1], xval_ref[first + mode])
        sums_ref[:, mode * nz : (mode + 2) * nz] = yz + x


def residual_kernel(
    weighted_ref, zlow_ref, zhigh_ref, ylow_ref, yhigh_ref, stencil_ref, taps_ref, coef_ref, right_ref, vectors_ref,
    _, residual_ref, spectral_ref,
):
    count, nx = weighted_ref.shape
    pieces = [ref[...] for ref in (weighted_ref, zlow_ref, zhigh_ref, ylow_ref, yhigh_ref)]
    missing = stencil_ref.shape[1] - sum(piece.shape[0] for piece in pieces)
    if missing:
        pieces.append(jnp.zeros((missing, nx), F32))
    high, low = split(jnp.concatenate(pieces, axis=0))
    both = mul(stencil_ref[...], high)
    both = both[: 2 * count] + both[2 * count :] + mul(stencil_ref[: 2 * count, :], low)
    for start in range(0, count, 8):
        mass = both[start : start + 8]
        stiff = both[count + start : count + start + 8]
        applied = None
        for offset in range(2 * REACH + 1):
            move = offset - REACH
            term = taps_ref[2 * offset] * mass + taps_ref[2 * offset + 1] * stiff
            term = pltpu.roll(term, -move % nx, 1) if move else term
            applied = term if applied is None else applied + term
        rows = pl.ds(start, 8)
        residual_ref[rows, :] = right_ref[rows, :] - coef_ref[rows, :] * applied
    high, low = split(residual_ref[...])
    product = mul_t(vectors_ref[...], jnp.concatenate([high, low], axis=0))
    spectral_ref[...] = (product[:nx, :count] + product[:nx, count:]) + (product[nx:, :count] + product[nx:, count:])


def modes_kernel(npy, npz, zhigh_ref, zlow_ref, ydown_ref, yup_ref, sums_ref, in_ref, out_ref):
    count = in_ref.shape[0] // (npy * npz)
    lanes = in_ref.shape[1]
    nz = sums_ref.shape[1] // count
    chunks = zhigh_ref.shape[1] // (2 * nz)
    rows = [
        jnp.concatenate([in_ref[pl.ds(b * count + j, npy, stride=npz * count), :] for b in range(npz)], axis=1)
        for j in range(count)
    ]
    zhigh, zlow = zhigh_ref[...], zlow_ref[...]

    def three(value, product):
        high, low = split(value)
        both = product(jnp.concatenate([high, low], axis=0), zhigh)
        return both[: count * npy] + both[count * npy :] + product(high, zlow)

    part = three(jnp.concatenate(rows, axis=0), mul)
    late = lax.broadcasted_iota(jnp.int32, (npy, 2 * nz), 1) >= nz

    def swap(value):
        return pltpu.roll(value, nz, 1)

    def tile(array, j, c):
        return array[j * npy : (j + 1) * npy, c * 2 * nz : (c + 1) * 2 * nz]

    pairs = []
    for j in range(0, count, 2):
        first = [tile(part, j, c) for c in range(chunks)]
        second = [tile(part, j + 1, c) for c in range(chunks)]
        even = [jnp.where(late, swap(second[c]), first[c]) for c in range(chunks)]
        odd = [jnp.where(late, second[c], swap(first[c])) for c in range(chunks)]
        pairs.append(jnp.concatenate(even + odd, axis=0))
    stacked = jnp.concatenate(pairs, axis=1)

    def four(value):
        high, low = split(value)
        return jnp.concatenate([high, low, high, low], axis=0)

    modes = mul(ydown_ref[...], four(stacked)) / sums_ref[...]
    restored = mul(yup_ref[...], four(modes))
    half = npy * chunks
    rows = []
    for pair in range(count // 2):
        block = restored[:, pair * 2 * nz : (pair + 1) * 2 * nz]
        even = [block[c * npy : (c + 1) * npy] for c in range(chunks)]
        odd = [block[half + c * npy : half + (c + 1) * npy] for c in range(chunks)]
        rows.append(jnp.concatenate([jnp.where(late, swap(odd[c]), even[c]) for c in range(chunks)], axis=1))
        rows.append(jnp.concatenate([jnp.where(late, odd[c], swap(even[c])) for c in range(chunks)], axis=1))
    back = three(jnp.concatenate(rows, axis=0), mul_t)
    for j in range(count):
        for b in range(npz):
            out_ref[pl.ds(b * count + j, npy, stride=npz * count), :] = back[
                j * npy : (j + 1) * npy, b * lanes : (b + 1) * lanes
            ]


def from_modes(spectral_ref, vectors_ref):
    nx, count = spectral_ref.shape
    high, low = split(spectral_ref[...].T)
    both = mul(jnp.concatenate([high, low], axis=0), vectors_ref[:nx, :])
    return both[:count] + both[count:] + mul(high, vectors_ref[nx:, :])


def update_kernel(ly, lz, spectral_ref, vectors_ref, field_ref, coef_ref, updated_ref, weighted_ref, low_ref, high_ref):
    updated = field_ref[...] + from_modes(spectral_ref, vectors_ref)
    updated_ref[...] = updated
    weighted = coef_ref[...] * updated
    weighted_ref[...] = weighted
    store_z_rims(ly, lz, weighted, low_ref, high_ref)


def last_update_kernel(spectral_ref, vectors_ref, field_ref, residual_ref, updated_hbm, residual_hbm, held, sem):
    leaving = pltpu.make_async_copy(residual_ref, residual_hbm, sem.at[0])
    leaving.start()
    held[...] = field_ref[...] + from_modes(spectral_ref, vectors_ref)
    fetch(((held, updated_hbm),), sem.at[pl.ds(1, 1)])
    leaving.wait()


def around(value, axis, step):
    count = lax.axis_size(axis)
    return lax.ppermute(value, axis, [(i, (i + step) % count) for i in range(count)])


def plain_modes(received, npy, npz, ly, lz, xvalues, yvalues, zvalues, yvectors, zvectors):
    count = received.shape[0] // (npy * npz)
    field = received.reshape(npy, npz, count, ly, lz).transpose(2, 0, 3, 1, 4).reshape(count, npy * ly, npz * lz)
    field = jnp.einsum("xyz,yj->xjz", field, yvectors, precision=HIGH)
    field = jnp.einsum("xyz,zk->xyk", field, zvectors, precision=HIGH)
    field = field / (yvalues[None, :, None] + zvalues[None, None, :] + xvalues[:, None, None])
    field = jnp.einsum("xjz,yj->xyz", field, yvectors, precision=HIGH)
    field = jnp.einsum("xyk,zk->xyz", field, zvectors, precision=HIGH)
    field = field.reshape(count, npy, ly, npz, lz).transpose(1, 3, 0, 2, 4)
    return field.reshape(npy * npz * count, ly * lz)


def shards(
    solution,
    right_side,
    span_index,
    coef_table,
    xaxis_bands,
    yaxis_bands,
    zaxis_bands,
    xaxis_vectors,
    yaxis_vectors,
    zaxis_vectors,
    xaxis_values,
    yaxis_values,
    zaxis_values,
):
    npy, npz = lax.axis_size("py"), lax.axis_size("pz")
    ly, lz, nx = solution.shape
    ny, nz = npy * ly, npz * lz
    count, devices = ly * lz, npy * npz
    modes = nx // devices
    field = solution.reshape(count, nx)
    right = right_side.reshape(count, nx)
    block, zrim, yrim = (count, nx), (ly * REACH, nx), (up8(REACH * lz + 2 * REACH * REACH), nx)
    cell = count * nx * 4
    dma = pltpu.SemaphoreType.DMA

    coef, weighted, zlow, zhigh = call(
        lambda *refs: coefficient_kernel(ly, lz, *refs),
        [(block, F32), (block, F32), (zrim, F32), (zrim, F32)],
        [HBM] * 3, count * nx * 16, 4 * cell,
        [pltpu.SMEM(coef_table.shape, F32), pltpu.VMEM(block, jnp.int32), pltpu.VMEM(block, F32), dma((3,))],
    )(coef_table, span_index.reshape(count, nx), field)

    points = point_columns(ly, lz)
    width = points.shape[1]
    bands = [array.transpose(1, 0, 2) for array in (yaxis_bands, zaxis_bands, xaxis_bands)]
    stencil, taps = call(
        lambda *refs: stencil_kernel(ly, lz, ny, nz, *refs),
        [((4 * count, width), BF16), ((2 * (2 * REACH + 1), 8, nx), F32)],
        [HBM] * 4 + [ANY], count * width * 60, 8 * count * width,
        [pltpu.VMEM(points.shape, jnp.int32)] + [pltpu.VMEM(array.shape, F32) for array in bands] + [dma((4,))],
    )(jnp.asarray(points), *bands, zlow)

    fast = (
        modes % 2 == 0 and npy % 8 == 0 and lz % 16 == 0 and ly % 2 == 0
        and 2 * nz == LANES and 2 * ny == LANES and count == LANES and nx % LANES == 0
    )
    if fast:
        zmat, ymat = (npz * count, ly * nz), (ny, 4 * ny)
        vectors, *tables = call(
            lambda *refs: tables_kernel(npy, npz, ly, lz, *refs),
            [((2 * nx, nx), BF16), (zmat, BF16), (zmat, BF16), (ymat, BF16), (ymat, BF16), ((ny, modes * nz), F32)],
            [HBM] * 6 + [ANY], npz * count * ly * nz * 8, npz * count * ly * nz * 4,
            [pltpu.VMEM(array.shape, F32) for array in (xaxis_vectors, yaxis_vectors, zaxis_vectors)]
            + [pltpu.SMEM((nx,), F32), pltpu.VMEM((1, ny), F32), pltpu.VMEM((1, nz), F32), dma((6,))],
        )(
            xaxis_vectors, yaxis_vectors, zaxis_vectors, xaxis_values,
            yaxis_values.reshape(1, ny), zaxis_values.reshape(1, nz), taps,
        )

        def precondition(received):
            return call(
                lambda *refs: modes_kernel(npy, npz, *refs),
                [((nx, count), F32)], [VMEM] * 6, 6 * 2 * count * nx * ly * nz, 2 * cell,
            )(*tables, received)[0]
    else:
        tables = [taps]
        vectors = call(
            xvectors_kernel, [((2 * nx, nx), BF16)], [HBM], nx * nx * 40, 8 * nx * nx,
            [pltpu.VMEM((nx, nx), F32), dma((1,))],
        )(xaxis_vectors)[0]
        part = lax.axis_index(BOTH)
        xpart = lax.dynamic_slice_in_dim(xaxis_values, part * modes, modes)

        def precondition(received):
            return plain_modes(
                received, npy, npz, ly, lz, xpart, yaxis_values, zaxis_values, yaxis_vectors, zaxis_vectors
            )

    for iteration in range(ITERS):
        last = iteration + 1 == ITERS
        from_low, from_high = around(zhigh, "pz", 1), around(zlow, "pz", -1)
        ylow, yhigh = call(
            lambda *refs: y_rims_kernel(ly, lz, *refs),
            [(yrim, F32)] * 2, [VMEM] * 3 + [ANY], nx, 4 * nx * 4 * yrim[0],
        )(weighted, from_low, from_high, taps)
        below, above = around(yhigh, "py", 1), around(ylow, "py", -1)
        residual, spectral = call(
            residual_kernel,
            [(block, F32), ((nx, count), F32)],
            [VMEM] * 10 + [ANY], 6 * count * nx * (nx + 2 * width), 5 * cell + 4 * nx * nx,
        )(weighted, from_low, from_high, below, above, stencil, taps, coef, right, vectors, tables[0])
        spectral = lax.all_to_all(spectral, BOTH, split_axis=0, concat_axis=0, tiled=True)
        spectral = precondition(spectral)
        spectral = lax.all_to_all(spectral, BOTH, split_axis=0, concat_axis=0, tiled=True)
        cost = (6 * count * nx * nx, 4 * cell + 4 * nx * nx)
        if not last:
            field, weighted, zlow, zhigh = call(
                lambda *refs: update_kernel(ly, lz, *refs),
                [(block, F32), (block, F32), (zrim, F32), (zrim, F32)], [VMEM] * 4, *cost,
            )(spectral, vectors, field, coef)
        else:
            field, residual = call(
                last_update_kernel, [(block, F32), (block, F32)], [VMEM] * 4, *cost,
                [pltpu.VMEM(block, F32), dma((2,))], [HBM] * 2,
            )(spectral, vectors, field, residual)
    return (field.reshape(solution.shape), residual.reshape(solution.shape))


def solution(mesh):
    return jax.shard_map(
        shards,
        mesh=mesh,
        in_specs=(
            P("py", "pz", None),
            P("py", "pz", None),
            P("py", "pz", None),
            P(),
            P(),
            P(None, None, "py"),
            P(None, None, "pz"),
            P(),
            P(),
            P(),
            P(),
            P(),
            P(),
        ),
        out_specs=(P("py", "pz", None), P("py", "pz", None)),
        check_vma=False,
    )
```

time: 98.7 us -> 94.8 us (0.960)
  blocking collectives: 40 us -> 54.5 us
  waiting for transfers between devices: 17.8 us -> 7.46 us
  starting transfers between devices: 19.3 us -> 14.4 us
  Pallas kernels: 13.3 us -> 11.2 us
    all_to_all x3 -> x4, blocking collectives: 40 us -> 54.5 us  [shards(): lax.all_to_all(spectral, BOTH, split_axis=0, concat_axis=0, tiled=True)]
    all_to_all x1 -> x0, waiting for transfers between devices: 8.69 us -> none  [shards(): lax.all_to_all(spectral, BOTH, split_axis=0, concat_axis=0, tiled=True)]
    all_to_all x1 -> x0, starting transfers between devices: 4.86 us -> none  [shards(): lax.all_to_all(spectral, BOTH, split_axis=0, concat_axis=0, tiled=True)]
    ppermute x8, waiting for transfers between devices: 9.16 us -> 7.46 us  [around(): lax.ppermute(value, axis, [(i, (i + step) % count) for i in range(count)])]
    pallas_call x2, Pallas kernels: 4.42 us -> 2.92 us  [precondition(): call(lambda *refs: modes_kernel(npy, npz, *refs), [((nx, count), F32)], [...]
    pallas_call x6 -> x5, Pallas kernels: 7.7 us -> 7.05 us  [the longest x2 3.37 us: shards(): call(residual_kernel, [(block, F32), ((nx, count), F32)], [VMEM] * 10 + [...]
    unnamed x34 -> x30, local copies, waits for them, and re-layouts: 6.67 us -> 6.04 us
  transfers between devices with their start and end apart: 9 -> 8, of which waited for: 5 -> 3; matrix products, arithmetic and copies ran while one was open for 0% -> 0% of each run, Pallas kernels for 2% -> 3%
where the time goes in v2:
time: 94.8 us; the launch traced here: 94.4 us
  blocking collectives  54.5 us (57%)
  starting transfers between devices  14.4 us (15%)
  Pallas kernels  11.2 us (12%)
  waiting for transfers between devices  7.46 us (8%)
  local copies, waits for them, and re-layouts  6.04 us (6%)
    all_to_all x4, blocking collectives, shards(): lax.all_to_all(spectral, BOTH, split_axis=0, concat_axis=0, tiled=True)  54.5 us
    ppermute x8, starting transfers between devices, around(): lax.ppermute(value, axis, [(i, (i + step) % count) for i in range(count)])  14.4 us
    ppermute x8, waiting for transfers between devices, around(): lax.ppermute(value, axis, [(i, (i + step) % count) for i in range(count)])  7.46 us
    unnamed x30, local copies, waits for them, and re-layouts  6.04 us
    pallas_call x2, Pallas kernels, shards(): call(residual_kernel, [(block, F32), ((nx, count), F32)], [VMEM] * 10 + [...  3.37 us
    pallas_call x2, Pallas kernels, precondition(): call(lambda *refs: modes_kernel(npy, npz, *refs), [((nx, count), F32)], [...  2.92 us
  transfers between devices with their start and end apart: 8, of which 3 were waited for; matrix products, arithmetic and copies ran while one was open for 0% of the time, Pallas kernels for 3%

profile of v2, /device:TPU:0, one launch (start us, length us, event | category | flops | bytes accessed | tf_op | source)
XLA Modules:
  0.0 94.4 jit_solution(14309425029376449509)
XLA Ops:
  0.6 0.6 copy-done.12
  1.3 0.9 %copy-done.1 = f32[8,16,512]{2,1,0:T(8,128)S(1)} copy-done((f32[8,16,512]{2,1,0:T(8,128)S(1)}, f32[8,16,512]{2,1,0:T(8,128)}, u32[]{:S(2)}) %copy-start.1) | copy-done | bytes 262168
  2.2 0.9 %copy-done.4 = s32[8,16,512]{2,1,0:T(8,128)S(1)} copy-done((s32[8,16,512]{2,1,0:T(8,128)S(1)}, s32[8,16,512]{2,1,0:T(8,128)}, u32[]{:S(2)}) %copy-start.4) | copy-done | bytes 262168
  3.2 0.7 shard_map.149
  3.9 3.1 %collective-permute-start = (f32[24,512]{1,0:T(8,128)S(1)}, f32[24,512]{1,0:T(8,128)S(1)}, u32[]{:S(2)}, u32[]{:S(2)}) collective-permute-start(f32[24,512]{1,0:T(8,128)S(1)} %get-tuple-element.35), channel_id=1, source_target_pairs={{0,1},{1,2},{2,3},{3,0},{4,5},{5,6},{6,7},{7,4},{8,9},{9,10},{10,1... | collective-permute-start | bytes 147464 | tf_op jit(solution)/shard_map/ppermute | solution.py:338
  7.0 2.1 %collective-permute-start.1 = (f32[24,512]{1,0:T(8,128)S(1)}, f32[24,512]{1,0:T(8,128)S(1)}, u32[]{:S(2)}, u32[]{:S(2)}) collective-permute-start(f32[24,512]{1,0:T(8,128)S(1)} %get-tuple-element.27.refs_4_), channel_id=1, source_target_pairs={{0,3},{1,0},{2,1},{3,2},{4,7},{5,4},{6,5},{7,6},{8,11},{9,8},{10,9... | collective-permute-start | bytes 147464 | tf_op jit(solution)/shard_map/ppermute | solution.py:338
  9.1 0.7 copy-done.7
  9.8 0.7 copy-done.8
  10.5 0.7 copy-done.9
  11.2 0.7 copy-done.10
  11.9 1.2 %shard_map.150 = (bf16[512,384]{1,0:T(8,128)(2,1)S(1)}, f32[14,8,512]{2,1,0:T(8,128)S(1)}) custom-call(s32[2,384]{1,0:T(2,128)S(1)} %copy-done.10, f32[7,2,8]{2,1,0:T(2,128)S(1)} %bitcast.32, f32[7,2,16]{2,1,0:T(2,128)S(1)} %bitcast.33, f32[7,2,512]{2,1,0:T(2,128)S(1)} %bitcast.31, f32[24,512]{1,0:T(8,128)S(1)} %get-tuple-element.27.refs_4_), custom_call_target="tpu_custom_call" | custom-call | flops 2949120 | bytes 393216 | tf_op jit(solution)/shard_map/pallas_call | solution.py:389
  13.2 0.1 collective-permute-start.2
  13.3 2.6 %collective-permute-start.3 = (f32[72,512]{1,0:T(8,128)S(1)}, f32[72,512]{1,0:T(8,128)S(1)}, u32[]{:S(2)}, u32[]{:S(2)}) collective-permute-start(f32[72,512]{1,0:T(8,128)S(1)} %get-tuple-element.37), channel_id=1, source_target_pairs={{0,28},{4,0},{8,4},{12,8},{16,12},{20,16},{24,20},{28,24},{1,29},{... | collective-permute-start | bytes 442376 | tf_op jit(solution)/shard_map/ppermute | solution.py:338
  16.0 0.6 copy-done.13
  16.6 1.3 %shard_map.151 = (bf16[1024,512]{1,0:T(8,128)(2,1)S(1)}, bf16[512,512]{1,0:T(8,128)(2,1)S(1)}, bf16[512,512]{1,0:T(8,128)(2,1)S(1)}, bf16[64,256]{1,0:T(8,128)(2...) custom-call(f32[512,512]{1,0:T(8,128)S(1)} %copy-done.3, f32[64,64]{1,0:T(8,128)S(1)} %copy-done.5, ...), custom_call_target="tpu_custom_call" | custom-call | flops 2097152 | bytes 1048576 | tf_op jit(solution)/shard_map/pallas_call | solution.py:402
  17.9 0.8 collective-permute-done.2.ylow_ref
  18.8 1.8 %shard_map.153 = (f32[128,512]{1,0:T(8,128)}, f32[512,128]{1,0:T(8,128)S(1)}) custom-call(f32[128,512]{1,0:T(8,128)S(1)} %get-tuple-element.34.refs_0_.weighted_ref, f32[24,512]{1,0:T(8,128)S(1)} %collective-permute-done.refs_1_.zlow_ref, f32[24,512]{1,0:T(8,128)S(1)} %collective-permute-done.1.refs_2_.zhigh_ref, ...), custom_call_target="tpu_custom_call" | custom-call | flops 503316480 | bytes 2359296 | tf_op jit(solution)/shard_map/pallas_call | solution.py:440
  20.6 14.5 %all_to_all.44 = f32[32,16,128]{2,1,0:T(8,128)S(1)} all-to-all(f32[32,16,128]{2,1,0:T(8,128)S(1)} %bitcast.30), channel_id=1, replica_groups=mesh['py'=8,'pz'=4] {'py','pz'}, dimensions={0} | all-to-all | bytes 524288 | tf_op jit(solution)/shard_map/all_to_all | solution.py:445
  35.0 1.5 %shard_map.154 = f32[512,128]{1,0:T(8,128)S(1)} custom-call(bf16[512,512]{1,0:T(8,128)(2,1)S(1)} %get-tuple-element.29._.refs_0_, bf16[512,512]{1,0:T(8,128)(2,1)S(1)} %get-tuple-element.30.refs_1_, bf16[64,256]{1,0:T(8,128)(2,1)S(1)} %get-tuple-element.31.refs_2_, bf16[64,256]{1,0:T(8,128)(2,1)S(1)} %get-tuple-element.32.refs_3_, ...), custom_call_target="tpu_custom_call" | custom-call | flops 402653184 | bytes 524288 | tf_op jit(solution)/shard_map/pallas_call | solution.py:414
  36.5 12.7 %all_to_all.45 = f32[32,16,128]{2,1,0:T(8,128)S(1)} all-to-all(f32[32,16,128]{2,1,0:T(8,128)S(1)} %bitcast.27), channel_id=1, replica_groups=mesh['py'=8,'pz'=4] {'py','pz'}, dimensions={0} | all-to-all | bytes 524288 | tf_op jit(solution)/shard_map/all_to_all | solution.py:447
  49.2 0.4 shard_map.155
  49.7 1.1 %collective-permute-start.4 = (f32[24,512]{1,0:T(8,128)S(1)}, f32[24,512]{1,0:T(8,128)S(1)}, u32[]{:S(2)}, u32[]{:S(2)}) collective-permute-start(f32[24,512]{1,0:T(8,128)S(1)} %get-tuple-element.43), channel_id=1, source_target_pairs={{0,1},{1,2},{2,3},{3,0},{4,5},{5,6},{6,7},{7,4},{8,9},{9,10},{10,1... | collective-permute-start | bytes 147464 | tf_op jit(solution)/shard_map/ppermute | solution.py:338
  50.8 2.8 %collective-permute-start.5 = (f32[24,512]{1,0:T(8,128)S(1)}, f32[24,512]{1,0:T(8,128)S(1)}, u32[]{:S(2)}, u32[]{:S(2)}) collective-permute-start(f32[24,512]{1,0:T(8,128)S(1)} %get-tuple-element.44), channel_id=1, source_target_pairs={{0,3},{1,0},{2,1},{3,2},{4,7},{5,4},{6,5},{7,6},{8,11},{9,8},{10,9... | collective-permute-start | bytes 147464 | tf_op jit(solution)/shard_map/ppermute | solution.py:338
  53.6 2.5 %collective-permute-done.4.refs_1_.zlow_ref = f32[24,512]{1,0:T(8,128)S(1)} collective-permute-done((f32[24,512]{1,0:T(8,128)S(1)}, f32[24,512]{1,0:T(8,128)S(1)}, u32[]{:S(2)}, u32[]{:S(2)}) %collective-permute-start.4) | collective-permute-done | bytes 49184 | tf_op jit(solution)/shard_map/ppermute | solution.py:338
  56.1 0.1 collective-permute-start.6
  56.2 2.6 %collective-permute-start.7 = (f32[72,512]{1,0:T(8,128)S(1)}, f32[72,512]{1,0:T(8,128)S(1)}, u32[]{:S(2)}, u32[]{:S(2)}) collective-permute-start(f32[72,512]{1,0:T(8,128)S(1)} %get-tuple-element.46), channel_id=1, source_target_pairs={{0,28},{4,0},{8,4},{12,8},{16,12},{20,16},{24,20},{28,24},{1,29},{... | collective-permute-start | bytes 442376 | tf_op jit(solution)/shard_map/ppermute | solution.py:338
  58.8 4.1 %collective-permute-done.6.ylow_ref = f32[72,512]{1,0:T(8,128)S(1)} collective-permute-done((f32[72,512]{1,0:T(8,128)S(1)}, f32[72,512]{1,0:T(8,128)S(1)}, u32[]{:S(2)}, u32[]{:S(2)}) %collective-permute-start.6) | collective-permute-done | bytes 147488 | tf_op jit(solution)/shard_map/ppermute | solution.py:338
  62.9 1.5 %shard_map.157 = (f32[128,512]{1,0:T(8,128)S(1)}, f32[512,128]{1,0:T(8,128)S(1)}) custom-call(f32[128,512]{1,0:T(8,128)S(1)} %get-tuple-element.42.refs_0_.weighted_ref, f32[24,512]{1,0:T(8,128)S(1)} %collective-permute-done.4.refs_1_.zlow_ref, f32[24,512]{1,0:T(8,128)S(1)} %collective-permute-done.5.refs_2_.zhigh_ref, ...), custom_call_target="tpu_custom_call" | custom-call | flops 503316480 | bytes 2359296 | tf_op jit(solution)/shard_map/pallas_call | solution.py:440
  64.5 14.5 %all_to_all.46 = f32[32,16,128]{2,1,0:T(8,128)S(1)} all-to-all(f32[32,16,128]{2,1,0:T(8,128)S(1)} %bitcast.29), channel_id=1, replica_groups=mesh['py'=8,'pz'=4] {'py','pz'}, dimensions={0} | all-to-all | bytes 524288 | tf_op jit(solution)/shard_map/all_to_all | solution.py:445
  79.0 1.5 %shard_map.158 = f32[512,128]{1,0:T(8,128)S(1)} custom-call(bf16[512,512]{1,0:T(8,128)(2,1)S(1)} %get-tuple-element.29._.refs_0_, bf16[512,512]{1,0:T(8,128)(2,1)S(1)} %get-tuple-element.30.refs_1_, bf16[64,256]{1,0:T(8,128)(2,1)S(1)} %get-tuple-element.31.refs_2_, bf16[64,256]{1,0:T(8,128)(2,1)S(1)} %get-tuple-element.32.refs_3_, ...), custom_call_target="tpu_custom_call" | custom-call | flops 402653184 | bytes 524288 | tf_op jit(solution)/shard_map/pallas_call | solution.py:414
  80.5 12.7 %all_to_all.47 = f32[32,16,128]{2,1,0:T(8,128)S(1)} all-to-all(f32[32,16,128]{2,1,0:T(8,128)S(1)} %bitcast.25), channel_id=1, replica_groups=mesh['py'=8,'pz'=4] {'py','pz'}, dimensions={0} | all-to-all | bytes 524288 | tf_op jit(solution)/shard_map/all_to_all | solution.py:447
  93.2 1.1 %shard_map.159 = (f32[128,512]{1,0:T(8,128)}, f32[128,512]{1,0:T(8,128)}) custom-call(f32[512,128]{1,0:T(8,128)S(1)} %bitcast.22, bf16[1024,512]{1,0:T(8,128)(2,1)S(1)} %get-tuple-element.40.vectors_ref.refs_1_, f32[128,512]{1,0:T(8,128)S(1)} %get-tuple-element.48.field_ref, f32[128,512]{1,0:T(8,128)S(1)} %get-tuple-element.49.residual_ref), custom_call_target="tpu_custom_call" | custom-call | flops 201326592 | bytes 2097152 | tf_op jit(solution)/shard_map/pallas_call | solution.py:455
  (29 shorter events, 0.1 us)
Async XLA Ops:
  0.6 0.7 copy-start.12
  1.3 0.9 %copy-start.1 = (f32[8,16,512]{2,1,0:T(8,128)S(1)}, f32[8,16,512]{2,1,0:T(8,128)}, u32[]{:S(2)}) copy-start(f32[8,16,512]{2,1,0:T(8,128)} %param.14) | copy-start | bytes 786436
  2.2 0.9 %copy-start.4 = (s32[8,16,512]{2,1,0:T(8,128)S(1)}, s32[8,16,512]{2,1,0:T(8,128)}, u32[]{:S(2)}) copy-start(s32[8,16,512]{2,1,0:T(8,128)} %param.16) | copy-start | bytes 786436
  3.2 12.7 %copy-start.3 = (f32[512,512]{1,0:T(8,128)S(1)}, f32[512,512]{1,0:T(8,128)}, u32[]{:S(2)}) copy-start(f32[512,512]{1,0:T(8,128)} %refs_0_.4) | copy-start | bytes 3145732
  3.9 9.2 %collective-permute-start = (f32[24,512]{1,0:T(8,128)S(1)}, f32[24,512]{1,0:T(8,128)S(1)}, u32[]{:S(2)}, u32[]{:S(2)}) collective-permute-start(f32[24,512]{1,0:T(8,128)S(1)} %get-tuple-element.35), channel_id=1, source_target_pairs={{0,1},{1,2},{2,3},{3,0},{4,5},{5,6},{6,7},{7,4},{8,9},{9,10},{10,1... | collective-permute-start | bytes 147464 | tf_op jit(solution)/shard_map/ppermute | solution.py:338
  7.0 6.2 %collective-permute-start.1 = (f32[24,512]{1,0:T(8,128)S(1)}, f32[24,512]{1,0:T(8,128)S(1)}, u32[]{:S(2)}, u32[]{:S(2)}) collective-permute-start(f32[24,512]{1,0:T(8,128)S(1)} %get-tuple-element.27.refs_4_), channel_id=1, source_target_pairs={{0,3},{1,0},{2,1},{3,2},{4,7},{5,4},{6,5},{7,6},{8,11},{9,8},{10,9... | collective-permute-start | bytes 147464 | tf_op jit(solution)/shard_map/ppermute | solution.py:338
  9.1 0.7 copy-start.7
  9.8 0.7 copy-start.8
  10.5 0.7 copy-start.9
  11.2 0.7 copy-start.10
  13.2 2.8 %copy-start.5 = (f32[64,64]{1,0:T(8,128)S(1)}, f32[64,64]{1,0:T(8,128)}, u32[]{:S(2)}) copy-start(f32[64,64]{1,0:T(8,128)} %refs_1_.1) | copy-start | bytes 49156
  13.2 2.8 %copy-start.6 = (f32[64,64]{1,0:T(8,128)S(1)}, f32[64,64]{1,0:T(8,128)}, u32[]{:S(2)}) copy-start(f32[64,64]{1,0:T(8,128)} %refs_2_.1) | copy-start | bytes 49156
  13.2 5.5 %collective-permute-start.2 = (f32[72,512]{1,0:T(8,128)S(1)}, f32[72,512]{1,0:T(8,128)S(1)}, u32[]{:S(2)}, u32[]{:S(2)}) collective-permute-start(f32[72,512]{1,0:T(8,128)S(1)} %get-tuple-element.36), channel_id=1, source_target_pairs={{0,4},{4,8},{8,12},{12,16},{16,20},{20,24},{24,28},{28,0},{1,5},{5... | collective-permute-start | bytes 442376 | tf_op jit(solution)/shard_map/ppermute | solution.py:338
  13.3 2.7 %copy-start.11 = (f32[512]{0:T(512)S(1)}, f32[512]{0:T(512)}, u32[]{:S(2)}) copy-start(f32[512]{0:T(512)} %refs_3_.1) | copy-start | bytes 6148
  13.3 5.4 %collective-permute-start.3 = (f32[72,512]{1,0:T(8,128)S(1)}, f32[72,512]{1,0:T(8,128)S(1)}, u32[]{:S(2)}, u32[]{:S(2)}) collective-permute-start(f32[72,512]{1,0:T(8,128)S(1)} %get-tuple-element.37), channel_id=1, source_target_pairs={{0,28},{4,0},{8,4},{12,8},{16,12},{20,16},{24,20},{28,24},{1,29},{... | collective-permute-start | bytes 442376 | tf_op jit(solution)/shard_map/ppermute | solution.py:338
  15.9 0.7 copy-start.13
  15.9 0.7 copy-start.14
  16.6 2.2 %copy-start = (f32[8,16,512]{2,1,0:T(8,128)S(1)}, f32[8,16,512]{2,1,0:T(8,128)}, u32[]{:S(2)}) copy-start(f32[8,16,512]{2,1,0:T(8,128)} %param.15) | copy-start | bytes 786436
  36.5 12.7 %copy-start.2 = (f32[8,16,512]{2,1,0:T(8,128)S(1)}, f32[8,16,512]{2,1,0:T(8,128)}, u32[]{:S(2)}) copy-start(f32[8,16,512]{2,1,0:T(8,128)} %param.14) | copy-start | bytes 786436
  49.7 6.4 %collective-permute-start.4 = (f32[24,512]{1,0:T(8,128)S(1)}, f32[24,512]{1,0:T(8,128)S(1)}, u32[]{:S(2)}, u32[]{:S(2)}) collective-permute-start(f32[24,512]{1,0:T(8,128)S(1)} %get-tuple-element.43), channel_id=1, source_target_pairs={{0,1},{1,2},{2,3},{3,0},{4,5},{5,6},{6,7},{7,4},{8,9},{9,10},{10,1... | collective-permute-start | bytes 147464 | tf_op jit(solution)/shard_map/ppermute | solution.py:338
  50.8 5.3 %collective-permute-start.5 = (f32[24,512]{1,0:T(8,128)S(1)}, f32[24,512]{1,0:T(8,128)S(1)}, u32[]{:S(2)}, u32[]{:S(2)}) collective-permute-start(f32[24,512]{1,0:T(8,128)S(1)} %get-tuple-element.44), channel_id=1, source_target_pairs={{0,3},{1,0},{2,1},{3,2},{4,7},{5,4},{6,5},{7,6},{8,11},{9,8},{10,9... | collective-permute-start | bytes 147464 | tf_op jit(solution)/shard_map/ppermute | solution.py:338
  56.1 6.8 %collective-permute-start.6 = (f32[72,512]{1,0:T(8,128)S(1)}, f32[72,512]{1,0:T(8,128)S(1)}, u32[]{:S(2)}, u32[]{:S(2)}) collective-permute-start(f32[72,512]{1,0:T(8,128)S(1)} %get-tuple-element.45), channel_id=1, source_target_pairs={{0,4},{4,8},{8,12},{12,16},{16,20},{20,24},{24,28},{28,0},{1,5},{5... | collective-permute-start | bytes 442376 | tf_op jit(solution)/shard_map/ppermute | solution.py:338
  56.2 6.7 %collective-permute-start.7 = (f32[72,512]{1,0:T(8,128)S(1)}, f32[72,512]{1,0:T(8,128)S(1)}, u32[]{:S(2)}, u32[]{:S(2)}) collective-permute-start(f32[72,512]{1,0:T(8,128)S(1)} %get-tuple-element.46), channel_id=1, source_target_pairs={{0,28},{4,0},{8,4},{12,8},{16,12},{20,16},{24,20},{28,24},{1,29},{... | collective-permute-start | bytes 442376 | tf_op jit(solution)/shard_map/ppermute | solution.py:338

commit v3 on v2

--- a/solution.py
+++ b/solution.py
@@ -39,6 +39,10 @@
         copy.start()
     for copy in copies:
         copy.wait()
+
+
+def in_hbm(*arrays):
+    return [pltpu.with_memory_space_constraint(array, pltpu.HBM) for array in arrays]
 
 
 def mul(left, right):
@@ -228,8 +232,9 @@
 
 def residual_kernel(
     weighted_ref, zlow_ref, zhigh_ref, ylow_ref, yhigh_ref, stencil_ref, taps_ref, coef_ref, right_ref, vectors_ref,
-    _, residual_ref, spectral_ref,
+    _, *results,
 ):
+    residual_ref, spectral_ref = results if results[0].shape == right_ref.shape else results[::-1]
     count, nx = weighted_ref.shape
     pieces = [ref[...] for ref in (weighted_ref, zlow_ref, zhigh_ref, ylow_ref, yhigh_ref)]
     missing = stencil_ref.shape[1] - sum(piece.shape[0] for piece in pieces)
@@ -381,7 +386,7 @@
         [(block, F32), (block, F32), (zrim, F32), (zrim, F32)],
         [HBM] * 3, count * nx * 16, 4 * cell,
         [pltpu.SMEM(coef_table.shape, F32), pltpu.VMEM(block, jnp.int32), pltpu.VMEM(block, F32), dma((3,))],
-    )(coef_table, span_index.reshape(count, nx), field)
+    )(*in_hbm(coef_table, span_index.reshape(count, nx), field))
 
     points = point_columns(ly, lz)
     width = points.shape[1]
@@ -391,7 +396,7 @@
         [((4 * count, width), BF16), ((2 * (2 * REACH + 1), 8, nx), F32)],
         [HBM] * 4 + [ANY], count * width * 60, 8 * count * width,
         [pltpu.VMEM(points.shape, jnp.int32)] + [pltpu.VMEM(array.shape, F32) for array in bands] + [dma((4,))],
-    )(jnp.asarray(points), *bands, zlow)
+    )(*in_hbm(jnp.asarray(points), *bands), zlow)
 
     fast = (
         modes % 2 == 0 and npy % 8 == 0 and lz % 16 == 0 and ly % 2 == 0
@@ -406,8 +411,11 @@
             [pltpu.VMEM(array.shape, F32) for array in (xaxis_vectors, yaxis_vectors, zaxis_vectors)]
             + [pltpu.SMEM((nx,), F32), pltpu.VMEM((1, ny), F32), pltpu.VMEM((1, nz), F32), dma((6,))],
         )(
-            xaxis_vectors, yaxis_vectors, zaxis_vectors, xaxis_values,
-            yaxis_values.reshape(1, ny), zaxis_values.reshape(1, nz), taps,
+            *in_hbm(
+                xaxis_vectors, yaxis_vectors, zaxis_vectors, xaxis_values,
+                yaxis_values.reshape(1, ny), zaxis_values.reshape(1, nz),
+            ),
+            taps,
         )
 
         def precondition(received):
@@ -420,7 +428,7 @@
         vectors = call(
             xvectors_kernel, [((2 * nx, nx), BF16)], [HBM], nx * nx * 40, 8 * nx * nx,
             [pltpu.VMEM((nx, nx), F32), dma((1,))],
-        )(xaxis_vectors)[0]
+        )(*in_hbm(xaxis_vectors))[0]
         part = lax.axis_index(BOTH)
         xpart = lax.dynamic_slice_in_dim(xaxis_values, part * modes, modes)
 
@@ -437,10 +445,11 @@
             [(yrim, F32)] * 2, [VMEM] * 3 + [ANY], nx, 4 * nx * 4 * yrim[0],
         )(weighted, from_low, from_high, taps)
         below, above = around(yhigh, "py", 1), around(ylow, "py", -1)
-        residual, spectral = call(
+        *residual, spectral = call(
             residual_kernel,
-            [(block, F32), ((nx, count), F32)],
+            [(block, F32)] * last + [((nx, count), F32)],
             [VMEM] * 10 + [ANY], 6 * count * nx * (nx + 2 * width), 5 * cell + 4 * nx * nx,
+            [pltpu.VMEM(block, F32)] * (not last),
         )(weighted, from_low, from_high, below, above, stencil, taps, coef, right, vectors, tables[0])
         spectral = lax.all_to_all(spectral, BOTH, split_axis=0, concat_axis=0, tiled=True)
         spectral = precondition(spectral)
@@ -455,7 +464,7 @@
             field, residual = call(
                 last_update_kernel, [(block, F32), (block, F32)], [VMEM] * 4, *cost,
                 [pltpu.VMEM(block, F32), dma((2,))], [HBM] * 2,
-            )(spectral, vectors, field, residual)
+            )(spectral, vectors, field, *residual)
     return (field.reshape(solution.shape), residual.reshape(solution.shape))
 
 

time: 94.8 us -> 92.3 us (0.974)
  local copies, waits for them, and re-layouts: 6.04 us -> 0.01 us
  Pallas kernels: 11.2 us -> 12.7 us
  blocking collectives: 54.5 us -> 56 us
    unnamed x30 -> x4, local copies, waits for them, and re-layouts: 6.04 us -> 0.01 us
    all_to_all x4, blocking collectives: 54.5 us -> 56 us  [shards(): lax.all_to_all(spectral, BOTH, split_axis=0, concat_axis=0, tiled=True)]
  transfers between devices with their start and end apart: 8 -> 8, of which waited for: 3 -> 5; matrix products, arithmetic and copies ran while one was open for 0% -> 0% of each run, Pallas kernels for 3% -> 4%
where the time goes in v3:
time: 92.3 us; the launch traced here: 92 us
  blocking collectives  56 us (61%)
  starting transfers between devices  14.4 us (16%)
  Pallas kernels  12.7 us (14%)
  waiting for transfers between devices  8.09 us (9%)
    all_to_all x4, blocking collectives, shards(): lax.all_to_all(spectral, BOTH, split_axis=0, concat_axis=0, tiled=True)  56 us
    ppermute x8, starting transfers between devices, around(): lax.ppermute(value, axis, [(i, (i + step) % count) for i in range(count)])  14.4 us
    ppermute x8, waiting for transfers between devices, around(): lax.ppermute(value, axis, [(i, (i + step) % count) for i in range(count)])  8.09 us
    pallas_call x2, Pallas kernels, shards(): call(residual_kernel, [(block, F32)] * last + [((nx, count), F32)], [VMEM...  3.09 us
    pallas_call x2, Pallas kernels, precondition(): call(lambda *refs: modes_kernel(npy, npz, *refs), [((nx, count), F32)], [...  2.92 us
    pallas_call x1, Pallas kernels, shards(): call(lambda *refs: stencil_kernel(ly, lz, ny, nz, *refs), [((4 * count, w...  1.99 us
    pallas_call x1, Pallas kernels, shards(): call(lambda *refs: tables_kernel(npy, npz, ly, lz, *refs), [((2 * nx, nx)...  1.87 us
  transfers between devices with their start and end apart: 8, of which 5 were waited for; matrix products, arithmetic and copies ran while one was open for 0% of the time, Pallas kernels for 4%

profile of v3, /device:TPU:0, one launch (start us, length us, event | category | flops | bytes accessed | tf_op | source)
XLA Modules:
  0.0 92.0 jit_solution(17498918468132820063)
XLA Ops:
  0.6 1.2 %shard_map.149 = (f32[128,512]{1,0:T(8,128)S(1)}, f32[128,512]{1,0:T(8,128)S(1)}, f32[24,512]{1,0:T(8,128)S(1)}, f32[24,512]{1,0:T(8,128)S(1)}) custom-call(f32[8]{0:T(128)} %refs_0_.3, s32[128,512]{1,0:T(8,128)} %bitcast.30, f32[128,512]{1,0:T(8,128)} %bitcast.20), custom_call_target="tpu_custom_call" | custom-call | flops 1048576 | bytes 1048576 | tf_op jit(solution)/shard_map/pallas_call | solution.py:384
  1.8 3.1 %collective-permute-start = (f32[24,512]{1,0:T(8,128)S(1)}, f32[24,512]{1,0:T(8,128)S(1)}, u32[]{:S(2)}, u32[]{:S(2)}) collective-permute-start(f32[24,512]{1,0:T(8,128)S(1)} %get-tuple-element.34), channel_id=1, source_target_pairs={{0,1},{1,2},{2,3},{3,0},{4,5},{5,6},{6,7},{7,4},{8,9},{9,10},{10,1... | collective-permute-start | bytes 147464 | tf_op jit(solution)/shard_map/ppermute | solution.py:343
  4.9 2.1 %collective-permute-start.1 = (f32[24,512]{1,0:T(8,128)S(1)}, f32[24,512]{1,0:T(8,128)S(1)}, u32[]{:S(2)}, u32[]{:S(2)}) collective-permute-start(f32[24,512]{1,0:T(8,128)S(1)} %get-tuple-element.26.refs_4_), channel_id=1, source_target_pairs={{0,3},{1,0},{2,1},{3,2},{4,7},{5,4},{6,5},{7,6},{8,11},{9,8},{10,9... | collective-permute-start | bytes 147464 | tf_op jit(solution)/shard_map/ppermute | solution.py:343
  7.0 2.0 %shard_map.150 = (bf16[512,384]{1,0:T(8,128)(2,1)S(1)}, f32[14,8,512]{2,1,0:T(8,128)S(1)}) custom-call(s32[2,384]{1,0:T(2,128)} %constant.2.clone.refs_0_, f32[7,2,8]{2,1,0:T(2,128)} %bitcast.32, f32[7,2,16]{2,1,0:T(2,128)} %bitcast.33, f32[7,2,512]{2,1,0:T(2,128)} %bitcast.31, f32[24,512]{1,0:T(8,128)S(1)} %get-tuple-element.26.refs_4_), custom_call_target="tpu_custom_call" | custom-call | flops 2949120 | bytes 393216 | tf_op jit(solution)/shard_map/pallas_call | solution.py:394
  9.0 0.1 collective-permute-done.refs_1_.zlow_ref
  9.1 0.4 collective-permute-done.1.refs_2_.zhigh_ref
  9.6 0.1 collective-permute-start.2
  9.6 2.6 %collective-permute-start.3 = (f32[72,512]{1,0:T(8,128)S(1)}, f32[72,512]{1,0:T(8,128)S(1)}, u32[]{:S(2)}, u32[]{:S(2)}) collective-permute-start(f32[72,512]{1,0:T(8,128)S(1)} %get-tuple-element.36), channel_id=1, source_target_pairs={{0,28},{4,0},{8,4},{12,8},{16,12},{20,16},{24,20},{28,24},{1,29},{... | collective-permute-start | bytes 442376 | tf_op jit(solution)/shard_map/ppermute | solution.py:343
  12.3 1.9 %shard_map.151 = (bf16[1024,512]{1,0:T(8,128)(2,1)S(1)}, bf16[512,512]{1,0:T(8,128)(2,1)S(1)}, bf16[512,512]{1,0:T(8,128)(2,1)S(1)}, bf16[64,256]{1,0:T(8,128)(2...) custom-call(f32[512,512]{1,0:T(8,128)} %refs_0_.4, f32[64,64]{1,0:T(8,128)} %refs_1_.1, f32[64,64]{1,0:T(8,128)} %refs_2_.1, ...), custom_call_target="tpu_custom_call" | custom-call | flops 2097152 | bytes 1048576 | tf_op jit(solution)/shard_map/pallas_call | solution.py:407
  14.1 0.9 %collective-permute-done.2.ylow_ref = f32[72,512]{1,0:T(8,128)S(1)} collective-permute-done((f32[72,512]{1,0:T(8,128)S(1)}, f32[72,512]{1,0:T(8,128)S(1)}, u32[]{:S(2)}, u32[]{:S(2)}) %collective-permute-start.2) | collective-permute-done | bytes 147488 | tf_op jit(solution)/shard_map/ppermute | solution.py:343
  15.1 0.0 collective-permute-done.3.yhigh_ref
  15.1 0.0 copy-done
  15.1 1.5 %shard_map.153 = f32[512,128]{1,0:T(8,128)S(1)} custom-call(f32[128,512]{1,0:T(8,128)S(1)} %get-tuple-element.33.refs_0_.weighted_ref, f32[24,512]{1,0:T(8,128)S(1)} %collective-permute-done.refs_1_.zlow_ref, f32[24,512]{1,0:T(8,128)S(1)} %collective-permute-done.1.refs_2_.zhigh_ref, f32[72,512]{1,0:T(8,128)S(1)} %collective-permute-done.2.ylow_ref, ...), custom_call_target="tpu_custom_call" | custom-call | flops 503316480 | bytes 2359296 | tf_op jit(solution)/shard_map/pallas_call | solution.py:448
  16.6 16.0 %all_to_all.44 = f32[32,16,128]{2,1,0:T(8,128)S(1)} all-to-all(f32[32,16,128]{2,1,0:T(8,128)S(1)} %bitcast.23), channel_id=1, replica_groups=mesh['py'=8,'pz'=4] {'py','pz'}, dimensions={0} | all-to-all | bytes 524288 | tf_op jit(solution)/shard_map/all_to_all | solution.py:454
  32.7 1.5 %shard_map.154 = f32[512,128]{1,0:T(8,128)S(1)} custom-call(bf16[512,512]{1,0:T(8,128)(2,1)S(1)} %get-tuple-element.28._.refs_0_, bf16[512,512]{1,0:T(8,128)(2,1)S(1)} %get-tuple-element.29.refs_1_, bf16[64,256]{1,0:T(8,128)(2,1)S(1)} %get-tuple-element.30.refs_2_, bf16[64,256]{1,0:T(8,128)(2,1)S(1)} %get-tuple-element.31.refs_3_, ...), custom_call_target="tpu_custom_call" | custom-call | flops 402653184 | bytes 524288 | tf_op jit(solution)/shard_map/pallas_call | solution.py:422
  34.1 0.0 copy-start.1
  34.1 12.7 %all_to_all.45 = f32[32,16,128]{2,1,0:T(8,128)S(1)} all-to-all(f32[32,16,128]{2,1,0:T(8,128)S(1)} %bitcast.28), channel_id=1, replica_groups=mesh['py'=8,'pz'=4] {'py','pz'}, dimensions={0} | all-to-all | bytes 524288 | tf_op jit(solution)/shard_map/all_to_all | solution.py:456
  46.9 0.0 copy-done.1
  46.9 0.4 shard_map.155
  47.3 1.1 %collective-permute-start.4 = (f32[24,512]{1,0:T(8,128)S(1)}, f32[24,512]{1,0:T(8,128)S(1)}, u32[]{:S(2)}, u32[]{:S(2)}) collective-permute-start(f32[24,512]{1,0:T(8,128)S(1)} %get-tuple-element.41), channel_id=1, source_target_pairs={{0,1},{1,2},{2,3},{3,0},{4,5},{5,6},{6,7},{7,4},{8,9},{9,10},{10,1... | collective-permute-start | bytes 147464 | tf_op jit(solution)/shard_map/ppermute | solution.py:343
  48.5 2.8 %collective-permute-start.5 = (f32[24,512]{1,0:T(8,128)S(1)}, f32[24,512]{1,0:T(8,128)S(1)}, u32[]{:S(2)}, u32[]{:S(2)}) collective-permute-start(f32[24,512]{1,0:T(8,128)S(1)} %get-tuple-element.42), channel_id=1, source_target_pairs={{0,3},{1,0},{2,1},{3,2},{4,7},{5,4},{6,5},{7,6},{8,11},{9,8},{10,9... | collective-permute-start | bytes 147464 | tf_op jit(solution)/shard_map/ppermute | solution.py:343
  51.2 2.5 %collective-permute-done.4.refs_1_.zlow_ref = f32[24,512]{1,0:T(8,128)S(1)} collective-permute-done((f32[24,512]{1,0:T(8,128)S(1)}, f32[24,512]{1,0:T(8,128)S(1)}, u32[]{:S(2)}, u32[]{:S(2)}) %collective-permute-start.4) | collective-permute-done | bytes 49184 | tf_op jit(solution)/shard_map/ppermute | solution.py:343
  53.7 0.0 collective-permute-done.5.refs_2_.zhigh_ref
  53.8 0.1 collective-permute-start.6
  53.8 2.6 %collective-permute-start.7 = (f32[72,512]{1,0:T(8,128)S(1)}, f32[72,512]{1,0:T(8,128)S(1)}, u32[]{:S(2)}, u32[]{:S(2)}) collective-permute-start(f32[72,512]{1,0:T(8,128)S(1)} %get-tuple-element.44), channel_id=1, source_target_pairs={{0,28},{4,0},{8,4},{12,8},{16,12},{20,16},{24,20},{28,24},{1,29},{... | collective-permute-start | bytes 442376 | tf_op jit(solution)/shard_map/ppermute | solution.py:343
  56.4 4.1 %collective-permute-done.6.ylow_ref = f32[72,512]{1,0:T(8,128)S(1)} collective-permute-done((f32[72,512]{1,0:T(8,128)S(1)}, f32[72,512]{1,0:T(8,128)S(1)}, u32[]{:S(2)}, u32[]{:S(2)}) %collective-permute-start.6) | collective-permute-done | bytes 147488 | tf_op jit(solution)/shard_map/ppermute | solution.py:343
  60.6 0.0 collective-permute-done.7.yhigh_ref
  60.6 1.5 %shard_map.157 = (f32[128,512]{1,0:T(8,128)S(1)}, f32[512,128]{1,0:T(8,128)S(1)}) custom-call(f32[128,512]{1,0:T(8,128)S(1)} %get-tuple-element.40.refs_0_.weighted_ref, f32[24,512]{1,0:T(8,128)S(1)} %collective-permute-done.4.refs_1_.zlow_ref, f32[24,512]{1,0:T(8,128)S(1)} %collective-permute-done.5.refs_2_.zhigh_ref, ...), custom_call_target="tpu_custom_call" | custom-call | flops 503316480 | bytes 2359296 | tf_op jit(solution)/shard_map/pallas_call | solution.py:448
  62.1 14.5 %all_to_all.46 = f32[32,16,128]{2,1,0:T(8,128)S(1)} all-to-all(f32[32,16,128]{2,1,0:T(8,128)S(1)} %bitcast.29), channel_id=1, replica_groups=mesh['py'=8,'pz'=4] {'py','pz'}, dimensions={0} | all-to-all | bytes 524288 | tf_op jit(solution)/shard_map/all_to_all | solution.py:454
  76.7 1.5 %shard_map.158 = f32[512,128]{1,0:T(8,128)S(1)} custom-call(bf16[512,512]{1,0:T(8,128)(2,1)S(1)} %get-tuple-element.28._.refs_0_, bf16[512,512]{1,0:T(8,128)(2,1)S(1)} %get-tuple-element.29.refs_1_, bf16[64,256]{1,0:T(8,128)(2,1)S(1)} %get-tuple-element.30.refs_2_, bf16[64,256]{1,0:T(8,128)(2,1)S(1)} %get-tuple-element.31.refs_3_, ...), custom_call_target="tpu_custom_call" | custom-call | flops 402653184 | bytes 524288 | tf_op jit(solution)/shard_map/pallas_call | solution.py:422
  78.1 12.7 %all_to_all.47 = f32[32,16,128]{2,1,0:T(8,128)S(1)} all-to-all(f32[32,16,128]{2,1,0:T(8,128)S(1)} %bitcast.26), channel_id=1, replica_groups=mesh['py'=8,'pz'=4] {'py','pz'}, dimensions={0} | all-to-all | bytes 524288 | tf_op jit(solution)/shard_map/all_to_all | solution.py:456
  90.8 1.1 %shard_map.159 = (f32[128,512]{1,0:T(8,128)}, f32[128,512]{1,0:T(8,128)}) custom-call(f32[512,128]{1,0:T(8,128)S(1)} %bitcast.22, bf16[1024,512]{1,0:T(8,128)(2,1)S(1)} %get-tuple-element.39.vectors_ref.refs_1_, f32[128,512]{1,0:T(8,128)S(1)} %get-tuple-element.46.field_ref, f32[128,512]{1,0:T(8,128)S(1)} %get-tuple-element.47.residual_ref), custom_call_target="tpu_custom_call" | custom-call | flops 201326592 | bytes 2097152 | tf_op jit(solution)/shard_map/pallas_call | solution.py:464
  (3 shorter events, 0.1 us)
Async XLA Ops:
  1.8 7.3 %collective-permute-start = (f32[24,512]{1,0:T(8,128)S(1)}, f32[24,512]{1,0:T(8,128)S(1)}, u32[]{:S(2)}, u32[]{:S(2)}) collective-permute-start(f32[24,512]{1,0:T(8,128)S(1)} %get-tuple-element.34), channel_id=1, source_target_pairs={{0,1},{1,2},{2,3},{3,0},{4,5},{5,6},{6,7},{7,4},{8,9},{9,10},{10,1... | collective-permute-start | bytes 147464 | tf_op jit(solution)/shard_map/ppermute | solution.py:343
  4.9 4.6 %collective-permute-start.1 = (f32[24,512]{1,0:T(8,128)S(1)}, f32[24,512]{1,0:T(8,128)S(1)}, u32[]{:S(2)}, u32[]{:S(2)}) collective-permute-start(f32[24,512]{1,0:T(8,128)S(1)} %get-tuple-element.26.refs_4_), channel_id=1, source_target_pairs={{0,3},{1,0},{2,1},{3,2},{4,7},{5,4},{6,5},{7,6},{8,11},{9,8},{10,9... | collective-permute-start | bytes 147464 | tf_op jit(solution)/shard_map/ppermute | solution.py:343
  9.6 5.5 %collective-permute-start.2 = (f32[72,512]{1,0:T(8,128)S(1)}, f32[72,512]{1,0:T(8,128)S(1)}, u32[]{:S(2)}, u32[]{:S(2)}) collective-permute-start(f32[72,512]{1,0:T(8,128)S(1)} %get-tuple-element.35), channel_id=1, source_target_pairs={{0,4},{4,8},{8,12},{12,16},{16,20},{20,24},{24,28},{28,0},{1,5},{5... | collective-permute-start | bytes 442376 | tf_op jit(solution)/shard_map/ppermute | solution.py:343
  9.6 5.5 %collective-permute-start.3 = (f32[72,512]{1,0:T(8,128)S(1)}, f32[72,512]{1,0:T(8,128)S(1)}, u32[]{:S(2)}, u32[]{:S(2)}) collective-permute-start(f32[72,512]{1,0:T(8,128)S(1)} %get-tuple-element.36), channel_id=1, source_target_pairs={{0,28},{4,0},{8,4},{12,8},{16,12},{20,16},{24,20},{28,24},{1,29},{... | collective-permute-start | bytes 442376 | tf_op jit(solution)/shard_map/ppermute | solution.py:343
  12.3 2.8 %copy-start = (f32[8,16,512]{2,1,0:T(8,128)S(1)}, f32[8,16,512]{2,1,0:T(8,128)}, u32[]{:S(2)}) copy-start(f32[8,16,512]{2,1,0:T(8,128)} %param.15) | copy-start | bytes 786436
  34.1 12.7 %copy-start.1 = (f32[8,16,512]{2,1,0:T(8,128)S(1)}, f32[8,16,512]{2,1,0:T(8,128)}, u32[]{:S(2)}) copy-start(f32[8,16,512]{2,1,0:T(8,128)} %param.14) | copy-start | bytes 786436
  47.3 6.4 %collective-permute-start.4 = (f32[24,512]{1,0:T(8,128)S(1)}, f32[24,512]{1,0:T(8,128)S(1)}, u32[]{:S(2)}, u32[]{:S(2)}) collective-permute-start(f32[24,512]{1,0:T(8,128)S(1)} %get-tuple-element.41), channel_id=1, source_target_pairs={{0,1},{1,2},{2,3},{3,0},{4,5},{5,6},{6,7},{7,4},{8,9},{9,10},{10,1... | collective-permute-start | bytes 147464 | tf_op jit(solution)/shard_map/ppermute | solution.py:343
  48.5 5.3 %collective-permute-start.5 = (f32[24,512]{1,0:T(8,128)S(1)}, f32[24,512]{1,0:T(8,128)S(1)}, u32[]{:S(2)}, u32[]{:S(2)}) collective-permute-start(f32[24,512]{1,0:T(8,128)S(1)} %get-tuple-element.42), channel_id=1, source_target_pairs={{0,3},{1,0},{2,1},{3,2},{4,7},{5,4},{6,5},{7,6},{8,11},{9,8},{10,9... | collective-permute-start | bytes 147464 | tf_op jit(solution)/shard_map/ppermute | solution.py:343
  53.8 6.8 %collective-permute-start.6 = (f32[72,512]{1,0:T(8,128)S(1)}, f32[72,512]{1,0:T(8,128)S(1)}, u32[]{:S(2)}, u32[]{:S(2)}) collective-permute-start(f32[72,512]{1,0:T(8,128)S(1)} %get-tuple-element.43), channel_id=1, source_target_pairs={{0,4},{4,8},{8,12},{12,16},{16,20},{20,24},{24,28},{28,0},{1,5},{5... | collective-permute-start | bytes 442376 | tf_op jit(solution)/shard_map/ppermute | solution.py:343
  53.8 6.7 %collective-permute-start.7 = (f32[72,512]{1,0:T(8,128)S(1)}, f32[72,512]{1,0:T(8,128)S(1)}, u32[]{:S(2)}, u32[]{:S(2)}) collective-permute-start(f32[72,512]{1,0:T(8,128)S(1)} %get-tuple-element.44), channel_id=1, source_target_pairs={{0,28},{4,0},{8,4},{12,8},{16,12},{20,16},{24,20},{28,24},{1,29},{... | collective-permute-start | bytes 442376 | tf_op jit(solution)/shard_map/ppermute | solution.py:343

commit v4 on v3

--- a/solution.py
+++ b/solution.py
@@ -72,9 +72,11 @@
 
 
 def coefficient_kernel(
-    ly, lz, table_ref, span_ref, field_ref, coef_ref, weighted_ref, low_ref, high_ref, table, span, field, sem
+    ly, lz, table_ref, span_ref, field_ref, coef_ref, weighted_ref, even_ref, odd_ref, table, span, field, sem
 ):
     fetch(((table_ref, table), (span_ref, span), (field_ref, field)), sem)
+    first = lax.rem(lax.axis_index("pz"), 2) == 0
+    half = ly * REACH
     entries = [table[entry] for entry in range(table_ref.shape[0])]
     for start in range(0, span.shape[0], lz):
         rows = pl.ds(start, lz)
@@ -85,18 +87,31 @@
         coef_ref[rows, :] = coef
         weighted = coef * field[rows, :]
         weighted_ref[rows, :] = weighted
-        rim = pl.ds(start // lz * REACH, REACH)
-        low_ref[rim, :] = weighted[:REACH]
-        high_ref[rim, :] = weighted[lz - REACH :]
-
-
-def y_rims_kernel(ly, lz, weighted_ref, zlow_ref, zhigh_ref, _, low_ref, high_ref):
+        for value, at in ((weighted, 0), (coef, half)):
+            rim = pl.ds(at + start // lz * REACH, REACH)
+            low, high = value[:REACH], value[lz - REACH :]
+            even_ref[rim, :] = jnp.where(first, high, low)
+            odd_ref[rim, :] = jnp.where(first, low, high)
+
+
+def store_y_rims(ly, lz, weighted_ref, zlow, zhigh, low_ref, high_ref):
     own, side = REACH * lz, REACH * REACH
     for ref, start, zstart in ((low_ref, 0, 0), (high_ref, (ly - REACH) * lz, (ly - REACH) * REACH)):
         ref[own:, :] = jnp.zeros((ref.shape[0] - own, ref.shape[1]), F32)
         ref[0:own, :] = weighted_ref[start : start + own, :]
-        ref[own : own + side, :] = zlow_ref[zstart : zstart + side, :]
-        ref[own + side : own + 2 * side, :] = zhigh_ref[zstart : zstart + side, :]
+        ref[own : own + side, :] = zlow[zstart : zstart + side, :]
+        ref[own + side : own + 2 * side, :] = zhigh[zstart : zstart + side, :]
+
+
+def y_rims_kernel(ly, lz, weighted_ref, even_ref, odd_ref, _, zlow_ref, zhigh_ref, low_ref, high_ref):
+    first = lax.rem(lax.axis_index("pz"), 2) == 0
+    zlow_ref[...] = jnp.where(first, odd_ref[...], even_ref[...])
+    zhigh_ref[...] = jnp.where(first, even_ref[...], odd_ref[...])
+    store_y_rims(ly, lz, weighted_ref, zlow_ref, zhigh_ref, low_ref, high_ref)
+
+
+def next_y_rims_kernel(ly, lz, weighted_ref, zlow_ref, zhigh_ref, low_ref, high_ref):
+    store_y_rims(ly, lz, weighted_ref, zlow_ref, zhigh_ref, low_ref, high_ref)
 
 
 def point_columns(ly, lz):
@@ -169,7 +184,7 @@
 
 def tables_kernel(
     npy, npz, ly, lz, xvec_hbm, yvec_hbm, zvec_hbm, xval_hbm, yval_hbm, zval_hbm, _,
-    xout_ref, zhigh_ref, zlow_ref, ydown_ref, yup_ref, sums_ref,
+    xout_ref, zhigh_ref, zlow_ref, ydown_ref, yup_ref, sums_ref, rimhigh_ref, rimlow_ref,
     xvec_ref, yvec_ref, zvec_ref, xval_ref, yval_ref, zval_ref, sem,
 ):
     fetch(
@@ -200,6 +215,19 @@
                 zhigh_ref[to] = high[block * lz : (block + 1) * lz, :]
                 zlow_ref[to] = low[block * lz : (block + 1) * lz, :]
 
+    shape = (rimhigh_ref.shape[0], 1)
+    row = lax.broadcasted_iota(jnp.int32, shape, 0)
+    block, spot = lax.div(row, LANES // 2), lax.rem(row, LANES // 2)
+    above = spot >= ly * REACH
+    spot = jnp.where(above, spot - ly * REACH, spot)
+    yrow = jnp.where(spot < ly * REACH, lax.div(spot, REACH), 2 * ly)
+    z = block * lz + lax.rem(spot, REACH) + jnp.where(above, lz, -REACH)
+    rim = exact((lax.broadcasted_iota(jnp.int32, (shape[0], nz), 1) == z).astype(F32), pair)
+    late = (lax.broadcasted_iota(jnp.int32, rim.shape, 1) >= nz).astype(jnp.int32)
+    for chunk in range(ly // 2):
+        columns = pl.ds(chunk * 2 * nz, 2 * nz)
+        rimhigh_ref[:, columns], rimlow_ref[:, columns] = split(jnp.where(yrow - 2 * chunk == late, rim, 0.0))
+
     def y_of(p):
         spot = lax.div(p, npy)
         return lax.rem(p, npy) * ly + 2 * lax.rem(spot, ly // 2) + lax.div(spot, ly // 2)
@@ -231,12 +259,11 @@
 
 
 def residual_kernel(
-    weighted_ref, zlow_ref, zhigh_ref, ylow_ref, yhigh_ref, stencil_ref, taps_ref, coef_ref, right_ref, vectors_ref,
-    _, *results,
+    zrim, weighted_ref, zlow_ref, zhigh_ref, ylow_ref, yhigh_ref, stencil_ref, taps_ref, coef_ref, right_ref, vectors_ref,
+    _, spectral_ref, residual_ref,
 ):
-    residual_ref, spectral_ref = results if results[0].shape == right_ref.shape else results[::-1]
     count, nx = weighted_ref.shape
-    pieces = [ref[...] for ref in (weighted_ref, zlow_ref, zhigh_ref, ylow_ref, yhigh_ref)]
+    pieces = [weighted_ref[...], zlow_ref[:zrim, :], zhigh_ref[:zrim, :], ylow_ref[...], yhigh_ref[...]]
     missing = stencil_ref.shape[1] - sum(piece.shape[0] for piece in pieces)
     if missing:
         pieces.append(jnp.zeros((missing, nx), F32))
@@ -259,7 +286,8 @@
     spectral_ref[...] = (product[:nx, :count] + product[:nx, count:]) + (product[nx:, :count] + product[nx:, count:])
 
 
-def modes_kernel(npy, npz, zhigh_ref, zlow_ref, ydown_ref, yup_ref, sums_ref, in_ref, out_ref):
+def modes_kernel(npy, npz, rims, *refs):
+    zhigh_ref, zlow_ref, ydown_ref, yup_ref, sums_ref, *rim_refs, in_ref, out_ref = refs
     count = in_ref.shape[0] // (npy * npz)
     lanes = in_ref.shape[1]
     nz = sums_ref.shape[1] // count
@@ -270,12 +298,12 @@
     ]
     zhigh, zlow = zhigh_ref[...], zlow_ref[...]
 
-    def three(value, product):
+    def three(value, product, whigh, wlow):
         high, low = split(value)
-        both = product(jnp.concatenate([high, low], axis=0), zhigh)
-        return both[: count * npy] + both[count * npy :] + product(high, zlow)
-
-    part = three(jnp.concatenate(rows, axis=0), mul)
+        both = product(jnp.concatenate([high, low], axis=0), whigh)
+        return both[: count * npy] + both[count * npy :] + product(high, wlow)
+
+    part = three(jnp.concatenate(rows, axis=0), mul, zhigh, zlow)
     late = lax.broadcasted_iota(jnp.int32, (npy, 2 * nz), 1) >= nz
 
     def swap(value):
@@ -307,19 +335,35 @@
         odd = [block[half + c * npy : half + (c + 1) * npy] for c in range(chunks)]
         rows.append(jnp.concatenate([jnp.where(late, swap(odd[c]), even[c]) for c in range(chunks)], axis=1))
         rows.append(jnp.concatenate([jnp.where(late, odd[c], swap(even[c])) for c in range(chunks)], axis=1))
-    back = three(jnp.concatenate(rows, axis=0), mul_t)
+    spectral = jnp.concatenate(rows, axis=0)
+    back = three(spectral, mul_t, zhigh, zlow)
+    size = out_ref.shape[0] // (npy * npz)
     for j in range(count):
         for b in range(npz):
-            out_ref[pl.ds(b * count + j, npy, stride=npz * count), :] = back[
+            out_ref[pl.ds(b * size + j, npy, stride=npz * size), :] = back[
                 j * npy : (j + 1) * npy, b * lanes : (b + 1) * lanes
             ]
+    if rims:
+        side = three(spectral, mul_t, rim_refs[0][...], rim_refs[1][...])
+        for j in range(count // 2):
+            for b in range(0, npz, 2):
+                first, second = (
+                    side[k * npy : (k + 1) * npy, b * lanes // 2 : b * lanes // 2 + lanes] for k in (j, j + count // 2)
+                )
+                at = b * size + count + j
+                out_ref[pl.ds(at, npy, stride=npz * size), :] = jnp.where(late, swap(second), first)
+                out_ref[pl.ds(at + size, npy, stride=npz * size), :] = jnp.where(late, second, swap(first))
+
+
+def transformed(points, vectors_ref):
+    rows, nx = points.shape
+    high, low = split(points)
+    both = mul(jnp.concatenate([high, low], axis=0), vectors_ref[:nx, :])
+    return both[:rows] + both[rows:] + mul(high, vectors_ref[nx:, :])
 
 
 def from_modes(spectral_ref, vectors_ref):
-    nx, count = spectral_ref.shape
-    high, low = split(spectral_ref[...].T)
-    both = mul(jnp.concatenate([high, low], axis=0), vectors_ref[:nx, :])
-    return both[:count] + both[count:] + mul(high, vectors_ref[nx:, :])
+    return transformed(spectral_ref[...].T, vectors_ref)
 
 
 def update_kernel(ly, lz, spectral_ref, vectors_ref, field_ref, coef_ref, updated_ref, weighted_ref, low_ref, high_ref):
@@ -330,12 +374,42 @@
     store_z_rims(ly, lz, weighted, low_ref, high_ref)
 
 
+def rim_update_kernel(
+    ly, lz, devices, spectral_ref, vectors_ref, field_ref, coef_ref, before_low_ref, before_high_ref,
+    updated_ref, weighted_ref, zlow_ref, zhigh_ref, low_ref, high_ref,
+):
+    nx = vectors_ref.shape[1]
+    modes = nx // devices
+    size = spectral_ref.shape[0] // devices
+    own, rims = [], []
+    for d in range(devices):
+        own.append(spectral_ref[d * size : d * size + modes, :])
+        rim = spectral_ref[d * size + modes : (d + 1) * size, :]
+        rims += [rim, pltpu.roll(rim, LANES // 2, 1)]
+    points = [jnp.concatenate(own, axis=0).T, jnp.concatenate(rims, axis=0).T[: LANES // 2]]
+    update = transformed(jnp.concatenate(points, axis=0), vectors_ref)
+    count, half = ly * lz, ly * REACH
+    updated = field_ref[...] + update[:count]
+    updated_ref[...] = updated
+    weighted_ref[...] = coef_ref[...] * updated
+    for side, (ref, before_ref) in enumerate(((zlow_ref, before_low_ref), (zhigh_ref, before_high_ref))):
+        start = count + side * half
+        ref[...] = before_ref[:half, :] + before_ref[half:, :] * update[start : start + half]
+    store_y_rims(ly, lz, weighted_ref, zlow_ref, zhigh_ref, low_ref, high_ref)
+
+
 def last_update_kernel(spectral_ref, vectors_ref, field_ref, residual_ref, updated_hbm, residual_hbm, held, sem):
     leaving = pltpu.make_async_copy(residual_ref, residual_hbm, sem.at[0])
     leaving.start()
     held[...] = field_ref[...] + from_modes(spectral_ref, vectors_ref)
     fetch(((held, updated_hbm),), sem.at[pl.ds(1, 1)])
     leaving.wait()
+
+
+def pairwise(value, axis, odd):
+    count = lax.axis_size(axis)
+    other = [((i + odd) ^ 1) - odd for i in range(count)]
+    return lax.ppermute(value, axis, [(i, j if 0 <= j < count else i) for i, j in enumerate(other)])
 
 
 def around(value, axis, step):
@@ -378,12 +452,13 @@
     field = solution.reshape(count, nx)
     right = right_side.reshape(count, nx)
     block, zrim, yrim = (count, nx), (ly * REACH, nx), (up8(REACH * lz + 2 * REACH * REACH), nx)
+    zrims = (2 * ly * REACH, nx)
     cell = count * nx * 4
     dma = pltpu.SemaphoreType.DMA
 
-    coef, weighted, zlow, zhigh = call(
+    coef, weighted, even, odd = call(
         lambda *refs: coefficient_kernel(ly, lz, *refs),
-        [(block, F32), (block, F32), (zrim, F32), (zrim, F32)],
+        [(block, F32), (block, F32), (zrims, F32), (zrims, F32)],
         [HBM] * 3, count * nx * 16, 4 * cell,
         [pltpu.SMEM(coef_table.shape, F32), pltpu.VMEM(block, jnp.int32), pltpu.VMEM(block, F32), dma((3,))],
     )(*in_hbm(coef_table, span_index.reshape(count, nx), field))
@@ -396,17 +471,18 @@
         [((4 * count, width), BF16), ((2 * (2 * REACH + 1), 8, nx), F32)],
         [HBM] * 4 + [ANY], count * width * 60, 8 * count * width,
         [pltpu.VMEM(points.shape, jnp.int32)] + [pltpu.VMEM(array.shape, F32) for array in bands] + [dma((4,))],
-    )(*in_hbm(jnp.asarray(points), *bands), zlow)
+    )(*in_hbm(jnp.asarray(points), *bands), even)
 
     fast = (
-        modes % 2 == 0 and npy % 8 == 0 and lz % 16 == 0 and ly % 2 == 0
+        modes % 16 == 0 and npz % 2 == 0 and 2 * ly * REACH <= LANES // 2 and npy % 8 == 0 and lz % 16 == 0 and ly % 2 == 0
         and 2 * nz == LANES and 2 * ny == LANES and count == LANES and nx % LANES == 0
     )
     if fast:
-        zmat, ymat = (npz * count, ly * nz), (ny, 4 * ny)
+        zmat, ymat, rmat = (npz * count, ly * nz), (ny, 4 * ny), (npz * LANES // 2, ly * nz)
         vectors, *tables = call(
             lambda *refs: tables_kernel(npy, npz, ly, lz, *refs),
-            [((2 * nx, nx), BF16), (zmat, BF16), (zmat, BF16), (ymat, BF16), (ymat, BF16), ((ny, modes * nz), F32)],
+            [((2 * nx, nx), BF16), (zmat, BF16), (zmat, BF16), (ymat, BF16), (ymat, BF16), ((ny, modes * nz), F32)]
+            + [(rmat, BF16)] * 2,
             [HBM] * 6 + [ANY], npz * count * ly * nz * 8, npz * count * ly * nz * 4,
             [pltpu.VMEM(array.shape, F32) for array in (xaxis_vectors, yaxis_vectors, zaxis_vectors)]
             + [pltpu.SMEM((nx,), F32), pltpu.VMEM((1, ny), F32), pltpu.VMEM((1, nz), F32), dma((6,))],
@@ -418,11 +494,12 @@
             taps,
         )
 
-        def precondition(received):
+        def precondition(received, rims):
+            size = modes * 3 // 2 if rims else modes
             return call(
-                lambda *refs: modes_kernel(npy, npz, *refs),
-                [((nx, count), F32)], [VMEM] * 6, 6 * 2 * count * nx * ly * nz, 2 * cell,
-            )(*tables, received)[0]
+                lambda *refs: modes_kernel(npy, npz, rims, *refs),
+                [((devices * size, count), F32)], [VMEM] * (8 if rims else 6), 6 * 2 * count * nx * ly * nz, 2 * cell,
+            )(*(tables if rims else tables[:5]), received)[0]
     else:
         tables = [taps]
         vectors = call(
@@ -432,39 +509,48 @@
         part = lax.axis_index(BOTH)
         xpart = lax.dynamic_slice_in_dim(xaxis_values, part * modes, modes)
 
-        def precondition(received):
+        def precondition(received, rims):
             return plain_modes(
                 received, npy, npz, ly, lz, xpart, yaxis_values, zaxis_values, yaxis_vectors, zaxis_vectors
             )
 
+    even, odd = pairwise(even, "pz", 0), pairwise(odd, "pz", 1)
+    zlow, zhigh, ylow, yhigh = call(
+        lambda *refs: y_rims_kernel(ly, lz, *refs),
+        [(zrims, F32)] * 2 + [(yrim, F32)] * 2, [VMEM] * 3 + [ANY], nx, 4 * nx * 4 * (yrim[0] + zrims[0]),
+    )(weighted, even, odd, taps)
     for iteration in range(ITERS):
         last = iteration + 1 == ITERS
-        from_low, from_high = around(zhigh, "pz", 1), around(zlow, "pz", -1)
-        ylow, yhigh = call(
-            lambda *refs: y_rims_kernel(ly, lz, *refs),
-            [(yrim, F32)] * 2, [VMEM] * 3 + [ANY], nx, 4 * nx * 4 * yrim[0],
-        )(weighted, from_low, from_high, taps)
         below, above = around(yhigh, "py", 1), around(ylow, "py", -1)
-        *residual, spectral = call(
-            residual_kernel,
-            [(block, F32)] * last + [((nx, count), F32)],
+        spectral, *residual = call(
+            lambda *refs: residual_kernel(zrim[0], *refs),
+            [((nx, count), F32)] + [(block, F32)] * last,
             [VMEM] * 10 + [ANY], 6 * count * nx * (nx + 2 * width), 5 * cell + 4 * nx * nx,
             [pltpu.VMEM(block, F32)] * (not last),
-        )(weighted, from_low, from_high, below, above, stencil, taps, coef, right, vectors, tables[0])
+        )(weighted, zlow, zhigh, below, above, stencil, taps, coef, right, vectors, tables[0])
         spectral = lax.all_to_all(spectral, BOTH, split_axis=0, concat_axis=0, tiled=True)
-        spectral = precondition(spectral)
+        spectral = precondition(spectral, not last)
         spectral = lax.all_to_all(spectral, BOTH, split_axis=0, concat_axis=0, tiled=True)
         cost = (6 * count * nx * nx, 4 * cell + 4 * nx * nx)
-        if not last:
-            field, weighted, zlow, zhigh = call(
-                lambda *refs: update_kernel(ly, lz, *refs),
-                [(block, F32), (block, F32), (zrim, F32), (zrim, F32)], [VMEM] * 4, *cost,
-            )(spectral, vectors, field, coef)
-        else:
+        if last:
             field, residual = call(
                 last_update_kernel, [(block, F32), (block, F32)], [VMEM] * 4, *cost,
                 [pltpu.VMEM(block, F32), dma((2,))], [HBM] * 2,
             )(spectral, vectors, field, *residual)
+        elif fast:
+            field, weighted, zlow, zhigh, ylow, yhigh = call(
+                lambda *refs: rim_update_kernel(ly, lz, devices, *refs),
+                [(block, F32)] * 2 + [(zrim, F32)] * 2 + [(yrim, F32)] * 2, [VMEM] * 6, *cost,
+            )(spectral, vectors, field, coef, zlow, zhigh)
+        else:
+            field, weighted, zlow, zhigh = call(
+                lambda *refs: update_kernel(ly, lz, *refs), [(block, F32)] * 2 + [(zrim, F32)] * 2, [VMEM] * 4, *cost,
+            )(spectral, vectors, field, coef)
+            zlow, zhigh = around(zhigh, "pz", 1), around(zlow, "pz", -1)
+            ylow, yhigh = call(
+                lambda *refs: next_y_rims_kernel(ly, lz, *refs),
+                [(yrim, F32)] * 2, [VMEM] * 3, nx, 4 * nx * 4 * yrim[0],
+            )(weighted, zlow, zhigh)
     return (field.reshape(solution.shape), residual.reshape(solution.shape))
 
 

time: 92.3 us -> 88.3 us (0.957)
  starting transfers between devices: 14.4 us -> 9.13 us
  blocking collectives: 56 us -> 60.8 us
  waiting for transfers between devices: 8.09 us -> 3.8 us
    ppermute x8 -> x4, starting transfers between devices: 14.4 us -> 5.39 us  [around(): lax.ppermute(value, axis, [(i, (i + step) % count) for i in range(count)])]
    all_to_all x4, blocking collectives: 56 us -> 60.8 us  [shards(): lax.all_to_all(spectral, BOTH, split_axis=0, concat_axis=0, tiled=True)]
    ppermute x8 -> x4, waiting for transfers between devices: 8.09 us -> 3.67 us  [around(): lax.ppermute(value, axis, [(i, (i + step) % count) for i in range(count)])]
    ppermute x0 -> x2, starting transfers between devices: none -> 3.74 us  [pairwise(): lax.ppermute(value, axis, [(i, j if 0 <= j < count else i) for i, j in en...]
    pallas_call x7 -> x6, Pallas kernels: 6.5 us -> 7.08 us  [the longest x2 3.33 us: precondition(): call(lambda *refs: modes_kernel(npy, npz, rims, *refs), [((devices * size...]
  transfers between devices with their start and end apart: 8 -> 6, of which waited for: 5 -> 3; matrix products, arithmetic and copies ran while one was open for 0% -> 0% of each run, Pallas kernels for 4% -> 5%
where the time goes in v4:
time: 88.3 us; the launch traced here: 88 us
  blocking collectives  60.8 us (69%)
  Pallas kernels  13.5 us (15%)
  starting transfers between devices  9.13 us (10%)
  waiting for transfers between devices  3.8 us (4%)
    all_to_all x4, blocking collectives, shards(): lax.all_to_all(spectral, BOTH, split_axis=0, concat_axis=0, tiled=True)  60.8 us
    ppermute x4, starting transfers between devices, around(): lax.ppermute(value, axis, [(i, (i + step) % count) for i in range(count)])  5.39 us
    ppermute x2, starting transfers between devices, pairwise(): lax.ppermute(value, axis, [(i, j if 0 <= j < count else i) for i, j in en...  3.74 us
    ppermute x4, waiting for transfers between devices, around(): lax.ppermute(value, axis, [(i, (i + step) % count) for i in range(count)])  3.67 us
    pallas_call x2, Pallas kernels, precondition(): call(lambda *refs: modes_kernel(npy, npz, rims, *refs), [((devices * size...  3.33 us
    pallas_call x2, Pallas kernels, shards(): call(lambda *refs: residual_kernel(zrim[0], *refs), [((nx, count), F32)]...  3.09 us
    pallas_call x1, Pallas kernels, shards(): call(lambda *refs: tables_kernel(npy, npz, ly, lz, *refs), [((2 * nx, nx)...  2.08 us
    pallas_call x1, Pallas kernels, shards(): call(lambda *refs: stencil_kernel(ly, lz, ny, nz, *refs), [((4 * count, w...  2 us
  transfers between devices with their start and end apart: 6, of which 3 were waited for; matrix products, arithmetic and copies ran while one was open for 0% of the time, Pallas kernels for 5%

profile of v4, /device:TPU:0, one launch (start us, length us, event | category | flops | bytes accessed | tf_op | source)
XLA Modules:
  0.0 88.0 jit_solution(12124952384481933601)
XLA Ops:
  0.6 1.2 %shard_map.149 = (f32[128,512]{1,0:T(8,128)S(1)}, f32[128,512]{1,0:T(8,128)S(1)}, f32[48,512]{1,0:T(8,128)S(1)}, f32[48,512]{1,0:T(8,128)S(1)}) custom-call(f32[8]{0:T(128)} %refs_0_.3, s32[128,512]{1,0:T(8,128)} %bitcast.30, f32[128,512]{1,0:T(8,128)} %bitcast.23), custom_call_target="tpu_custom_call" | custom-call | flops 1048576 | bytes 1048576 | tf_op jit(solution)/shard_map/pallas_call | solution.py:459
  1.9 3.1 %collective-permute-start = (f32[48,512]{1,0:T(8,128)S(1)}, f32[48,512]{1,0:T(8,128)S(1)}, u32[]{:S(2)}, u32[]{:S(2)}) collective-permute-start(f32[48,512]{1,0:T(8,128)S(1)} %get-tuple-element.30.refs_4_), channel_id=1, source_target_pairs={{0,1},{1,0},{2,3},{3,2},{4,5},{5,4},{6,7},{7,6},{8,9},{9,8},{10,11... | collective-permute-start | bytes 294920 | tf_op jit(solution)/shard_map/ppermute | solution.py:412
  5.0 0.7 collective-permute-start.1
  5.6 2.0 %shard_map.150 = (bf16[512,384]{1,0:T(8,128)(2,1)S(1)}, f32[14,8,512]{2,1,0:T(8,128)S(1)}) custom-call(s32[2,384]{1,0:T(2,128)} %constant.2.clone.refs_0_, f32[7,2,8]{2,1,0:T(2,128)} %bitcast.32, f32[7,2,16]{2,1,0:T(2,128)} %bitcast.33, f32[7,2,512]{2,1,0:T(2,128)} %bitcast.31, f32[48,512]{1,0:T(8,128)S(1)} %get-tuple-element.30.refs_4_), custom_call_target="tpu_custom_call" | custom-call | flops 2949120 | bytes 393216 | tf_op jit(solution)/shard_map/pallas_call | solution.py:469
  7.6 0.1 collective-permute-done.refs_1_
  7.8 0.0 collective-permute-done.1.refs_2_
  7.8 0.1 collective-permute-start.2
  7.9 2.6 %collective-permute-start.3 = (f32[72,512]{1,0:T(8,128)S(1)}, f32[72,512]{1,0:T(8,128)S(1)}, u32[]{:S(2)}, u32[]{:S(2)}) collective-permute-start(f32[72,512]{1,0:T(8,128)S(1)} %get-tuple-element.44), channel_id=1, source_target_pairs={{0,28},{4,0},{8,4},{12,8},{16,12},{20,16},{24,20},{28,24},{1,29},{... | collective-permute-start | bytes 442376 | tf_op jit(solution)/shard_map/ppermute | solution.py:417
  10.5 0.0 copy-start
  10.5 2.1 %shard_map.151 = (bf16[1024,512]{1,0:T(8,128)(2,1)S(1)}, bf16[512,512]{1,0:T(8,128)(2,1)S(1)}, bf16[512,512]{1,0:T(8,128)(2,1)S(1)}, bf16[64,256]{1,0:T(8,128)(2...) custom-call(f32[512,512]{1,0:T(8,128)} %refs_0_.4, ...), custom_call_target="tpu_custom_call" | custom-call | flops 2097152 | bytes 1048576 | tf_op jit(solution)/shard_map/pallas_call | solution.py:482
  12.6 0.7 collective-permute-done.2.refs_3_
  13.3 0.0 collective-permute-done.3.refs_4_
  13.3 0.0 copy-done
  13.3 1.5 %shard_map.153 = f32[512,128]{1,0:T(8,128)S(1)} custom-call(f32[128,512]{1,0:T(8,128)S(1)} %get-tuple-element.39.refs_0_, f32[48,512]{1,0:T(8,128)S(1)} %get-tuple-element.41.refs_1_.refs_4_, f32[48,512]{1,0:T(8,128)S(1)} %get-tuple-element.42.refs_2_.refs_5_, f32[72,512]{1,0:T(8,128)S(1)} %collective-permute-done.2.refs_3_, ...), custom_call_target="tpu_custom_call" | custom-call | flops 503316480 | bytes 2359296 | tf_op jit(solution)/shard_map/pallas_call | solution.py:525
  14.9 18.8 %all_to_all.44 = f32[32,16,128]{2,1,0:T(8,128)S(1)} all-to-all(f32[32,16,128]{2,1,0:T(8,128)S(1)} %bitcast.22), channel_id=1, replica_groups=mesh['py'=8,'pz'=4] {'py','pz'}, dimensions={0} | all-to-all | bytes 524288 | tf_op jit(solution)/shard_map/all_to_all | solution.py:531
  33.7 1.9 %shard_map.154 = f32[768,128]{1,0:T(8,128)S(1)} custom-call(bf16[512,512]{1,0:T(8,128)(2,1)S(1)} %get-tuple-element.32.refs_10_.refs_0_, bf16[512,512]{1,0:T(8,128)(2,1)S(1)} %get-tuple-element.33.refs_1_, bf16[64,256]{1,0:T(8,128)(2,1)S(1)} %get-tuple-element.34.refs_2_, bf16[64,256]{1,0:T(8,128)(2,1)S(1)} %get-tuple-element.35.refs_3_, ...), custom_call_target="tpu_custom_call" | custom-call | flops 402653184 | bytes 524288 | tf_op jit(solution)/shard_map/pallas_call | solution.py:499
  35.6 0.0 copy-start.1
  35.6 14.4 %all_to_all.45 = f32[32,24,128]{2,1,0:T(8,128)S(1)} all-to-all(f32[32,24,128]{2,1,0:T(8,128)S(1)} %bitcast.18), channel_id=1, replica_groups=mesh['py'=8,'pz'=4] {'py','pz'}, dimensions={0} | all-to-all | bytes 786432 | tf_op jit(solution)/shard_map/all_to_all | solution.py:533
  50.0 0.0 copy-done.1
  50.0 0.6 shard_map.155
  50.6 1.2 %collective-permute-start.4 = (f32[72,512]{1,0:T(8,128)S(1)}, f32[72,512]{1,0:T(8,128)S(1)}, u32[]{:S(2)}, u32[]{:S(2)}) collective-permute-start(f32[72,512]{1,0:T(8,128)S(1)} %get-tuple-element.51), channel_id=1, source_target_pairs={{0,4},{4,8},{8,12},{12,16},{16,20},{20,24},{24,28},{28,0},{1,5},{5... | collective-permute-start | bytes 442376 | tf_op jit(solution)/shard_map/ppermute | solution.py:417
  51.8 1.5 %collective-permute-start.5 = (f32[72,512]{1,0:T(8,128)S(1)}, f32[72,512]{1,0:T(8,128)S(1)}, u32[]{:S(2)}, u32[]{:S(2)}) collective-permute-start(f32[72,512]{1,0:T(8,128)S(1)} %get-tuple-element.52), channel_id=1, source_target_pairs={{0,28},{4,0},{8,4},{12,8},{16,12},{20,16},{24,20},{28,24},{1,29},{... | collective-permute-start | bytes 442376 | tf_op jit(solution)/shard_map/ppermute | solution.py:417
  53.3 2.9 %collective-permute-done.4.refs_3_ = f32[72,512]{1,0:T(8,128)S(1)} collective-permute-done((f32[72,512]{1,0:T(8,128)S(1)}, f32[72,512]{1,0:T(8,128)S(1)}, u32[]{:S(2)}, u32[]{:S(2)}) %collective-permute-start.4) | collective-permute-done | bytes 147488 | tf_op jit(solution)/shard_map/ppermute | solution.py:417
  56.2 0.0 collective-permute-done.5.refs_4_
  56.2 1.5 %shard_map.156 = (f32[512,128]{1,0:T(8,128)S(1)}, f32[128,512]{1,0:T(8,128)S(1)}) custom-call(f32[128,512]{1,0:T(8,128)S(1)} %get-tuple-element.48.refs_0_, f32[24,512]{1,0:T(8,128)S(1)} %get-tuple-element.49.refs_1_, f32[24,512]{1,0:T(8,128)S(1)} %get-tuple-element.50.refs_2_, f32[72,512]{1,0:T(8,128)S(1)} %collective-permute-done.4.refs_3_, ...), custom_call_target="tpu_custom_call" | custom-call | flops 503316480 | bytes 2359296 | tf_op jit(solution)/shard_map/pallas_call | solution.py:525
  57.8 14.9 %all_to_all.46 = f32[32,16,128]{2,1,0:T(8,128)S(1)} all-to-all(f32[32,16,128]{2,1,0:T(8,128)S(1)} %bitcast.29), channel_id=1, replica_groups=mesh['py'=8,'pz'=4] {'py','pz'}, dimensions={0} | all-to-all | bytes 524288 | tf_op jit(solution)/shard_map/all_to_all | solution.py:531
  72.7 1.5 %shard_map.157 = f32[512,128]{1,0:T(8,128)S(1)} custom-call(bf16[512,512]{1,0:T(8,128)(2,1)S(1)} %get-tuple-element.32.refs_10_.refs_0_, bf16[512,512]{1,0:T(8,128)(2,1)S(1)} %get-tuple-element.33.refs_1_, bf16[64,256]{1,0:T(8,128)(2,1)S(1)} %get-tuple-element.34.refs_2_, bf16[64,256]{1,0:T(8,128)(2,1)S(1)} %get-tuple-element.35.refs_3_, ...), custom_call_target="tpu_custom_call" | custom-call | flops 402653184 | bytes 524288 | tf_op jit(solution)/shard_map/pallas_call | solution.py:499
  74.2 12.7 %all_to_all.47 = f32[32,16,128]{2,1,0:T(8,128)S(1)} all-to-all(f32[32,16,128]{2,1,0:T(8,128)S(1)} %bitcast.28), channel_id=1, replica_groups=mesh['py'=8,'pz'=4] {'py','pz'}, dimensions={0} | all-to-all | bytes 524288 | tf_op jit(solution)/shard_map/all_to_all | solution.py:533
  86.9 1.1 %shard_map.158 = (f32[128,512]{1,0:T(8,128)}, f32[128,512]{1,0:T(8,128)}) custom-call(f32[512,128]{1,0:T(8,128)S(1)} %bitcast.25, bf16[1024,512]{1,0:T(8,128)(2,1)S(1)} %get-tuple-element.47.refs_9_.refs_1_.vectors_ref, f32[128,512]{1,0:T(8,128)S(1)} %get-tuple-element.54.field_ref, f32[128,512]{1,0:T(8,128)S(1)} %get-tuple-element.55.residual_ref), custom_call_target="tpu_custom_call" | custom-call | flops 201326592 | bytes 2097152 | tf_op jit(solution)/shard_map/pallas_call | solution.py:536
  (1 shorter events, 0.0 us)
Async XLA Ops:
  1.9 5.9 %collective-permute-start = (f32[48,512]{1,0:T(8,128)S(1)}, f32[48,512]{1,0:T(8,128)S(1)}, u32[]{:S(2)}, u32[]{:S(2)}) collective-permute-start(f32[48,512]{1,0:T(8,128)S(1)} %get-tuple-element.30.refs_4_), channel_id=1, source_target_pairs={{0,1},{1,0},{2,3},{3,2},{4,5},{5,4},{6,7},{7,6},{8,9},{9,8},{10,11... | collective-permute-start | bytes 294920 | tf_op jit(solution)/shard_map/ppermute | solution.py:412
  5.0 2.8 %collective-permute-start.1 = (f32[48,512]{1,0:T(8,128)S(1)}, f32[48,512]{1,0:T(8,128)S(1)}, u32[]{:S(2)}, u32[]{:S(2)}) collective-permute-start(f32[48,512]{1,0:T(8,128)S(1)} %get-tuple-element.40), channel_id=1, source_target_pairs={{0,0},{1,2},{2,1},{3,3},{4,4},{5,6},{6,5},{7,7},{8,8},{9,10},{10,9... | collective-permute-start | bytes 294920 | tf_op jit(solution)/shard_map/ppermute | solution.py:412
  7.8 5.5 %collective-permute-start.2 = (f32[72,512]{1,0:T(8,128)S(1)}, f32[72,512]{1,0:T(8,128)S(1)}, u32[]{:S(2)}, u32[]{:S(2)}) collective-permute-start(f32[72,512]{1,0:T(8,128)S(1)} %get-tuple-element.43), channel_id=1, source_target_pairs={{0,4},{4,8},{8,12},{12,16},{16,20},{20,24},{24,28},{28,0},{1,5},{5... | collective-permute-start | bytes 442376 | tf_op jit(solution)/shard_map/ppermute | solution.py:417
  7.9 5.5 %collective-permute-start.3 = (f32[72,512]{1,0:T(8,128)S(1)}, f32[72,512]{1,0:T(8,128)S(1)}, u32[]{:S(2)}, u32[]{:S(2)}) collective-permute-start(f32[72,512]{1,0:T(8,128)S(1)} %get-tuple-element.44), channel_id=1, source_target_pairs={{0,28},{4,0},{8,4},{12,8},{16,12},{20,16},{24,20},{28,24},{1,29},{... | collective-permute-start | bytes 442376 | tf_op jit(solution)/shard_map/ppermute | solution.py:417
  10.5 2.8 %copy-start = (f32[8,16,512]{2,1,0:T(8,128)S(1)}, f32[8,16,512]{2,1,0:T(8,128)}, u32[]{:S(2)}) copy-start(f32[8,16,512]{2,1,0:T(8,128)} %param.15) | copy-start | bytes 786436
  35.6 14.4 %copy-start.1 = (f32[8,16,512]{2,1,0:T(8,128)S(1)}, f32[8,16,512]{2,1,0:T(8,128)}, u32[]{:S(2)}) copy-start(f32[8,16,512]{2,1,0:T(8,128)} %param.14) | copy-start | bytes 786436
  50.6 5.6 %collective-permute-start.4 = (f32[72,512]{1,0:T(8,128)S(1)}, f32[72,512]{1,0:T(8,128)S(1)}, u32[]{:S(2)}, u32[]{:S(2)}) collective-permute-start(f32[72,512]{1,0:T(8,128)S(1)} %get-tuple-element.51), channel_id=1, source_target_pairs={{0,4},{4,8},{8,12},{12,16},{16,20},{20,24},{24,28},{28,0},{1,5},{5... | collective-permute-start | bytes 442376 | tf_op jit(solution)/shard_map/ppermute | solution.py:417
  51.8 4.4 %collective-permute-start.5 = (f32[72,512]{1,0:T(8,128)S(1)}, f32[72,512]{1,0:T(8,128)S(1)}, u32[]{:S(2)}, u32[]{:S(2)}) collective-permute-start(f32[72,512]{1,0:T(8,128)S(1)} %get-tuple-element.52), channel_id=1, source_target_pairs={{0,28},{4,0},{8,4},{12,8},{16,12},{20,16},{24,20},{28,24},{1,29},{... | collective-permute-start | bytes 442376 | tf_op jit(solution)/shard_map/ppermute | solution.py:417

commit v5 on v4

--- a/solution.py
+++ b/solution.py
@@ -94,40 +94,45 @@
             odd_ref[rim, :] = jnp.where(first, low, high)
 
 
-def store_y_rims(ly, lz, weighted_ref, zlow, zhigh, low_ref, high_ref):
+def store_y_rims(ly, lz, weighted_ref, zlow, zhigh, odd_ref, even_ref):
+    first = lax.rem(lax.axis_index("py"), 2) == 0
     own, side = REACH * lz, REACH * REACH
-    for ref, start, zstart in ((low_ref, 0, 0), (high_ref, (ly - REACH) * lz, (ly - REACH) * REACH)):
-        ref[own:, :] = jnp.zeros((ref.shape[0] - own, ref.shape[1]), F32)
-        ref[0:own, :] = weighted_ref[start : start + own, :]
-        ref[own : own + side, :] = zlow[zstart : zstart + side, :]
-        ref[own + side : own + 2 * side, :] = zhigh[zstart : zstart + side, :]
-
-
-def y_rims_kernel(ly, lz, weighted_ref, even_ref, odd_ref, _, zlow_ref, zhigh_ref, low_ref, high_ref):
+    for at, count, ref, start, step in ((0, own, weighted_ref, ly - REACH, lz),) + tuple(
+        (own + k * side, side, ref, ly - REACH, REACH) for k, ref in enumerate((zlow, zhigh))
+    ):
+        low, high = ref[:count, :], ref[start * step : start * step + count, :]
+        even_ref[at : at + count, :] = jnp.where(first, high, low)
+        odd_ref[at : at + count, :] = jnp.where(first, low, high)
+    end = own + 2 * side
+    for ref in (even_ref, odd_ref):
+        ref[end:, :] = jnp.zeros((ref.shape[0] - end, ref.shape[1]), F32)
+
+
+def y_rims_kernel(ly, lz, weighted_ref, odd_ref, even_ref, _, zlow_ref, zhigh_ref, yodd_ref, yeven_ref):
     first = lax.rem(lax.axis_index("pz"), 2) == 0
     zlow_ref[...] = jnp.where(first, odd_ref[...], even_ref[...])
     zhigh_ref[...] = jnp.where(first, even_ref[...], odd_ref[...])
-    store_y_rims(ly, lz, weighted_ref, zlow_ref, zhigh_ref, low_ref, high_ref)
-
-
-def next_y_rims_kernel(ly, lz, weighted_ref, zlow_ref, zhigh_ref, low_ref, high_ref):
-    store_y_rims(ly, lz, weighted_ref, zlow_ref, zhigh_ref, low_ref, high_ref)
+    store_y_rims(ly, lz, weighted_ref, zlow_ref, zhigh_ref, yodd_ref, yeven_ref)
+
+
+def next_y_rims_kernel(ly, lz, weighted_ref, zlow_ref, zhigh_ref, yodd_ref, yeven_ref):
+    store_y_rims(ly, lz, weighted_ref, zlow_ref, zhigh_ref, yodd_ref, yeven_ref)
 
 
 def point_columns(ly, lz):
-    own = [(y, z) for y in range(ly) for z in range(lz)]
     below, above = range(-REACH, 0), range(REACH)
-    zlow = [(y, z) for y in range(ly) for z in below]
-    zhigh = [(y, lz + z) for y in range(ly) for z in above]
-    sides = []
-    for ys in (below, [ly + y for y in above]):
-        rim = [(y, z) for y in ys for z in range(lz)]
-        rim += [(y, z) for y in ys for z in below]
-        rim += [(y, lz + z) for y in ys for z in above]
-        sides += rim + [(1 << 20, 1 << 20)] * (up8(len(rim)) - len(rim))
-    points = own + zlow + zhigh + sides
-    points += [(1 << 20, 1 << 20)] * (-len(points) % 128)
-    return np.array(points, np.int32).T.copy()
+    halves = []
+    for half in range(2):
+        first = 0 if half == 0 else ly // 2 - REACH
+        points = [(first + y, z) for y in range(ly // 2 + REACH) for z in range(lz)]
+        points += [(y, z) for y in range(ly) for z in below]
+        points += [(y, lz + z) for y in range(ly) for z in above]
+        ys = below if half == 0 else [ly + y for y in above]
+        points += [(y, z) for y in ys for z in range(lz)]
+        points += [(y, z) for y in ys for z in below]
+        points += [(y, lz + z) for y in ys for z in above]
+        halves += points + [(1 << 20, 1 << 20)] * (-len(points) % LANES)
+    return np.array(halves, np.int32).T.copy()
 
 
 def stencil_kernel(
@@ -140,30 +145,31 @@
         ),
         sem,
     )
-    count = ly * lz
-    rows = lax.broadcasted_iota(jnp.int32, (count, 1), 0)
-    yrow, zrow = lax.div(rows, lz), lax.rem(rows, lz)
-    factors = []
-    for bands_ref, length, row, column, first, whole in (
-        (ybands_ref, ly, yrow, points_ref[0:1, :], lax.axis_index("py") * ly, ny),
-        (zbands_ref, lz, zrow, points_ref[1:2, :], lax.axis_index("pz") * lz, nz),
-    ):
-        pick = (lax.broadcasted_iota(jnp.int32, (count, length), 1) == row).astype(F32)
-        spot = column + first
-        inside = (spot >= 0) & (spot < whole)
-        distance = jnp.where(inside, column, 1 << 20) - row
-        here = [distance == offset - REACH for offset in range(2 * REACH + 1)]
-        for matrix in range(2):
-            taps = exact(pick, bands_ref[:, matrix, :], (1, 1))
-            dense = jnp.zeros(distance.shape, F32)
-            for offset in range(2 * REACH + 1):
-                dense = jnp.where(here[offset], taps[:, offset : offset + 1], dense)
-            factors.append(dense)
-    ystiff, ymass, zstiff, zmass = factors
-    for part, value in enumerate((ymass * zmass, ystiff * zmass + ymass * zstiff)):
-        high, low = split(value)
-        out_ref[part * count : (part + 1) * count, :] = high
-        out_ref[(part + 2) * count : (part + 3) * count, :] = low
+    count = ly * lz // 2
+    width = out_ref.shape[1]
+    for half in range(2):
+        rows = lax.broadcasted_iota(jnp.int32, (count, 1), 0) + half * count
+        columns = pl.ds(half * width, width)
+        factors = []
+        for bands_ref, length, row, column, first, whole in (
+            (ybands_ref, ly, lax.div(rows, lz), points_ref[0:1, columns], lax.axis_index("py") * ly, ny),
+            (zbands_ref, lz, lax.rem(rows, lz), points_ref[1:2, columns], lax.axis_index("pz") * lz, nz),
+        ):
+            pick = (lax.broadcasted_iota(jnp.int32, (count, length), 1) == row).astype(F32)
+            spot = column + first
+            inside = (spot >= 0) & (spot < whole)
+            distance = jnp.where(inside, column, 1 << 20) - row
+            here = [distance == offset - REACH for offset in range(2 * REACH + 1)]
+            for matrix in range(2):
+                taps = exact(pick, bands_ref[:, matrix, :], (1, 1))
+                dense = jnp.zeros(distance.shape, F32)
+                for offset in range(2 * REACH + 1):
+                    dense = jnp.where(here[offset], taps[:, offset : offset + 1], dense)
+                factors.append(dense)
+        ystiff, ymass, zstiff, zmass = factors
+        for part, value in enumerate((ymass * zmass, ystiff * zmass + ymass * zstiff)):
+            at = (4 * half + part) * count
+            out_ref[at : at + count, :], out_ref[at + 2 * count : at + 3 * count, :] = split(value)
     nx = xbands_ref.shape[2]
     lane = lax.broadcasted_iota(jnp.int32, (1, nx), 1)
     for offset in range(2 * REACH + 1):
@@ -259,20 +265,29 @@
 
 
 def residual_kernel(
-    zrim, weighted_ref, zlow_ref, zhigh_ref, ylow_ref, yhigh_ref, stencil_ref, taps_ref, coef_ref, right_ref, vectors_ref,
+    lz, zrim, weighted_ref, zlow_ref, zhigh_ref, yodd_ref, yeven_ref, stencil_ref, taps_ref, coef_ref, right_ref, vectors_ref,
     _, spectral_ref, residual_ref,
 ):
     count, nx = weighted_ref.shape
-    pieces = [weighted_ref[...], zlow_ref[:zrim, :], zhigh_ref[:zrim, :], ylow_ref[...], yhigh_ref[...]]
-    missing = stencil_ref.shape[1] - sum(piece.shape[0] for piece in pieces)
-    if missing:
-        pieces.append(jnp.zeros((missing, nx), F32))
-    high, low = split(jnp.concatenate(pieces, axis=0))
-    both = mul(stencil_ref[...], high)
-    both = both[: 2 * count] + both[2 * count :] + mul(stencil_ref[: 2 * count, :], low)
+    part, need = count // 2, weighted_ref.shape[0] // 2 + REACH * lz
+    own = split(weighted_ref[...])
+    zrims = split(jnp.concatenate([zlow_ref[:zrim, :], zhigh_ref[:zrim, :]], axis=0))
+    fields = []
+    even = lax.rem(lax.axis_index("py"), 2) == 0
+    below, above = jnp.where(even, yodd_ref[...], yeven_ref[...]), jnp.where(even, yeven_ref[...], yodd_ref[...])
+    for half, rim in enumerate((below, above)):
+        missing = stencil_ref.shape[1] - need - 2 * zrim - rim.shape[0]
+        yrim = split(jnp.concatenate([rim, jnp.zeros((missing, nx), F32)], axis=0) if missing else rim)
+        first = half * (count - need)
+        high, low = (
+            jnp.concatenate([own[k][first : first + need], zrims[k], yrim[k]], axis=0) for k in range(2)
+        )
+        stencil = stencil_ref[4 * half * part : 4 * (half + 1) * part, :]
+        both = mul(stencil, high)
+        both = both[: 2 * part] + both[2 * part :] + mul(stencil[: 2 * part], low)
+        fields.append((both[:part], both[part:]))
     for start in range(0, count, 8):
-        mass = both[start : start + 8]
-        stiff = both[count + start : count + start + 8]
+        mass, stiff = (field[start % part : start % part + 8] for field in fields[start // part])
         applied = None
         for offset in range(2 * REACH + 1):
             move = offset - REACH
@@ -282,8 +297,9 @@
         rows = pl.ds(start, 8)
         residual_ref[rows, :] = right_ref[rows, :] - coef_ref[rows, :] * applied
     high, low = split(residual_ref[...])
-    product = mul_t(vectors_ref[...], jnp.concatenate([high, low], axis=0))
-    spectral_ref[...] = (product[:nx, :count] + product[:nx, count:]) + (product[nx:, :count] + product[nx:, count:])
+    product = mul_t(jnp.concatenate([high, low], axis=0), vectors_ref[:nx, :])
+    product = product[:count] + product[count:] + mul_t(high, vectors_ref[nx:, :])
+    spectral_ref[...] = product.T
 
 
 def modes_kernel(npy, npz, rims, *refs):
@@ -376,7 +392,7 @@
 
 def rim_update_kernel(
     ly, lz, devices, spectral_ref, vectors_ref, field_ref, coef_ref, before_low_ref, before_high_ref,
-    updated_ref, weighted_ref, zlow_ref, zhigh_ref, low_ref, high_ref,
+    updated_ref, weighted_ref, zlow_ref, zhigh_ref, yodd_ref, yeven_ref,
 ):
     nx = vectors_ref.shape[1]
     modes = nx // devices
@@ -395,7 +411,7 @@
     for side, (ref, before_ref) in enumerate(((zlow_ref, before_low_ref), (zhigh_ref, before_high_ref))):
         start = count + side * half
         ref[...] = before_ref[:half, :] + before_ref[half:, :] * update[start : start + half]
-    store_y_rims(ly, lz, weighted_ref, zlow_ref, zhigh_ref, low_ref, high_ref)
+    store_y_rims(ly, lz, weighted_ref, zlow_ref, zhigh_ref, yodd_ref, yeven_ref)
 
 
 def last_update_kernel(spectral_ref, vectors_ref, field_ref, residual_ref, updated_hbm, residual_hbm, held, sem):
@@ -410,6 +426,11 @@
     count = lax.axis_size(axis)
     other = [((i + odd) ^ 1) - odd for i in range(count)]
     return lax.ppermute(value, axis, [(i, j if 0 <= j < count else i) for i, j in enumerate(other)])
+
+
+def paired(value, axis):
+    count = lax.axis_size(axis)
+    return lax.ppermute(value, axis, [(i, (i + 1 if i % 2 else i - 1) % count) for i in range(count)])
 
 
 def around(value, axis, step):
@@ -464,7 +485,7 @@
     )(*in_hbm(coef_table, span_index.reshape(count, nx), field))
 
     points = point_columns(ly, lz)
-    width = points.shape[1]
+    width = points.shape[1] // 2
     bands = [array.transpose(1, 0, 2) for array in (yaxis_bands, zaxis_bands, xaxis_bands)]
     stencil, taps = call(
         lambda *refs: stencil_kernel(ly, lz, ny, nz, *refs),
@@ -515,19 +536,19 @@
             )
 
     even, odd = pairwise(even, "pz", 0), pairwise(odd, "pz", 1)
-    zlow, zhigh, ylow, yhigh = call(
+    zlow, zhigh, yodd, yeven = call(
         lambda *refs: y_rims_kernel(ly, lz, *refs),
         [(zrims, F32)] * 2 + [(yrim, F32)] * 2, [VMEM] * 3 + [ANY], nx, 4 * nx * 4 * (yrim[0] + zrims[0]),
-    )(weighted, even, odd, taps)
+    )(weighted, odd, even, taps)
     for iteration in range(ITERS):
         last = iteration + 1 == ITERS
-        below, above = around(yhigh, "py", 1), around(ylow, "py", -1)
+        yodd, yeven = paired(yodd, "py"), pairwise(yeven, "py", 0)
         spectral, *residual = call(
-            lambda *refs: residual_kernel(zrim[0], *refs),
+            lambda *refs: residual_kernel(lz, zrim[0], *refs),
             [((nx, count), F32)] + [(block, F32)] * last,
             [VMEM] * 10 + [ANY], 6 * count * nx * (nx + 2 * width), 5 * cell + 4 * nx * nx,
             [pltpu.VMEM(block, F32)] * (not last),
-        )(weighted, zlow, zhigh, below, above, stencil, taps, coef, right, vectors, tables[0])
+        )(weighted, zlow, zhigh, yodd, yeven, stencil, taps, coef, right, vectors, tables[0])
         spectral = lax.all_to_all(spectral, BOTH, split_axis=0, concat_axis=0, tiled=True)
         spectral = precondition(spectral, not last)
         spectral = lax.all_to_all(spectral, BOTH, split_axis=0, concat_axis=0, tiled=True)
@@ -538,7 +559,7 @@
                 [pltpu.VMEM(block, F32), dma((2,))], [HBM] * 2,
             )(spectral, vectors, field, *residual)
         elif fast:
-            field, weighted, zlow, zhigh, ylow, yhigh = call(
+            field, weighted, zlow, zhigh, yodd, yeven = call(
                 lambda *refs: rim_update_kernel(ly, lz, devices, *refs),
                 [(block, F32)] * 2 + [(zrim, F32)] * 2 + [(yrim, F32)] * 2, [VMEM] * 6, *cost,
             )(spectral, vectors, field, coef, zlow, zhigh)
@@ -547,7 +568,7 @@
                 lambda *refs: update_kernel(ly, lz, *refs), [(block, F32)] * 2 + [(zrim, F32)] * 2, [VMEM] * 4, *cost,
             )(spectral, vectors, field, coef)
             zlow, zhigh = around(zhigh, "pz", 1), around(zlow, "pz", -1)
-            ylow, yhigh = call(
+            yodd, yeven = call(
                 lambda *refs: next_y_rims_kernel(ly, lz, *refs),
                 [(yrim, F32)] * 2, [VMEM] * 3, nx, 4 * nx * 4 * yrim[0],
             )(weighted, zlow, zhigh)

time: 88.3 us -> 85.7 us (0.971)
  blocking collectives: 60.8 us -> 53.8 us
  waiting for transfers between devices: 3.8 us -> 7.84 us
  starting transfers between devices: 9.13 us -> 10.3 us
    all_to_all x4, blocking collectives: 60.8 us -> 53.8 us  [shards(): lax.all_to_all(spectral, BOTH, split_axis=0, concat_axis=0, tiled=True)]
    ppermute x2 -> x4, starting transfers between devices: 3.74 us -> 7.45 us  [pairwise(): lax.ppermute(value, axis, [(i, j if 0 <= j < count else i) for i, j in en...]
    ppermute x4 -> x2, waiting for transfers between devices: 3.67 us -> 7.08 us  [paired(): lax.ppermute(value, axis, [(i, (i + 1 if i % 2 else i - 1) % count) for i...]
    ppermute x4 -> x2, starting transfers between devices: 5.39 us -> 2.89 us  [paired(): lax.ppermute(value, axis, [(i, (i + 1 if i % 2 else i - 1) % count) for i...]
where the time goes in v5:
time: 85.7 us; the launch traced here: 85.4 us
  blocking collectives  53.8 us (63%)
  Pallas kernels  12.7 us (15%)
  starting transfers between devices  10.3 us (12%)
  waiting for transfers between devices  7.84 us (9%)
    all_to_all x4, blocking collectives, shards(): lax.all_to_all(spectral, BOTH, split_axis=0, concat_axis=0, tiled=True)  53.8 us
    ppermute x4, starting transfers between devices, pairwise(): lax.ppermute(value, axis, [(i, j if 0 <= j < count else i) for i, j in en...  7.45 us
    ppermute x2, waiting for transfers between devices, paired(): lax.ppermute(value, axis, [(i, (i + 1 if i % 2 else i - 1) % count) for i...  7.08 us
    pallas_call x2, Pallas kernels, precondition(): call(lambda *refs: modes_kernel(npy, npz, rims, *refs), [((devices * size...  3.34 us
    ppermute x2, starting transfers between devices, paired(): lax.ppermute(value, axis, [(i, (i + 1 if i % 2 else i - 1) % count) for i...  2.89 us
    pallas_call x2, Pallas kernels, shards(): call(lambda *refs: residual_kernel(lz, zrim[0], *refs), [((nx, count), F3...  2.37 us
    pallas_call x1, Pallas kernels, shards(): call(lambda *refs: tables_kernel(npy, npz, ly, lz, *refs), [((2 * nx, nx)...  2.08 us
    pallas_call x1, Pallas kernels, shards(): call(lambda *refs: stencil_kernel(ly, lz, ny, nz, *refs), [((4 * count, w...  1.82 us
  transfers between devices with their start and end apart: 6, of which 3 were waited for; matrix products, arithmetic and copies ran while one was open for 0% of the time, Pallas kernels for 5%

profile of v5, /device:TPU:0, one launch (start us, length us, event | category | flops | bytes accessed | tf_op | source)
XLA Modules:
  0.0 85.4 jit_solution(14753579856327585473)
XLA Ops:
  0.6 1.2 %shard_map.149 = (f32[128,512]{1,0:T(8,128)S(1)}, f32[128,512]{1,0:T(8,128)S(1)}, f32[48,512]{1,0:T(8,128)S(1)}, f32[48,512]{1,0:T(8,128)S(1)}) custom-call(f32[8]{0:T(128)} %refs_0_.3, s32[128,512]{1,0:T(8,128)} %bitcast.30, f32[128,512]{1,0:T(8,128)} %bitcast.22), custom_call_target="tpu_custom_call" | custom-call | flops 1048576 | bytes 1048576 | tf_op jit(solution)/shard_map/pallas_call | solution.py:480
  1.9 0.7 collective-permute-start
  2.6 5.9 %collective-permute-start.1 = (f32[48,512]{1,0:T(8,128)S(1)}, f32[48,512]{1,0:T(8,128)S(1)}, u32[]{:S(2)}, u32[]{:S(2)}) collective-permute-start(f32[48,512]{1,0:T(8,128)S(1)} %get-tuple-element.30.refs_4_), channel_id=1, source_target_pairs={{0,1},{1,0},{2,3},{3,2},{4,5},{5,4},{6,7},{7,6},{8,9},{9,8},{10,11... | collective-permute-start | bytes 294920 | tf_op jit(solution)/shard_map/ppermute | solution.py:428
  8.5 1.8 %shard_map.150 = (bf16[512,256]{1,0:T(8,128)(2,1)S(1)}, f32[14,8,512]{2,1,0:T(8,128)S(1)}) custom-call(s32[2,512]{1,0:T(2,128)} %constant.2.clone.refs_0_, f32[7,2,8]{2,1,0:T(2,128)} %bitcast.32, f32[7,2,16]{2,1,0:T(2,128)} %bitcast.33, f32[7,2,512]{2,1,0:T(2,128)} %bitcast.31, f32[48,512]{1,0:T(8,128)S(1)} %get-tuple-element.30.refs_4_), custom_call_target="tpu_custom_call" | custom-call | flops 1966080 | bytes 262144 | tf_op jit(solution)/shard_map/pallas_call | solution.py:490
  10.3 0.0 collective-permute-done.refs_1_
  10.3 0.8 collective-permute-done.1.refs_2_
  11.1 0.1 shard_map.152
  11.1 0.8 collective-permute-start.2
  11.9 0.9 %collective-permute-start.3 = (f32[72,512]{1,0:T(8,128)S(1)}, f32[72,512]{1,0:T(8,128)S(1)}, u32[]{:S(2)}, u32[]{:S(2)}) collective-permute-start(f32[72,512]{1,0:T(8,128)S(1)} %get-tuple-element.44), channel_id=1, source_target_pairs={{0,4},{4,0},{8,12},{12,8},{16,20},{20,16},{24,28},{28,24},{1,5},{5... | collective-permute-start | bytes 442376 | tf_op jit(solution)/shard_map/ppermute | solution.py:428
  12.8 0.0 copy-start
  12.8 2.1 %shard_map.151 = (bf16[1024,512]{1,0:T(8,128)(2,1)S(1)}, bf16[512,512]{1,0:T(8,128)(2,1)S(1)}, bf16[512,512]{1,0:T(8,128)(2,1)S(1)}, bf16[64,256]{1,0:T(8,128)(2...) custom-call(f32[512,512]{1,0:T(8,128)} %refs_0_.4, ...), custom_call_target="tpu_custom_call" | custom-call | flops 2097152 | bytes 1048576 | tf_op jit(solution)/shard_map/pallas_call | solution.py:503
  14.9 3.2 %collective-permute-done.2.refs_3_ = f32[72,512]{1,0:T(8,128)S(1)} collective-permute-done((f32[72,512]{1,0:T(8,128)S(1)}, f32[72,512]{1,0:T(8,128)S(1)}, u32[]{:S(2)}, u32[]{:S(2)}) %collective-permute-start.2) | collective-permute-done | bytes 147488 | tf_op jit(solution)/shard_map/ppermute | solution.py:433
  18.1 0.0 collective-permute-done.3.refs_4_
  18.1 0.0 copy-done
  18.1 1.2 %shard_map.153 = f32[512,128]{1,0:T(8,128)S(1)} custom-call(f32[128,512]{1,0:T(8,128)S(1)} %get-tuple-element.39.refs_0_, f32[48,512]{1,0:T(8,128)S(1)} %get-tuple-element.41.refs_1_.refs_4_, f32[48,512]{1,0:T(8,128)S(1)} %get-tuple-element.42.refs_2_.refs_5_, f32[72,512]{1,0:T(8,128)S(1)} %collective-permute-done.2.refs_3_, ...), custom_call_target="tpu_custom_call" | custom-call | flops 402653184 | bytes 2359296 | tf_op jit(solution)/shard_map/pallas_call | solution.py:546
  19.3 12.6 %all_to_all.44 = f32[32,16,128]{2,1,0:T(8,128)S(1)} all-to-all(f32[32,16,128]{2,1,0:T(8,128)S(1)} %bitcast.26), channel_id=1, replica_groups=mesh['py'=8,'pz'=4] {'py','pz'}, dimensions={0} | all-to-all | bytes 524288 | tf_op jit(solution)/shard_map/all_to_all | solution.py:552
  31.9 1.9 %shard_map.154 = f32[768,128]{1,0:T(8,128)S(1)} custom-call(bf16[512,512]{1,0:T(8,128)(2,1)S(1)} %get-tuple-element.32.refs_10_.refs_0_, bf16[512,512]{1,0:T(8,128)(2,1)S(1)} %get-tuple-element.33.refs_1_, bf16[64,256]{1,0:T(8,128)(2,1)S(1)} %get-tuple-element.34.refs_2_, bf16[64,256]{1,0:T(8,128)(2,1)S(1)} %get-tuple-element.35.refs_3_, ...), custom_call_target="tpu_custom_call" | custom-call | flops 402653184 | bytes 524288 | tf_op jit(solution)/shard_map/pallas_call | solution.py:520
  33.8 0.0 copy-start.1
  33.8 14.4 %all_to_all.45 = f32[32,24,128]{2,1,0:T(8,128)S(1)} all-to-all(f32[32,24,128]{2,1,0:T(8,128)S(1)} %bitcast.18), channel_id=1, replica_groups=mesh['py'=8,'pz'=4] {'py','pz'}, dimensions={0} | all-to-all | bytes 786432 | tf_op jit(solution)/shard_map/all_to_all | solution.py:554
  48.2 0.0 copy-done.1
  48.2 0.6 shard_map.155
  48.8 2.1 %collective-permute-start.4 = (f32[72,512]{1,0:T(8,128)S(1)}, f32[72,512]{1,0:T(8,128)S(1)}, u32[]{:S(2)}, u32[]{:S(2)}) collective-permute-start(f32[72,512]{1,0:T(8,128)S(1)} %get-tuple-element.51), channel_id=1, source_target_pairs={{0,28},{4,8},{8,4},{12,16},{16,12},{20,24},{24,20},{28,0},{1,29},{... | collective-permute-start | bytes 442376 | tf_op jit(solution)/shard_map/ppermute | solution.py:433
  50.9 0.0 collective-permute-start.5
  50.9 3.8 %collective-permute-done.4.refs_3_ = f32[72,512]{1,0:T(8,128)S(1)} collective-permute-done((f32[72,512]{1,0:T(8,128)S(1)}, f32[72,512]{1,0:T(8,128)S(1)}, u32[]{:S(2)}, u32[]{:S(2)}) %collective-permute-start.4) | collective-permute-done | bytes 147488 | tf_op jit(solution)/shard_map/ppermute | solution.py:433
  54.7 0.0 collective-permute-done.5.refs_4_
  54.7 1.2 %shard_map.156 = (f32[512,128]{1,0:T(8,128)S(1)}, f32[128,512]{1,0:T(8,128)S(1)}) custom-call(f32[128,512]{1,0:T(8,128)S(1)} %get-tuple-element.48.refs_0_, f32[24,512]{1,0:T(8,128)S(1)} %get-tuple-element.49.refs_1_, f32[24,512]{1,0:T(8,128)S(1)} %get-tuple-element.50.refs_2_, f32[72,512]{1,0:T(8,128)S(1)} %collective-permute-done.4.refs_3_, ...), custom_call_target="tpu_custom_call" | custom-call | flops 402653184 | bytes 2359296 | tf_op jit(solution)/shard_map/pallas_call | solution.py:546
  55.9 14.2 %all_to_all.46 = f32[32,16,128]{2,1,0:T(8,128)S(1)} all-to-all(f32[32,16,128]{2,1,0:T(8,128)S(1)} %bitcast.29), channel_id=1, replica_groups=mesh['py'=8,'pz'=4] {'py','pz'}, dimensions={0} | all-to-all | bytes 524288 | tf_op jit(solution)/shard_map/all_to_all | solution.py:552
  70.1 1.5 %shard_map.157 = f32[512,128]{1,0:T(8,128)S(1)} custom-call(bf16[512,512]{1,0:T(8,128)(2,1)S(1)} %get-tuple-element.32.refs_10_.refs_0_, bf16[512,512]{1,0:T(8,128)(2,1)S(1)} %get-tuple-element.33.refs_1_, bf16[64,256]{1,0:T(8,128)(2,1)S(1)} %get-tuple-element.34.refs_2_, bf16[64,256]{1,0:T(8,128)(2,1)S(1)} %get-tuple-element.35.refs_3_, ...), custom_call_target="tpu_custom_call" | custom-call | flops 402653184 | bytes 524288 | tf_op jit(solution)/shard_map/pallas_call | solution.py:520
  71.6 12.7 %all_to_all.47 = f32[32,16,128]{2,1,0:T(8,128)S(1)} all-to-all(f32[32,16,128]{2,1,0:T(8,128)S(1)} %bitcast.28), channel_id=1, replica_groups=mesh['py'=8,'pz'=4] {'py','pz'}, dimensions={0} | all-to-all | bytes 524288 | tf_op jit(solution)/shard_map/all_to_all | solution.py:554
  84.3 1.1 %shard_map.158 = (f32[128,512]{1,0:T(8,128)}, f32[128,512]{1,0:T(8,128)}) custom-call(f32[512,128]{1,0:T(8,128)S(1)} %bitcast.24, bf16[1024,512]{1,0:T(8,128)(2,1)S(1)} %get-tuple-element.47.refs_9_.refs_1_.vectors_ref, f32[128,512]{1,0:T(8,128)S(1)} %get-tuple-element.54.field_ref, f32[128,512]{1,0:T(8,128)S(1)} %get-tuple-element.55.residual_ref), custom_call_target="tpu_custom_call" | custom-call | flops 201326592 | bytes 2097152 | tf_op jit(solution)/shard_map/pallas_call | solution.py:557
Async XLA Ops:
  1.9 8.4 %collective-permute-start = (f32[48,512]{1,0:T(8,128)S(1)}, f32[48,512]{1,0:T(8,128)S(1)}, u32[]{:S(2)}, u32[]{:S(2)}) collective-permute-start(f32[48,512]{1,0:T(8,128)S(1)} %get-tuple-element.40), channel_id=1, source_target_pairs={{0,0},{1,2},{2,1},{3,3},{4,4},{5,6},{6,5},{7,7},{8,8},{9,10},{10,9... | collective-permute-start | bytes 294920 | tf_op jit(solution)/shard_map/ppermute | solution.py:428
  2.6 8.5 %collective-permute-start.1 = (f32[48,512]{1,0:T(8,128)S(1)}, f32[48,512]{1,0:T(8,128)S(1)}, u32[]{:S(2)}, u32[]{:S(2)}) collective-permute-start(f32[48,512]{1,0:T(8,128)S(1)} %get-tuple-element.30.refs_4_), channel_id=1, source_target_pairs={{0,1},{1,0},{2,3},{3,2},{4,5},{5,4},{6,7},{7,6},{8,9},{9,8},{10,11... | collective-permute-start | bytes 294920 | tf_op jit(solution)/shard_map/ppermute | solution.py:428
  11.1 7.0 %collective-permute-start.2 = (f32[72,512]{1,0:T(8,128)S(1)}, f32[72,512]{1,0:T(8,128)S(1)}, u32[]{:S(2)}, u32[]{:S(2)}) collective-permute-start(f32[72,512]{1,0:T(8,128)S(1)} %get-tuple-element.43), channel_id=1, source_target_pairs={{0,28},{4,8},{8,4},{12,16},{16,12},{20,24},{24,20},{28,0},{1,29},{... | collective-permute-start | bytes 442376 | tf_op jit(solution)/shard_map/ppermute | solution.py:433
  11.9 6.2 %collective-permute-start.3 = (f32[72,512]{1,0:T(8,128)S(1)}, f32[72,512]{1,0:T(8,128)S(1)}, u32[]{:S(2)}, u32[]{:S(2)}) collective-permute-start(f32[72,512]{1,0:T(8,128)S(1)} %get-tuple-element.44), channel_id=1, source_target_pairs={{0,4},{4,0},{8,12},{12,8},{16,20},{20,16},{24,28},{28,24},{1,5},{5... | collective-permute-start | bytes 442376 | tf_op jit(solution)/shard_map/ppermute | solution.py:428
  12.8 5.3 %copy-start = (f32[8,16,512]{2,1,0:T(8,128)S(1)}, f32[8,16,512]{2,1,0:T(8,128)}, u32[]{:S(2)}) copy-start(f32[8,16,512]{2,1,0:T(8,128)} %param.15) | copy-start | bytes 786436
  33.8 14.4 %copy-start.1 = (f32[8,16,512]{2,1,0:T(8,128)S(1)}, f32[8,16,512]{2,1,0:T(8,128)}, u32[]{:S(2)}) copy-start(f32[8,16,512]{2,1,0:T(8,128)} %param.14) | copy-start | bytes 786436
  48.8 5.9 %collective-permute-start.4 = (f32[72,512]{1,0:T(8,128)S(1)}, f32[72,512]{1,0:T(8,128)S(1)}, u32[]{:S(2)}, u32[]{:S(2)}) collective-permute-start(f32[72,512]{1,0:T(8,128)S(1)} %get-tuple-element.51), channel_id=1, source_target_pairs={{0,28},{4,8},{8,4},{12,16},{16,12},{20,24},{24,20},{28,0},{1,29},{... | collective-permute-start | bytes 442376 | tf_op jit(solution)/shard_map/ppermute | solution.py:433
  50.9 3.8 %collective-permute-start.5 = (f32[72,512]{1,0:T(8,128)S(1)}, f32[72,512]{1,0:T(8,128)S(1)}, u32[]{:S(2)}, u32[]{:S(2)}) collective-permute-start(f32[72,512]{1,0:T(8,128)S(1)} %get-tuple-element.52), channel_id=1, source_target_pairs={{0,4},{4,0},{8,12},{12,8},{16,20},{20,16},{24,28},{28,24},{1,5},{5... | collective-permute-start | bytes 442376 | tf_op jit(solution)/shard_map/ppermute | solution.py:428

commit v6 on v5

--- a/solution.py
+++ b/solution.py
@@ -215,12 +215,11 @@
     zlow_ref[...] = jnp.zeros(zlow_ref.shape, BF16)
     for parity in range(2):
         high, low = split(jnp.where(half == (parity == 1), pair, 0.0))
-        for yl in range(parity, ly, 2):
+        for yl in range(parity, ly // 2, 2):
             for block in range(npz):
-                to = (pl.ds((block * ly + yl) * lz, lz), pl.ds(yl // 2 * 2 * nz, 2 * nz))
+                to = (pl.ds((block * ly // 2 + yl) * lz, lz), pl.ds(yl // 2 * 2 * nz, 2 * nz))
                 zhigh_ref[to] = high[block * lz : (block + 1) * lz, :]
                 zlow_ref[to] = low[block * lz : (block + 1) * lz, :]
-
     shape = (rimhigh_ref.shape[0], 1)
     row = lax.broadcasted_iota(jnp.int32, shape, 0)
     block, spot = lax.div(row, LANES // 2), lax.rem(row, LANES // 2)
@@ -303,38 +302,50 @@
 
 
 def modes_kernel(npy, npz, rims, *refs):
-    zhigh_ref, zlow_ref, ydown_ref, yup_ref, sums_ref, *rim_refs, in_ref, out_ref = refs
+    zhigh_ref, zlow_ref, ydown_ref, yup_ref, sums_ref, *rim_refs, in_ref, out_ref, turn_ref = refs
     count = in_ref.shape[0] // (npy * npz)
-    lanes = in_ref.shape[1]
+    size = out_ref.shape[0] // (npy * npz)
     nz = sums_ref.shape[1] // count
-    chunks = zhigh_ref.shape[1] // (2 * nz)
-    rows = [
-        jnp.concatenate([in_ref[pl.ds(b * count + j, npy, stride=npz * count), :] for b in range(npz)], axis=1)
-        for j in range(count)
-    ]
+    width = zhigh_ref.shape[1]
+    chunks = 2 * width // LANES
+    step = turn_ref.shape[0] // (npy * chunks)
     zhigh, zlow = zhigh_ref[...], zlow_ref[...]
 
     def three(value, product, whigh, wlow):
+        rows = value.shape[0]
         high, low = split(value)
         both = product(jnp.concatenate([high, low], axis=0), whigh)
-        return both[: count * npy] + both[count * npy :] + product(high, wlow)
-
-    part = three(jnp.concatenate(rows, axis=0), mul, zhigh, zlow)
-    late = lax.broadcasted_iota(jnp.int32, (npy, 2 * nz), 1) >= nz
-
-    def swap(value):
-        return pltpu.roll(value, nz, 1)
-
-    def tile(array, j, c):
-        return array[j * npy : (j + 1) * npy, c * 2 * nz : (c + 1) * 2 * nz]
-
+        return both[:rows] + both[rows:] + product(high, wlow)
+
+    def early(first, second):
+        late = lax.broadcasted_iota(jnp.int32, first.shape, 1) >= LANES // 2
+        return jnp.where(late, pltpu.roll(second, LANES // 2, 1), first)
+
+    def later(first, second):
+        late = lax.broadcasted_iota(jnp.int32, first.shape, 1) >= LANES // 2
+        return jnp.where(late, second, pltpu.roll(first, LANES // 2, 1))
+
+    def by_mode(mode, chunk):
+        return pl.ds(chunk * npy * step + mode, npy, stride=step)
+
+    def by_device(device, chunk):
+        return pl.ds((chunk * npy + device) * step, count)
+
+    halves = [[], []]
+    for p in range(npy):
+        blocks = [in_ref[(p * npz + b) * count : (p * npz + b + 1) * count, :] for b in range(npz)]
+        for half, joined in zip(halves, (early, later)):
+            half.append(jnp.concatenate([joined(blocks[b], blocks[b + 1]) for b in range(0, npz, 2)], axis=1))
+    part = three(jnp.concatenate(halves[0] + halves[1], axis=0), mul, zhigh, zlow)
+    for chunk in range(chunks):
+        half, lane = divmod(chunk * LANES, width)
+        for p in range(npy):
+            row = (half * npy + p) * count
+            turn_ref[by_device(p, chunk), :] = part[row : row + count, lane : lane + LANES]
     pairs = []
-    for j in range(0, count, 2):
-        first = [tile(part, j, c) for c in range(chunks)]
-        second = [tile(part, j + 1, c) for c in range(chunks)]
-        even = [jnp.where(late, swap(second[c]), first[c]) for c in range(chunks)]
-        odd = [jnp.where(late, second[c], swap(first[c])) for c in range(chunks)]
-        pairs.append(jnp.concatenate(even + odd, axis=0))
+    for mode in range(0, count, 2):
+        tiles = [(turn_ref[by_mode(mode, c), :], turn_ref[by_mode(mode + 1, c), :]) for c in range(chunks)]
+        pairs.append(jnp.concatenate([early(*tile) for tile in tiles] + [later(*tile) for tile in tiles], axis=0))
     stacked = jnp.concatenate(pairs, axis=1)
 
     def four(value):
@@ -343,32 +354,44 @@
 
     modes = mul(ydown_ref[...], four(stacked)) / sums_ref[...]
     restored = mul(yup_ref[...], four(modes))
-    half = npy * chunks
-    rows = []
-    for pair in range(count // 2):
-        block = restored[:, pair * 2 * nz : (pair + 1) * 2 * nz]
-        even = [block[c * npy : (c + 1) * npy] for c in range(chunks)]
-        odd = [block[half + c * npy : half + (c + 1) * npy] for c in range(chunks)]
-        rows.append(jnp.concatenate([jnp.where(late, swap(odd[c]), even[c]) for c in range(chunks)], axis=1))
-        rows.append(jnp.concatenate([jnp.where(late, odd[c], swap(even[c])) for c in range(chunks)], axis=1))
+    for mode in range(0, count, 2):
+        block = restored[:, mode * nz : (mode + 2) * nz]
+        for c in range(chunks):
+            even = block[c * npy : (c + 1) * npy]
+            odd = block[(chunks + c) * npy : (chunks + c + 1) * npy]
+            turn_ref[by_mode(mode, c), :] = early(even, odd)
+            turn_ref[by_mode(mode + 1, c), :] = later(even, odd)
+    rows = [
+        jnp.concatenate(
+            [turn_ref[by_device(p, half * chunks // 2 + c), :] for c in range(chunks // 2)], axis=1
+        )
+        for half in range(2)
+        for p in range(npy)
+    ]
     spectral = jnp.concatenate(rows, axis=0)
     back = three(spectral, mul_t, zhigh, zlow)
-    size = out_ref.shape[0] // (npy * npz)
-    for j in range(count):
-        for b in range(npz):
-            out_ref[pl.ds(b * size + j, npy, stride=npz * size), :] = back[
-                j * npy : (j + 1) * npy, b * lanes : (b + 1) * lanes
-            ]
+    total = npy * count
     if rims:
-        side = three(spectral, mul_t, rim_refs[0][...], rim_refs[1][...])
-        for j in range(count // 2):
-            for b in range(0, npz, 2):
-                first, second = (
-                    side[k * npy : (k + 1) * npy, b * lanes // 2 : b * lanes // 2 + lanes] for k in (j, j + count // 2)
-                )
-                at = b * size + count + j
-                out_ref[pl.ds(at, npy, stride=npz * size), :] = jnp.where(late, swap(second), first)
-                out_ref[pl.ds(at + size, npy, stride=npz * size), :] = jnp.where(late, second, swap(first))
+        side = [
+            three(spectral[half * total : (half + 1) * total], mul_t, *(ref[:, pl.ds(half * width, width)] for ref in rim_refs))
+            for half in range(2)
+        ]
+        side = side[0] + side[1]
+    for p in range(npy):
+        for b in range(0, npz, 2):
+            first, second = (
+                back[k * total + p * count : k * total + (p + 1) * count, b * LANES // 2 : b * LANES // 2 + LANES]
+                for k in range(2)
+            )
+            at = (p * npz + b) * size
+            out_ref[at : at + count, :] = early(first, second)
+            out_ref[at + size : at + size + count, :] = later(first, second)
+            if rims:
+                row, middle = p * count, p * count + count // 2
+                first = side[row:middle, b * LANES // 2 : b * LANES // 2 + LANES]
+                second = side[middle : row + count, b * LANES // 2 : b * LANES // 2 + LANES]
+                out_ref[at + count : at + size, :] = early(first, second)
+                out_ref[at + size + count : at + 2 * size, :] = later(first, second)
 
 
 def transformed(points, vectors_ref):
@@ -431,6 +454,21 @@
 def paired(value, axis):
     count = lax.axis_size(axis)
     return lax.ppermute(value, axis, [(i, (i + 1 if i % 2 else i - 1) % count) for i in range(count)])
+
+
+def odd_pairs(value, axis, other):
+    count, across = lax.axis_size(axis), lax.axis_size(other)
+    first = BOTH.index(axis) == 0
+
+    def spot(i, k):
+        return i * across + k if first else k * count + i
+
+    pairs = []
+    for i in range(count):
+        for k in range(across):
+            j = i + 1 if i % 2 else i - 1
+            pairs.append((spot(i, k), spot(j, k) if 0 <= j < count else spot(i, k ^ 1)))
+    return lax.ppermute(value, BOTH, pairs)
 
 
 def around(value, axis, step):
@@ -495,11 +533,11 @@
     )(*in_hbm(jnp.asarray(points), *bands), even)
 
     fast = (
-        modes % 16 == 0 and npz % 2 == 0 and 2 * ly * REACH <= LANES // 2 and npy % 8 == 0 and lz % 16 == 0 and ly % 2 == 0
+        modes % 16 == 0 and npz % 2 == 0 and 2 * ly * REACH <= LANES // 2 and npy % 8 == 0 and lz % 16 == 0 and ly % 4 == 0
         and 2 * nz == LANES and 2 * ny == LANES and count == LANES and nx % LANES == 0
     )
     if fast:
-        zmat, ymat, rmat = (npz * count, ly * nz), (ny, 4 * ny), (npz * LANES // 2, ly * nz)
+        zmat, ymat, rmat = (npz * count // 2, ly * nz // 2), (ny, 4 * ny), (npz * LANES // 2, ly * nz)
         vectors, *tables = call(
             lambda *refs: tables_kernel(npy, npz, ly, lz, *refs),
             [((2 * nx, nx), BF16), (zmat, BF16), (zmat, BF16), (ymat, BF16), (ymat, BF16), ((ny, modes * nz), F32)]
@@ -520,6 +558,7 @@
             return call(
                 lambda *refs: modes_kernel(npy, npz, rims, *refs),
                 [((devices * size, count), F32)], [VMEM] * (8 if rims else 6), 6 * 2 * count * nx * ly * nz, 2 * cell,
+                [pltpu.VMEM((ly * nz // LANES * npy * (modes + 8), LANES), F32)],
             )(*(tables if rims else tables[:5]), received)[0]
     else:
         tables = [taps]
@@ -535,7 +574,7 @@
                 received, npy, npz, ly, lz, xpart, yaxis_values, zaxis_values, yaxis_vectors, zaxis_vectors
             )
 
-    even, odd = pairwise(even, "pz", 0), pairwise(odd, "pz", 1)
+    even, odd = pairwise(even, "pz", 0), odd_pairs(odd, "pz", "py")
     zlow, zhigh, yodd, yeven = call(
         lambda *refs: y_rims_kernel(ly, lz, *refs),
         [(zrims, F32)] * 2 + [(yrim, F32)] * 2, [VMEM] * 3 + [ANY], nx, 4 * nx * 4 * (yrim[0] + zrims[0]),

time: 85.7 us -> 85 us (level)
  starting transfers between devices: 10.3 us -> 8.43 us
  blocking collectives: 53.8 us -> 55.6 us
    ppermute x4 -> x3, starting transfers between devices: 7.45 us -> 5.02 us  [pairwise(): lax.ppermute(value, axis, [(i, j if 0 <= j < count else i) for i, j in en...]
    all_to_all x4, blocking collectives: 53.8 us -> 55.6 us  [shards(): lax.all_to_all(spectral, BOTH, split_axis=0, concat_axis=0, tiled=True)]
where the time goes in v6:
time: 85 us; the launch traced here: 84.7 us
  blocking collectives  55.6 us (65%)
  Pallas kernels  12 us (14%)
  starting transfers between devices  8.43 us (10%)
  waiting for transfers between devices  7.91 us (9%)
    all_to_all x4, blocking collectives, shards(): lax.all_to_all(spectral, BOTH, split_axis=0, concat_axis=0, tiled=True)  55.6 us
    ppermute x2, waiting for transfers between devices, paired(): lax.ppermute(value, axis, [(i, (i + 1 if i % 2 else i - 1) % count) for i...  7.15 us
    ppermute x3, starting transfers between devices, pairwise(): lax.ppermute(value, axis, [(i, j if 0 <= j < count else i) for i, j in en...  5.02 us
    ppermute x2, starting transfers between devices, paired(): lax.ppermute(value, axis, [(i, (i + 1 if i % 2 else i - 1) % count) for i...  2.89 us
    pallas_call x2, Pallas kernels, precondition(): call(lambda *refs: modes_kernel(npy, npz, rims, *refs), [((devices * size...  2.76 us
    pallas_call x2, Pallas kernels, shards(): call(lambda *refs: residual_kernel(lz, zrim[0], *refs), [((nx, count), F3...  2.38 us
    pallas_call x1, Pallas kernels, shards(): call(lambda *refs: tables_kernel(npy, npz, ly, lz, *refs), [((2 * nx, nx)...  2.01 us
    pallas_call x1, Pallas kernels, shards(): call(lambda *refs: stencil_kernel(ly, lz, ny, nz, *refs), [((4 * count, w...  1.82 us
  transfers between devices with their start and end apart: 6, of which 3 were waited for; matrix products, arithmetic and copies ran while one was open for 0% of the time, Pallas kernels for 5%

profile of v6, /device:TPU:0, one launch (start us, length us, event | category | flops | bytes accessed | tf_op | source)
XLA Modules:
  0.0 84.7 jit_solution(3672219663565442980)
XLA Ops:
  0.6 1.2 %shard_map.149 = (f32[128,512]{1,0:T(8,128)S(1)}, f32[128,512]{1,0:T(8,128)S(1)}, f32[48,512]{1,0:T(8,128)S(1)}, f32[48,512]{1,0:T(8,128)S(1)}) custom-call(f32[8]{0:T(128)} %refs_0_.3, s32[128,512]{1,0:T(8,128)} %bitcast.30, f32[128,512]{1,0:T(8,128)} %bitcast.20), custom_call_target="tpu_custom_call" | custom-call | flops 1048576 | bytes 1048576 | tf_op jit(solution)/shard_map/pallas_call | solution.py:518
  1.9 0.5 collective-permute-start
  2.4 4.1 %collective-permute-start.1 = (f32[48,512]{1,0:T(8,128)S(1)}, f32[48,512]{1,0:T(8,128)S(1)}, u32[]{:S(2)}, u32[]{:S(2)}) collective-permute-start(f32[48,512]{1,0:T(8,128)S(1)} %get-tuple-element.30.refs_4_), channel_id=1, source_target_pairs={{0,1},{1,0},{2,3},{3,2},{4,5},{5,4},{6,7},{7,6},{8,9},{9,8},{10,11... | collective-permute-start | bytes 294920 | tf_op jit(solution)/shard_map/ppermute | solution.py:451
  6.5 1.8 %shard_map.150 = (bf16[512,256]{1,0:T(8,128)(2,1)S(1)}, f32[14,8,512]{2,1,0:T(8,128)S(1)}) custom-call(s32[2,512]{1,0:T(2,128)} %constant.2.clone.refs_0_, f32[7,2,8]{2,1,0:T(2,128)} %bitcast.32, f32[7,2,16]{2,1,0:T(2,128)} %bitcast.33, f32[7,2,512]{2,1,0:T(2,128)} %bitcast.31, f32[48,512]{1,0:T(8,128)S(1)} %get-tuple-element.30.refs_4_), custom_call_target="tpu_custom_call" | custom-call | flops 1966080 | bytes 262144 | tf_op jit(solution)/shard_map/pallas_call | solution.py:528
  8.4 0.0 collective-permute-done.refs_1_
  8.4 0.8 collective-permute-done.1.refs_2_
  9.1 0.1 shard_map.152
  9.2 0.8 collective-permute-start.2
  10.0 0.9 %collective-permute-start.3 = (f32[72,512]{1,0:T(8,128)S(1)}, f32[72,512]{1,0:T(8,128)S(1)}, u32[]{:S(2)}, u32[]{:S(2)}) collective-permute-start(f32[72,512]{1,0:T(8,128)S(1)} %get-tuple-element.44), channel_id=1, source_target_pairs={{0,4},{4,0},{8,12},{12,8},{16,20},{20,16},{24,28},{28,24},{1,5},{5... | collective-permute-start | bytes 442376 | tf_op jit(solution)/shard_map/ppermute | solution.py:451
  10.9 0.0 copy-start.1
  10.9 2.0 %shard_map.151 = (bf16[1024,512]{1,0:T(8,128)(2,1)S(1)}, bf16[256,256]{1,0:T(8,128)(2,1)S(1)}, bf16[256,256]{1,0:T(8,128)(2,1)S(1)}, bf16[64,256]{1,0:T(8,128)(2...) custom-call(f32[512,512]{1,0:T(8,128)} %refs_0_.4, ...), custom_call_target="tpu_custom_call" | custom-call | flops 2097152 | bytes 1048576 | tf_op jit(solution)/shard_map/pallas_call | solution.py:541
  12.9 3.3 %collective-permute-done.2.refs_3_ = f32[72,512]{1,0:T(8,128)S(1)} collective-permute-done((f32[72,512]{1,0:T(8,128)S(1)}, f32[72,512]{1,0:T(8,128)S(1)}, u32[]{:S(2)}, u32[]{:S(2)}) %collective-permute-start.2) | collective-permute-done | bytes 147488 | tf_op jit(solution)/shard_map/ppermute | solution.py:456
  16.2 0.0 collective-permute-done.3.refs_4_
  16.2 0.0 copy-done.1
  16.2 1.2 %shard_map.153 = f32[512,128]{1,0:T(8,128)S(1)} custom-call(f32[128,512]{1,0:T(8,128)S(1)} %get-tuple-element.39.refs_0_, f32[48,512]{1,0:T(8,128)S(1)} %get-tuple-element.41.refs_1_.refs_4_, f32[48,512]{1,0:T(8,128)S(1)} %get-tuple-element.42.refs_2_.refs_5_, f32[72,512]{1,0:T(8,128)S(1)} %collective-permute-done.2.refs_3_, ...), custom_call_target="tpu_custom_call" | custom-call | flops 402653184 | bytes 2359296 | tf_op jit(solution)/shard_map/pallas_call | solution.py:585
  17.4 14.3 %all_to_all.44 = f32[32,16,128]{2,1,0:T(8,128)S(1)} all-to-all(f32[32,16,128]{2,1,0:T(8,128)S(1)} %bitcast.24), channel_id=1, replica_groups=mesh['py'=8,'pz'=4] {'py','pz'}, dimensions={0} | all-to-all | bytes 524288 | tf_op jit(solution)/shard_map/all_to_all | solution.py:591
  31.7 1.4 %shard_map.154 = f32[768,128]{1,0:T(8,128)S(1)} custom-call(bf16[256,256]{1,0:T(8,128)(2,1)S(1)} %get-tuple-element.32.refs_10_.refs_0_, bf16[256,256]{1,0:T(8,128)(2,1)S(1)} %get-tuple-element.33.refs_1_, bf16[64,256]{1,0:T(8,128)(2,1)S(1)} %get-tuple-element.34.refs_2_, bf16[64,256]{1,0:T(8,128)(2,1)S(1)} %get-tuple-element.35.refs_3_, ...), custom_call_target="tpu_custom_call" | custom-call | flops 402653184 | bytes 524288 | tf_op jit(solution)/shard_map/pallas_call | solution.py:558
  33.2 0.0 copy-start
  33.2 14.4 %all_to_all.45 = f32[32,24,128]{2,1,0:T(8,128)S(1)} all-to-all(f32[32,24,128]{2,1,0:T(8,128)S(1)} %bitcast.18), channel_id=1, replica_groups=mesh['py'=8,'pz'=4] {'py','pz'}, dimensions={0} | all-to-all | bytes 786432 | tf_op jit(solution)/shard_map/all_to_all | solution.py:593
  47.5 0.0 copy-done
  47.5 0.6 shard_map.155
  48.2 2.1 %collective-permute-start.4 = (f32[72,512]{1,0:T(8,128)S(1)}, f32[72,512]{1,0:T(8,128)S(1)}, u32[]{:S(2)}, u32[]{:S(2)}) collective-permute-start(f32[72,512]{1,0:T(8,128)S(1)} %get-tuple-element.51), channel_id=1, source_target_pairs={{0,28},{4,8},{8,4},{12,16},{16,12},{20,24},{24,20},{28,0},{1,29},{... | collective-permute-start | bytes 442376 | tf_op jit(solution)/shard_map/ppermute | solution.py:456
  50.3 0.0 collective-permute-start.5
  50.3 3.8 %collective-permute-done.4.refs_3_ = f32[72,512]{1,0:T(8,128)S(1)} collective-permute-done((f32[72,512]{1,0:T(8,128)S(1)}, f32[72,512]{1,0:T(8,128)S(1)}, u32[]{:S(2)}, u32[]{:S(2)}) %collective-permute-start.4) | collective-permute-done | bytes 147488 | tf_op jit(solution)/shard_map/ppermute | solution.py:456
  54.1 0.0 collective-permute-done.5.refs_4_
  54.1 1.2 %shard_map.156 = (f32[512,128]{1,0:T(8,128)S(1)}, f32[128,512]{1,0:T(8,128)S(1)}) custom-call(f32[128,512]{1,0:T(8,128)S(1)} %get-tuple-element.48.refs_0_, f32[24,512]{1,0:T(8,128)S(1)} %get-tuple-element.49.refs_1_, f32[24,512]{1,0:T(8,128)S(1)} %get-tuple-element.50.refs_2_, f32[72,512]{1,0:T(8,128)S(1)} %collective-permute-done.4.refs_3_, ...), custom_call_target="tpu_custom_call" | custom-call | flops 402653184 | bytes 2359296 | tf_op jit(solution)/shard_map/pallas_call | solution.py:585
  55.3 14.2 %all_to_all.46 = f32[32,16,128]{2,1,0:T(8,128)S(1)} all-to-all(f32[32,16,128]{2,1,0:T(8,128)S(1)} %bitcast.27), channel_id=1, replica_groups=mesh['py'=8,'pz'=4] {'py','pz'}, dimensions={0} | all-to-all | bytes 524288 | tf_op jit(solution)/shard_map/all_to_all | solution.py:591
  69.5 1.3 %shard_map.157 = f32[512,128]{1,0:T(8,128)S(1)} custom-call(bf16[256,256]{1,0:T(8,128)(2,1)S(1)} %get-tuple-element.32.refs_10_.refs_0_, bf16[256,256]{1,0:T(8,128)(2,1)S(1)} %get-tuple-element.33.refs_1_, bf16[64,256]{1,0:T(8,128)(2,1)S(1)} %get-tuple-element.34.refs_2_, bf16[64,256]{1,0:T(8,128)(2,1)S(1)} %get-tuple-element.35.refs_3_, ...), custom_call_target="tpu_custom_call" | custom-call | flops 402653184 | bytes 524288 | tf_op jit(solution)/shard_map/pallas_call | solution.py:558
  70.8 12.7 %all_to_all.47 = f32[32,16,128]{2,1,0:T(8,128)S(1)} all-to-all(f32[32,16,128]{2,1,0:T(8,128)S(1)} %bitcast.29), channel_id=1, replica_groups=mesh['py'=8,'pz'=4] {'py','pz'}, dimensions={0} | all-to-all | bytes 524288 | tf_op jit(solution)/shard_map/all_to_all | solution.py:593
  83.5 1.1 %shard_map.158 = (f32[128,512]{1,0:T(8,128)}, f32[128,512]{1,0:T(8,128)}) custom-call(f32[512,128]{1,0:T(8,128)S(1)} %bitcast.22, bf16[1024,512]{1,0:T(8,128)(2,1)S(1)} %get-tuple-element.47.refs_9_.refs_1_.vectors_ref, f32[128,512]{1,0:T(8,128)S(1)} %get-tuple-element.54.field_ref, f32[128,512]{1,0:T(8,128)S(1)} %get-tuple-element.55.residual_ref), custom_call_target="tpu_custom_call" | custom-call | flops 201326592 | bytes 2097152 | tf_op jit(solution)/shard_map/pallas_call | solution.py:596
Async XLA Ops:
  1.9 6.5 %collective-permute-start = (f32[48,512]{1,0:T(8,128)S(1)}, f32[48,512]{1,0:T(8,128)S(1)}, u32[]{:S(2)}, u32[]{:S(2)}) collective-permute-start(f32[48,512]{1,0:T(8,128)S(1)} %get-tuple-element.40), channel_id=1, source_target_pairs={{0,4},{4,0},{8,12},{12,8},{16,20},{20,16},{24,28},{28,24},{1,2},{5... | collective-permute-start | bytes 294920 | tf_op jit(solution)/shard_map/ppermute | solution.py:471
  2.4 6.7 %collective-permute-start.1 = (f32[48,512]{1,0:T(8,128)S(1)}, f32[48,512]{1,0:T(8,128)S(1)}, u32[]{:S(2)}, u32[]{:S(2)}) collective-permute-start(f32[48,512]{1,0:T(8,128)S(1)} %get-tuple-element.30.refs_4_), channel_id=1, source_target_pairs={{0,1},{1,0},{2,3},{3,2},{4,5},{5,4},{6,7},{7,6},{8,9},{9,8},{10,11... | collective-permute-start | bytes 294920 | tf_op jit(solution)/shard_map/ppermute | solution.py:451
  9.2 7.0 %collective-permute-start.2 = (f32[72,512]{1,0:T(8,128)S(1)}, f32[72,512]{1,0:T(8,128)S(1)}, u32[]{:S(2)}, u32[]{:S(2)}) collective-permute-start(f32[72,512]{1,0:T(8,128)S(1)} %get-tuple-element.43), channel_id=1, source_target_pairs={{0,28},{4,8},{8,4},{12,16},{16,12},{20,24},{24,20},{28,0},{1,29},{... | collective-permute-start | bytes 442376 | tf_op jit(solution)/shard_map/ppermute | solution.py:456
  10.0 6.2 %collective-permute-start.3 = (f32[72,512]{1,0:T(8,128)S(1)}, f32[72,512]{1,0:T(8,128)S(1)}, u32[]{:S(2)}, u32[]{:S(2)}) collective-permute-start(f32[72,512]{1,0:T(8,128)S(1)} %get-tuple-element.44), channel_id=1, source_target_pairs={{0,4},{4,0},{8,12},{12,8},{16,20},{20,16},{24,28},{28,24},{1,5},{5... | collective-permute-start | bytes 442376 | tf_op jit(solution)/shard_map/ppermute | solution.py:451
  10.9 5.3 %copy-start.1 = (f32[8,16,512]{2,1,0:T(8,128)S(1)}, f32[8,16,512]{2,1,0:T(8,128)}, u32[]{:S(2)}) copy-start(f32[8,16,512]{2,1,0:T(8,128)} %param.15) | copy-start | bytes 786436
  33.2 14.4 %copy-start = (f32[8,16,512]{2,1,0:T(8,128)S(1)}, f32[8,16,512]{2,1,0:T(8,128)}, u32[]{:S(2)}) copy-start(f32[8,16,512]{2,1,0:T(8,128)} %param.14) | copy-start | bytes 786436
  48.2 5.9 %collective-permute-start.4 = (f32[72,512]{1,0:T(8,128)S(1)}, f32[72,512]{1,0:T(8,128)S(1)}, u32[]{:S(2)}, u32[]{:S(2)}) collective-permute-start(f32[72,512]{1,0:T(8,128)S(1)} %get-tuple-element.51), channel_id=1, source_target_pairs={{0,28},{4,8},{8,4},{12,16},{16,12},{20,24},{24,20},{28,0},{1,29},{... | collective-permute-start | bytes 442376 | tf_op jit(solution)/shard_map/ppermute | solution.py:456
  50.3 3.8 %collective-permute-start.5 = (f32[72,512]{1,0:T(8,128)S(1)}, f32[72,512]{1,0:T(8,128)S(1)}, u32[]{:S(2)}, u32[]{:S(2)}) collective-permute-start(f32[72,512]{1,0:T(8,128)S(1)} %get-tuple-element.52), channel_id=1, source_target_pairs={{0,4},{4,0},{8,12},{12,8},{16,20},{20,16},{24,28},{28,24},{1,5},{5... | collective-permute-start | bytes 442376 | tf_op jit(solution)/shard_map/ppermute | solution.py:451

commit v7 on v6

--- a/solution.py
+++ b/solution.py
@@ -72,10 +72,11 @@
 
 
 def coefficient_kernel(
-    ly, lz, table_ref, span_ref, field_ref, coef_ref, weighted_ref, even_ref, odd_ref, table, span, field, sem
+    ly, lz, table_ref, span_ref, field_ref, coef_ref, weighted_ref, even_ref, odd_ref, yodd_ref, yeven_ref,
+    table, span, field, sem,
 ):
     fetch(((table_ref, table), (span_ref, span), (field_ref, field)), sem)
-    first = lax.rem(lax.axis_index("pz"), 2) == 0
+    first = lax.rem(lax.axis_index("py") + lax.axis_index("pz"), 2) == 1
     half = ly * REACH
     entries = [table[entry] for entry in range(table_ref.shape[0])]
     for start in range(0, span.shape[0], lz):
@@ -92,31 +93,39 @@
             low, high = value[:REACH], value[lz - REACH :]
             even_ref[rim, :] = jnp.where(first, high, low)
             odd_ref[rim, :] = jnp.where(first, low, high)
-
-
-def store_y_rims(ly, lz, weighted_ref, zlow, zhigh, odd_ref, even_ref):
+    store_y_rims(own_rim(ly, lz, weighted_ref), yodd_ref, yeven_ref)
+
+
+def store_y_rims(pieces, odd_ref, even_ref):
     first = lax.rem(lax.axis_index("py"), 2) == 0
-    own, side = REACH * lz, REACH * REACH
-    for at, count, ref, start, step in ((0, own, weighted_ref, ly - REACH, lz),) + tuple(
-        (own + k * side, side, ref, ly - REACH, REACH) for k, ref in enumerate((zlow, zhigh))
-    ):
-        low, high = ref[:count, :], ref[start * step : start * step + count, :]
+    at = 0
+    for value, count, rows in pieces:
+        low, high = value[:count, :], value[rows - count : rows, :]
         even_ref[at : at + count, :] = jnp.where(first, high, low)
         odd_ref[at : at + count, :] = jnp.where(first, low, high)
-    end = own + 2 * side
-    for ref in (even_ref, odd_ref):
-        ref[end:, :] = jnp.zeros((ref.shape[0] - end, ref.shape[1]), F32)
-
-
-def y_rims_kernel(ly, lz, weighted_ref, odd_ref, even_ref, _, zlow_ref, zhigh_ref, yodd_ref, yeven_ref):
-    first = lax.rem(lax.axis_index("pz"), 2) == 0
+        at += count
+    if at < even_ref.shape[0]:
+        for ref in (even_ref, odd_ref):
+            ref[at:, :] = jnp.zeros((ref.shape[0] - at, ref.shape[1]), F32)
+
+
+def own_rim(ly, lz, weighted):
+    return [(weighted, REACH * lz, ly * lz)]
+
+
+def corners(ly, zlow, zhigh):
+    return [(value, REACH * REACH, ly * REACH) for value in (zlow, zhigh)]
+
+
+def y_rims_kernel(ly, odd_ref, even_ref, _, zlow_ref, zhigh_ref, yodd_ref, yeven_ref):
+    first = lax.rem(lax.axis_index("py") + lax.axis_index("pz"), 2) == 1
     zlow_ref[...] = jnp.where(first, odd_ref[...], even_ref[...])
     zhigh_ref[...] = jnp.where(first, even_ref[...], odd_ref[...])
-    store_y_rims(ly, lz, weighted_ref, zlow_ref, zhigh_ref, yodd_ref, yeven_ref)
+    store_y_rims(corners(ly, zlow_ref, zhigh_ref), yodd_ref, yeven_ref)
 
 
 def next_y_rims_kernel(ly, lz, weighted_ref, zlow_ref, zhigh_ref, yodd_ref, yeven_ref):
-    store_y_rims(ly, lz, weighted_ref, zlow_ref, zhigh_ref, yodd_ref, yeven_ref)
+    store_y_rims(own_rim(ly, lz, weighted_ref) + corners(ly, zlow_ref, zhigh_ref), yodd_ref, yeven_ref)
 
 
 def point_columns(ly, lz):
@@ -263,17 +272,18 @@
         sums_ref[:, mode * nz : (mode + 2) * nz] = yz + x
 
 
-def residual_kernel(
-    lz, zrim, weighted_ref, zlow_ref, zhigh_ref, yodd_ref, yeven_ref, stencil_ref, taps_ref, coef_ref, right_ref, vectors_ref,
-    _, spectral_ref, residual_ref,
-):
+def residual_kernel(lz, zrim, parts, *refs):
+    weighted_ref, zlow_ref, zhigh_ref, *refs = refs
+    yodd_refs, yeven_refs, refs = refs[:parts], refs[parts : 2 * parts], refs[2 * parts :]
+    stencil_ref, taps_ref, coef_ref, right_ref, vectors_ref, _, spectral_ref, residual_ref = refs
     count, nx = weighted_ref.shape
     part, need = count // 2, weighted_ref.shape[0] // 2 + REACH * lz
     own = split(weighted_ref[...])
     zrims = split(jnp.concatenate([zlow_ref[:zrim, :], zhigh_ref[:zrim, :]], axis=0))
     fields = []
     even = lax.rem(lax.axis_index("py"), 2) == 0
-    below, above = jnp.where(even, yodd_ref[...], yeven_ref[...]), jnp.where(even, yeven_ref[...], yodd_ref[...])
+    yodd, yeven = (jnp.concatenate([ref[...] for ref in refs], axis=0) for refs in (yodd_refs, yeven_refs))
+    below, above = jnp.where(even, yodd, yeven), jnp.where(even, yeven, yodd)
     for half, rim in enumerate((below, above)):
         missing = stencil_ref.shape[1] - need - 2 * zrim - rim.shape[0]
         yrim = split(jnp.concatenate([rim, jnp.zeros((missing, nx), F32)], axis=0) if missing else rim)
@@ -434,7 +444,7 @@
     for side, (ref, before_ref) in enumerate(((zlow_ref, before_low_ref), (zhigh_ref, before_high_ref))):
         start = count + side * half
         ref[...] = before_ref[:half, :] + before_ref[half:, :] * update[start : start + half]
-    store_y_rims(ly, lz, weighted_ref, zlow_ref, zhigh_ref, yodd_ref, yeven_ref)
+    store_y_rims(own_rim(ly, lz, weighted_ref) + corners(ly, zlow_ref, zhigh_ref), yodd_ref, yeven_ref)
 
 
 def last_update_kernel(spectral_ref, vectors_ref, field_ref, residual_ref, updated_hbm, residual_hbm, held, sem):
@@ -468,6 +478,17 @@
         for k in range(across):
             j = i + 1 if i % 2 else i - 1
             pairs.append((spot(i, k), spot(j, k) if 0 <= j < count else spot(i, k ^ 1)))
+    return lax.ppermute(value, BOTH, pairs)
+
+
+def staggered(value, parity):
+    across, count = lax.axis_size("py"), lax.axis_size("pz")
+    pairs = []
+    for i in range(across):
+        for k in range(count):
+            j = k + 1 if (i + k) % 2 == parity else k - 1
+            other = i ^ 2 if i ^ 2 < across else i
+            pairs.append((i * count + k, i * count + j if 0 <= j < count else other * count + k))
     return lax.ppermute(value, BOTH, pairs)
 
 
@@ -515,9 +536,9 @@
     cell = count * nx * 4
     dma = pltpu.SemaphoreType.DMA
 
-    coef, weighted, even, odd = call(
+    coef, weighted, even, odd, yodd, yeven = call(
         lambda *refs: coefficient_kernel(ly, lz, *refs),
-        [(block, F32), (block, F32), (zrims, F32), (zrims, F32)],
+        [(block, F32)] * 2 + [(zrims, F32)] * 2 + [((REACH * lz, nx), F32)] * 2,
         [HBM] * 3, count * nx * 16, 4 * cell,
         [pltpu.SMEM(coef_table.shape, F32), pltpu.VMEM(block, jnp.int32), pltpu.VMEM(block, F32), dma((3,))],
     )(*in_hbm(coef_table, span_index.reshape(count, nx), field))
@@ -574,20 +595,23 @@
                 received, npy, npz, ly, lz, xpart, yaxis_values, zaxis_values, yaxis_vectors, zaxis_vectors
             )
 
-    even, odd = pairwise(even, "pz", 0), odd_pairs(odd, "pz", "py")
-    zlow, zhigh, yodd, yeven = call(
-        lambda *refs: y_rims_kernel(ly, lz, *refs),
-        [(zrims, F32)] * 2 + [(yrim, F32)] * 2, [VMEM] * 3 + [ANY], nx, 4 * nx * 4 * (yrim[0] + zrims[0]),
-    )(weighted, odd, even, taps)
+    even, odd = staggered(even, 1), staggered(odd, 0)
+    zlow, zhigh, *corner = call(
+        lambda *refs: y_rims_kernel(ly, *refs),
+        [(zrims, F32)] * 2 + [((up8(2 * REACH * REACH), nx), F32)] * 2,
+        [VMEM] * 2 + [ANY], nx, 4 * nx * 4 * zrims[0],
+    )(odd, even, taps)
+    yodd, yeven = [yodd, corner[0]], [yeven, corner[1]]
     for iteration in range(ITERS):
         last = iteration + 1 == ITERS
-        yodd, yeven = paired(yodd, "py"), pairwise(yeven, "py", 0)
+        yodd, yeven = [paired(value, "py") for value in yodd], [pairwise(value, "py", 0) for value in yeven]
+        parts = len(yodd)
         spectral, *residual = call(
-            lambda *refs: residual_kernel(lz, zrim[0], *refs),
+            lambda *refs: residual_kernel(lz, zrim[0], parts, *refs),
             [((nx, count), F32)] + [(block, F32)] * last,
-            [VMEM] * 10 + [ANY], 6 * count * nx * (nx + 2 * width), 5 * cell + 4 * nx * nx,
+            [VMEM] * (8 + 2 * parts) + [ANY], 6 * count * nx * (nx + 2 * width), 5 * cell + 4 * nx * nx,
             [pltpu.VMEM(block, F32)] * (not last),
-        )(weighted, zlow, zhigh, yodd, yeven, stencil, taps, coef, right, vectors, tables[0])
+        )(weighted, zlow, zhigh, *yodd, *yeven, stencil, taps, coef, right, vectors, tables[0])
         spectral = lax.all_to_all(spectral, BOTH, split_axis=0, concat_axis=0, tiled=True)
         spectral = precondition(spectral, not last)
         spectral = lax.all_to_all(spectral, BOTH, split_axis=0, concat_axis=0, tiled=True)
@@ -598,7 +622,7 @@
                 [pltpu.VMEM(block, F32), dma((2,))], [HBM] * 2,
             )(spectral, vectors, field, *residual)
         elif fast:
-            field, weighted, zlow, zhigh, yodd, yeven = call(
+            field, weighted, zlow, zhigh, *yrims = call(
                 lambda *refs: rim_update_kernel(ly, lz, devices, *refs),
                 [(block, F32)] * 2 + [(zrim, F32)] * 2 + [(yrim, F32)] * 2, [VMEM] * 6, *cost,
             )(spectral, vectors, field, coef, zlow, zhigh)
@@ -607,10 +631,11 @@
                 lambda *refs: update_kernel(ly, lz, *refs), [(block, F32)] * 2 + [(zrim, F32)] * 2, [VMEM] * 4, *cost,
             )(spectral, vectors, field, coef)
             zlow, zhigh = around(zhigh, "pz", 1), around(zlow, "pz", -1)
-            yodd, yeven = call(
+            yrims = call(
                 lambda *refs: next_y_rims_kernel(ly, lz, *refs),
                 [(yrim, F32)] * 2, [VMEM] * 3, nx, 4 * nx * 4 * yrim[0],
             )(weighted, zlow, zhigh)
+        yodd, yeven = ([value] for value in yrims) if not last else (None, None)
     return (field.reshape(solution.shape), residual.reshape(solution.shape))
 
 

time: 85 us -> 83.4 us (0.981)
  waiting for transfers between devices: 7.91 us -> 3.85 us
  starting transfers between devices: 8.43 us -> 10.6 us
    ppermute x1 -> x2, starting transfers between devices: 0.52 us -> 4.58 us  [staggered(): return lax.ppermute(value, BOTH, pairs)]
    ppermute x3, starting transfers between devices: 5.02 us -> 0.99 us  [pairwise(): lax.ppermute(value, axis, [(i, j if 0 <= j < count else i) for i, j in en...]
    ppermute x2 -> x3, waiting for transfers between devices: 7.15 us -> 3.83 us  [paired(): lax.ppermute(value, axis, [(i, (i + 1 if i % 2 else i - 1) % count) for i...]
    ppermute x2 -> x3, starting transfers between devices: 2.89 us -> 5.06 us  [paired(): lax.ppermute(value, axis, [(i, (i + 1 if i % 2 else i - 1) % count) for i...]
  transfers between devices with their start and end apart: 6 -> 8, of which waited for: 3 -> 1; matrix products, arithmetic and copies ran while one was open for 0% -> 0% of each run, Pallas kernels for 5% -> 5%
where the time goes in v7:
time: 83.4 us; the launch traced here: 83.1 us
  blocking collectives  55.8 us (67%)
  Pallas kernels  12 us (14%)
  starting transfers between devices  10.6 us (13%)
  waiting for transfers between devices  3.85 us (5%)
    all_to_all x4, blocking collectives, shards(): lax.all_to_all(spectral, BOTH, split_axis=0, concat_axis=0, tiled=True)  55.8 us
    ppermute x3, starting transfers between devices, paired(): lax.ppermute(value, axis, [(i, (i + 1 if i % 2 else i - 1) % count) for i...  5.06 us
    ppermute x2, starting transfers between devices, staggered(): return lax.ppermute(value, BOTH, pairs)  4.58 us
    ppermute x3, waiting for transfers between devices, paired(): lax.ppermute(value, axis, [(i, (i + 1 if i % 2 else i - 1) % count) for i...  3.83 us
    pallas_call x2, Pallas kernels, precondition(): call(lambda *refs: modes_kernel(npy, npz, rims, *refs), [((devices * size...  2.76 us
    pallas_call x2, Pallas kernels, shards(): call(lambda *refs: residual_kernel(lz, zrim[0], parts, *refs), [((nx, cou...  2.38 us
    pallas_call x1, Pallas kernels, shards(): call(lambda *refs: tables_kernel(npy, npz, ly, lz, *refs), [((2 * nx, nx)...  2.01 us
    pallas_call x1, Pallas kernels, shards(): call(lambda *refs: stencil_kernel(ly, lz, ny, nz, *refs), [((4 * count, w...  1.81 us
  transfers between devices with their start and end apart: 8, of which 1 were waited for; matrix products, arithmetic and copies ran while one was open for 0% of the time, Pallas kernels for 5%

profile of v7, /device:TPU:0, one launch (start us, length us, event | category | flops | bytes accessed | tf_op | source)
XLA Modules:
  0.0 83.1 jit_solution(4349151560737137548)
XLA Ops:
  0.6 1.3 %shard_map.149 = (f32[128,512]{1,0:T(8,128)S(1)}, f32[128,512]{1,0:T(8,128)S(1)}, f32[48,512]{1,0:T(8,128)S(1)}, f32[48,512]{1,0:T(8,128)S(1)}, f32[48,512]{1,0:T(8,128)S(1)}, /*index=5*/f32[48,512]{1,0:T(8,128)S(1)}) custom-call(f32[8]{0:T(128)} %refs_0_.3, s32[128,512]{1,0:T(8,128)} %bitcast.30, f32[128,512]{1,0:T(8,128)} %bitcast.20), custom_call_target="tpu_custom_call" | custom-call | flops 1048576 | bytes 1048576 | tf_op jit(solution)/shard_map/pallas_call | solution.py:539
  1.9 3.1 %collective-permute-start = (f32[48,512]{1,0:T(8,128)S(1)}, f32[48,512]{1,0:T(8,128)S(1)}, u32[]{:S(2)}, u32[]{:S(2)}) collective-permute-start(f32[48,512]{1,0:T(8,128)S(1)} %get-tuple-element.42), channel_id=1, source_target_pairs={{0,1},{1,0},{2,3},{3,2},{4,12},{5,6},{6,5},{7,15},{8,9},{9,8},{10,... | collective-permute-start | bytes 294920 | tf_op jit(solution)/shard_map/ppermute | solution.py:492
  5.0 1.5 %collective-permute-start.1 = (f32[48,512]{1,0:T(8,128)S(1)}, f32[48,512]{1,0:T(8,128)S(1)}, u32[]{:S(2)}, u32[]{:S(2)}) collective-permute-start(f32[48,512]{1,0:T(8,128)S(1)} %get-tuple-element.32.refs_4_), channel_id=1, source_target_pairs={{0,8},{1,2},{2,1},{3,11},{4,5},{5,4},{6,7},{7,6},{8,0},{9,10},{10,... | collective-permute-start | bytes 294920 | tf_op jit(solution)/shard_map/ppermute | solution.py:492
  6.5 1.4 %collective-permute-start.2 = (f32[48,512]{1,0:T(8,128)S(1)}, f32[48,512]{1,0:T(8,128)S(1)}, u32[]{:S(2)}, u32[]{:S(2)}) collective-permute-start(f32[48,512]{1,0:T(8,128)S(1)} %get-tuple-element.45), channel_id=1, source_target_pairs={{0,28},{4,8},{8,4},{12,16},{16,12},{20,24},{24,20},{28,0},{1,29},{... | collective-permute-start | bytes 294920 | tf_op jit(solution)/shard_map/ppermute | solution.py:466
  7.9 0.0 collective-permute-start.4
  7.9 1.8 %shard_map.150 = (bf16[512,256]{1,0:T(8,128)(2,1)S(1)}, f32[14,8,512]{2,1,0:T(8,128)S(1)}) custom-call(s32[2,512]{1,0:T(2,128)} %constant.2.clone.refs_0_, f32[7,2,8]{2,1,0:T(2,128)} %bitcast.32, f32[7,2,16]{2,1,0:T(2,128)} %bitcast.33, f32[7,2,512]{2,1,0:T(2,128)} %bitcast.31, f32[48,512]{1,0:T(8,128)S(1)} %get-tuple-element.32.refs_4_), custom_call_target="tpu_custom_call" | custom-call | flops 1966080 | bytes 262144 | tf_op jit(solution)/shard_map/pallas_call | solution.py:549
  9.7 0.0 collective-permute-done.refs_0_
  9.7 0.0 collective-permute-done.1.refs_1_
  9.8 1.6 %collective-permute-start.3 = (f32[24,512]{1,0:T(8,128)S(1)}, f32[24,512]{1,0:T(8,128)S(1)}, u32[]{:S(2)}, u32[]{:S(2)}) collective-permute-start(f32[24,512]{1,0:T(8,128)S(1)} %get-tuple-element.46), channel_id=1, source_target_pairs={{0,28},{4,8},{8,4},{12,16},{16,12},{20,24},{24,20},{28,0},{1,29},{... | collective-permute-start | bytes 147464 | tf_op jit(solution)/shard_map/ppermute | solution.py:466
  11.3 1.0 %collective-permute-start.5 = (f32[24,512]{1,0:T(8,128)S(1)}, f32[24,512]{1,0:T(8,128)S(1)}, u32[]{:S(2)}, u32[]{:S(2)}) collective-permute-start(f32[24,512]{1,0:T(8,128)S(1)} %get-tuple-element.48), channel_id=1, source_target_pairs={{0,4},{4,0},{8,12},{12,8},{16,20},{20,16},{24,28},{28,24},{1,5},{5... | collective-permute-start | bytes 147464 | tf_op jit(solution)/shard_map/ppermute | solution.py:461
  12.3 2.0 %shard_map.151 = (bf16[1024,512]{1,0:T(8,128)(2,1)S(1)}, bf16[256,256]{1,0:T(8,128)(2,1)S(1)}, bf16[256,256]{1,0:T(8,128)(2,1)S(1)}, bf16[64,256]{1,0:T(8,128)(2...) custom-call(f32[512,512]{1,0:T(8,128)} %refs_0_.4, ...), custom_call_target="tpu_custom_call" | custom-call | flops 2097152 | bytes 1048576 | tf_op jit(solution)/shard_map/pallas_call | solution.py:562
  14.4 0.0 collective-permute-done.2.refs_3_
  14.4 0.0 collective-permute-done.4.refs_5_
  14.4 0.0 collective-permute-done.3.refs_4_
  14.4 0.0 collective-permute-done.5.refs_6_
  14.4 0.0 copy-done.1
  14.4 1.2 %shard_map.153 = f32[512,128]{1,0:T(8,128)S(1)} custom-call(f32[128,512]{1,0:T(8,128)S(1)} %get-tuple-element.41.refs_0_, f32[48,512]{1,0:T(8,128)S(1)} %get-tuple-element.43.refs_1_.refs_4_, f32[48,512]{1,0:T(8,128)S(1)} %get-tuple-element.44.refs_2_.refs_5_, f32[48,512]{1,0:T(8,128)S(1)} %collective-permute-done.2.refs_3_, ...), custom_call_target="tpu_custom_call" | custom-call | flops 402653184 | bytes 2359296 | tf_op jit(solution)/shard_map/pallas_call | solution.py:609
  15.6 14.6 %all_to_all.44 = f32[32,16,128]{2,1,0:T(8,128)S(1)} all-to-all(f32[32,16,128]{2,1,0:T(8,128)S(1)} %bitcast.23), channel_id=1, replica_groups=mesh['py'=8,'pz'=4] {'py','pz'}, dimensions={0} | all-to-all | bytes 524288 | tf_op jit(solution)/shard_map/all_to_all | solution.py:615
  30.2 1.4 %shard_map.154 = f32[768,128]{1,0:T(8,128)S(1)} custom-call(bf16[256,256]{1,0:T(8,128)(2,1)S(1)} %get-tuple-element.34.refs_12_.refs_0_.refs_10_, bf16[256,256]{1,0:T(8,128)(2,1)S(1)} %get-tuple-element.35.refs_1_, bf16[64,256]{1,0:T(8,128)(2,1)S(1)} %get-tuple-element.36.refs_2_, bf16[64,256]{1,0:T(8,128)(2,1)S(1)} %get-tuple-element.37.refs_3_, ...), custom_call_target="tpu_custom_call" | custom-call | flops 402653184 | bytes 524288 | tf_op jit(solution)/shard_map/pallas_call | solution.py:579
  31.6 0.0 copy-start
  31.6 14.4 %all_to_all.45 = f32[32,24,128]{2,1,0:T(8,128)S(1)} all-to-all(f32[32,24,128]{2,1,0:T(8,128)S(1)} %bitcast.18), channel_id=1, replica_groups=mesh['py'=8,'pz'=4] {'py','pz'}, dimensions={0} | all-to-all | bytes 786432 | tf_op jit(solution)/shard_map/all_to_all | solution.py:617
  46.0 0.0 copy-done
  46.0 0.6 shard_map.155
  46.6 2.1 %collective-permute-start.6 = (f32[72,512]{1,0:T(8,128)S(1)}, f32[72,512]{1,0:T(8,128)S(1)}, u32[]{:S(2)}, u32[]{:S(2)}) collective-permute-start(f32[72,512]{1,0:T(8,128)S(1)} %get-tuple-element.55), channel_id=1, source_target_pairs={{0,28},{4,8},{8,4},{12,16},{16,12},{20,24},{24,20},{28,0},{1,29},{... | collective-permute-start | bytes 442376 | tf_op jit(solution)/shard_map/ppermute | solution.py:466
  48.7 0.0 collective-permute-start.7
  48.7 3.8 %collective-permute-done.6.refs_3_ = f32[72,512]{1,0:T(8,128)S(1)} collective-permute-done((f32[72,512]{1,0:T(8,128)S(1)}, f32[72,512]{1,0:T(8,128)S(1)}, u32[]{:S(2)}, u32[]{:S(2)}) %collective-permute-start.6) | collective-permute-done | bytes 147488 | tf_op jit(solution)/shard_map/ppermute | solution.py:466
  52.5 0.0 collective-permute-done.7.refs_4_
  52.5 1.2 %shard_map.156 = (f32[512,128]{1,0:T(8,128)S(1)}, f32[128,512]{1,0:T(8,128)S(1)}) custom-call(f32[128,512]{1,0:T(8,128)S(1)} %get-tuple-element.52.refs_0_, f32[24,512]{1,0:T(8,128)S(1)} %get-tuple-element.53.refs_1_, f32[24,512]{1,0:T(8,128)S(1)} %get-tuple-element.54.refs_2_, f32[72,512]{1,0:T(8,128)S(1)} %collective-permute-done.6.refs_3_, ...), custom_call_target="tpu_custom_call" | custom-call | flops 402653184 | bytes 2359296 | tf_op jit(solution)/shard_map/pallas_call | solution.py:609
  53.7 14.2 %all_to_all.46 = f32[32,16,128]{2,1,0:T(8,128)S(1)} all-to-all(f32[32,16,128]{2,1,0:T(8,128)S(1)} %bitcast.27), channel_id=1, replica_groups=mesh['py'=8,'pz'=4] {'py','pz'}, dimensions={0} | all-to-all | bytes 524288 | tf_op jit(solution)/shard_map/all_to_all | solution.py:615
  67.9 1.3 %shard_map.157 = f32[512,128]{1,0:T(8,128)S(1)} custom-call(bf16[256,256]{1,0:T(8,128)(2,1)S(1)} %get-tuple-element.34.refs_12_.refs_0_.refs_10_, bf16[256,256]{1,0:T(8,128)(2,1)S(1)} %get-tuple-element.35.refs_1_, bf16[64,256]{1,0:T(8,128)(2,1)S(1)} %get-tuple-element.36.refs_2_, bf16[64,256]{1,0:T(8,128)(2,1)S(1)} %get-tuple-element.37.refs_3_, ...), custom_call_target="tpu_custom_call" | custom-call | flops 402653184 | bytes 524288 | tf_op jit(solution)/shard_map/pallas_call | solution.py:579
  69.2 12.7 %all_to_all.47 = f32[32,16,128]{2,1,0:T(8,128)S(1)} all-to-all(f32[32,16,128]{2,1,0:T(8,128)S(1)} %bitcast.29), channel_id=1, replica_groups=mesh['py'=8,'pz'=4] {'py','pz'}, dimensions={0} | all-to-all | bytes 524288 | tf_op jit(solution)/shard_map/all_to_all | solution.py:617
  82.0 1.1 %shard_map.158 = (f32[128,512]{1,0:T(8,128)}, f32[128,512]{1,0:T(8,128)}) custom-call(f32[512,128]{1,0:T(8,128)S(1)} %bitcast.22, bf16[1024,512]{1,0:T(8,128)(2,1)S(1)} %get-tuple-element.51.refs_11_.refs_1_.refs_9_.vectors_ref, f32[128,512]{1,0:T(8,128)S(1)} %get-tuple-element.58.field_ref, f32[128,512]{1,0:T(8,128)S(1)} %get-tuple-element.59.residual_ref), custom_call_target="tpu_custom_call" | custom-call | flops 201326592 | bytes 2097152 | tf_op jit(solution)/shard_map/pallas_call | solution.py:620
  (2 shorter events, 0.0 us)
Async XLA Ops:
  1.9 7.8 %collective-permute-start = (f32[48,512]{1,0:T(8,128)S(1)}, f32[48,512]{1,0:T(8,128)S(1)}, u32[]{:S(2)}, u32[]{:S(2)}) collective-permute-start(f32[48,512]{1,0:T(8,128)S(1)} %get-tuple-element.42), channel_id=1, source_target_pairs={{0,1},{1,0},{2,3},{3,2},{4,12},{5,6},{6,5},{7,15},{8,9},{9,8},{10,... | collective-permute-start | bytes 294920 | tf_op jit(solution)/shard_map/ppermute | solution.py:492
  5.0 4.7 %collective-permute-start.1 = (f32[48,512]{1,0:T(8,128)S(1)}, f32[48,512]{1,0:T(8,128)S(1)}, u32[]{:S(2)}, u32[]{:S(2)}) collective-permute-start(f32[48,512]{1,0:T(8,128)S(1)} %get-tuple-element.32.refs_4_), channel_id=1, source_target_pairs={{0,8},{1,2},{2,1},{3,11},{4,5},{5,4},{6,7},{7,6},{8,0},{9,10},{10,... | collective-permute-start | bytes 294920 | tf_op jit(solution)/shard_map/ppermute | solution.py:492
  6.5 7.9 %collective-permute-start.2 = (f32[48,512]{1,0:T(8,128)S(1)}, f32[48,512]{1,0:T(8,128)S(1)}, u32[]{:S(2)}, u32[]{:S(2)}) collective-permute-start(f32[48,512]{1,0:T(8,128)S(1)} %get-tuple-element.45), channel_id=1, source_target_pairs={{0,28},{4,8},{8,4},{12,16},{16,12},{20,24},{24,20},{28,0},{1,29},{... | collective-permute-start | bytes 294920 | tf_op jit(solution)/shard_map/ppermute | solution.py:466
  7.9 6.5 %collective-permute-start.4 = (f32[48,512]{1,0:T(8,128)S(1)}, f32[48,512]{1,0:T(8,128)S(1)}, u32[]{:S(2)}, u32[]{:S(2)}) collective-permute-start(f32[48,512]{1,0:T(8,128)S(1)} %get-tuple-element.47), channel_id=1, source_target_pairs={{0,4},{4,0},{8,12},{12,8},{16,20},{20,16},{24,28},{28,24},{1,5},{5... | collective-permute-start | bytes 294920 | tf_op jit(solution)/shard_map/ppermute | solution.py:461
  9.8 4.6 %collective-permute-start.3 = (f32[24,512]{1,0:T(8,128)S(1)}, f32[24,512]{1,0:T(8,128)S(1)}, u32[]{:S(2)}, u32[]{:S(2)}) collective-permute-start(f32[24,512]{1,0:T(8,128)S(1)} %get-tuple-element.46), channel_id=1, source_target_pairs={{0,28},{4,8},{8,4},{12,16},{16,12},{20,24},{24,20},{28,0},{1,29},{... | collective-permute-start | bytes 147464 | tf_op jit(solution)/shard_map/ppermute | solution.py:466
  11.3 3.0 %collective-permute-start.5 = (f32[24,512]{1,0:T(8,128)S(1)}, f32[24,512]{1,0:T(8,128)S(1)}, u32[]{:S(2)}, u32[]{:S(2)}) collective-permute-start(f32[24,512]{1,0:T(8,128)S(1)} %get-tuple-element.48), channel_id=1, source_target_pairs={{0,4},{4,0},{8,12},{12,8},{16,20},{20,16},{24,28},{28,24},{1,5},{5... | collective-permute-start | bytes 147464 | tf_op jit(solution)/shard_map/ppermute | solution.py:461
  12.3 2.1 %copy-start.1 = (f32[8,16,512]{2,1,0:T(8,128)S(1)}, f32[8,16,512]{2,1,0:T(8,128)}, u32[]{:S(2)}) copy-start(f32[8,16,512]{2,1,0:T(8,128)} %param.15) | copy-start | bytes 786436
  31.6 14.4 %copy-start = (f32[8,16,512]{2,1,0:T(8,128)S(1)}, f32[8,16,512]{2,1,0:T(8,128)}, u32[]{:S(2)}) copy-start(f32[8,16,512]{2,1,0:T(8,128)} %param.14) | copy-start | bytes 786436
  46.6 5.9 %collective-permute-start.6 = (f32[72,512]{1,0:T(8,128)S(1)}, f32[72,512]{1,0:T(8,128)S(1)}, u32[]{:S(2)}, u32[]{:S(2)}) collective-permute-start(f32[72,512]{1,0:T(8,128)S(1)} %get-tuple-element.55), channel_id=1, source_target_pairs={{0,28},{4,8},{8,4},{12,16},{16,12},{20,24},{24,20},{28,0},{1,29},{... | collective-permute-start | bytes 442376 | tf_op jit(solution)/shard_map/ppermute | solution.py:466
  48.7 3.8 %collective-permute-start.7 = (f32[72,512]{1,0:T(8,128)S(1)}, f32[72,512]{1,0:T(8,128)S(1)}, u32[]{:S(2)}, u32[]{:S(2)}) collective-permute-start(f32[72,512]{1,0:T(8,128)S(1)} %get-tuple-element.56), channel_id=1, source_target_pairs={{0,4},{4,0},{8,12},{12,8},{16,20},{20,16},{24,28},{28,24},{1,5},{5... | collective-permute-start | bytes 442376 | tf_op jit(solution)/shard_map/ppermute | solution.py:461

commit v8 on v7

--- a/solution.py
+++ b/solution.py
@@ -71,11 +71,12 @@
         high_ref[y * REACH : (y + 1) * REACH, :] = weighted[(y + 1) * lz - REACH : (y + 1) * lz, :]
 
 
-def coefficient_kernel(
-    ly, lz, table_ref, span_ref, field_ref, coef_ref, weighted_ref, even_ref, odd_ref, yodd_ref, yeven_ref,
-    table, span, field, sem,
-):
-    fetch(((table_ref, table), (span_ref, span), (field_ref, field)), sem)
+def coefficient_kernel(ly, lz, small, *refs):
+    table_ref, span_ref, field_ref, *refs = refs
+    sources, refs = refs[:small], refs[small:]
+    coef_ref, weighted_ref, even_ref, odd_ref, yodd_ref, yeven_ref, *refs = refs
+    targets, (table, span, field, sem) = refs[:small], refs[small:]
+    fetch([(table_ref, table), (span_ref, span), (field_ref, field), *zip(sources, targets)], sem)
     first = lax.rem(lax.axis_index("py") + lax.axis_index("pz"), 2) == 1
     half = ly * REACH
     entries = [table[entry] for entry in range(table_ref.shape[0])]
@@ -94,6 +95,11 @@
             even_ref[rim, :] = jnp.where(first, high, low)
             odd_ref[rim, :] = jnp.where(first, low, high)
     store_y_rims(own_rim(ly, lz, weighted_ref), yodd_ref, yeven_ref)
+    ybands = targets[1]
+    for ref in (yodd_ref, yeven_ref):
+        for matrix in range(2):
+            at = REACH * lz + 8 * matrix
+            ref[at : at + ybands.shape[0], :ly] = ybands[:, matrix, :]
 
 
 def store_y_rims(pieces, odd_ref, even_ref):
@@ -144,16 +150,11 @@
     return np.array(halves, np.int32).T.copy()
 
 
-def stencil_kernel(
-    ly, lz, ny, nz, points_hbm, ybands_hbm, zbands_hbm, xbands_hbm, _, out_ref, taps_ref,
-    points_ref, ybands_ref, zbands_ref, xbands_ref, sem,
-):
-    fetch(
-        (
-            (points_hbm, points_ref), (ybands_hbm, ybands_ref), (zbands_hbm, zbands_ref), (xbands_hbm, xbands_ref),
-        ),
-        sem,
-    )
+def stencil_kernel(ly, lz, ny, nz, later, points_ref, ybands_ref, zbands_ref, *refs):
+    sources, (_, out_ref, *refs) = refs[:later], refs[later:]
+    copies = [pltpu.make_async_copy(*pair, refs[-1].at[i]) for i, pair in enumerate(zip(sources, refs[:later]))]
+    for copy in copies:
+        copy.start()
     count = ly * lz // 2
     width = out_ref.shape[1]
     for half in range(2):
@@ -179,6 +180,11 @@
         for part, value in enumerate((ymass * zmass, ystiff * zmass + ymass * zstiff)):
             at = (4 * half + part) * count
             out_ref[at : at + count, :], out_ref[at + 2 * count : at + 3 * count, :] = split(value)
+    for copy in copies:
+        copy.wait()
+
+
+def store_taps(xbands_ref, taps_ref):
     nx = xbands_ref.shape[2]
     lane = lax.broadcasted_iota(jnp.int32, (1, nx), 1)
     for offset in range(2 * REACH + 1):
@@ -190,7 +196,13 @@
             taps_ref[2 * offset + matrix] = jnp.broadcast_to(jnp.where(inside, band, 0.0), (8, nx))
 
 
-def xvectors_kernel(source, out_ref, held, sem):
+def doubled(size):
+    row = lax.broadcasted_iota(jnp.int32, (size, 2 * size), 0)
+    return (row == lax.rem(lax.broadcasted_iota(jnp.int32, (size, 2 * size), 1), size)).astype(F32)
+
+
+def xvectors_kernel(source, xbands_ref, out_ref, taps_ref, held, sem):
+    store_taps(xbands_ref, taps_ref)
     fetch(((source, held),), sem)
     high, low = split(held[...].T)
     out_ref[: high.shape[0], :] = high
@@ -198,27 +210,18 @@
 
 
 def tables_kernel(
-    npy, npz, ly, lz, xvec_hbm, yvec_hbm, zvec_hbm, xval_hbm, yval_hbm, zval_hbm, _,
-    xout_ref, zhigh_ref, zlow_ref, ydown_ref, yup_ref, sums_ref, rimhigh_ref, rimlow_ref,
-    xvec_ref, yvec_ref, zvec_ref, xval_ref, yval_ref, zval_ref, sem,
+    npy, npz, ly, lz, xvec_ref, yvec_ref, zvec_ref, yval_ref, zval_ref, xbands_ref, xval_hbm, _,
+    xout_ref, taps_ref, sums_ref, zhigh_ref, zlow_ref, ydown_ref, yup_ref, rimhigh_ref, rimlow_ref, xval_ref, sem,
 ):
-    fetch(
-        (
-            (xvec_hbm, xvec_ref), (yvec_hbm, yvec_ref), (zvec_hbm, zvec_ref),
-            (xval_hbm, xval_ref), (yval_hbm, yval_ref), (zval_hbm, zval_ref),
-        ),
-        sem,
-    )
+    fetching = pltpu.make_async_copy(xval_hbm, xval_ref, sem.at[0])
+    fetching.start()
+    store_taps(xbands_ref, taps_ref)
     ny, nz = npy * ly, npz * lz
     nx = xvec_ref.shape[0]
     high, low = split(xvec_ref[...].T)
     xout_ref[:nx, :] = high
     xout_ref[nx:, :] = low
-    twice = (
-        lax.broadcasted_iota(jnp.int32, (nz, 2 * nz), 0)
-        == lax.rem(lax.broadcasted_iota(jnp.int32, (nz, 2 * nz), 1), nz)
-    ).astype(F32)
-    pair = exact(zvec_ref[...], twice)
+    pair = exact(zvec_ref[...], doubled(nz))
     half = lax.broadcasted_iota(jnp.int32, pair.shape, 1) >= nz
     zhigh_ref[...] = jnp.zeros(zhigh_ref.shape, BF16)
     zlow_ref[...] = jnp.zeros(zlow_ref.shape, BF16)
@@ -260,59 +263,148 @@
     ).astype(F32)
     copies = (row == lax.rem(lane, ny)).astype(F32)
     yup_ref[...] = four(exact(exact(order, yvec_ref[...]), copies))
+    fetching.wait()
     square = (ny, ny)
     diagonal = lax.broadcasted_iota(jnp.int32, square, 0) == lax.broadcasted_iota(jnp.int32, square, 1)
     ycolumn = jnp.sum(jnp.where(diagonal, yval_ref[...], 0.0), axis=1, keepdims=True)
-    yz = ycolumn + exact(jnp.broadcast_to(zval_ref[...], (8, nz)), twice)[0:1]
+    yz = ycolumn + exact(jnp.broadcast_to(zval_ref[...], (8, nz)), doubled(nz))[0:1]
     late = lax.broadcasted_iota(jnp.int32, (1, 2 * nz), 1) >= nz
-    modes = nx // (npy * npz)
-    first = (lax.axis_index("py") * npz + lax.axis_index("pz")) * modes
+    modes = sums_ref.shape[1] // nz
+    first = (lax.axis_index("py") * (nz // lz) + lax.axis_index("pz")) * modes
     for mode in range(0, modes, 2):
         x = jnp.where(late, xval_ref[first + mode + 1], xval_ref[first + mode])
         sums_ref[:, mode * nz : (mode + 2) * nz] = yz + x
+
+
+def y_sides(odd, even):
+    first = lax.rem(lax.axis_index("py"), 2) == 0
+    return jnp.where(first, odd, even), jnp.where(first, even, odd)
+
+
+def three_products(matrix, high, low):
+    rows = matrix.shape[0] // 2
+    both = mul(matrix, high)
+    return both[:rows] + both[rows:] + mul(matrix[:rows], low)
+
+
+def yz_fields(lz, zrim, weighted_ref, zlow_ref, zhigh_ref, sides, stencil_ref):
+    count, nx = weighted_ref.shape
+    part, need = count // 2, count // 2 + REACH * lz
+    own = split(weighted_ref[...])
+    zrims = split(jnp.concatenate([zlow_ref[:zrim, :], zhigh_ref[:zrim, :]], axis=0))
+    left = stencil_ref.shape[1] - need - 2 * zrim
+    fields = []
+    for half in range(2):
+        if sides is None:
+            yrim = [jnp.zeros((left, nx), BF16)] * 2
+        else:
+            rim = sides[half]
+            missing = left - rim.shape[0]
+            yrim = split(jnp.concatenate([rim, jnp.zeros((missing, nx), F32)], axis=0) if missing else rim)
+        first = half * (count - need)
+        high, low = (
+            jnp.concatenate([own[k][first : first + need], zrims[k], yrim[k]], axis=0) for k in range(2)
+        )
+        both = three_products(stencil_ref[4 * half * part : 4 * (half + 1) * part, :], high, low)
+        fields.append((both[:part], both[part:]))
+    return fields
+
+
+def x_banded(taps_ref, mass, stiff):
+    nx = mass.shape[1]
+    applied = None
+    for offset in range(2 * REACH + 1):
+        move = offset - REACH
+        term = taps_ref[2 * offset] * mass + taps_ref[2 * offset + 1] * stiff
+        term = pltpu.roll(term, -move % nx, 1) if move else term
+        applied = term if applied is None else applied + term
+    return applied
+
+
+def store_modes(points, vectors_ref, spectral_ref):
+    count, nx = points.shape
+    high, low = split(points)
+    product = mul_t(jnp.concatenate([high, low], axis=0), vectors_ref[:nx, :])
+    spectral_ref[...] = (product[:count] + product[count:] + mul_t(high, vectors_ref[nx:, :])).T
 
 
 def residual_kernel(lz, zrim, parts, *refs):
     weighted_ref, zlow_ref, zhigh_ref, *refs = refs
     yodd_refs, yeven_refs, refs = refs[:parts], refs[parts : 2 * parts], refs[2 * parts :]
     stencil_ref, taps_ref, coef_ref, right_ref, vectors_ref, _, spectral_ref, residual_ref = refs
-    count, nx = weighted_ref.shape
-    part, need = count // 2, weighted_ref.shape[0] // 2 + REACH * lz
-    own = split(weighted_ref[...])
-    zrims = split(jnp.concatenate([zlow_ref[:zrim, :], zhigh_ref[:zrim, :]], axis=0))
-    fields = []
-    even = lax.rem(lax.axis_index("py"), 2) == 0
-    yodd, yeven = (jnp.concatenate([ref[...] for ref in refs], axis=0) for refs in (yodd_refs, yeven_refs))
-    below, above = jnp.where(even, yodd, yeven), jnp.where(even, yeven, yodd)
-    for half, rim in enumerate((below, above)):
-        missing = stencil_ref.shape[1] - need - 2 * zrim - rim.shape[0]
-        yrim = split(jnp.concatenate([rim, jnp.zeros((missing, nx), F32)], axis=0) if missing else rim)
-        first = half * (count - need)
-        high, low = (
-            jnp.concatenate([own[k][first : first + need], zrims[k], yrim[k]], axis=0) for k in range(2)
-        )
-        stencil = stencil_ref[4 * half * part : 4 * (half + 1) * part, :]
-        both = mul(stencil, high)
-        both = both[: 2 * part] + both[2 * part :] + mul(stencil[: 2 * part], low)
-        fields.append((both[:part], both[part:]))
-    for start in range(0, count, 8):
+    if parts == 2:
+        (yodd_ref, odd_corner_ref), (yeven_ref, even_corner_ref) = yodd_refs, yeven_refs
+        own = REACH * lz
+        yodd = jnp.concatenate([yodd_ref[:own, :], odd_corner_ref[...]], axis=0)
+        yeven = jnp.concatenate([yeven_ref[:own, :], even_corner_ref[...]], axis=0)
+    else:
+        yodd, yeven = yodd_refs[0][...], yeven_refs[0][...]
+    fields = yz_fields(lz, zrim, weighted_ref, zlow_ref, zhigh_ref, y_sides(yodd, yeven), stencil_ref)
+    part = weighted_ref.shape[0] // 2
+    for start in range(0, 2 * part, 8):
         mass, stiff = (field[start % part : start % part + 8] for field in fields[start // part])
-        applied = None
-        for offset in range(2 * REACH + 1):
-            move = offset - REACH
-            term = taps_ref[2 * offset] * mass + taps_ref[2 * offset + 1] * stiff
-            term = pltpu.roll(term, -move % nx, 1) if move else term
-            applied = term if applied is None else applied + term
         rows = pl.ds(start, 8)
-        residual_ref[rows, :] = right_ref[rows, :] - coef_ref[rows, :] * applied
-    high, low = split(residual_ref[...])
-    product = mul_t(jnp.concatenate([high, low], axis=0), vectors_ref[:nx, :])
-    product = product[:count] + product[count:] + mul_t(high, vectors_ref[nx:, :])
-    spectral_ref[...] = product.T
+        residual_ref[rows, :] = right_ref[rows, :] - coef_ref[rows, :] * x_banded(taps_ref, mass, stiff)
+    store_modes(residual_ref[...], vectors_ref, spectral_ref)
+
+
+def own_part_kernel(lz, zrim, weighted_ref, zlow_ref, zhigh_ref, stencil_ref, taps_ref, applied_ref):
+    fields = yz_fields(lz, zrim, weighted_ref, zlow_ref, zhigh_ref, None, stencil_ref)
+    part = weighted_ref.shape[0] // 2
+    for start in range(0, 2 * part, 8):
+        mass, stiff = (field[start % part : start % part + 8] for field in fields[start // part])
+        applied_ref[pl.ds(start, 8), :] = x_banded(taps_ref, mass, stiff)
+
+
+def joined_residual_kernel(applied_ref, yodd_ref, yeven_ref, coef_ref, right_ref, vectors_ref, spectral_ref, residual_ref):
+    count, rim = applied_ref.shape[0], yodd_ref.shape[0]
+    for at, side in zip((0, count - rim), y_sides(yodd_ref[...], yeven_ref[...])):
+        rows = pl.ds(at, rim)
+        residual_ref[rows, :] = right_ref[rows, :] - coef_ref[rows, :] * (applied_ref[rows, :] + side)
+    rows = pl.ds(rim, count - 2 * rim)
+    residual_ref[rows, :] = right_ref[rows, :] - coef_ref[rows, :] * applied_ref[rows, :]
+    store_modes(residual_ref[...], vectors_ref, spectral_ref)
+
+
+def outward_kernel(ly, lz, nz, zbands_ref, yodd_ref, yeven_ref, _, out_ref):
+    rim, side = REACH * lz, REACH * REACH
+    width = out_ref.shape[1]
+    row = lax.broadcasted_iota(jnp.int32, (rim, 1), 0)
+    column = lax.broadcasted_iota(jnp.int32, (1, width), 1)
+    spot = jnp.where(column < rim + side, column - rim, column - rim - side)
+    yin = jnp.where(column < rim, lax.div(column, lz), lax.div(spot, REACH))
+    zin = jnp.where(
+        column < rim, lax.rem(column, lz), lax.rem(spot, REACH) + jnp.where(column < rim + side, -REACH, lz)
+    )
+    place = zin + lax.axis_index("pz") * lz
+    inside = (column < rim + 2 * side) & (place >= 0) & (place < nz)
+    yout, zout = lax.div(row, lz), lax.rem(row, lz)
+
+    def dense(taps, tap):
+        value = jnp.zeros(tap.shape, F32)
+        for k in range(2 * REACH + 1):
+            value = jnp.where(tap == k, taps[:, k : k + 1], value)
+        return value
+
+    def picked(length, at, bands):
+        return exact((lax.broadcasted_iota(jnp.int32, (rim, length), 1) == at).astype(F32), bands, (1, 1))
+
+    ztap = jnp.where(inside, zin - zout + REACH, -1)
+    zstiff, zmass = (dense(picked(lz, zout, zbands_ref[:, matrix, :]), ztap) for matrix in range(2))
+    sides = y_sides(yodd_ref[rim : rim + 16, :ly], yeven_ref[rim : rim + 16, :ly])
+    spot, count = lax.axis_index("py"), lax.axis_size("py")
+    for k, (bands, at, shift, there) in enumerate(
+        ((sides[0], yout + ly - REACH, 2 * REACH, spot > 0), (sides[1], yout, 0, spot < count - 1))
+    ):
+        ytap = jnp.where(there, yin - yout + shift, -1)
+        ystiff, ymass = (dense(picked(ly, at, bands[8 * matrix : 8 * matrix + 8]), ytap) for matrix in range(2))
+        for part, value in enumerate((ymass * zmass, ystiff * zmass + ymass * zstiff)):
+            start = (4 * k + part) * rim
+            out_ref[start : start + rim, :], out_ref[start + 2 * rim : start + 3 * rim, :] = split(value)
 
 
 def modes_kernel(npy, npz, rims, *refs):
-    zhigh_ref, zlow_ref, ydown_ref, yup_ref, sums_ref, *rim_refs, in_ref, out_ref, turn_ref = refs
+    sums_ref, zhigh_ref, zlow_ref, ydown_ref, yup_ref, *rim_refs, in_ref, out_ref, turn_ref = refs
     count = in_ref.shape[0] // (npy * npz)
     size = out_ref.shape[0] // (npy * npz)
     nz = sums_ref.shape[1] // count
@@ -425,7 +517,7 @@
 
 def rim_update_kernel(
     ly, lz, devices, spectral_ref, vectors_ref, field_ref, coef_ref, before_low_ref, before_high_ref,
-    updated_ref, weighted_ref, zlow_ref, zhigh_ref, yodd_ref, yeven_ref,
+    outward_ref, taps_ref, updated_ref, weighted_ref, zlow_ref, zhigh_ref, yodd_ref, yeven_ref, below_ref, above_ref,
 ):
     nx = vectors_ref.shape[1]
     modes = nx // devices
@@ -444,7 +536,21 @@
     for side, (ref, before_ref) in enumerate(((zlow_ref, before_low_ref), (zhigh_ref, before_high_ref))):
         start = count + side * half
         ref[...] = before_ref[:half, :] + before_ref[half:, :] * update[start : start + half]
-    store_y_rims(own_rim(ly, lz, weighted_ref) + corners(ly, zlow_ref, zhigh_ref), yodd_ref, yeven_ref)
+    at = 0
+    for value, rows, whole in own_rim(ly, lz, weighted_ref) + corners(ly, zlow_ref, zhigh_ref):
+        below_ref[at : at + rows, :] = value[:rows, :]
+        above_ref[at : at + rows, :] = value[whole - rows : whole, :]
+        at += rows
+    rim, adds = yodd_ref.shape[0], []
+    for k, ref in enumerate((below_ref, above_ref)):
+        ref[at:, :] = jnp.zeros((ref.shape[0] - at, nx), F32)
+        both = three_products(outward_ref[4 * k * rim : 4 * (k + 1) * rim, :], *split(ref[...]))
+        adds.append((both[:rim], both[rim:]))
+    first = lax.rem(lax.axis_index("py"), 2) == 0
+    for start in range(0, rim, 8):
+        below, above = (x_banded(taps_ref, *(field[start : start + 8] for field in fields)) for fields in adds)
+        yodd_ref[start : start + 8, :] = jnp.where(first, below, above)
+        yeven_ref[start : start + 8, :] = jnp.where(first, above, below)
 
 
 def last_update_kernel(spectral_ref, vectors_ref, field_ref, residual_ref, updated_hbm, residual_hbm, held, sem):
@@ -536,43 +642,49 @@
     cell = count * nx * 4
     dma = pltpu.SemaphoreType.DMA
 
-    coef, weighted, even, odd, yodd, yeven = call(
-        lambda *refs: coefficient_kernel(ly, lz, *refs),
-        [(block, F32)] * 2 + [(zrims, F32)] * 2 + [((REACH * lz, nx), F32)] * 2,
-        [HBM] * 3, count * nx * 16, 4 * cell,
-        [pltpu.SMEM(coef_table.shape, F32), pltpu.VMEM(block, jnp.int32), pltpu.VMEM(block, F32), dma((3,))],
-    )(*in_hbm(coef_table, span_index.reshape(count, nx), field))
-
     points = point_columns(ly, lz)
     width = points.shape[1] // 2
-    bands = [array.transpose(1, 0, 2) for array in (yaxis_bands, zaxis_bands, xaxis_bands)]
-    stencil, taps = call(
-        lambda *refs: stencil_kernel(ly, lz, ny, nz, *refs),
-        [((4 * count, width), BF16), ((2 * (2 * REACH + 1), 8, nx), F32)],
-        [HBM] * 4 + [ANY], count * width * 60, 8 * count * width,
-        [pltpu.VMEM(points.shape, jnp.int32)] + [pltpu.VMEM(array.shape, F32) for array in bands] + [dma((4,))],
-    )(*in_hbm(jnp.asarray(points), *bands), even)
-
+    small = [jnp.asarray(points), *(array.transpose(1, 0, 2) for array in (yaxis_bands, zaxis_bands, xaxis_bands))]
     fast = (
         modes % 16 == 0 and npz % 2 == 0 and 2 * ly * REACH <= LANES // 2 and npy % 8 == 0 and lz % 16 == 0 and ly % 4 == 0
         and 2 * nz == LANES and 2 * ny == LANES and count == LANES and nx % LANES == 0
     )
+    later = [xaxis_vectors, yaxis_vectors, zaxis_vectors, yaxis_values.reshape(1, ny), zaxis_values.reshape(1, nz)] * fast
+
+    coef, weighted, even, odd, yodd, yeven, *small = call(
+        lambda *refs: coefficient_kernel(ly, lz, len(small), *refs),
+        [(block, F32)] * 2 + [(zrims, F32)] * 2 + [((REACH * lz + 16, nx), F32)] * 2
+        + [(array.shape, array.dtype) for array in small],
+        [HBM] * (3 + len(small)), count * nx * 16, 4 * cell,
+        [pltpu.SMEM(coef_table.shape, F32), pltpu.VMEM(block, jnp.int32), pltpu.VMEM(block, F32)]
+        + [dma((3 + len(small),))],
+    )(*in_hbm(coef_table, span_index.reshape(count, nx), field, *small))
+
+    *bands, xbands = small
+    stencil, *held = call(
+        lambda *refs: stencil_kernel(ly, lz, ny, nz, len(later), *refs),
+        [((4 * count, width), BF16)] + [(array.shape, F32) for array in later],
+        [VMEM] * 3 + [HBM] * len(later) + [ANY], count * width * 60, 8 * count * width,
+        [dma((len(later),))] * fast,
+    )(*bands, *in_hbm(*later), even)
+
+    even, odd = staggered(even, 1), staggered(odd, 0)
+    zlow, zhigh, *corner = call(
+        lambda *refs: y_rims_kernel(ly, *refs),
+        [(zrims, F32)] * 2 + [((up8(2 * REACH * REACH), nx), F32)] * 2,
+        [VMEM] * 2 + [ANY], nx, 4 * nx * 4 * zrims[0],
+    )(odd, even, stencil)
+    yodd, yeven = [yodd, corner[0]], [yeven, corner[1]]
+
     if fast:
         zmat, ymat, rmat = (npz * count // 2, ly * nz // 2), (ny, 4 * ny), (npz * LANES // 2, ly * nz)
-        vectors, *tables = call(
+        vectors, taps, *tables = call(
             lambda *refs: tables_kernel(npy, npz, ly, lz, *refs),
-            [((2 * nx, nx), BF16), (zmat, BF16), (zmat, BF16), (ymat, BF16), (ymat, BF16), ((ny, modes * nz), F32)]
-            + [(rmat, BF16)] * 2,
-            [HBM] * 6 + [ANY], npz * count * ly * nz * 8, npz * count * ly * nz * 4,
-            [pltpu.VMEM(array.shape, F32) for array in (xaxis_vectors, yaxis_vectors, zaxis_vectors)]
-            + [pltpu.SMEM((nx,), F32), pltpu.VMEM((1, ny), F32), pltpu.VMEM((1, nz), F32), dma((6,))],
-        )(
-            *in_hbm(
-                xaxis_vectors, yaxis_vectors, zaxis_vectors, xaxis_values,
-                yaxis_values.reshape(1, ny), zaxis_values.reshape(1, nz),
-            ),
-            taps,
-        )
+            [((2 * nx, nx), BF16), ((2 * (2 * REACH + 1), 8, nx), F32), ((ny, modes * nz), F32)]
+            + [(zmat, BF16), (zmat, BF16), (ymat, BF16), (ymat, BF16), (rmat, BF16), (rmat, BF16)],
+            [VMEM] * 6 + [HBM, ANY], npz * count * ly * nz * 8, npz * count * ly * nz * 4,
+            [pltpu.SMEM((nx,), F32), dma((1,))],
+        )(*held, xbands, *in_hbm(xaxis_values), corner[0])
 
         def precondition(received, rims):
             size = modes * 3 // 2 if rims else modes
@@ -582,11 +694,11 @@
                 [pltpu.VMEM((ly * nz // LANES * npy * (modes + 8), LANES), F32)],
             )(*(tables if rims else tables[:5]), received)[0]
     else:
+        vectors, taps = call(
+            xvectors_kernel, [((2 * nx, nx), BF16), ((2 * (2 * REACH + 1), 8, nx), F32)], [HBM, VMEM],
+            nx * nx * 40, 8 * nx * nx, [pltpu.VMEM((nx, nx), F32), dma((1,))],
+        )(*in_hbm(xaxis_vectors), xbands)
         tables = [taps]
-        vectors = call(
-            xvectors_kernel, [((2 * nx, nx), BF16)], [HBM], nx * nx * 40, 8 * nx * nx,
-            [pltpu.VMEM((nx, nx), F32), dma((1,))],
-        )(*in_hbm(xaxis_vectors))[0]
         part = lax.axis_index(BOTH)
         xpart = lax.dynamic_slice_in_dim(xaxis_values, part * modes, modes)
 
@@ -595,23 +707,31 @@
                 received, npy, npz, ly, lz, xpart, yaxis_values, zaxis_values, yaxis_vectors, zaxis_vectors
             )
 
-    even, odd = staggered(even, 1), staggered(odd, 0)
-    zlow, zhigh, *corner = call(
-        lambda *refs: y_rims_kernel(ly, *refs),
-        [(zrims, F32)] * 2 + [((up8(2 * REACH * REACH), nx), F32)] * 2,
-        [VMEM] * 2 + [ANY], nx, 4 * nx * 4 * zrims[0],
-    )(odd, even, taps)
-    yodd, yeven = [yodd, corner[0]], [yeven, corner[1]]
+    outward = None
     for iteration in range(ITERS):
         last = iteration + 1 == ITERS
         yodd, yeven = [paired(value, "py") for value in yodd], [pairwise(value, "py", 0) for value in yeven]
         parts = len(yodd)
-        spectral, *residual = call(
-            lambda *refs: residual_kernel(lz, zrim[0], parts, *refs),
-            [((nx, count), F32)] + [(block, F32)] * last,
-            [VMEM] * (8 + 2 * parts) + [ANY], 6 * count * nx * (nx + 2 * width), 5 * cell + 4 * nx * nx,
-            [pltpu.VMEM(block, F32)] * (not last),
-        )(weighted, zlow, zhigh, *yodd, *yeven, stencil, taps, coef, right, vectors, tables[0])
+        if fast and iteration == 0:
+            outward = call(
+                lambda *refs: outward_kernel(ly, lz, nz, *refs),
+                [((8 * REACH * lz, LANES), BF16)], [VMEM] * 3 + [ANY], 1 << 20, 1 << 18,
+            )(bands[2], yodd[0], yeven[0], tables[0])[0]
+        outs = [((nx, count), F32)] + [(block, F32)] * last
+        scratch = [pltpu.VMEM(block, F32)] * (not last)
+        cost = (6 * count * nx * (nx + 2 * width), 5 * cell + 4 * nx * nx)
+        if fast and iteration > 0:
+            applied = call(
+                lambda *refs: own_part_kernel(lz, zrim[0], *refs), [(block, F32)], [VMEM] * 5, *cost,
+            )(weighted, zlow, zhigh, stencil, taps)[0]
+            spectral, *residual = call(joined_residual_kernel, outs, [VMEM] * 6, *cost, scratch)(
+                applied, *yodd, *yeven, coef, right, vectors
+            )
+        else:
+            spectral, *residual = call(
+                lambda *refs: residual_kernel(lz, zrim[0], parts, *refs),
+                outs, [VMEM] * (8 + 2 * parts) + [ANY], *cost, scratch,
+            )(weighted, zlow, zhigh, *yodd, *yeven, stencil, taps, coef, right, vectors, outward if fast else tables[0])
         spectral = lax.all_to_all(spectral, BOTH, split_axis=0, concat_axis=0, tiled=True)
         spectral = precondition(spectral, not last)
         spectral = lax.all_to_all(spectral, BOTH, split_axis=0, concat_axis=0, tiled=True)
@@ -624,8 +744,9 @@
         elif fast:
             field, weighted, zlow, zhigh, *yrims = call(
                 lambda *refs: rim_update_kernel(ly, lz, devices, *refs),
-                [(block, F32)] * 2 + [(zrim, F32)] * 2 + [(yrim, F32)] * 2, [VMEM] * 6, *cost,
-            )(spectral, vectors, field, coef, zlow, zhigh)
+                [(block, F32)] * 2 + [(zrim, F32)] * 2 + [((REACH * lz, nx), F32)] * 2, [VMEM] * 8, *cost,
+                [pltpu.VMEM((LANES, nx), F32)] * 2,
+            )(spectral, vectors, field, coef, zlow, zhigh, outward, taps)
         else:
             field, weighted, zlow, zhigh = call(
                 lambda *refs: update_kernel(ly, lz, *refs), [(block, F32)] * 2 + [(zrim, F32)] * 2, [VMEM] * 4, *cost,

time: 83.4 us -> 82.5 us (0.989)
    pallas_call x1, Pallas kernels: 2.01 us -> 0.96 us  [shards(): call(lambda *refs: tables_kernel(npy, npz, ly, lz, *refs), [((2 * nx, nx)...]
    ppermute x3, starting transfers between devices: 5.06 us -> 4.17 us  [paired(): lax.ppermute(value, axis, [(i, (i + 1 if i % 2 else i - 1) % count) for i...]
    pallas_call x4 -> x6, Pallas kernels: 5.45 us -> 5.99 us  [the longest x1 1.39 us: shards(): call(lambda *refs: stencil_kernel(ly, lz, ny, nz, len(later), *refs), [((...]
  transfers between devices with their start and end apart: 8 -> 8, of which waited for: 1 -> 3; matrix products, arithmetic and copies ran while one was open for 0% -> 0% of each run, Pallas kernels for 5% -> 5%
where the time goes in v8:
time: 82.5 us; the launch traced here: 82.2 us
  blocking collectives  55.7 us (68%)
  Pallas kernels  12.2 us (15%)
  starting transfers between devices  10.2 us (12%)
  waiting for transfers between devices  3.44 us (4%)
    all_to_all x4, blocking collectives, shards(): lax.all_to_all(spectral, BOTH, split_axis=0, concat_axis=0, tiled=True)  55.7 us
    ppermute x2, starting transfers between devices, staggered(): return lax.ppermute(value, BOTH, pairs)  4.67 us
    ppermute x3, starting transfers between devices, paired(): lax.ppermute(value, axis, [(i, (i + 1 if i % 2 else i - 1) % count) for i...  4.17 us
    ppermute x3, waiting for transfers between devices, paired(): lax.ppermute(value, axis, [(i, (i + 1 if i % 2 else i - 1) % count) for i...  3.42 us
    pallas_call x2, Pallas kernels, precondition(): call(lambda *refs: modes_kernel(npy, npz, rims, *refs), [((devices * size...  2.76 us
  transfers between devices with their start and end apart: 8, of which 3 were waited for; matrix products, arithmetic and copies ran while one was open for 0% of the time, Pallas kernels for 5%

profile of v8, /device:TPU:0, one launch (start us, length us, event | category | flops | bytes accessed | tf_op | source)
XLA Modules:
  0.0 82.2 jit_solution(7033691358585737401)
XLA Ops:
  0.6 1.3 %shard_map.149 = (f32[128,512]{1,0:T(8,128)S(1)}, f32[128,512]{1,0:T(8,128)S(1)}, f32[48,512]{1,0:T(8,128)S(1)}, f32[48,512]{1,0:T(8,128)S(1)}, f32[64,512]{1,0:...) custom-call(f32[8]{0:T(128)} %refs_0_.1, ...), custom_call_target="tpu_custom_call" | custom-call | flops 1048576 | bytes 1048576 | tf_op jit(solution)/shard_map/pallas_call | solution.py:654
  2.0 3.0 %collective-permute-start.1 = (f32[48,512]{1,0:T(8,128)S(1)}, f32[48,512]{1,0:T(8,128)S(1)}, u32[]{:S(2)}, u32[]{:S(2)}) collective-permute-start(f32[48,512]{1,0:T(8,128)S(1)} %get-tuple-element.44.refs_8_), channel_id=1, source_target_pairs={{0,8},{1,2},{2,1},{3,11},{4,5},{5,4},{6,7},{7,6},{8,0},{9,10},{10,... | collective-permute-start | bytes 294920 | tf_op jit(solution)/shard_map/ppermute | solution.py:598
  5.0 1.7 %collective-permute-start = (f32[48,512]{1,0:T(8,128)S(1)}, f32[48,512]{1,0:T(8,128)S(1)}, u32[]{:S(2)}, u32[]{:S(2)}) collective-permute-start(f32[48,512]{1,0:T(8,128)S(1)} %get-tuple-element.51), channel_id=1, source_target_pairs={{0,1},{1,0},{2,3},{3,2},{4,12},{5,6},{6,5},{7,15},{8,9},{9,8},{10,... | collective-permute-start | bytes 294920 | tf_op jit(solution)/shard_map/ppermute | solution.py:598
  6.6 0.3 collective-permute-start.2
  6.9 1.3 %collective-permute-start.4 = (f32[64,512]{1,0:T(8,128)S(1)}, f32[64,512]{1,0:T(8,128)S(1)}, u32[]{:S(2)}, u32[]{:S(2)}) collective-permute-start(f32[64,512]{1,0:T(8,128)S(1)} %get-tuple-element.65), channel_id=1, source_target_pairs={{0,4},{4,0},{8,12},{12,8},{16,20},{20,16},{24,28},{28,24},{1,5},{5... | collective-permute-start | bytes 393224 | tf_op jit(solution)/shard_map/ppermute | solution.py:567
  8.2 1.4 %shard_map.150 = (bf16[512,256]{1,0:T(8,128)(2,1)S(1)}, f32[512,512]{1,0:T(8,128)S(1)}, f32[64,64]{1,0:T(8,128)S(1)}, f32[64,64]{1,0:T(8,128)S(1)}, f32[1,64]{1,0:T(1,128)S(1)}, /*index=5*/f32[1,64]{1,0:T(1,128)S(1)}) custom-call(s32[2,512]{1,0:T(2,128)S(1)} %get-tuple-element.41.refs_0_, f32[7,2,8]{2,1,0:T(2,128)S(1)} %get-tuple-element.42.refs_1_, ...), custom_call_target="tpu_custom_call" | custom-call | flops 1966080 | bytes 262144 | tf_op jit(solution)/shard_map/pallas_call | solution.py:664
  9.6 0.0 collective-permute-done.1.refs_1_
  9.6 0.0 collective-permute-done.refs_0_
  9.7 1.8 %collective-permute-start.3 = (f32[24,512]{1,0:T(8,128)S(1)}, f32[24,512]{1,0:T(8,128)S(1)}, u32[]{:S(2)}, u32[]{:S(2)}) collective-permute-start(f32[24,512]{1,0:T(8,128)S(1)} %get-tuple-element.53.refs_7_), channel_id=1, source_target_pairs={{0,28},{4,8},{8,4},{12,16},{16,12},{20,24},{24,20},{28,0},{1,29},{... | collective-permute-start | bytes 147464 | tf_op jit(solution)/shard_map/ppermute | solution.py:572
  11.5 0.0 collective-permute-start.5
  11.5 1.0 %shard_map.152 = (bf16[1024,512]{1,0:T(8,128)(2,1)S(1)}, f32[14,8,512]{2,1,0:T(8,128)S(1)}, f32[64,1024]{1,0:T(8,128)S(1)}, bf16[256,256]{1,0:T(8,128)(2,1)S(1)}...) custom-call(f32[512,512]{1,0:T(8,128)S(1)} %get-tuple-element.45.ref, ...), custom_call_target="tpu_custom_call" | custom-call | flops 2097152 | bytes 1048576 | tf_op jit(solution)/shard_map/pallas_call | solution.py:681
  12.5 0.7 collective-permute-done.2.refs_1_.refs_3_
  13.2 0.0 collective-permute-done.4.refs_2_.refs_5_
  13.2 0.6 shard_map.153.refs_12_.refs_6_
  13.9 0.6 collective-permute-done.3.refs_4_
  14.5 0.0 collective-permute-done.5.refs_6_
  14.5 1.3 %shard_map.154 = f32[512,128]{1,0:T(8,128)S(1)} custom-call(f32[128,512]{1,0:T(8,128)S(1)} %get-tuple-element.61.refs_0_, f32[48,512]{1,0:T(8,128)S(1)} %get-tuple-element.62.refs_1_.refs_4_, f32[48,512]{1,0:T(8,128)S(1)} %get-tuple-element.63.refs_2_.refs_5_, f32[64,512]{1,0:T(8,128)S(1)} %collective-permute-done.2.refs_1_.refs_3_, ...), custom_call_target="tpu_custom_call" | custom-call | flops 402653184 | bytes 2359296 | tf_op jit(solution)/shard_map/pallas_call | solution.py:731
  15.7 14.6 %all_to_all.44 = f32[32,16,128]{2,1,0:T(8,128)S(1)} all-to-all(f32[32,16,128]{2,1,0:T(8,128)S(1)} %bitcast.21), channel_id=1, replica_groups=mesh['py'=8,'pz'=4] {'py','pz'}, dimensions={0} | all-to-all | bytes 524288 | tf_op jit(solution)/shard_map/all_to_all | solution.py:735
  30.3 1.4 %shard_map.155 = f32[768,128]{1,0:T(8,128)S(1)} custom-call(f32[64,1024]{1,0:T(8,128)S(1)} %get-tuple-element.54.refs_3_.refs_0_, bf16[256,256]{1,0:T(8,128)(2,1)S(1)} %get-tuple-element.55.refs_1_, bf16[256,256]{1,0:T(8,128)(2,1)S(1)} %get-tuple-element.56.refs_2_, bf16[64,256]{1,0:T(8,128)(2,1)S(1)} %get-tuple-element.57.refs_3_, ...), custom_call_target="tpu_custom_call" | custom-call | flops 402653184 | bytes 524288 | tf_op jit(solution)/shard_map/pallas_call | solution.py:691
  31.7 0.0 copy-start
  31.8 14.4 %all_to_all.45 = f32[32,24,128]{2,1,0:T(8,128)S(1)} all-to-all(f32[32,24,128]{2,1,0:T(8,128)S(1)} %bitcast.19), channel_id=1, replica_groups=mesh['py'=8,'pz'=4] {'py','pz'}, dimensions={0} | all-to-all | bytes 786432 | tf_op jit(solution)/shard_map/all_to_all | solution.py:737
  46.1 1.3 %shard_map.156 = (f32[128,512]{1,0:T(8,128)S(1)}, f32[128,512]{1,0:T(8,128)S(1)}, f32[24,512]{1,0:T(8,128)S(1)}, f32[24,512]{1,0:T(8,128)S(1)}, f32[48,512]{1,0:T(8,128)S(1)}, /*index=5*/f32[48,512]{1,0:T(8,128)S(1)}) custom-call(f32[768,128]{1,0:T(8,128)S(1)} %bitcast.18, bf16[1024,512]{1,0:T(8,128)(2,1)S(1)} %get-tuple-element.69.refs_11_.refs_1_.vectors_ref, ...), custom_call_target="tpu_custom_call" | custom-call | flops 201326592 | bytes 2097152 | tf_op jit(solution)/shard_map/pallas_call | solution.py:745
  47.4 2.1 %collective-permute-start.6 = (f32[48,512]{1,0:T(8,128)S(1)}, f32[48,512]{1,0:T(8,128)S(1)}, u32[]{:S(2)}, u32[]{:S(2)}) collective-permute-start(f32[48,512]{1,0:T(8,128)S(1)} %get-tuple-element.73), channel_id=1, source_target_pairs={{0,28},{4,8},{8,4},{12,16},{16,12},{20,24},{24,20},{28,0},{1,29},{... | collective-permute-start | bytes 294920 | tf_op jit(solution)/shard_map/ppermute | solution.py:572
  49.5 0.0 collective-permute-start.7
  49.5 0.8 shard_map.157.applied_ref
  50.3 2.1 %collective-permute-done.6.yodd_ref = f32[48,512]{1,0:T(8,128)S(1)} collective-permute-done((f32[48,512]{1,0:T(8,128)S(1)}, f32[48,512]{1,0:T(8,128)S(1)}, u32[]{:S(2)}, u32[]{:S(2)}) %collective-permute-start.6) | collective-permute-done | bytes 98336 | tf_op jit(solution)/shard_map/ppermute | solution.py:572
  52.4 0.0 collective-permute-done.7.yeven_ref
  52.4 0.6 shard_map.158
  53.0 14.0 %all_to_all.46 = f32[32,16,128]{2,1,0:T(8,128)S(1)} all-to-all(f32[32,16,128]{2,1,0:T(8,128)S(1)} %bitcast.27), channel_id=1, replica_groups=mesh['py'=8,'pz'=4] {'py','pz'}, dimensions={0} | all-to-all | bytes 524288 | tf_op jit(solution)/shard_map/all_to_all | solution.py:735
  67.0 1.3 %shard_map.159 = f32[512,128]{1,0:T(8,128)S(1)} custom-call(f32[64,1024]{1,0:T(8,128)S(1)} %get-tuple-element.54.refs_3_.refs_0_, bf16[256,256]{1,0:T(8,128)(2,1)S(1)} %get-tuple-element.55.refs_1_, bf16[256,256]{1,0:T(8,128)(2,1)S(1)} %get-tuple-element.56.refs_2_, bf16[64,256]{1,0:T(8,128)(2,1)S(1)} %get-tuple-element.57.refs_3_, ...), custom_call_target="tpu_custom_call" | custom-call | flops 402653184 | bytes 524288 | tf_op jit(solution)/shard_map/pallas_call | solution.py:691
  68.3 12.7 %all_to_all.47 = f32[32,16,128]{2,1,0:T(8,128)S(1)} all-to-all(f32[32,16,128]{2,1,0:T(8,128)S(1)} %bitcast.29), channel_id=1, replica_groups=mesh['py'=8,'pz'=4] {'py','pz'}, dimensions={0} | all-to-all | bytes 524288 | tf_op jit(solution)/shard_map/all_to_all | solution.py:737
  81.1 1.1 %shard_map.160 = (f32[128,512]{1,0:T(8,128)}, f32[128,512]{1,0:T(8,128)}) custom-call(f32[512,128]{1,0:T(8,128)S(1)} %bitcast.20, bf16[1024,512]{1,0:T(8,128)(2,1)S(1)} %get-tuple-element.69.refs_11_.refs_1_.vectors_ref, f32[128,512]{1,0:T(8,128)S(1)} %get-tuple-element.76.field_ref, f32[128,512]{1,0:T(8,128)S(1)} %get-tuple-element.77.residual_ref), custom_call_target="tpu_custom_call" | custom-call | flops 201326592 | bytes 2097152 | tf_op jit(solution)/shard_map/pallas_call | solution.py:740
  (4 shorter events, 0.1 us)
Async XLA Ops:
  2.0 7.7 %collective-permute-start.1 = (f32[48,512]{1,0:T(8,128)S(1)}, f32[48,512]{1,0:T(8,128)S(1)}, u32[]{:S(2)}, u32[]{:S(2)}) collective-permute-start(f32[48,512]{1,0:T(8,128)S(1)} %get-tuple-element.44.refs_8_), channel_id=1, source_target_pairs={{0,8},{1,2},{2,1},{3,11},{4,5},{5,4},{6,7},{7,6},{8,0},{9,10},{10,... | collective-permute-start | bytes 294920 | tf_op jit(solution)/shard_map/ppermute | solution.py:598
  5.0 4.7 %collective-permute-start = (f32[48,512]{1,0:T(8,128)S(1)}, f32[48,512]{1,0:T(8,128)S(1)}, u32[]{:S(2)}, u32[]{:S(2)}) collective-permute-start(f32[48,512]{1,0:T(8,128)S(1)} %get-tuple-element.51), channel_id=1, source_target_pairs={{0,1},{1,0},{2,3},{3,2},{4,12},{5,6},{6,5},{7,15},{8,9},{9,8},{10,... | collective-permute-start | bytes 294920 | tf_op jit(solution)/shard_map/ppermute | solution.py:598
  6.6 6.6 %collective-permute-start.2 = (f32[64,512]{1,0:T(8,128)S(1)}, f32[64,512]{1,0:T(8,128)S(1)}, u32[]{:S(2)}, u32[]{:S(2)}) collective-permute-start(f32[64,512]{1,0:T(8,128)S(1)} %get-tuple-element.64), channel_id=1, source_target_pairs={{0,28},{4,8},{8,4},{12,16},{16,12},{20,24},{24,20},{28,0},{1,29},{... | collective-permute-start | bytes 393224 | tf_op jit(solution)/shard_map/ppermute | solution.py:572
  6.9 6.3 %collective-permute-start.4 = (f32[64,512]{1,0:T(8,128)S(1)}, f32[64,512]{1,0:T(8,128)S(1)}, u32[]{:S(2)}, u32[]{:S(2)}) collective-permute-start(f32[64,512]{1,0:T(8,128)S(1)} %get-tuple-element.65), channel_id=1, source_target_pairs={{0,4},{4,0},{8,12},{12,8},{16,20},{20,16},{24,28},{28,24},{1,5},{5... | collective-permute-start | bytes 393224 | tf_op jit(solution)/shard_map/ppermute | solution.py:567
  9.7 4.8 %collective-permute-start.3 = (f32[24,512]{1,0:T(8,128)S(1)}, f32[24,512]{1,0:T(8,128)S(1)}, u32[]{:S(2)}, u32[]{:S(2)}) collective-permute-start(f32[24,512]{1,0:T(8,128)S(1)} %get-tuple-element.53.refs_7_), channel_id=1, source_target_pairs={{0,28},{4,8},{8,4},{12,16},{16,12},{20,24},{24,20},{28,0},{1,29},{... | collective-permute-start | bytes 147464 | tf_op jit(solution)/shard_map/ppermute | solution.py:572
  11.5 3.0 %collective-permute-start.5 = (f32[24,512]{1,0:T(8,128)S(1)}, f32[24,512]{1,0:T(8,128)S(1)}, u32[]{:S(2)}, u32[]{:S(2)}) collective-permute-start(f32[24,512]{1,0:T(8,128)S(1)} %get-tuple-element.66), channel_id=1, source_target_pairs={{0,4},{4,0},{8,12},{12,8},{16,20},{20,16},{24,28},{28,24},{1,5},{5... | collective-permute-start | bytes 147464 | tf_op jit(solution)/shard_map/ppermute | solution.py:567
  13.2 1.3 %copy-start.1 = (f32[8,16,512]{2,1,0:T(8,128)S(1)}, f32[8,16,512]{2,1,0:T(8,128)}, u32[]{:S(2)}) copy-start(f32[8,16,512]{2,1,0:T(8,128)} %param.15) | copy-start | bytes 786436
  31.7 14.4 %copy-start = (f32[8,16,512]{2,1,0:T(8,128)S(1)}, f32[8,16,512]{2,1,0:T(8,128)}, u32[]{:S(2)}) copy-start(f32[8,16,512]{2,1,0:T(8,128)} %param.14) | copy-start | bytes 786436
  47.4 5.0 %collective-permute-start.6 = (f32[48,512]{1,0:T(8,128)S(1)}, f32[48,512]{1,0:T(8,128)S(1)}, u32[]{:S(2)}, u32[]{:S(2)}) collective-permute-start(f32[48,512]{1,0:T(8,128)S(1)} %get-tuple-element.73), channel_id=1, source_target_pairs={{0,28},{4,8},{8,4},{12,16},{16,12},{20,24},{24,20},{28,0},{1,29},{... | collective-permute-start | bytes 294920 | tf_op jit(solution)/shard_map/ppermute | solution.py:572
  49.5 2.9 %collective-permute-start.7 = (f32[48,512]{1,0:T(8,128)S(1)}, f32[48,512]{1,0:T(8,128)S(1)}, u32[]{:S(2)}, u32[]{:S(2)}) collective-permute-start(f32[48,512]{1,0:T(8,128)S(1)} %get-tuple-element.74), channel_id=1, source_target_pairs={{0,4},{4,0},{8,12},{12,8},{16,20},{20,16},{24,28},{28,24},{1,5},{5... | collective-permute-start | bytes 294920 | tf_op jit(solution)/shard_map/ppermute | solution.py:567

commit v9 on v8

--- a/solution.py
+++ b/solution.py
@@ -249,20 +249,20 @@
         spot = lax.div(p, npy)
         return lax.rem(p, npy) * ly + 2 * lax.rem(spot, ly // 2) + lax.div(spot, ly // 2)
 
-    def four(array):
+    def parts(array):
         high, low = split(array)
         late = lax.broadcasted_iota(jnp.int32, array.shape, 1) >= 2 * ny
         return jnp.where(late, low.astype(F32), high.astype(F32)).astype(BF16)
 
-    lane = lax.broadcasted_iota(jnp.int32, (ny, 4 * ny), 1)
-    row = lax.broadcasted_iota(jnp.int32, (ny, 4 * ny), 0)
+    lane = lax.broadcasted_iota(jnp.int32, (ny, 3 * ny), 1)
+    row = lax.broadcasted_iota(jnp.int32, (ny, 3 * ny), 0)
     moved = (row == y_of(lax.rem(lane, ny))).astype(F32)
-    ydown_ref[...] = four(exact(yvec_ref[...].T, moved))
+    ydown_ref[...] = parts(exact(yvec_ref[...].T, moved))
     order = (
         lax.broadcasted_iota(jnp.int32, (ny, ny), 1) == y_of(lax.broadcasted_iota(jnp.int32, (ny, ny), 0))
     ).astype(F32)
     copies = (row == lax.rem(lane, ny)).astype(F32)
-    yup_ref[...] = four(exact(exact(order, yvec_ref[...]), copies))
+    yup_ref[...] = parts(exact(exact(order, yvec_ref[...]), copies))
     fetching.wait()
     square = (ny, ny)
     diagonal = lax.broadcasted_iota(jnp.int32, square, 0) == lax.broadcasted_iota(jnp.int32, square, 1)
@@ -450,12 +450,12 @@
         pairs.append(jnp.concatenate([early(*tile) for tile in tiles] + [later(*tile) for tile in tiles], axis=0))
     stacked = jnp.concatenate(pairs, axis=1)
 
-    def four(value):
+    def stack(value):
         high, low = split(value)
-        return jnp.concatenate([high, low, high, low], axis=0)
-
-    modes = mul(ydown_ref[...], four(stacked)) / sums_ref[...]
-    restored = mul(yup_ref[...], four(modes))
+        return jnp.concatenate([high, low, high], axis=0)
+
+    modes = mul(ydown_ref[...], stack(stacked)) / sums_ref[...]
+    restored = mul(yup_ref[...], stack(modes))
     for mode in range(0, count, 2):
         block = restored[:, mode * nz : (mode + 2) * nz]
         for c in range(chunks):
@@ -475,7 +475,10 @@
     total = npy * count
     if rims:
         side = [
-            three(spectral[half * total : (half + 1) * total], mul_t, *(ref[:, pl.ds(half * width, width)] for ref in rim_refs))
+            three(
+                spectral[half * total : (half + 1) * total], mul_t,
+                *(ref[:, pl.ds(half * width, width)] for ref in rim_refs),
+            )
             for half in range(2)
         ]
         side = side[0] + side[1]
@@ -572,21 +575,6 @@
     return lax.ppermute(value, axis, [(i, (i + 1 if i % 2 else i - 1) % count) for i in range(count)])
 
 
-def odd_pairs(value, axis, other):
-    count, across = lax.axis_size(axis), lax.axis_size(other)
-    first = BOTH.index(axis) == 0
-
-    def spot(i, k):
-        return i * across + k if first else k * count + i
-
-    pairs = []
-    for i in range(count):
-        for k in range(across):
-            j = i + 1 if i % 2 else i - 1
-            pairs.append((spot(i, k), spot(j, k) if 0 <= j < count else spot(i, k ^ 1)))
-    return lax.ppermute(value, BOTH, pairs)
-
-
 def staggered(value, parity):
     across, count = lax.axis_size("py"), lax.axis_size("pz")
     pairs = []
@@ -677,7 +665,7 @@
     yodd, yeven = [yodd, corner[0]], [yeven, corner[1]]
 
     if fast:
-        zmat, ymat, rmat = (npz * count // 2, ly * nz // 2), (ny, 4 * ny), (npz * LANES // 2, ly * nz)
+        zmat, ymat, rmat = (npz * count // 2, ly * nz // 2), (ny, 3 * ny), (npz * LANES // 2, ly * nz)
         vectors, taps, *tables = call(
             lambda *refs: tables_kernel(npy, npz, ly, lz, *refs),
             [((2 * nx, nx), BF16), ((2 * (2 * REACH + 1), 8, nx), F32), ((ny, modes * nz), F32)]
@@ -691,7 +679,7 @@
             return call(
                 lambda *refs: modes_kernel(npy, npz, rims, *refs),
                 [((devices * size, count), F32)], [VMEM] * (8 if rims else 6), 6 * 2 * count * nx * ly * nz, 2 * cell,
-                [pltpu.VMEM((ly * nz // LANES * npy * (modes + 8), LANES), F32)],
+                [pltpu.VMEM(((ly * nz // LANES * npy + 1) * (modes + 8), LANES), F32)],
             )(*(tables if rims else tables[:5]), received)[0]
     else:
         vectors, taps = call(
@@ -707,7 +695,6 @@
                 received, npy, npz, ly, lz, xpart, yaxis_values, zaxis_values, yaxis_vectors, zaxis_vectors
             )
 
-    outward = None
     for iteration in range(ITERS):
         last = iteration + 1 == ITERS
         yodd, yeven = [paired(value, "py") for value in yodd], [pairwise(value, "py", 0) for value in yeven]

time: 82.5 us -> 82.3 us (level)
  no operation moved by 1% of the time
where the time goes in v9:
time: 82.3 us; the launch traced here: 82.1 us
  blocking collectives  55.7 us (68%)
  Pallas kernels  12 us (15%)
  starting transfers between devices  10.2 us (12%)
  waiting for transfers between devices  3.44 us (4%)
    all_to_all x4, blocking collectives, shards(): lax.all_to_all(spectral, BOTH, split_axis=0, concat_axis=0, tiled=True)  55.7 us
    ppermute x2, starting transfers between devices, staggered(): return lax.ppermute(value, BOTH, pairs)  4.67 us
    ppermute x3, starting transfers between devices, paired(): lax.ppermute(value, axis, [(i, (i + 1 if i % 2 else i - 1) % count) for i...  4.16 us
    ppermute x3, waiting for transfers between devices, paired(): lax.ppermute(value, axis, [(i, (i + 1 if i % 2 else i - 1) % count) for i...  3.43 us
    pallas_call x2, Pallas kernels, precondition(): call(lambda *refs: modes_kernel(npy, npz, rims, *refs), [((devices * size...  2.63 us
  transfers between devices with their start and end apart: 8, of which 3 were waited for; matrix products, arithmetic and copies ran while one was open for 0% of the time, Pallas kernels for 5%

profile of v9, /device:TPU:0, one launch (start us, length us, event | category | flops | bytes accessed | tf_op | source)
XLA Modules:
  0.0 82.1 jit_solution(7602109748451034776)
XLA Ops:
  0.6 1.3 %shard_map.149 = (f32[128,512]{1,0:T(8,128)S(1)}, f32[128,512]{1,0:T(8,128)S(1)}, f32[48,512]{1,0:T(8,128)S(1)}, f32[48,512]{1,0:T(8,128)S(1)}, f32[64,512]{1,0:...) custom-call(f32[8]{0:T(128)} %refs_0_.1, ...), custom_call_target="tpu_custom_call" | custom-call | flops 1048576 | bytes 1048576 | tf_op jit(solution)/shard_map/pallas_call | solution.py:642
  2.0 3.0 %collective-permute-start.1 = (f32[48,512]{1,0:T(8,128)S(1)}, f32[48,512]{1,0:T(8,128)S(1)}, u32[]{:S(2)}, u32[]{:S(2)}) collective-permute-start(f32[48,512]{1,0:T(8,128)S(1)} %get-tuple-element.44.refs_8_), channel_id=1, source_target_pairs={{0,8},{1,2},{2,1},{3,11},{4,5},{5,4},{6,7},{7,6},{8,0},{9,10},{10,... | collective-permute-start | bytes 294920 | tf_op jit(solution)/shard_map/ppermute | solution.py:586
  5.0 1.7 %collective-permute-start = (f32[48,512]{1,0:T(8,128)S(1)}, f32[48,512]{1,0:T(8,128)S(1)}, u32[]{:S(2)}, u32[]{:S(2)}) collective-permute-start(f32[48,512]{1,0:T(8,128)S(1)} %get-tuple-element.51), channel_id=1, source_target_pairs={{0,1},{1,0},{2,3},{3,2},{4,12},{5,6},{6,5},{7,15},{8,9},{9,8},{10,... | collective-permute-start | bytes 294920 | tf_op jit(solution)/shard_map/ppermute | solution.py:586
  6.6 0.3 collective-permute-start.2
  6.9 1.3 %collective-permute-start.4 = (f32[64,512]{1,0:T(8,128)S(1)}, f32[64,512]{1,0:T(8,128)S(1)}, u32[]{:S(2)}, u32[]{:S(2)}) collective-permute-start(f32[64,512]{1,0:T(8,128)S(1)} %get-tuple-element.65), channel_id=1, source_target_pairs={{0,4},{4,0},{8,12},{12,8},{16,20},{20,16},{24,28},{28,24},{1,5},{5... | collective-permute-start | bytes 393224 | tf_op jit(solution)/shard_map/ppermute | solution.py:570
  8.2 1.4 %shard_map.150 = (bf16[512,256]{1,0:T(8,128)(2,1)S(1)}, f32[512,512]{1,0:T(8,128)S(1)}, f32[64,64]{1,0:T(8,128)S(1)}, f32[64,64]{1,0:T(8,128)S(1)}, f32[1,64]{1,0:T(1,128)S(1)}, /*index=5*/f32[1,64]{1,0:T(1,128)S(1)}) custom-call(s32[2,512]{1,0:T(2,128)S(1)} %get-tuple-element.41.refs_0_, f32[7,2,8]{2,1,0:T(2,128)S(1)} %get-tuple-element.42.refs_1_, ...), custom_call_target="tpu_custom_call" | custom-call | flops 1966080 | bytes 262144 | tf_op jit(solution)/shard_map/pallas_call | solution.py:652
  9.6 0.0 collective-permute-done.1.refs_1_
  9.6 0.0 collective-permute-done.refs_0_
  9.7 1.8 %collective-permute-start.3 = (f32[24,512]{1,0:T(8,128)S(1)}, f32[24,512]{1,0:T(8,128)S(1)}, u32[]{:S(2)}, u32[]{:S(2)}) collective-permute-start(f32[24,512]{1,0:T(8,128)S(1)} %get-tuple-element.53.refs_7_), channel_id=1, source_target_pairs={{0,28},{4,8},{8,4},{12,16},{16,12},{20,24},{24,20},{28,0},{1,29},{... | collective-permute-start | bytes 147464 | tf_op jit(solution)/shard_map/ppermute | solution.py:575
  11.5 0.0 collective-permute-start.5
  11.5 1.0 %shard_map.152 = (bf16[1024,512]{1,0:T(8,128)(2,1)S(1)}, f32[14,8,512]{2,1,0:T(8,128)S(1)}, f32[64,1024]{1,0:T(8,128)S(1)}, bf16[256,256]{1,0:T(8,128)(2,1)S(1)}...) custom-call(f32[512,512]{1,0:T(8,128)S(1)} %get-tuple-element.45.ref, ...), custom_call_target="tpu_custom_call" | custom-call | flops 2097152 | bytes 1048576 | tf_op jit(solution)/shard_map/pallas_call | solution.py:669
  12.5 0.7 collective-permute-done.2.refs_1_.refs_3_
  13.2 0.0 collective-permute-done.4.refs_2_.refs_5_
  13.2 0.6 shard_map.153.refs_12_.refs_6_
  13.9 0.6 collective-permute-done.3.refs_4_
  14.5 0.0 collective-permute-done.5.refs_6_
  14.5 1.3 %shard_map.154 = f32[512,128]{1,0:T(8,128)S(1)} custom-call(f32[128,512]{1,0:T(8,128)S(1)} %get-tuple-element.61.refs_0_, f32[48,512]{1,0:T(8,128)S(1)} %get-tuple-element.62.refs_1_.refs_4_, f32[48,512]{1,0:T(8,128)S(1)} %get-tuple-element.63.refs_2_.refs_5_, f32[64,512]{1,0:T(8,128)S(1)} %collective-permute-done.2.refs_1_.refs_3_, ...), custom_call_target="tpu_custom_call" | custom-call | flops 402653184 | bytes 2359296 | tf_op jit(solution)/shard_map/pallas_call | solution.py:718
  15.7 14.6 %all_to_all.44 = f32[32,16,128]{2,1,0:T(8,128)S(1)} all-to-all(f32[32,16,128]{2,1,0:T(8,128)S(1)} %bitcast.21), channel_id=1, replica_groups=mesh['py'=8,'pz'=4] {'py','pz'}, dimensions={0} | all-to-all | bytes 524288 | tf_op jit(solution)/shard_map/all_to_all | solution.py:722
  30.3 1.4 %shard_map.155 = f32[768,128]{1,0:T(8,128)S(1)} custom-call(f32[64,1024]{1,0:T(8,128)S(1)} %get-tuple-element.54.refs_3_.refs_0_, bf16[256,256]{1,0:T(8,128)(2,1)S(1)} %get-tuple-element.55.refs_1_, bf16[256,256]{1,0:T(8,128)(2,1)S(1)} %get-tuple-element.56.refs_2_, bf16[64,192]{1,0:T(8,128)(2,1)S(1)} %get-tuple-element.57.refs_3_, ...), custom_call_target="tpu_custom_call" | custom-call | flops 402653184 | bytes 524288 | tf_op jit(solution)/shard_map/pallas_call | solution.py:679
  31.7 0.0 copy-start
  31.7 14.4 %all_to_all.45 = f32[32,24,128]{2,1,0:T(8,128)S(1)} all-to-all(f32[32,24,128]{2,1,0:T(8,128)S(1)} %bitcast.19), channel_id=1, replica_groups=mesh['py'=8,'pz'=4] {'py','pz'}, dimensions={0} | all-to-all | bytes 786432 | tf_op jit(solution)/shard_map/all_to_all | solution.py:724
  46.0 1.3 %shard_map.156 = (f32[128,512]{1,0:T(8,128)S(1)}, f32[128,512]{1,0:T(8,128)S(1)}, f32[24,512]{1,0:T(8,128)S(1)}, f32[24,512]{1,0:T(8,128)S(1)}, f32[48,512]{1,0:T(8,128)S(1)}, /*index=5*/f32[48,512]{1,0:T(8,128)S(1)}) custom-call(f32[768,128]{1,0:T(8,128)S(1)} %bitcast.18, bf16[1024,512]{1,0:T(8,128)(2,1)S(1)} %get-tuple-element.69.refs_11_.refs_1_.vectors_ref, ...), custom_call_target="tpu_custom_call" | custom-call | flops 201326592 | bytes 2097152 | tf_op jit(solution)/shard_map/pallas_call | solution.py:732
  47.3 2.1 %collective-permute-start.6 = (f32[48,512]{1,0:T(8,128)S(1)}, f32[48,512]{1,0:T(8,128)S(1)}, u32[]{:S(2)}, u32[]{:S(2)}) collective-permute-start(f32[48,512]{1,0:T(8,128)S(1)} %get-tuple-element.73), channel_id=1, source_target_pairs={{0,28},{4,8},{8,4},{12,16},{16,12},{20,24},{24,20},{28,0},{1,29},{... | collective-permute-start | bytes 294920 | tf_op jit(solution)/shard_map/ppermute | solution.py:575
  49.4 0.0 collective-permute-start.7
  49.4 0.8 shard_map.157.applied_ref
  50.2 2.1 %collective-permute-done.6.yodd_ref = f32[48,512]{1,0:T(8,128)S(1)} collective-permute-done((f32[48,512]{1,0:T(8,128)S(1)}, f32[48,512]{1,0:T(8,128)S(1)}, u32[]{:S(2)}, u32[]{:S(2)}) %collective-permute-start.6) | collective-permute-done | bytes 98336 | tf_op jit(solution)/shard_map/ppermute | solution.py:575
  52.3 0.0 collective-permute-done.7.yeven_ref
  52.3 0.6 shard_map.158
  52.9 14.0 %all_to_all.46 = f32[32,16,128]{2,1,0:T(8,128)S(1)} all-to-all(f32[32,16,128]{2,1,0:T(8,128)S(1)} %bitcast.27), channel_id=1, replica_groups=mesh['py'=8,'pz'=4] {'py','pz'}, dimensions={0} | all-to-all | bytes 524288 | tf_op jit(solution)/shard_map/all_to_all | solution.py:722
  66.9 1.3 %shard_map.159 = f32[512,128]{1,0:T(8,128)S(1)} custom-call(f32[64,1024]{1,0:T(8,128)S(1)} %get-tuple-element.54.refs_3_.refs_0_, bf16[256,256]{1,0:T(8,128)(2,1)S(1)} %get-tuple-element.55.refs_1_, bf16[256,256]{1,0:T(8,128)(2,1)S(1)} %get-tuple-element.56.refs_2_, bf16[64,192]{1,0:T(8,128)(2,1)S(1)} %get-tuple-element.57.refs_3_, ...), custom_call_target="tpu_custom_call" | custom-call | flops 402653184 | bytes 524288 | tf_op jit(solution)/shard_map/pallas_call | solution.py:679
  68.2 12.7 %all_to_all.47 = f32[32,16,128]{2,1,0:T(8,128)S(1)} all-to-all(f32[32,16,128]{2,1,0:T(8,128)S(1)} %bitcast.29), channel_id=1, replica_groups=mesh['py'=8,'pz'=4] {'py','pz'}, dimensions={0} | all-to-all | bytes 524288 | tf_op jit(solution)/shard_map/all_to_all | solution.py:724
  80.9 1.1 %shard_map.160 = (f32[128,512]{1,0:T(8,128)}, f32[128,512]{1,0:T(8,128)}) custom-call(f32[512,128]{1,0:T(8,128)S(1)} %bitcast.20, bf16[1024,512]{1,0:T(8,128)(2,1)S(1)} %get-tuple-element.69.refs_11_.refs_1_.vectors_ref, f32[128,512]{1,0:T(8,128)S(1)} %get-tuple-element.76.field_ref, f32[128,512]{1,0:T(8,128)S(1)} %get-tuple-element.77.residual_ref), custom_call_target="tpu_custom_call" | custom-call | flops 201326592 | bytes 2097152 | tf_op jit(solution)/shard_map/pallas_call | solution.py:727
  (4 shorter events, 0.1 us)
Async XLA Ops:
  2.0 7.7 %collective-permute-start.1 = (f32[48,512]{1,0:T(8,128)S(1)}, f32[48,512]{1,0:T(8,128)S(1)}, u32[]{:S(2)}, u32[]{:S(2)}) collective-permute-start(f32[48,512]{1,0:T(8,128)S(1)} %get-tuple-element.44.refs_8_), channel_id=1, source_target_pairs={{0,8},{1,2},{2,1},{3,11},{4,5},{5,4},{6,7},{7,6},{8,0},{9,10},{10,... | collective-permute-start | bytes 294920 | tf_op jit(solution)/shard_map/ppermute | solution.py:586
  5.0 4.7 %collective-permute-start = (f32[48,512]{1,0:T(8,128)S(1)}, f32[48,512]{1,0:T(8,128)S(1)}, u32[]{:S(2)}, u32[]{:S(2)}) collective-permute-start(f32[48,512]{1,0:T(8,128)S(1)} %get-tuple-element.51), channel_id=1, source_target_pairs={{0,1},{1,0},{2,3},{3,2},{4,12},{5,6},{6,5},{7,15},{8,9},{9,8},{10,... | collective-permute-start | bytes 294920 | tf_op jit(solution)/shard_map/ppermute | solution.py:586
  6.6 6.6 %collective-permute-start.2 = (f32[64,512]{1,0:T(8,128)S(1)}, f32[64,512]{1,0:T(8,128)S(1)}, u32[]{:S(2)}, u32[]{:S(2)}) collective-permute-start(f32[64,512]{1,0:T(8,128)S(1)} %get-tuple-element.64), channel_id=1, source_target_pairs={{0,28},{4,8},{8,4},{12,16},{16,12},{20,24},{24,20},{28,0},{1,29},{... | collective-permute-start | bytes 393224 | tf_op jit(solution)/shard_map/ppermute | solution.py:575
  6.9 6.3 %collective-permute-start.4 = (f32[64,512]{1,0:T(8,128)S(1)}, f32[64,512]{1,0:T(8,128)S(1)}, u32[]{:S(2)}, u32[]{:S(2)}) collective-permute-start(f32[64,512]{1,0:T(8,128)S(1)} %get-tuple-element.65), channel_id=1, source_target_pairs={{0,4},{4,0},{8,12},{12,8},{16,20},{20,16},{24,28},{28,24},{1,5},{5... | collective-permute-start | bytes 393224 | tf_op jit(solution)/shard_map/ppermute | solution.py:570
  9.7 4.8 %collective-permute-start.3 = (f32[24,512]{1,0:T(8,128)S(1)}, f32[24,512]{1,0:T(8,128)S(1)}, u32[]{:S(2)}, u32[]{:S(2)}) collective-permute-start(f32[24,512]{1,0:T(8,128)S(1)} %get-tuple-element.53.refs_7_), channel_id=1, source_target_pairs={{0,28},{4,8},{8,4},{12,16},{16,12},{20,24},{24,20},{28,0},{1,29},{... | collective-permute-start | bytes 147464 | tf_op jit(solution)/shard_map/ppermute | solution.py:575
  11.5 3.0 %collective-permute-start.5 = (f32[24,512]{1,0:T(8,128)S(1)}, f32[24,512]{1,0:T(8,128)S(1)}, u32[]{:S(2)}, u32[]{:S(2)}) collective-permute-start(f32[24,512]{1,0:T(8,128)S(1)} %get-tuple-element.66), channel_id=1, source_target_pairs={{0,4},{4,0},{8,12},{12,8},{16,20},{20,16},{24,28},{28,24},{1,5},{5... | collective-permute-start | bytes 147464 | tf_op jit(solution)/shard_map/ppermute | solution.py:570
  13.2 1.3 %copy-start.1 = (f32[8,16,512]{2,1,0:T(8,128)S(1)}, f32[8,16,512]{2,1,0:T(8,128)}, u32[]{:S(2)}) copy-start(f32[8,16,512]{2,1,0:T(8,128)} %param.15) | copy-start | bytes 786436
  31.7 14.4 %copy-start = (f32[8,16,512]{2,1,0:T(8,128)S(1)}, f32[8,16,512]{2,1,0:T(8,128)}, u32[]{:S(2)}) copy-start(f32[8,16,512]{2,1,0:T(8,128)} %param.14) | copy-start | bytes 786436
  47.3 5.0 %collective-permute-start.6 = (f32[48,512]{1,0:T(8,128)S(1)}, f32[48,512]{1,0:T(8,128)S(1)}, u32[]{:S(2)}, u32[]{:S(2)}) collective-permute-start(f32[48,512]{1,0:T(8,128)S(1)} %get-tuple-element.73), channel_id=1, source_target_pairs={{0,28},{4,8},{8,4},{12,16},{16,12},{20,24},{24,20},{28,0},{1,29},{... | collective-permute-start | bytes 294920 | tf_op jit(solution)/shard_map/ppermute | solution.py:575
  49.4 2.9 %collective-permute-start.7 = (f32[48,512]{1,0:T(8,128)S(1)}, f32[48,512]{1,0:T(8,128)S(1)}, u32[]{:S(2)}, u32[]{:S(2)}) collective-permute-start(f32[48,512]{1,0:T(8,128)S(1)} %get-tuple-element.74), channel_id=1, source_target_pairs={{0,4},{4,0},{8,12},{12,8},{16,20},{20,16},{24,28},{28,24},{1,5},{5... | collective-permute-start | bytes 294920 | tf_op jit(solution)/shard_map/ppermute | solution.py:570

commit v10 on v9

--- a/solution.py
+++ b/solution.py
@@ -77,7 +77,7 @@
     coef_ref, weighted_ref, even_ref, odd_ref, yodd_ref, yeven_ref, *refs = refs
     targets, (table, span, field, sem) = refs[:small], refs[small:]
     fetch([(table_ref, table), (span_ref, span), (field_ref, field), *zip(sources, targets)], sem)
-    first = lax.rem(lax.axis_index("py") + lax.axis_index("pz"), 2) == 1
+    first = lax.rem(lax.axis_index("pz"), 2) == 0
     half = ly * REACH
     entries = [table[entry] for entry in range(table_ref.shape[0])]
     for start in range(0, span.shape[0], lz):
@@ -124,7 +124,7 @@
 
 
 def y_rims_kernel(ly, odd_ref, even_ref, _, zlow_ref, zhigh_ref, yodd_ref, yeven_ref):
-    first = lax.rem(lax.axis_index("py") + lax.axis_index("pz"), 2) == 1
+    first = lax.rem(lax.axis_index("pz"), 2) == 0
     zlow_ref[...] = jnp.where(first, odd_ref[...], even_ref[...])
     zhigh_ref[...] = jnp.where(first, even_ref[...], odd_ref[...])
     store_y_rims(corners(ly, zlow_ref, zhigh_ref), yodd_ref, yeven_ref)
@@ -575,14 +575,13 @@
     return lax.ppermute(value, axis, [(i, (i + 1 if i % 2 else i - 1) % count) for i in range(count)])
 
 
-def staggered(value, parity):
+def odd_pairs(value):
     across, count = lax.axis_size("py"), lax.axis_size("pz")
     pairs = []
     for i in range(across):
         for k in range(count):
-            j = k + 1 if (i + k) % 2 == parity else k - 1
-            other = i ^ 2 if i ^ 2 < across else i
-            pairs.append((i * count + k, i * count + j if 0 <= j < count else other * count + k))
+            j = k + 1 if k % 2 else k - 1
+            pairs.append((i * count + k, i * count + j if 0 <= j < count else (i ^ 1) * count + k))
     return lax.ppermute(value, BOTH, pairs)
 
 
@@ -656,7 +655,7 @@
         [dma((len(later),))] * fast,
     )(*bands, *in_hbm(*later), even)
 
-    even, odd = staggered(even, 1), staggered(odd, 0)
+    even, odd = pairwise(even, "pz", 0), odd_pairs(odd)
     zlow, zhigh, *corner = call(
         lambda *refs: y_rims_kernel(ly, *refs),
         [(zrims, F32)] * 2 + [((up8(2 * REACH * REACH), nx), F32)] * 2,

time: 82.3 us -> 81.4 us (0.989)
  starting transfers between devices: 10.2 us -> 8.46 us
  waiting for transfers between devices: 3.44 us -> 4.49 us
    ppermute x2 -> x1, starting transfers between devices: 4.67 us -> 0.01 us  [odd_pairs(): return lax.ppermute(value, BOTH, pairs)]
    ppermute x3 -> x4, starting transfers between devices: 1.33 us -> 3.1 us  [pairwise(): lax.ppermute(value, axis, [(i, j if 0 <= j < count else i) for i, j in en...]
    ppermute x3, starting transfers between devices: 4.16 us -> 5.35 us  [paired(): lax.ppermute(value, axis, [(i, (i + 1 if i % 2 else i - 1) % count) for i...]
    ppermute x3, waiting for transfers between devices: 3.43 us -> 4.48 us  [paired(): lax.ppermute(value, axis, [(i, (i + 1 if i % 2 else i - 1) % count) for i...]
where the time goes in v10:
time: 81.4 us; the launch traced here: 81.2 us
  blocking collectives  55.4 us (68%)
  Pallas kernels  12 us (15%)
  starting transfers between devices  8.46 us (10%)
  waiting for transfers between devices  4.49 us (6%)
    all_to_all x4, blocking collectives, shards(): lax.all_to_all(spectral, BOTH, split_axis=0, concat_axis=0, tiled=True)  55.4 us
    ppermute x3, starting transfers between devices, paired(): lax.ppermute(value, axis, [(i, (i + 1 if i % 2 else i - 1) % count) for i...  5.35 us
    ppermute x3, waiting for transfers between devices, paired(): lax.ppermute(value, axis, [(i, (i + 1 if i % 2 else i - 1) % count) for i...  4.48 us
    ppermute x4, starting transfers between devices, pairwise(): lax.ppermute(value, axis, [(i, j if 0 <= j < count else i) for i, j in en...  3.1 us
    pallas_call x2, Pallas kernels, precondition(): call(lambda *refs: modes_kernel(npy, npz, rims, *refs), [((devices * size...  2.63 us
  transfers between devices with their start and end apart: 8, of which 3 were waited for; matrix products, arithmetic and copies ran while one was open for 0% of the time, Pallas kernels for 5%

profile of v10, /device:TPU:0, one launch (start us, length us, event | category | flops | bytes accessed | tf_op | source)
XLA Modules:
  0.0 81.2 jit_solution(6812109592901323045)
XLA Ops:
  0.6 1.3 %shard_map.149 = (f32[128,512]{1,0:T(8,128)S(1)}, f32[128,512]{1,0:T(8,128)S(1)}, f32[48,512]{1,0:T(8,128)S(1)}, f32[48,512]{1,0:T(8,128)S(1)}, f32[64,512]{1,0:...) custom-call(f32[8]{0:T(128)} %refs_0_.1, ...), custom_call_target="tpu_custom_call" | custom-call | flops 1048576 | bytes 1048576 | tf_op jit(solution)/shard_map/pallas_call | solution.py:641
  2.0 3.1 %collective-permute-start.1 = (f32[48,512]{1,0:T(8,128)S(1)}, f32[48,512]{1,0:T(8,128)S(1)}, u32[]{:S(2)}, u32[]{:S(2)}) collective-permute-start(f32[48,512]{1,0:T(8,128)S(1)} %get-tuple-element.44.refs_8_), channel_id=1, source_target_pairs={{0,1},{1,0},{2,3},{3,2},{4,5},{5,4},{6,7},{7,6},{8,9},{9,8},{10,11... | collective-permute-start | bytes 294920 | tf_op jit(solution)/shard_map/ppermute | solution.py:570
  5.0 0.0 collective-permute-start
  5.0 2.6 %collective-permute-start.2 = (f32[64,512]{1,0:T(8,128)S(1)}, f32[64,512]{1,0:T(8,128)S(1)}, u32[]{:S(2)}, u32[]{:S(2)}) collective-permute-start(f32[64,512]{1,0:T(8,128)S(1)} %get-tuple-element.64), channel_id=1, source_target_pairs={{0,28},{4,8},{8,4},{12,16},{16,12},{20,24},{24,20},{28,0},{1,29},{... | collective-permute-start | bytes 393224 | tf_op jit(solution)/shard_map/ppermute | solution.py:575
  7.6 0.0 collective-permute-start.4
  7.6 1.4 %shard_map.150 = (bf16[512,256]{1,0:T(8,128)(2,1)S(1)}, f32[512,512]{1,0:T(8,128)S(1)}, f32[64,64]{1,0:T(8,128)S(1)}, f32[64,64]{1,0:T(8,128)S(1)}, f32[1,64]{1,0:T(1,128)S(1)}, /*index=5*/f32[1,64]{1,0:T(1,128)S(1)}) custom-call(s32[2,512]{1,0:T(2,128)S(1)} %get-tuple-element.41.refs_0_, f32[7,2,8]{2,1,0:T(2,128)S(1)} %get-tuple-element.42.refs_1_, ...), custom_call_target="tpu_custom_call" | custom-call | flops 1966080 | bytes 262144 | tf_op jit(solution)/shard_map/pallas_call | solution.py:651
  9.0 0.0 collective-permute-done.1.refs_1_
  9.0 0.0 collective-permute-done.refs_0_
  9.1 0.7 collective-permute-start.3
  9.8 0.0 collective-permute-start.5
  9.8 1.0 %shard_map.152 = (bf16[1024,512]{1,0:T(8,128)(2,1)S(1)}, f32[14,8,512]{2,1,0:T(8,128)S(1)}, f32[64,1024]{1,0:T(8,128)S(1)}, bf16[256,256]{1,0:T(8,128)(2,1)S(1)}...) custom-call(f32[512,512]{1,0:T(8,128)S(1)} %get-tuple-element.45.ref, ...), custom_call_target="tpu_custom_call" | custom-call | flops 2097152 | bytes 1048576 | tf_op jit(solution)/shard_map/pallas_call | solution.py:668
  10.8 0.3 collective-permute-done.2.refs_1_.refs_3_
  11.0 0.0 collective-permute-done.4.refs_2_.refs_5_
  11.0 0.6 shard_map.153.refs_12_.refs_6_
  11.7 2.1 %collective-permute-done.3.refs_4_ = f32[24,512]{1,0:T(8,128)S(1)} collective-permute-done((f32[24,512]{1,0:T(8,128)S(1)}, f32[24,512]{1,0:T(8,128)S(1)}, u32[]{:S(2)}, u32[]{:S(2)}) %collective-permute-start.3) | collective-permute-done | bytes 49184 | tf_op jit(solution)/shard_map/ppermute | solution.py:575
  13.8 0.0 collective-permute-done.5.refs_6_
  13.8 1.3 %shard_map.154 = f32[512,128]{1,0:T(8,128)S(1)} custom-call(f32[128,512]{1,0:T(8,128)S(1)} %get-tuple-element.61.refs_0_, f32[48,512]{1,0:T(8,128)S(1)} %get-tuple-element.62.refs_1_.refs_4_, f32[48,512]{1,0:T(8,128)S(1)} %get-tuple-element.63.refs_2_.refs_5_, f32[64,512]{1,0:T(8,128)S(1)} %collective-permute-done.2.refs_1_.refs_3_, ...), custom_call_target="tpu_custom_call" | custom-call | flops 402653184 | bytes 2359296 | tf_op jit(solution)/shard_map/pallas_call | solution.py:717
  15.1 14.3 %all_to_all.44 = f32[32,16,128]{2,1,0:T(8,128)S(1)} all-to-all(f32[32,16,128]{2,1,0:T(8,128)S(1)} %bitcast.21), channel_id=1, replica_groups=mesh['py'=8,'pz'=4] {'py','pz'}, dimensions={0} | all-to-all | bytes 524288 | tf_op jit(solution)/shard_map/all_to_all | solution.py:721
  29.4 1.4 %shard_map.155 = f32[768,128]{1,0:T(8,128)S(1)} custom-call(f32[64,1024]{1,0:T(8,128)S(1)} %get-tuple-element.54.refs_3_.refs_0_, bf16[256,256]{1,0:T(8,128)(2,1)S(1)} %get-tuple-element.55.refs_1_, bf16[256,256]{1,0:T(8,128)(2,1)S(1)} %get-tuple-element.56.refs_2_, bf16[64,192]{1,0:T(8,128)(2,1)S(1)} %get-tuple-element.57.refs_3_, ...), custom_call_target="tpu_custom_call" | custom-call | flops 402653184 | bytes 524288 | tf_op jit(solution)/shard_map/pallas_call | solution.py:678
  30.8 0.0 copy-start
  30.8 14.4 %all_to_all.45 = f32[32,24,128]{2,1,0:T(8,128)S(1)} all-to-all(f32[32,24,128]{2,1,0:T(8,128)S(1)} %bitcast.19), channel_id=1, replica_groups=mesh['py'=8,'pz'=4] {'py','pz'}, dimensions={0} | all-to-all | bytes 786432 | tf_op jit(solution)/shard_map/all_to_all | solution.py:723
  45.1 1.3 %shard_map.156 = (f32[128,512]{1,0:T(8,128)S(1)}, f32[128,512]{1,0:T(8,128)S(1)}, f32[24,512]{1,0:T(8,128)S(1)}, f32[24,512]{1,0:T(8,128)S(1)}, f32[48,512]{1,0:T(8,128)S(1)}, /*index=5*/f32[48,512]{1,0:T(8,128)S(1)}) custom-call(f32[768,128]{1,0:T(8,128)S(1)} %bitcast.18, bf16[1024,512]{1,0:T(8,128)(2,1)S(1)} %get-tuple-element.69.refs_11_.refs_1_.vectors_ref, ...), custom_call_target="tpu_custom_call" | custom-call | flops 201326592 | bytes 2097152 | tf_op jit(solution)/shard_map/pallas_call | solution.py:731
  46.4 2.1 %collective-permute-start.6 = (f32[48,512]{1,0:T(8,128)S(1)}, f32[48,512]{1,0:T(8,128)S(1)}, u32[]{:S(2)}, u32[]{:S(2)}) collective-permute-start(f32[48,512]{1,0:T(8,128)S(1)} %get-tuple-element.73), channel_id=1, source_target_pairs={{0,28},{4,8},{8,4},{12,16},{16,12},{20,24},{24,20},{28,0},{1,29},{... | collective-permute-start | bytes 294920 | tf_op jit(solution)/shard_map/ppermute | solution.py:575
  48.5 0.0 collective-permute-start.7
  48.5 0.8 %shard_map.157.applied_ref = f32[128,512]{1,0:T(8,128)S(1)} custom-call(f32[128,512]{1,0:T(8,128)S(1)} %get-tuple-element.70.refs_0_, f32[24,512]{1,0:T(8,128)S(1)} %get-tuple-element.71.refs_1_, f32[24,512]{1,0:T(8,128)S(1)} %get-tuple-element.72.refs_2_, bf16[512,256]{1,0:T(8,128)(2,1)S(1)} %get-tuple-element.52.refs_2_.refs_7_.refs_3_, ...), custom_call_target="tpu_custom_call" | custom-call | flops 402653184 | bytes 2359296 | tf_op jit(solution)/shard_map/pallas_call | solution.py:710
  49.3 2.1 %collective-permute-done.6.yodd_ref = f32[48,512]{1,0:T(8,128)S(1)} collective-permute-done((f32[48,512]{1,0:T(8,128)S(1)}, f32[48,512]{1,0:T(8,128)S(1)}, u32[]{:S(2)}, u32[]{:S(2)}) %collective-permute-start.6) | collective-permute-done | bytes 98336 | tf_op jit(solution)/shard_map/ppermute | solution.py:575
  51.4 0.0 collective-permute-done.7.yeven_ref
  51.4 0.6 shard_map.158
  52.0 14.0 %all_to_all.46 = f32[32,16,128]{2,1,0:T(8,128)S(1)} all-to-all(f32[32,16,128]{2,1,0:T(8,128)S(1)} %bitcast.27), channel_id=1, replica_groups=mesh['py'=8,'pz'=4] {'py','pz'}, dimensions={0} | all-to-all | bytes 524288 | tf_op jit(solution)/shard_map/all_to_all | solution.py:721
  66.0 1.3 %shard_map.159 = f32[512,128]{1,0:T(8,128)S(1)} custom-call(f32[64,1024]{1,0:T(8,128)S(1)} %get-tuple-element.54.refs_3_.refs_0_, bf16[256,256]{1,0:T(8,128)(2,1)S(1)} %get-tuple-element.55.refs_1_, bf16[256,256]{1,0:T(8,128)(2,1)S(1)} %get-tuple-element.56.refs_2_, bf16[64,192]{1,0:T(8,128)(2,1)S(1)} %get-tuple-element.57.refs_3_, ...), custom_call_target="tpu_custom_call" | custom-call | flops 402653184 | bytes 524288 | tf_op jit(solution)/shard_map/pallas_call | solution.py:678
  67.3 12.7 %all_to_all.47 = f32[32,16,128]{2,1,0:T(8,128)S(1)} all-to-all(f32[32,16,128]{2,1,0:T(8,128)S(1)} %bitcast.29), channel_id=1, replica_groups=mesh['py'=8,'pz'=4] {'py','pz'}, dimensions={0} | all-to-all | bytes 524288 | tf_op jit(solution)/shard_map/all_to_all | solution.py:723
  80.0 1.1 %shard_map.160 = (f32[128,512]{1,0:T(8,128)}, f32[128,512]{1,0:T(8,128)}) custom-call(f32[512,128]{1,0:T(8,128)S(1)} %bitcast.20, bf16[1024,512]{1,0:T(8,128)(2,1)S(1)} %get-tuple-element.69.refs_11_.refs_1_.vectors_ref, f32[128,512]{1,0:T(8,128)S(1)} %get-tuple-element.76.field_ref, f32[128,512]{1,0:T(8,128)S(1)} %get-tuple-element.77.residual_ref), custom_call_target="tpu_custom_call" | custom-call | flops 201326592 | bytes 2097152 | tf_op jit(solution)/shard_map/pallas_call | solution.py:726
  (4 shorter events, 0.1 us)
Async XLA Ops:
  2.0 7.1 %collective-permute-start.1 = (f32[48,512]{1,0:T(8,128)S(1)}, f32[48,512]{1,0:T(8,128)S(1)}, u32[]{:S(2)}, u32[]{:S(2)}) collective-permute-start(f32[48,512]{1,0:T(8,128)S(1)} %get-tuple-element.44.refs_8_), channel_id=1, source_target_pairs={{0,1},{1,0},{2,3},{3,2},{4,5},{5,4},{6,7},{7,6},{8,9},{9,8},{10,11... | collective-permute-start | bytes 294920 | tf_op jit(solution)/shard_map/ppermute | solution.py:570
  5.0 4.0 %collective-permute-start = (f32[48,512]{1,0:T(8,128)S(1)}, f32[48,512]{1,0:T(8,128)S(1)}, u32[]{:S(2)}, u32[]{:S(2)}) collective-permute-start(f32[48,512]{1,0:T(8,128)S(1)} %get-tuple-element.51), channel_id=1, source_target_pairs={{0,4},{1,2},{2,1},{3,7},{4,0},{5,6},{6,5},{7,3},{8,12},{9,10},{10,... | collective-permute-start | bytes 294920 | tf_op jit(solution)/shard_map/ppermute | solution.py:585
  5.0 6.0 %collective-permute-start.2 = (f32[64,512]{1,0:T(8,128)S(1)}, f32[64,512]{1,0:T(8,128)S(1)}, u32[]{:S(2)}, u32[]{:S(2)}) collective-permute-start(f32[64,512]{1,0:T(8,128)S(1)} %get-tuple-element.64), channel_id=1, source_target_pairs={{0,28},{4,8},{8,4},{12,16},{16,12},{20,24},{24,20},{28,0},{1,29},{... | collective-permute-start | bytes 393224 | tf_op jit(solution)/shard_map/ppermute | solution.py:575
  7.6 3.4 %collective-permute-start.4 = (f32[64,512]{1,0:T(8,128)S(1)}, f32[64,512]{1,0:T(8,128)S(1)}, u32[]{:S(2)}, u32[]{:S(2)}) collective-permute-start(f32[64,512]{1,0:T(8,128)S(1)} %get-tuple-element.65), channel_id=1, source_target_pairs={{0,4},{4,0},{8,12},{12,8},{16,20},{20,16},{24,28},{28,24},{1,5},{5... | collective-permute-start | bytes 393224 | tf_op jit(solution)/shard_map/ppermute | solution.py:570
  9.1 4.7 %collective-permute-start.3 = (f32[24,512]{1,0:T(8,128)S(1)}, f32[24,512]{1,0:T(8,128)S(1)}, u32[]{:S(2)}, u32[]{:S(2)}) collective-permute-start(f32[24,512]{1,0:T(8,128)S(1)} %get-tuple-element.53.refs_7_), channel_id=1, source_target_pairs={{0,28},{4,8},{8,4},{12,16},{16,12},{20,24},{24,20},{28,0},{1,29},{... | collective-permute-start | bytes 147464 | tf_op jit(solution)/shard_map/ppermute | solution.py:575
  9.8 4.0 %collective-permute-start.5 = (f32[24,512]{1,0:T(8,128)S(1)}, f32[24,512]{1,0:T(8,128)S(1)}, u32[]{:S(2)}, u32[]{:S(2)}) collective-permute-start(f32[24,512]{1,0:T(8,128)S(1)} %get-tuple-element.66), channel_id=1, source_target_pairs={{0,4},{4,0},{8,12},{12,8},{16,20},{20,16},{24,28},{28,24},{1,5},{5... | collective-permute-start | bytes 147464 | tf_op jit(solution)/shard_map/ppermute | solution.py:570
  11.0 2.8 %copy-start.1 = (f32[8,16,512]{2,1,0:T(8,128)S(1)}, f32[8,16,512]{2,1,0:T(8,128)}, u32[]{:S(2)}) copy-start(f32[8,16,512]{2,1,0:T(8,128)} %param.15) | copy-start | bytes 786436
  30.8 14.4 %copy-start = (f32[8,16,512]{2,1,0:T(8,128)S(1)}, f32[8,16,512]{2,1,0:T(8,128)}, u32[]{:S(2)}) copy-start(f32[8,16,512]{2,1,0:T(8,128)} %param.14) | copy-start | bytes 786436
  46.4 5.0 %collective-permute-start.6 = (f32[48,512]{1,0:T(8,128)S(1)}, f32[48,512]{1,0:T(8,128)S(1)}, u32[]{:S(2)}, u32[]{:S(2)}) collective-permute-start(f32[48,512]{1,0:T(8,128)S(1)} %get-tuple-element.73), channel_id=1, source_target_pairs={{0,28},{4,8},{8,4},{12,16},{16,12},{20,24},{24,20},{28,0},{1,29},{... | collective-permute-start | bytes 294920 | tf_op jit(solution)/shard_map/ppermute | solution.py:575
  48.5 2.9 %collective-permute-start.7 = (f32[48,512]{1,0:T(8,128)S(1)}, f32[48,512]{1,0:T(8,128)S(1)}, u32[]{:S(2)}, u32[]{:S(2)}) collective-permute-start(f32[48,512]{1,0:T(8,128)S(1)} %get-tuple-element.74), channel_id=1, source_target_pairs={{0,4},{4,0},{8,12},{12,8},{16,20},{20,16},{24,28},{28,24},{1,5},{5... | collective-permute-start | bytes 294920 | tf_op jit(solution)/shard_map/ppermute | solution.py:570

commit v11 on v10

--- a/solution.py
+++ b/solution.py
@@ -76,11 +76,23 @@
     sources, refs = refs[:small], refs[small:]
     coef_ref, weighted_ref, even_ref, odd_ref, yodd_ref, yeven_ref, *refs = refs
     targets, (table, span, field, sem) = refs[:small], refs[small:]
-    fetch([(table_ref, table), (span_ref, span), (field_ref, field), *zip(sources, targets)], sem)
+    count = span.shape[0]
+    pieces = [pl.ds(start, count // 4) for start in range(0, count, count // 4)]
+    pairs = [(table_ref, table)]
+    for piece in pieces:
+        pairs += [(span_ref.at[piece, :], span.at[piece, :]), (field_ref.at[piece, :], field.at[piece, :])]
+    pairs += list(zip(sources, targets))
+    copies = [pltpu.make_async_copy(*pair, sem.at[i]) for i, pair in enumerate(pairs)]
+    for copy in copies:
+        copy.start()
+    copies[0].wait()
     first = lax.rem(lax.axis_index("pz"), 2) == 0
     half = ly * REACH
     entries = [table[entry] for entry in range(table_ref.shape[0])]
     for start in range(0, span.shape[0], lz):
+        if start % (count // 4) == 0:
+            for copy in copies[1 + start * 8 // count : 3 + start * 8 // count]:
+                copy.wait()
         rows = pl.ds(start, lz)
         index = span[rows, :]
         coef = jnp.full(index.shape, entries[0], F32)
@@ -95,6 +107,8 @@
             even_ref[rim, :] = jnp.where(first, high, low)
             odd_ref[rim, :] = jnp.where(first, low, high)
     store_y_rims(own_rim(ly, lz, weighted_ref), yodd_ref, yeven_ref)
+    for copy in copies[1 + 2 * len(pieces) :]:
+        copy.wait()
     ybands = targets[1]
     for ref in (yodd_ref, yeven_ref):
         for matrix in range(2):
@@ -570,9 +584,15 @@
     return lax.ppermute(value, axis, [(i, j if 0 <= j < count else i) for i, j in enumerate(other)])
 
 
-def paired(value, axis):
-    count = lax.axis_size(axis)
-    return lax.ppermute(value, axis, [(i, (i + 1 if i % 2 else i - 1) % count) for i in range(count)])
+def paired(value, near):
+    across, count = lax.axis_size("py"), lax.axis_size("pz")
+    pairs = []
+    for i in range(across):
+        for k in range(count):
+            j = i + 1 if i % 2 else i - 1
+            end = i * count + (k ^ 1) if near and k ^ 1 < count else j % across * count + k
+            pairs.append((i * count + k, j * count + k if 0 <= j < across else end))
+    return lax.ppermute(value, BOTH, pairs)
 
 
 def odd_pairs(value):
@@ -644,7 +664,7 @@
         + [(array.shape, array.dtype) for array in small],
         [HBM] * (3 + len(small)), count * nx * 16, 4 * cell,
         [pltpu.SMEM(coef_table.shape, F32), pltpu.VMEM(block, jnp.int32), pltpu.VMEM(block, F32)]
-        + [dma((3 + len(small),))],
+        + [dma((9 + len(small),))],
     )(*in_hbm(coef_table, span_index.reshape(count, nx), field, *small))
 
     *bands, xbands = small
@@ -696,7 +716,7 @@
 
     for iteration in range(ITERS):
         last = iteration + 1 == ITERS
-        yodd, yeven = [paired(value, "py") for value in yodd], [pairwise(value, "py", 0) for value in yeven]
+        yodd, yeven = [paired(value, iteration > 0) for value in yodd], [pairwise(value, "py", 0) for value in yeven]
         parts = len(yodd)
         if fast and iteration == 0:
             outward = call(

time: 81.4 us -> 81.4 us (level)
  no operation moved by 1% of the time
where the time goes in v11:
time: 81.4 us; the launch traced here: 81.1 us
  blocking collectives  55.5 us (68%)
  Pallas kernels  12 us (15%)
  starting transfers between devices  8.72 us (11%)
  waiting for transfers between devices  4.17 us (5%)
    all_to_all x4, blocking collectives, shards(): lax.all_to_all(spectral, BOTH, split_axis=0, concat_axis=0, tiled=True)  55.5 us
    ppermute x3, starting transfers between devices, paired(): return lax.ppermute(value, BOTH, pairs)  5.62 us
    ppermute x3, waiting for transfers between devices, paired(): return lax.ppermute(value, BOTH, pairs)  4.16 us
    ppermute x4, starting transfers between devices, pairwise(): lax.ppermute(value, axis, [(i, j if 0 <= j < count else i) for i, j in en...  3.1 us
    pallas_call x2, Pallas kernels, precondition(): call(lambda *refs: modes_kernel(npy, npz, rims, *refs), [((devices * size...  2.63 us
  transfers between devices with their start and end apart: 8, of which 3 were waited for; matrix products, arithmetic and copies ran while one was open for 0% of the time, Pallas kernels for 5%

profile of v11, /device:TPU:0, one launch (start us, length us, event | category | flops | bytes accessed | tf_op | source)
XLA Modules:
  0.0 81.1 jit_solution(7898566226463296119)
XLA Ops:
  0.6 1.3 %shard_map.149 = (f32[128,512]{1,0:T(8,128)S(1)}, f32[128,512]{1,0:T(8,128)S(1)}, f32[48,512]{1,0:T(8,128)S(1)}, f32[48,512]{1,0:T(8,128)S(1)}, f32[64,512]{1,0:...) custom-call(f32[8]{0:T(128)} %refs_0_.1, ...), custom_call_target="tpu_custom_call" | custom-call | flops 1048576 | bytes 1048576 | tf_op jit(solution)/shard_map/pallas_call | solution.py:661
  1.9 3.1 %collective-permute-start.1 = (f32[48,512]{1,0:T(8,128)S(1)}, f32[48,512]{1,0:T(8,128)S(1)}, u32[]{:S(2)}, u32[]{:S(2)}) collective-permute-start(f32[48,512]{1,0:T(8,128)S(1)} %get-tuple-element.44.refs_8_), channel_id=1, source_target_pairs={{0,1},{1,0},{2,3},{3,2},{4,5},{5,4},{6,7},{7,6},{8,9},{9,8},{10,11... | collective-permute-start | bytes 294920 | tf_op jit(solution)/shard_map/ppermute | solution.py:584
  5.0 0.0 collective-permute-start
  5.0 2.6 %collective-permute-start.2 = (f32[64,512]{1,0:T(8,128)S(1)}, f32[64,512]{1,0:T(8,128)S(1)}, u32[]{:S(2)}, u32[]{:S(2)}) collective-permute-start(f32[64,512]{1,0:T(8,128)S(1)} %get-tuple-element.64), channel_id=1, source_target_pairs={{0,28},{1,29},{2,30},{3,31},{4,8},{5,9},{6,10},{7,11},{8,4},{9,5},... | collective-permute-start | bytes 393224 | tf_op jit(solution)/shard_map/ppermute | solution.py:595
  7.5 0.0 collective-permute-start.4
  7.6 1.4 %shard_map.150 = (bf16[512,256]{1,0:T(8,128)(2,1)S(1)}, f32[512,512]{1,0:T(8,128)S(1)}, f32[64,64]{1,0:T(8,128)S(1)}, f32[64,64]{1,0:T(8,128)S(1)}, f32[1,64]{1,0:T(1,128)S(1)}, /*index=5*/f32[1,64]{1,0:T(1,128)S(1)}) custom-call(s32[2,512]{1,0:T(2,128)S(1)} %get-tuple-element.41.refs_0_, f32[7,2,8]{2,1,0:T(2,128)S(1)} %get-tuple-element.42.refs_1_, ...), custom_call_target="tpu_custom_call" | custom-call | flops 1966080 | bytes 262144 | tf_op jit(solution)/shard_map/pallas_call | solution.py:671
  9.0 0.0 collective-permute-done.1.refs_1_
  9.0 0.0 collective-permute-done.refs_0_
  9.0 0.7 collective-permute-start.3
  9.7 0.0 collective-permute-start.5
  9.7 1.0 %shard_map.152 = (bf16[1024,512]{1,0:T(8,128)(2,1)S(1)}, f32[14,8,512]{2,1,0:T(8,128)S(1)}, f32[64,1024]{1,0:T(8,128)S(1)}, bf16[256,256]{1,0:T(8,128)(2,1)S(1)}...) custom-call(f32[512,512]{1,0:T(8,128)S(1)} %get-tuple-element.45.ref, ...), custom_call_target="tpu_custom_call" | custom-call | flops 2097152 | bytes 1048576 | tf_op jit(solution)/shard_map/pallas_call | solution.py:688
  10.7 0.3 collective-permute-done.2.refs_1_.refs_3_
  11.0 0.0 collective-permute-done.4.refs_2_.refs_5_
  11.0 0.6 shard_map.153.refs_12_.refs_6_
  11.6 2.1 %collective-permute-done.3.refs_4_ = f32[24,512]{1,0:T(8,128)S(1)} collective-permute-done((f32[24,512]{1,0:T(8,128)S(1)}, f32[24,512]{1,0:T(8,128)S(1)}, u32[]{:S(2)}, u32[]{:S(2)}) %collective-permute-start.3) | collective-permute-done | bytes 49184 | tf_op jit(solution)/shard_map/ppermute | solution.py:595
  13.8 0.0 collective-permute-done.5.refs_6_
  13.8 1.3 %shard_map.154 = f32[512,128]{1,0:T(8,128)S(1)} custom-call(f32[128,512]{1,0:T(8,128)S(1)} %get-tuple-element.61.refs_0_, f32[48,512]{1,0:T(8,128)S(1)} %get-tuple-element.62.refs_1_.refs_4_, f32[48,512]{1,0:T(8,128)S(1)} %get-tuple-element.63.refs_2_.refs_5_, f32[64,512]{1,0:T(8,128)S(1)} %collective-permute-done.2.refs_1_.refs_3_, ...), custom_call_target="tpu_custom_call" | custom-call | flops 402653184 | bytes 2359296 | tf_op jit(solution)/shard_map/pallas_call | solution.py:737
  15.0 14.3 %all_to_all.44 = f32[32,16,128]{2,1,0:T(8,128)S(1)} all-to-all(f32[32,16,128]{2,1,0:T(8,128)S(1)} %bitcast.21), channel_id=1, replica_groups=mesh['py'=8,'pz'=4] {'py','pz'}, dimensions={0} | all-to-all | bytes 524288 | tf_op jit(solution)/shard_map/all_to_all | solution.py:741
  29.3 1.4 %shard_map.155 = f32[768,128]{1,0:T(8,128)S(1)} custom-call(f32[64,1024]{1,0:T(8,128)S(1)} %get-tuple-element.54.refs_3_.refs_0_, bf16[256,256]{1,0:T(8,128)(2,1)S(1)} %get-tuple-element.55.refs_1_, bf16[256,256]{1,0:T(8,128)(2,1)S(1)} %get-tuple-element.56.refs_2_, bf16[64,192]{1,0:T(8,128)(2,1)S(1)} %get-tuple-element.57.refs_3_, ...), custom_call_target="tpu_custom_call" | custom-call | flops 402653184 | bytes 524288 | tf_op jit(solution)/shard_map/pallas_call | solution.py:698
  30.7 0.0 copy-start
  30.7 14.4 %all_to_all.45 = f32[32,24,128]{2,1,0:T(8,128)S(1)} all-to-all(f32[32,24,128]{2,1,0:T(8,128)S(1)} %bitcast.19), channel_id=1, replica_groups=mesh['py'=8,'pz'=4] {'py','pz'}, dimensions={0} | all-to-all | bytes 786432 | tf_op jit(solution)/shard_map/all_to_all | solution.py:743
  45.1 1.3 %shard_map.156 = (f32[128,512]{1,0:T(8,128)S(1)}, f32[128,512]{1,0:T(8,128)S(1)}, f32[24,512]{1,0:T(8,128)S(1)}, f32[24,512]{1,0:T(8,128)S(1)}, f32[48,512]{1,0:T(8,128)S(1)}, /*index=5*/f32[48,512]{1,0:T(8,128)S(1)}) custom-call(f32[768,128]{1,0:T(8,128)S(1)} %bitcast.18, bf16[1024,512]{1,0:T(8,128)(2,1)S(1)} %get-tuple-element.69.refs_11_.refs_1_.vectors_ref, ...), custom_call_target="tpu_custom_call" | custom-call | flops 201326592 | bytes 2097152 | tf_op jit(solution)/shard_map/pallas_call | solution.py:751
  46.4 2.3 %collective-permute-start.6 = (f32[48,512]{1,0:T(8,128)S(1)}, f32[48,512]{1,0:T(8,128)S(1)}, u32[]{:S(2)}, u32[]{:S(2)}) collective-permute-start(f32[48,512]{1,0:T(8,128)S(1)} %get-tuple-element.73), channel_id=1, source_target_pairs={{0,1},{1,0},{2,3},{3,2},{4,8},{5,9},{6,10},{7,11},{8,4},{9,5},{10,... | collective-permute-start | bytes 294920 | tf_op jit(solution)/shard_map/ppermute | solution.py:595
  48.7 0.0 collective-permute-start.7
  48.7 0.8 %shard_map.157.applied_ref = f32[128,512]{1,0:T(8,128)S(1)} custom-call(f32[128,512]{1,0:T(8,128)S(1)} %get-tuple-element.70.refs_0_, f32[24,512]{1,0:T(8,128)S(1)} %get-tuple-element.71.refs_1_, f32[24,512]{1,0:T(8,128)S(1)} %get-tuple-element.72.refs_2_, bf16[512,256]{1,0:T(8,128)(2,1)S(1)} %get-tuple-element.52.refs_2_.refs_7_.refs_3_, ...), custom_call_target="tpu_custom_call" | custom-call | flops 402653184 | bytes 2359296 | tf_op jit(solution)/shard_map/pallas_call | solution.py:730
  49.5 1.8 %collective-permute-done.6.yodd_ref = f32[48,512]{1,0:T(8,128)S(1)} collective-permute-done((f32[48,512]{1,0:T(8,128)S(1)}, f32[48,512]{1,0:T(8,128)S(1)}, u32[]{:S(2)}, u32[]{:S(2)}) %collective-permute-start.6) | collective-permute-done | bytes 98336 | tf_op jit(solution)/shard_map/ppermute | solution.py:595
  51.3 0.0 collective-permute-done.7.yeven_ref
  51.3 0.6 shard_map.158
  51.9 14.1 %all_to_all.46 = f32[32,16,128]{2,1,0:T(8,128)S(1)} all-to-all(f32[32,16,128]{2,1,0:T(8,128)S(1)} %bitcast.27), channel_id=1, replica_groups=mesh['py'=8,'pz'=4] {'py','pz'}, dimensions={0} | all-to-all | bytes 524288 | tf_op jit(solution)/shard_map/all_to_all | solution.py:741
  66.0 1.3 %shard_map.159 = f32[512,128]{1,0:T(8,128)S(1)} custom-call(f32[64,1024]{1,0:T(8,128)S(1)} %get-tuple-element.54.refs_3_.refs_0_, bf16[256,256]{1,0:T(8,128)(2,1)S(1)} %get-tuple-element.55.refs_1_, bf16[256,256]{1,0:T(8,128)(2,1)S(1)} %get-tuple-element.56.refs_2_, bf16[64,192]{1,0:T(8,128)(2,1)S(1)} %get-tuple-element.57.refs_3_, ...), custom_call_target="tpu_custom_call" | custom-call | flops 402653184 | bytes 524288 | tf_op jit(solution)/shard_map/pallas_call | solution.py:698
  67.2 12.7 %all_to_all.47 = f32[32,16,128]{2,1,0:T(8,128)S(1)} all-to-all(f32[32,16,128]{2,1,0:T(8,128)S(1)} %bitcast.29), channel_id=1, replica_groups=mesh['py'=8,'pz'=4] {'py','pz'}, dimensions={0} | all-to-all | bytes 524288 | tf_op jit(solution)/shard_map/all_to_all | solution.py:743
  80.0 1.1 %shard_map.160 = (f32[128,512]{1,0:T(8,128)}, f32[128,512]{1,0:T(8,128)}) custom-call(f32[512,128]{1,0:T(8,128)S(1)} %bitcast.20, bf16[1024,512]{1,0:T(8,128)(2,1)S(1)} %get-tuple-element.69.refs_11_.refs_1_.vectors_ref, f32[128,512]{1,0:T(8,128)S(1)} %get-tuple-element.76.field_ref, f32[128,512]{1,0:T(8,128)S(1)} %get-tuple-element.77.residual_ref), custom_call_target="tpu_custom_call" | custom-call | flops 201326592 | bytes 2097152 | tf_op jit(solution)/shard_map/pallas_call | solution.py:746
  (4 shorter events, 0.1 us)
Async XLA Ops:
  1.9 7.1 %collective-permute-start.1 = (f32[48,512]{1,0:T(8,128)S(1)}, f32[48,512]{1,0:T(8,128)S(1)}, u32[]{:S(2)}, u32[]{:S(2)}) collective-permute-start(f32[48,512]{1,0:T(8,128)S(1)} %get-tuple-element.44.refs_8_), channel_id=1, source_target_pairs={{0,1},{1,0},{2,3},{3,2},{4,5},{5,4},{6,7},{7,6},{8,9},{9,8},{10,11... | collective-permute-start | bytes 294920 | tf_op jit(solution)/shard_map/ppermute | solution.py:584
  5.0 4.0 %collective-permute-start = (f32[48,512]{1,0:T(8,128)S(1)}, f32[48,512]{1,0:T(8,128)S(1)}, u32[]{:S(2)}, u32[]{:S(2)}) collective-permute-start(f32[48,512]{1,0:T(8,128)S(1)} %get-tuple-element.51), channel_id=1, source_target_pairs={{0,4},{1,2},{2,1},{3,7},{4,0},{5,6},{6,5},{7,3},{8,12},{9,10},{10,... | collective-permute-start | bytes 294920 | tf_op jit(solution)/shard_map/ppermute | solution.py:605
  5.0 6.0 %collective-permute-start.2 = (f32[64,512]{1,0:T(8,128)S(1)}, f32[64,512]{1,0:T(8,128)S(1)}, u32[]{:S(2)}, u32[]{:S(2)}) collective-permute-start(f32[64,512]{1,0:T(8,128)S(1)} %get-tuple-element.64), channel_id=1, source_target_pairs={{0,28},{1,29},{2,30},{3,31},{4,8},{5,9},{6,10},{7,11},{8,4},{9,5},... | collective-permute-start | bytes 393224 | tf_op jit(solution)/shard_map/ppermute | solution.py:595
  7.5 3.4 %collective-permute-start.4 = (f32[64,512]{1,0:T(8,128)S(1)}, f32[64,512]{1,0:T(8,128)S(1)}, u32[]{:S(2)}, u32[]{:S(2)}) collective-permute-start(f32[64,512]{1,0:T(8,128)S(1)} %get-tuple-element.65), channel_id=1, source_target_pairs={{0,4},{4,0},{8,12},{12,8},{16,20},{20,16},{24,28},{28,24},{1,5},{5... | collective-permute-start | bytes 393224 | tf_op jit(solution)/shard_map/ppermute | solution.py:584
  9.0 4.7 %collective-permute-start.3 = (f32[24,512]{1,0:T(8,128)S(1)}, f32[24,512]{1,0:T(8,128)S(1)}, u32[]{:S(2)}, u32[]{:S(2)}) collective-permute-start(f32[24,512]{1,0:T(8,128)S(1)} %get-tuple-element.53.refs_7_), channel_id=1, source_target_pairs={{0,28},{1,29},{2,30},{3,31},{4,8},{5,9},{6,10},{7,11},{8,4},{9,5},... | collective-permute-start | bytes 147464 | tf_op jit(solution)/shard_map/ppermute | solution.py:595
  9.7 4.0 %collective-permute-start.5 = (f32[24,512]{1,0:T(8,128)S(1)}, f32[24,512]{1,0:T(8,128)S(1)}, u32[]{:S(2)}, u32[]{:S(2)}) collective-permute-start(f32[24,512]{1,0:T(8,128)S(1)} %get-tuple-element.66), channel_id=1, source_target_pairs={{0,4},{4,0},{8,12},{12,8},{16,20},{20,16},{24,28},{28,24},{1,5},{5... | collective-permute-start | bytes 147464 | tf_op jit(solution)/shard_map/ppermute | solution.py:584
  11.0 2.8 %copy-start.1 = (f32[8,16,512]{2,1,0:T(8,128)S(1)}, f32[8,16,512]{2,1,0:T(8,128)}, u32[]{:S(2)}) copy-start(f32[8,16,512]{2,1,0:T(8,128)} %param.15) | copy-start | bytes 786436
  30.7 14.4 %copy-start = (f32[8,16,512]{2,1,0:T(8,128)S(1)}, f32[8,16,512]{2,1,0:T(8,128)}, u32[]{:S(2)}) copy-start(f32[8,16,512]{2,1,0:T(8,128)} %param.14) | copy-start | bytes 786436
  46.4 4.9 %collective-permute-start.6 = (f32[48,512]{1,0:T(8,128)S(1)}, f32[48,512]{1,0:T(8,128)S(1)}, u32[]{:S(2)}, u32[]{:S(2)}) collective-permute-start(f32[48,512]{1,0:T(8,128)S(1)} %get-tuple-element.73), channel_id=1, source_target_pairs={{0,1},{1,0},{2,3},{3,2},{4,8},{5,9},{6,10},{7,11},{8,4},{9,5},{10,... | collective-permute-start | bytes 294920 | tf_op jit(solution)/shard_map/ppermute | solution.py:595
  48.7 2.6 %collective-permute-start.7 = (f32[48,512]{1,0:T(8,128)S(1)}, f32[48,512]{1,0:T(8,128)S(1)}, u32[]{:S(2)}, u32[]{:S(2)}) collective-permute-start(f32[48,512]{1,0:T(8,128)S(1)} %get-tuple-element.74), channel_id=1, source_target_pairs={{0,4},{4,0},{8,12},{12,8},{16,20},{20,16},{24,28},{28,24},{1,5},{5... | collective-permute-start | bytes 294920 | tf_op jit(solution)/shard_map/ppermute | solution.py:584

commit v12 on v10

--- a/solution.py
+++ b/solution.py
@@ -556,12 +556,17 @@
         yeven_ref[start : start + 8, :] = jnp.where(first, above, below)
 
 
-def last_update_kernel(spectral_ref, vectors_ref, field_ref, residual_ref, updated_hbm, residual_hbm, held, sem):
+def last_modes_kernel(npy, npz, *refs):
+    *tables, residual_ref, in_ref, out_ref, residual_hbm, turn_ref, sem = refs
     leaving = pltpu.make_async_copy(residual_ref, residual_hbm, sem.at[0])
     leaving.start()
+    modes_kernel(npy, npz, False, *tables, in_ref, out_ref, turn_ref)
+    leaving.wait()
+
+
+def last_update_kernel(spectral_ref, vectors_ref, field_ref, updated_hbm, held, sem):
     held[...] = field_ref[...] + from_modes(spectral_ref, vectors_ref)
-    fetch(((held, updated_hbm),), sem.at[pl.ds(1, 1)])
-    leaving.wait()
+    fetch(((held, updated_hbm),), sem)
 
 
 def pairwise(value, axis, odd):
@@ -673,13 +678,20 @@
             [pltpu.SMEM((nx,), F32), dma((1,))],
         )(*held, xbands, *in_hbm(xaxis_values), corner[0])
 
-        def precondition(received, rims):
+        def precondition(received, rims, residual):
+            turn = pltpu.VMEM(((ly * nz // LANES * npy + 1) * (modes + 8), LANES), F32)
+            if not rims:
+                return call(
+                    lambda *refs: last_modes_kernel(npy, npz, *refs),
+                    [((nx, count), F32), (block, F32)], [VMEM] * 7, 6 * 2 * count * nx * ly * nz, 4 * cell,
+                    [turn, dma((1,))], [VMEM, HBM],
+                )(*tables[:5], *residual, received)
             size = modes * 3 // 2 if rims else modes
             return call(
                 lambda *refs: modes_kernel(npy, npz, rims, *refs),
                 [((devices * size, count), F32)], [VMEM] * (8 if rims else 6), 6 * 2 * count * nx * ly * nz, 2 * cell,
-                [pltpu.VMEM(((ly * nz // LANES * npy + 1) * (modes + 8), LANES), F32)],
-            )(*(tables if rims else tables[:5]), received)[0]
+                [turn],
+            )(*(tables if rims else tables[:5]), received)[0], None
     else:
         vectors, taps = call(
             xvectors_kernel, [((2 * nx, nx), BF16), ((2 * (2 * REACH + 1), 8, nx), F32)], [HBM, VMEM],
@@ -689,10 +701,10 @@
         part = lax.axis_index(BOTH)
         xpart = lax.dynamic_slice_in_dim(xaxis_values, part * modes, modes)
 
-        def precondition(received, rims):
+        def precondition(received, rims, residual):
             return plain_modes(
                 received, npy, npz, ly, lz, xpart, yaxis_values, zaxis_values, yaxis_vectors, zaxis_vectors
-            )
+            ), *(residual or [None])
 
     for iteration in range(ITERS):
         last = iteration + 1 == ITERS
@@ -719,14 +731,13 @@
                 outs, [VMEM] * (8 + 2 * parts) + [ANY], *cost, scratch,
             )(weighted, zlow, zhigh, *yodd, *yeven, stencil, taps, coef, right, vectors, outward if fast else tables[0])
         spectral = lax.all_to_all(spectral, BOTH, split_axis=0, concat_axis=0, tiled=True)
-        spectral = precondition(spectral, not last)
+        spectral, residual = precondition(spectral, not last, residual)
         spectral = lax.all_to_all(spectral, BOTH, split_axis=0, concat_axis=0, tiled=True)
         cost = (6 * count * nx * nx, 4 * cell + 4 * nx * nx)
         if last:
-            field, residual = call(
-                last_update_kernel, [(block, F32), (block, F32)], [VMEM] * 4, *cost,
-                [pltpu.VMEM(block, F32), dma((2,))], [HBM] * 2,
-            )(spectral, vectors, field, *residual)
+            field = call(
+                last_update_kernel, [(block, F32)], [VMEM] * 3, *cost, [pltpu.VMEM(block, F32), dma((1,))], [HBM],
+            )(spectral, vectors, field)[0]
         elif fast:
             field, weighted, zlow, zhigh, *yrims = call(
                 lambda *refs: rim_update_kernel(ly, lz, devices, *refs),

time: 81.4 us -> 81.4 us (level)
    pallas_call x1 -> x2, Pallas kernels: 1.14 us -> 2.4 us  [the longest x1 1.27 us: precondition(): call(lambda *refs: last_modes_kernel(npy, npz, *refs), [((nx, count), F32...]
    pallas_call x2 -> x1, Pallas kernels: 2.63 us -> 1.37 us  [precondition(): call(lambda *refs: modes_kernel(npy, npz, rims, *refs), [((devices * size...]
where the time goes in v12:
time: 81.4 us; the launch traced here: 81.2 us
  blocking collectives  55.4 us (68%)
  Pallas kernels  12 us (15%)
  starting transfers between devices  8.46 us (10%)
  waiting for transfers between devices  4.49 us (6%)
    all_to_all x4, blocking collectives, shards(): lax.all_to_all(spectral, BOTH, split_axis=0, concat_axis=0, tiled=True)  55.4 us
    ppermute x3, starting transfers between devices, paired(): lax.ppermute(value, axis, [(i, (i + 1 if i % 2 else i - 1) % count) for i...  5.35 us
    ppermute x3, waiting for transfers between devices, paired(): lax.ppermute(value, axis, [(i, (i + 1 if i % 2 else i - 1) % count) for i...  4.48 us
    ppermute x4, starting transfers between devices, pairwise(): lax.ppermute(value, axis, [(i, j if 0 <= j < count else i) for i, j in en...  3.1 us
  transfers between devices with their start and end apart: 8, of which 3 were waited for; matrix products, arithmetic and copies ran while one was open for 0% of the time, Pallas kernels for 5%

profile of v12, /device:TPU:0, one launch (start us, length us, event | category | flops | bytes accessed | tf_op | source)
XLA Modules:
  0.0 81.2 jit_solution(10510453661028327990)
XLA Ops:
  0.6 1.3 %shard_map.149 = (f32[128,512]{1,0:T(8,128)S(1)}, f32[128,512]{1,0:T(8,128)S(1)}, f32[48,512]{1,0:T(8,128)S(1)}, f32[48,512]{1,0:T(8,128)S(1)}, f32[64,512]{1,0:...) custom-call(f32[8]{0:T(128)} %refs_0_.1, ...), custom_call_target="tpu_custom_call" | custom-call | flops 1048576 | bytes 1048576 | tf_op jit(solution)/shard_map/pallas_call | solution.py:646
  2.0 3.1 %collective-permute-start.1 = (f32[48,512]{1,0:T(8,128)S(1)}, f32[48,512]{1,0:T(8,128)S(1)}, u32[]{:S(2)}, u32[]{:S(2)}) collective-permute-start(f32[48,512]{1,0:T(8,128)S(1)} %get-tuple-element.44.refs_8_), channel_id=1, source_target_pairs={{0,1},{1,0},{2,3},{3,2},{4,5},{5,4},{6,7},{7,6},{8,9},{9,8},{10,11... | collective-permute-start | bytes 294920 | tf_op jit(solution)/shard_map/ppermute | solution.py:575
  5.0 0.0 collective-permute-start
  5.0 2.6 %collective-permute-start.2 = (f32[64,512]{1,0:T(8,128)S(1)}, f32[64,512]{1,0:T(8,128)S(1)}, u32[]{:S(2)}, u32[]{:S(2)}) collective-permute-start(f32[64,512]{1,0:T(8,128)S(1)} %get-tuple-element.64), channel_id=1, source_target_pairs={{0,28},{4,8},{8,4},{12,16},{16,12},{20,24},{24,20},{28,0},{1,29},{... | collective-permute-start | bytes 393224 | tf_op jit(solution)/shard_map/ppermute | solution.py:580
  7.6 0.0 collective-permute-start.4
  7.6 1.4 %shard_map.150 = (bf16[512,256]{1,0:T(8,128)(2,1)S(1)}, f32[512,512]{1,0:T(8,128)S(1)}, f32[64,64]{1,0:T(8,128)S(1)}, f32[64,64]{1,0:T(8,128)S(1)}, f32[1,64]{1,0:T(1,128)S(1)}, /*index=5*/f32[1,64]{1,0:T(1,128)S(1)}) custom-call(s32[2,512]{1,0:T(2,128)S(1)} %get-tuple-element.41.refs_0_, f32[7,2,8]{2,1,0:T(2,128)S(1)} %get-tuple-element.42.refs_1_, ...), custom_call_target="tpu_custom_call" | custom-call | flops 1966080 | bytes 262144 | tf_op jit(solution)/shard_map/pallas_call | solution.py:656
  9.0 0.0 collective-permute-done.1.refs_1_
  9.0 0.0 collective-permute-done.refs_0_
  9.1 0.7 collective-permute-start.3
  9.8 0.0 collective-permute-start.5
  9.8 1.0 %shard_map.152 = (bf16[1024,512]{1,0:T(8,128)(2,1)S(1)}, f32[14,8,512]{2,1,0:T(8,128)S(1)}, f32[64,1024]{1,0:T(8,128)S(1)}, bf16[256,256]{1,0:T(8,128)(2,1)S(1)}...) custom-call(f32[512,512]{1,0:T(8,128)S(1)} %get-tuple-element.45.ref, ...), custom_call_target="tpu_custom_call" | custom-call | flops 2097152 | bytes 1048576 | tf_op jit(solution)/shard_map/pallas_call | solution.py:673
  10.8 0.3 collective-permute-done.2.refs_1_.refs_3_
  11.0 0.0 collective-permute-done.4.refs_2_.refs_5_
  11.0 0.6 shard_map.153.refs_12_.refs_6_
  11.7 2.1 %collective-permute-done.3.refs_4_ = f32[24,512]{1,0:T(8,128)S(1)} collective-permute-done((f32[24,512]{1,0:T(8,128)S(1)}, f32[24,512]{1,0:T(8,128)S(1)}, u32[]{:S(2)}, u32[]{:S(2)}) %collective-permute-start.3) | collective-permute-done | bytes 49184 | tf_op jit(solution)/shard_map/ppermute | solution.py:580
  13.8 0.0 collective-permute-done.5.refs_6_
  13.8 1.3 %shard_map.154 = f32[512,128]{1,0:T(8,128)S(1)} custom-call(f32[128,512]{1,0:T(8,128)S(1)} %get-tuple-element.61.refs_0_, f32[48,512]{1,0:T(8,128)S(1)} %get-tuple-element.62.refs_1_.refs_4_, f32[48,512]{1,0:T(8,128)S(1)} %get-tuple-element.63.refs_2_.refs_5_, f32[64,512]{1,0:T(8,128)S(1)} %collective-permute-done.2.refs_1_.refs_3_, ...), custom_call_target="tpu_custom_call" | custom-call | flops 402653184 | bytes 2359296 | tf_op jit(solution)/shard_map/pallas_call | solution.py:729
  15.1 14.3 %all_to_all.44 = f32[32,16,128]{2,1,0:T(8,128)S(1)} all-to-all(f32[32,16,128]{2,1,0:T(8,128)S(1)} %bitcast.20), channel_id=1, replica_groups=mesh['py'=8,'pz'=4] {'py','pz'}, dimensions={0} | all-to-all | bytes 524288 | tf_op jit(solution)/shard_map/all_to_all | solution.py:733
  29.4 1.4 %shard_map.155 = f32[768,128]{1,0:T(8,128)S(1)} custom-call(f32[64,1024]{1,0:T(8,128)S(1)} %get-tuple-element.54.refs_3_.refs_0_, bf16[256,256]{1,0:T(8,128)(2,1)S(1)} %get-tuple-element.55.refs_1_, bf16[256,256]{1,0:T(8,128)(2,1)S(1)} %get-tuple-element.56.refs_2_, bf16[64,192]{1,0:T(8,128)(2,1)S(1)} %get-tuple-element.57.refs_3_, ...), custom_call_target="tpu_custom_call" | custom-call | flops 402653184 | bytes 524288 | tf_op jit(solution)/shard_map/pallas_call | solution.py:690
  30.8 0.0 copy-start
  30.8 14.4 %all_to_all.45 = f32[32,24,128]{2,1,0:T(8,128)S(1)} all-to-all(f32[32,24,128]{2,1,0:T(8,128)S(1)} %bitcast.19), channel_id=1, replica_groups=mesh['py'=8,'pz'=4] {'py','pz'}, dimensions={0} | all-to-all | bytes 786432 | tf_op jit(solution)/shard_map/all_to_all | solution.py:735
  45.1 1.3 %shard_map.156 = (f32[128,512]{1,0:T(8,128)S(1)}, f32[128,512]{1,0:T(8,128)S(1)}, f32[24,512]{1,0:T(8,128)S(1)}, f32[24,512]{1,0:T(8,128)S(1)}, f32[48,512]{1,0:T(8,128)S(1)}, /*index=5*/f32[48,512]{1,0:T(8,128)S(1)}) custom-call(f32[768,128]{1,0:T(8,128)S(1)} %bitcast.18, bf16[1024,512]{1,0:T(8,128)(2,1)S(1)} %get-tuple-element.69.refs_11_.refs_1_.vectors_ref, ...), custom_call_target="tpu_custom_call" | custom-call | flops 201326592 | bytes 2097152 | tf_op jit(solution)/shard_map/pallas_call | solution.py:742
  46.4 2.1 %collective-permute-start.6 = (f32[48,512]{1,0:T(8,128)S(1)}, f32[48,512]{1,0:T(8,128)S(1)}, u32[]{:S(2)}, u32[]{:S(2)}) collective-permute-start(f32[48,512]{1,0:T(8,128)S(1)} %get-tuple-element.73), channel_id=1, source_target_pairs={{0,28},{4,8},{8,4},{12,16},{16,12},{20,24},{24,20},{28,0},{1,29},{... | collective-permute-start | bytes 294920 | tf_op jit(solution)/shard_map/ppermute | solution.py:580
  48.5 0.0 collective-permute-start.7
  48.5 0.8 %shard_map.157.applied_ref = f32[128,512]{1,0:T(8,128)S(1)} custom-call(f32[128,512]{1,0:T(8,128)S(1)} %get-tuple-element.70.refs_0_, f32[24,512]{1,0:T(8,128)S(1)} %get-tuple-element.71.refs_1_, f32[24,512]{1,0:T(8,128)S(1)} %get-tuple-element.72.refs_2_, bf16[512,256]{1,0:T(8,128)(2,1)S(1)} %get-tuple-element.52.refs_2_.refs_7_.refs_3_, ...), custom_call_target="tpu_custom_call" | custom-call | flops 402653184 | bytes 2359296 | tf_op jit(solution)/shard_map/pallas_call | solution.py:722
  49.3 2.1 %collective-permute-done.6.yodd_ref = f32[48,512]{1,0:T(8,128)S(1)} collective-permute-done((f32[48,512]{1,0:T(8,128)S(1)}, f32[48,512]{1,0:T(8,128)S(1)}, u32[]{:S(2)}, u32[]{:S(2)}) %collective-permute-start.6) | collective-permute-done | bytes 98336 | tf_op jit(solution)/shard_map/ppermute | solution.py:580
  51.4 0.0 collective-permute-done.7.yeven_ref
  51.4 0.6 shard_map.158
  52.0 14.0 %all_to_all.46 = f32[32,16,128]{2,1,0:T(8,128)S(1)} all-to-all(f32[32,16,128]{2,1,0:T(8,128)S(1)} %bitcast.29), channel_id=1, replica_groups=mesh['py'=8,'pz'=4] {'py','pz'}, dimensions={0} | all-to-all | bytes 524288 | tf_op jit(solution)/shard_map/all_to_all | solution.py:733
  66.0 1.3 %shard_map.159 = (f32[512,128]{1,0:T(8,128)S(1)}, f32[128,512]{1,0:T(8,128)}) custom-call(f32[64,1024]{1,0:T(8,128)S(1)} %get-tuple-element.54.refs_3_.refs_0_, bf16[256,256]{1,0:T(8,128)(2,1)S(1)} %get-tuple-element.55.refs_1_, bf16[256,256]{1,0:T(8,128)(2,1)S(1)} %get-tuple-element.56.refs_2_, bf16[64,192]{1,0:T(8,128)(2,1)S(1)} %get-tuple-element.57.refs_3_, ...), custom_call_target="tpu_custom_call" | custom-call | flops 402653184 | bytes 1048576 | tf_op jit(solution)/shard_map/pallas_call | solution.py:684
  67.3 12.7 %all_to_all.47 = f32[32,16,128]{2,1,0:T(8,128)S(1)} all-to-all(f32[32,16,128]{2,1,0:T(8,128)S(1)} %bitcast.28), channel_id=1, replica_groups=mesh['py'=8,'pz'=4] {'py','pz'}, dimensions={0} | all-to-all | bytes 524288 | tf_op jit(solution)/shard_map/all_to_all | solution.py:735
  80.0 1.1 %shard_map.160 = f32[128,512]{1,0:T(8,128)} custom-call(f32[512,128]{1,0:T(8,128)S(1)} %bitcast.22, bf16[1024,512]{1,0:T(8,128)(2,1)S(1)} %get-tuple-element.69.refs_11_.refs_1_.vectors_ref, f32[128,512]{1,0:T(8,128)S(1)} %get-tuple-element.78.field_ref), custom_call_target="tpu_custom_call" | custom-call | flops 201326592 | bytes 2097152 | tf_op jit(solution)/shard_map/pallas_call | solution.py:738
  (4 shorter events, 0.1 us)
Async XLA Ops:
  2.0 7.1 %collective-permute-start.1 = (f32[48,512]{1,0:T(8,128)S(1)}, f32[48,512]{1,0:T(8,128)S(1)}, u32[]{:S(2)}, u32[]{:S(2)}) collective-permute-start(f32[48,512]{1,0:T(8,128)S(1)} %get-tuple-element.44.refs_8_), channel_id=1, source_target_pairs={{0,1},{1,0},{2,3},{3,2},{4,5},{5,4},{6,7},{7,6},{8,9},{9,8},{10,11... | collective-permute-start | bytes 294920 | tf_op jit(solution)/shard_map/ppermute | solution.py:575
  5.0 4.0 %collective-permute-start = (f32[48,512]{1,0:T(8,128)S(1)}, f32[48,512]{1,0:T(8,128)S(1)}, u32[]{:S(2)}, u32[]{:S(2)}) collective-permute-start(f32[48,512]{1,0:T(8,128)S(1)} %get-tuple-element.51), channel_id=1, source_target_pairs={{0,4},{1,2},{2,1},{3,7},{4,0},{5,6},{6,5},{7,3},{8,12},{9,10},{10,... | collective-permute-start | bytes 294920 | tf_op jit(solution)/shard_map/ppermute | solution.py:590
  5.0 6.0 %collective-permute-start.2 = (f32[64,512]{1,0:T(8,128)S(1)}, f32[64,512]{1,0:T(8,128)S(1)}, u32[]{:S(2)}, u32[]{:S(2)}) collective-permute-start(f32[64,512]{1,0:T(8,128)S(1)} %get-tuple-element.64), channel_id=1, source_target_pairs={{0,28},{4,8},{8,4},{12,16},{16,12},{20,24},{24,20},{28,0},{1,29},{... | collective-permute-start | bytes 393224 | tf_op jit(solution)/shard_map/ppermute | solution.py:580
  7.6 3.4 %collective-permute-start.4 = (f32[64,512]{1,0:T(8,128)S(1)}, f32[64,512]{1,0:T(8,128)S(1)}, u32[]{:S(2)}, u32[]{:S(2)}) collective-permute-start(f32[64,512]{1,0:T(8,128)S(1)} %get-tuple-element.65), channel_id=1, source_target_pairs={{0,4},{4,0},{8,12},{12,8},{16,20},{20,16},{24,28},{28,24},{1,5},{5... | collective-permute-start | bytes 393224 | tf_op jit(solution)/shard_map/ppermute | solution.py:575
  9.1 4.7 %collective-permute-start.3 = (f32[24,512]{1,0:T(8,128)S(1)}, f32[24,512]{1,0:T(8,128)S(1)}, u32[]{:S(2)}, u32[]{:S(2)}) collective-permute-start(f32[24,512]{1,0:T(8,128)S(1)} %get-tuple-element.53.refs_7_), channel_id=1, source_target_pairs={{0,28},{4,8},{8,4},{12,16},{16,12},{20,24},{24,20},{28,0},{1,29},{... | collective-permute-start | bytes 147464 | tf_op jit(solution)/shard_map/ppermute | solution.py:580
  9.8 4.0 %collective-permute-start.5 = (f32[24,512]{1,0:T(8,128)S(1)}, f32[24,512]{1,0:T(8,128)S(1)}, u32[]{:S(2)}, u32[]{:S(2)}) collective-permute-start(f32[24,512]{1,0:T(8,128)S(1)} %get-tuple-element.66), channel_id=1, source_target_pairs={{0,4},{4,0},{8,12},{12,8},{16,20},{20,16},{24,28},{28,24},{1,5},{5... | collective-permute-start | bytes 147464 | tf_op jit(solution)/shard_map/ppermute | solution.py:575
  11.0 2.8 %copy-start.1 = (f32[8,16,512]{2,1,0:T(8,128)S(1)}, f32[8,16,512]{2,1,0:T(8,128)}, u32[]{:S(2)}) copy-start(f32[8,16,512]{2,1,0:T(8,128)} %param.15) | copy-start | bytes 786436
  30.8 14.4 %copy-start = (f32[8,16,512]{2,1,0:T(8,128)S(1)}, f32[8,16,512]{2,1,0:T(8,128)}, u32[]{:S(2)}) copy-start(f32[8,16,512]{2,1,0:T(8,128)} %param.14) | copy-start | bytes 786436
  46.4 5.0 %collective-permute-start.6 = (f32[48,512]{1,0:T(8,128)S(1)}, f32[48,512]{1,0:T(8,128)S(1)}, u32[]{:S(2)}, u32[]{:S(2)}) collective-permute-start(f32[48,512]{1,0:T(8,128)S(1)} %get-tuple-element.73), channel_id=1, source_target_pairs={{0,28},{4,8},{8,4},{12,16},{16,12},{20,24},{24,20},{28,0},{1,29},{... | collective-permute-start | bytes 294920 | tf_op jit(solution)/shard_map/ppermute | solution.py:580
  48.5 2.9 %collective-permute-start.7 = (f32[48,512]{1,0:T(8,128)S(1)}, f32[48,512]{1,0:T(8,128)S(1)}, u32[]{:S(2)}, u32[]{:S(2)}) collective-permute-start(f32[48,512]{1,0:T(8,128)S(1)} %get-tuple-element.74), channel_id=1, source_target_pairs={{0,4},{4,0},{8,12},{12,8},{16,20},{20,16},{24,28},{28,24},{1,5},{5... | collective-permute-start | bytes 294920 | tf_op jit(solution)/shard_map/ppermute | solution.py:575

commit v13 on v10

--- a/solution.py
+++ b/solution.py
@@ -413,9 +413,8 @@
     step = turn_ref.shape[0] // (npy * chunks)
     zhigh, zlow = zhigh_ref[...], zlow_ref[...]
 
-    def three(value, product, whigh, wlow):
-        rows = value.shape[0]
-        high, low = split(value)
+    def three(high, low, product, whigh, wlow):
+        rows = high.shape[0]
         both = product(jnp.concatenate([high, low], axis=0), whigh)
         return both[:rows] + both[rows:] + product(high, wlow)
 
@@ -438,7 +437,7 @@
         blocks = [in_ref[(p * npz + b) * count : (p * npz + b + 1) * count, :] for b in range(npz)]
         for half, joined in zip(halves, (early, later)):
             half.append(jnp.concatenate([joined(blocks[b], blocks[b + 1]) for b in range(0, npz, 2)], axis=1))
-    part = three(jnp.concatenate(halves[0] + halves[1], axis=0), mul, zhigh, zlow)
+    part = three(*split(jnp.concatenate(halves[0] + halves[1], axis=0)), mul, zhigh, zlow)
     for chunk in range(chunks):
         half, lane = divmod(chunk * LANES, width)
         for p in range(npy):
@@ -470,13 +469,13 @@
         for half in range(2)
         for p in range(npy)
     ]
-    spectral = jnp.concatenate(rows, axis=0)
-    back = three(spectral, mul_t, zhigh, zlow)
+    spectral = split(jnp.concatenate(rows, axis=0))
+    back = three(*spectral, mul_t, zhigh, zlow)
     total = npy * count
     if rims:
         side = [
             three(
-                spectral[half * total : (half + 1) * total], mul_t,
+                *(piece[half * total : (half + 1) * total] for piece in spectral), mul_t,
                 *(ref[:, pl.ds(half * width, width)] for ref in rim_refs),
             )
             for half in range(2)

time: 81.4 us -> 81.4 us (level)
  no operation moved by 1% of the time
where the time goes in v13:
time: 81.4 us; the launch traced here: 81.2 us
  blocking collectives  55.4 us (68%)
  Pallas kernels  12 us (15%)
  starting transfers between devices  8.46 us (10%)
  waiting for transfers between devices  4.49 us (6%)
    all_to_all x4, blocking collectives, shards(): lax.all_to_all(spectral, BOTH, split_axis=0, concat_axis=0, tiled=True)  55.4 us
    ppermute x3, starting transfers between devices, paired(): lax.ppermute(value, axis, [(i, (i + 1 if i % 2 else i - 1) % count) for i...  5.35 us
    ppermute x3, waiting for transfers between devices, paired(): lax.ppermute(value, axis, [(i, (i + 1 if i % 2 else i - 1) % count) for i...  4.48 us
    ppermute x4, starting transfers between devices, pairwise(): lax.ppermute(value, axis, [(i, j if 0 <= j < count else i) for i, j in en...  3.1 us
    pallas_call x2, Pallas kernels, precondition(): call(lambda *refs: modes_kernel(npy, npz, rims, *refs), [((devices * size...  2.63 us
  transfers between devices with their start and end apart: 8, of which 3 were waited for; matrix products, arithmetic and copies ran while one was open for 0% of the time, Pallas kernels for 5%

profile of v13, /device:TPU:0, one launch (start us, length us, event | category | flops | bytes accessed | tf_op | source)
XLA Modules:
  0.0 81.2 jit_solution(6812109592901323045)
XLA Ops:
  0.6 1.3 %shard_map.149 = (f32[128,512]{1,0:T(8,128)S(1)}, f32[128,512]{1,0:T(8,128)S(1)}, f32[48,512]{1,0:T(8,128)S(1)}, f32[48,512]{1,0:T(8,128)S(1)}, f32[64,512]{1,0:...) custom-call(f32[8]{0:T(128)} %refs_0_.1, ...), custom_call_target="tpu_custom_call" | custom-call | flops 1048576 | bytes 1048576 | tf_op jit(solution)/shard_map/pallas_call | solution.py:640
  2.0 3.1 %collective-permute-start.1 = (f32[48,512]{1,0:T(8,128)S(1)}, f32[48,512]{1,0:T(8,128)S(1)}, u32[]{:S(2)}, u32[]{:S(2)}) collective-permute-start(f32[48,512]{1,0:T(8,128)S(1)} %get-tuple-element.44.refs_8_), channel_id=1, source_target_pairs={{0,1},{1,0},{2,3},{3,2},{4,5},{5,4},{6,7},{7,6},{8,9},{9,8},{10,11... | collective-permute-start | bytes 294920 | tf_op jit(solution)/shard_map/ppermute | solution.py:569
  5.0 0.0 collective-permute-start
  5.0 2.6 %collective-permute-start.2 = (f32[64,512]{1,0:T(8,128)S(1)}, f32[64,512]{1,0:T(8,128)S(1)}, u32[]{:S(2)}, u32[]{:S(2)}) collective-permute-start(f32[64,512]{1,0:T(8,128)S(1)} %get-tuple-element.64), channel_id=1, source_target_pairs={{0,28},{4,8},{8,4},{12,16},{16,12},{20,24},{24,20},{28,0},{1,29},{... | collective-permute-start | bytes 393224 | tf_op jit(solution)/shard_map/ppermute | solution.py:574
  7.6 0.0 collective-permute-start.4
  7.6 1.4 %shard_map.150 = (bf16[512,256]{1,0:T(8,128)(2,1)S(1)}, f32[512,512]{1,0:T(8,128)S(1)}, f32[64,64]{1,0:T(8,128)S(1)}, f32[64,64]{1,0:T(8,128)S(1)}, f32[1,64]{1,0:T(1,128)S(1)}, /*index=5*/f32[1,64]{1,0:T(1,128)S(1)}) custom-call(s32[2,512]{1,0:T(2,128)S(1)} %get-tuple-element.41.refs_0_, f32[7,2,8]{2,1,0:T(2,128)S(1)} %get-tuple-element.42.refs_1_, ...), custom_call_target="tpu_custom_call" | custom-call | flops 1966080 | bytes 262144 | tf_op jit(solution)/shard_map/pallas_call | solution.py:650
  9.0 0.0 collective-permute-done.1.refs_1_
  9.0 0.0 collective-permute-done.refs_0_
  9.1 0.7 collective-permute-start.3
  9.8 0.0 collective-permute-start.5
  9.8 1.0 %shard_map.152 = (bf16[1024,512]{1,0:T(8,128)(2,1)S(1)}, f32[14,8,512]{2,1,0:T(8,128)S(1)}, f32[64,1024]{1,0:T(8,128)S(1)}, bf16[256,256]{1,0:T(8,128)(2,1)S(1)}...) custom-call(f32[512,512]{1,0:T(8,128)S(1)} %get-tuple-element.45.ref, ...), custom_call_target="tpu_custom_call" | custom-call | flops 2097152 | bytes 1048576 | tf_op jit(solution)/shard_map/pallas_call | solution.py:667
  10.8 0.3 collective-permute-done.2.refs_1_.refs_3_
  11.0 0.0 collective-permute-done.4.refs_2_.refs_5_
  11.0 0.6 shard_map.153.refs_12_.refs_6_
  11.7 2.1 %collective-permute-done.3.refs_4_ = f32[24,512]{1,0:T(8,128)S(1)} collective-permute-done((f32[24,512]{1,0:T(8,128)S(1)}, f32[24,512]{1,0:T(8,128)S(1)}, u32[]{:S(2)}, u32[]{:S(2)}) %collective-permute-start.3) | collective-permute-done | bytes 49184 | tf_op jit(solution)/shard_map/ppermute | solution.py:574
  13.8 0.0 collective-permute-done.5.refs_6_
  13.8 1.3 %shard_map.154 = f32[512,128]{1,0:T(8,128)S(1)} custom-call(f32[128,512]{1,0:T(8,128)S(1)} %get-tuple-element.61.refs_0_, f32[48,512]{1,0:T(8,128)S(1)} %get-tuple-element.62.refs_1_.refs_4_, f32[48,512]{1,0:T(8,128)S(1)} %get-tuple-element.63.refs_2_.refs_5_, f32[64,512]{1,0:T(8,128)S(1)} %collective-permute-done.2.refs_1_.refs_3_, ...), custom_call_target="tpu_custom_call" | custom-call | flops 402653184 | bytes 2359296 | tf_op jit(solution)/shard_map/pallas_call | solution.py:716
  15.1 14.3 %all_to_all.44 = f32[32,16,128]{2,1,0:T(8,128)S(1)} all-to-all(f32[32,16,128]{2,1,0:T(8,128)S(1)} %bitcast.21), channel_id=1, replica_groups=mesh['py'=8,'pz'=4] {'py','pz'}, dimensions={0} | all-to-all | bytes 524288 | tf_op jit(solution)/shard_map/all_to_all | solution.py:720
  29.4 1.4 %shard_map.155 = f32[768,128]{1,0:T(8,128)S(1)} custom-call(f32[64,1024]{1,0:T(8,128)S(1)} %get-tuple-element.54.refs_3_.refs_0_, bf16[256,256]{1,0:T(8,128)(2,1)S(1)} %get-tuple-element.55.refs_1_, bf16[256,256]{1,0:T(8,128)(2,1)S(1)} %get-tuple-element.56.refs_2_, bf16[64,192]{1,0:T(8,128)(2,1)S(1)} %get-tuple-element.57.refs_3_, ...), custom_call_target="tpu_custom_call" | custom-call | flops 402653184 | bytes 524288 | tf_op jit(solution)/shard_map/pallas_call | solution.py:677
  30.8 0.0 copy-start
  30.8 14.4 %all_to_all.45 = f32[32,24,128]{2,1,0:T(8,128)S(1)} all-to-all(f32[32,24,128]{2,1,0:T(8,128)S(1)} %bitcast.19), channel_id=1, replica_groups=mesh['py'=8,'pz'=4] {'py','pz'}, dimensions={0} | all-to-all | bytes 786432 | tf_op jit(solution)/shard_map/all_to_all | solution.py:722
  45.1 1.3 %shard_map.156 = (f32[128,512]{1,0:T(8,128)S(1)}, f32[128,512]{1,0:T(8,128)S(1)}, f32[24,512]{1,0:T(8,128)S(1)}, f32[24,512]{1,0:T(8,128)S(1)}, f32[48,512]{1,0:T(8,128)S(1)}, /*index=5*/f32[48,512]{1,0:T(8,128)S(1)}) custom-call(f32[768,128]{1,0:T(8,128)S(1)} %bitcast.18, bf16[1024,512]{1,0:T(8,128)(2,1)S(1)} %get-tuple-element.69.refs_11_.refs_1_.vectors_ref, ...), custom_call_target="tpu_custom_call" | custom-call | flops 201326592 | bytes 2097152 | tf_op jit(solution)/shard_map/pallas_call | solution.py:730
  46.4 2.1 %collective-permute-start.6 = (f32[48,512]{1,0:T(8,128)S(1)}, f32[48,512]{1,0:T(8,128)S(1)}, u32[]{:S(2)}, u32[]{:S(2)}) collective-permute-start(f32[48,512]{1,0:T(8,128)S(1)} %get-tuple-element.73), channel_id=1, source_target_pairs={{0,28},{4,8},{8,4},{12,16},{16,12},{20,24},{24,20},{28,0},{1,29},{... | collective-permute-start | bytes 294920 | tf_op jit(solution)/shard_map/ppermute | solution.py:574
  48.5 0.0 collective-permute-start.7
  48.5 0.8 %shard_map.157.applied_ref = f32[128,512]{1,0:T(8,128)S(1)} custom-call(f32[128,512]{1,0:T(8,128)S(1)} %get-tuple-element.70.refs_0_, f32[24,512]{1,0:T(8,128)S(1)} %get-tuple-element.71.refs_1_, f32[24,512]{1,0:T(8,128)S(1)} %get-tuple-element.72.refs_2_, bf16[512,256]{1,0:T(8,128)(2,1)S(1)} %get-tuple-element.52.refs_2_.refs_7_.refs_3_, ...), custom_call_target="tpu_custom_call" | custom-call | flops 402653184 | bytes 2359296 | tf_op jit(solution)/shard_map/pallas_call | solution.py:709
  49.3 2.1 %collective-permute-done.6.yodd_ref = f32[48,512]{1,0:T(8,128)S(1)} collective-permute-done((f32[48,512]{1,0:T(8,128)S(1)}, f32[48,512]{1,0:T(8,128)S(1)}, u32[]{:S(2)}, u32[]{:S(2)}) %collective-permute-start.6) | collective-permute-done | bytes 98336 | tf_op jit(solution)/shard_map/ppermute | solution.py:574
  51.4 0.0 collective-permute-done.7.yeven_ref
  51.4 0.6 shard_map.158
  52.0 14.0 %all_to_all.46 = f32[32,16,128]{2,1,0:T(8,128)S(1)} all-to-all(f32[32,16,128]{2,1,0:T(8,128)S(1)} %bitcast.27), channel_id=1, replica_groups=mesh['py'=8,'pz'=4] {'py','pz'}, dimensions={0} | all-to-all | bytes 524288 | tf_op jit(solution)/shard_map/all_to_all | solution.py:720
  66.0 1.3 %shard_map.159 = f32[512,128]{1,0:T(8,128)S(1)} custom-call(f32[64,1024]{1,0:T(8,128)S(1)} %get-tuple-element.54.refs_3_.refs_0_, bf16[256,256]{1,0:T(8,128)(2,1)S(1)} %get-tuple-element.55.refs_1_, bf16[256,256]{1,0:T(8,128)(2,1)S(1)} %get-tuple-element.56.refs_2_, bf16[64,192]{1,0:T(8,128)(2,1)S(1)} %get-tuple-element.57.refs_3_, ...), custom_call_target="tpu_custom_call" | custom-call | flops 402653184 | bytes 524288 | tf_op jit(solution)/shard_map/pallas_call | solution.py:677
  67.3 12.7 %all_to_all.47 = f32[32,16,128]{2,1,0:T(8,128)S(1)} all-to-all(f32[32,16,128]{2,1,0:T(8,128)S(1)} %bitcast.29), channel_id=1, replica_groups=mesh['py'=8,'pz'=4] {'py','pz'}, dimensions={0} | all-to-all | bytes 524288 | tf_op jit(solution)/shard_map/all_to_all | solution.py:722
  80.0 1.1 %shard_map.160 = (f32[128,512]{1,0:T(8,128)}, f32[128,512]{1,0:T(8,128)}) custom-call(f32[512,128]{1,0:T(8,128)S(1)} %bitcast.20, bf16[1024,512]{1,0:T(8,128)(2,1)S(1)} %get-tuple-element.69.refs_11_.refs_1_.vectors_ref, f32[128,512]{1,0:T(8,128)S(1)} %get-tuple-element.76.field_ref, f32[128,512]{1,0:T(8,128)S(1)} %get-tuple-element.77.residual_ref), custom_call_target="tpu_custom_call" | custom-call | flops 201326592 | bytes 2097152 | tf_op jit(solution)/shard_map/pallas_call | solution.py:725
  (4 shorter events, 0.1 us)
Async XLA Ops:
  2.0 7.1 %collective-permute-start.1 = (f32[48,512]{1,0:T(8,128)S(1)}, f32[48,512]{1,0:T(8,128)S(1)}, u32[]{:S(2)}, u32[]{:S(2)}) collective-permute-start(f32[48,512]{1,0:T(8,128)S(1)} %get-tuple-element.44.refs_8_), channel_id=1, source_target_pairs={{0,1},{1,0},{2,3},{3,2},{4,5},{5,4},{6,7},{7,6},{8,9},{9,8},{10,11... | collective-permute-start | bytes 294920 | tf_op jit(solution)/shard_map/ppermute | solution.py:569
  5.0 4.0 %collective-permute-start = (f32[48,512]{1,0:T(8,128)S(1)}, f32[48,512]{1,0:T(8,128)S(1)}, u32[]{:S(2)}, u32[]{:S(2)}) collective-permute-start(f32[48,512]{1,0:T(8,128)S(1)} %get-tuple-element.51), channel_id=1, source_target_pairs={{0,4},{1,2},{2,1},{3,7},{4,0},{5,6},{6,5},{7,3},{8,12},{9,10},{10,... | collective-permute-start | bytes 294920 | tf_op jit(solution)/shard_map/ppermute | solution.py:584
  5.0 6.0 %collective-permute-start.2 = (f32[64,512]{1,0:T(8,128)S(1)}, f32[64,512]{1,0:T(8,128)S(1)}, u32[]{:S(2)}, u32[]{:S(2)}) collective-permute-start(f32[64,512]{1,0:T(8,128)S(1)} %get-tuple-element.64), channel_id=1, source_target_pairs={{0,28},{4,8},{8,4},{12,16},{16,12},{20,24},{24,20},{28,0},{1,29},{... | collective-permute-start | bytes 393224 | tf_op jit(solution)/shard_map/ppermute | solution.py:574
  7.6 3.4 %collective-permute-start.4 = (f32[64,512]{1,0:T(8,128)S(1)}, f32[64,512]{1,0:T(8,128)S(1)}, u32[]{:S(2)}, u32[]{:S(2)}) collective-permute-start(f32[64,512]{1,0:T(8,128)S(1)} %get-tuple-element.65), channel_id=1, source_target_pairs={{0,4},{4,0},{8,12},{12,8},{16,20},{20,16},{24,28},{28,24},{1,5},{5... | collective-permute-start | bytes 393224 | tf_op jit(solution)/shard_map/ppermute | solution.py:569
  9.1 4.7 %collective-permute-start.3 = (f32[24,512]{1,0:T(8,128)S(1)}, f32[24,512]{1,0:T(8,128)S(1)}, u32[]{:S(2)}, u32[]{:S(2)}) collective-permute-start(f32[24,512]{1,0:T(8,128)S(1)} %get-tuple-element.53.refs_7_), channel_id=1, source_target_pairs={{0,28},{4,8},{8,4},{12,16},{16,12},{20,24},{24,20},{28,0},{1,29},{... | collective-permute-start | bytes 147464 | tf_op jit(solution)/shard_map/ppermute | solution.py:574
  9.8 4.0 %collective-permute-start.5 = (f32[24,512]{1,0:T(8,128)S(1)}, f32[24,512]{1,0:T(8,128)S(1)}, u32[]{:S(2)}, u32[]{:S(2)}) collective-permute-start(f32[24,512]{1,0:T(8,128)S(1)} %get-tuple-element.66), channel_id=1, source_target_pairs={{0,4},{4,0},{8,12},{12,8},{16,20},{20,16},{24,28},{28,24},{1,5},{5... | collective-permute-start | bytes 147464 | tf_op jit(solution)/shard_map/ppermute | solution.py:569
  11.0 2.8 %copy-start.1 = (f32[8,16,512]{2,1,0:T(8,128)S(1)}, f32[8,16,512]{2,1,0:T(8,128)}, u32[]{:S(2)}) copy-start(f32[8,16,512]{2,1,0:T(8,128)} %param.15) | copy-start | bytes 786436
  30.8 14.4 %copy-start = (f32[8,16,512]{2,1,0:T(8,128)S(1)}, f32[8,16,512]{2,1,0:T(8,128)}, u32[]{:S(2)}) copy-start(f32[8,16,512]{2,1,0:T(8,128)} %param.14) | copy-start | bytes 786436
  46.4 5.0 %collective-permute-start.6 = (f32[48,512]{1,0:T(8,128)S(1)}, f32[48,512]{1,0:T(8,128)S(1)}, u32[]{:S(2)}, u32[]{:S(2)}) collective-permute-start(f32[48,512]{1,0:T(8,128)S(1)} %get-tuple-element.73), channel_id=1, source_target_pairs={{0,28},{4,8},{8,4},{12,16},{16,12},{20,24},{24,20},{28,0},{1,29},{... | collective-permute-start | bytes 294920 | tf_op jit(solution)/shard_map/ppermute | solution.py:574
  48.5 2.9 %collective-permute-start.7 = (f32[48,512]{1,0:T(8,128)S(1)}, f32[48,512]{1,0:T(8,128)S(1)}, u32[]{:S(2)}, u32[]{:S(2)}) collective-permute-start(f32[48,512]{1,0:T(8,128)S(1)} %get-tuple-element.74), channel_id=1, source_target_pairs={{0,4},{4,0},{8,12},{12,8},{16,20},{20,16},{24,28},{28,24},{1,5},{5... | collective-permute-start | bytes 294920 | tf_op jit(solution)/shard_map/ppermute | solution.py:569

commit v14 on v10

--- a/solution.py
+++ b/solution.py
@@ -570,9 +570,15 @@
     return lax.ppermute(value, axis, [(i, j if 0 <= j < count else i) for i, j in enumerate(other)])
 
 
-def paired(value, axis):
-    count = lax.axis_size(axis)
-    return lax.ppermute(value, axis, [(i, (i + 1 if i % 2 else i - 1) % count) for i in range(count)])
+def paired(value, near):
+    across, count = lax.axis_size("py"), lax.axis_size("pz")
+    pairs = []
+    for i in range(across):
+        for k in range(count):
+            j = i + 1 if i % 2 else i - 1
+            end = i * count + (k ^ 1) if near and k ^ 1 < count else j % across * count + k
+            pairs.append((i * count + k, j * count + k if 0 <= j < across else end))
+    return lax.ppermute(value, BOTH, pairs)
 
 
 def odd_pairs(value):
@@ -696,7 +702,7 @@
 
     for iteration in range(ITERS):
         last = iteration + 1 == ITERS
-        yodd, yeven = [paired(value, "py") for value in yodd], [pairwise(value, "py", 0) for value in yeven]
+        yodd, yeven = [paired(value, k > 0) for k, value in enumerate(yodd)], [pairwise(value, "py", 0) for value in yeven]
         parts = len(yodd)
         if fast and iteration == 0:
             outward = call(

time: 81.4 us -> 81.4 us (level)
  waiting for transfers between devices: 4.49 us -> 2.52 us
  starting transfers between devices: 8.46 us -> 10 us
    ppermute x3, waiting for transfers between devices: 4.48 us -> 2.51 us  [paired(): return lax.ppermute(value, BOTH, pairs)]
    ppermute x3, starting transfers between devices: 5.35 us -> 6.9 us  [paired(): return lax.ppermute(value, BOTH, pairs)]
  transfers between devices with their start and end apart: 8 -> 8, of which waited for: 3 -> 2; matrix products, arithmetic and copies ran while one was open for 0% -> 0% of each run, Pallas kernels for 5% -> 5%
where the time goes in v14:
time: 81.4 us; the launch traced here: 81.2 us
  blocking collectives  55.8 us (69%)
  Pallas kernels  12 us (15%)
  starting transfers between devices  10 us (12%)
  waiting for transfers between devices  2.52 us (3%)
    all_to_all x4, blocking collectives, shards(): lax.all_to_all(spectral, BOTH, split_axis=0, concat_axis=0, tiled=True)  55.8 us
    ppermute x3, starting transfers between devices, paired(): return lax.ppermute(value, BOTH, pairs)  6.9 us
    ppermute x4, starting transfers between devices, pairwise(): lax.ppermute(value, axis, [(i, j if 0 <= j < count else i) for i, j in en...  3.1 us
    pallas_call x2, Pallas kernels, precondition(): call(lambda *refs: modes_kernel(npy, npz, rims, *refs), [((devices * size...  2.63 us
    ppermute x3, waiting for transfers between devices, paired(): return lax.ppermute(value, BOTH, pairs)  2.51 us
  transfers between devices with their start and end apart: 8, of which 2 were waited for; matrix products, arithmetic and copies ran while one was open for 0% of the time, Pallas kernels for 5%

profile of v14, /device:TPU:0, one launch (start us, length us, event | category | flops | bytes accessed | tf_op | source)
XLA Modules:
  0.0 81.2 jit_solution(9815107937335302919)
XLA Ops:
  0.6 1.3 %shard_map.149 = (f32[128,512]{1,0:T(8,128)S(1)}, f32[128,512]{1,0:T(8,128)S(1)}, f32[48,512]{1,0:T(8,128)S(1)}, f32[48,512]{1,0:T(8,128)S(1)}, f32[64,512]{1,0:...) custom-call(f32[8]{0:T(128)} %refs_0_.1, ...), custom_call_target="tpu_custom_call" | custom-call | flops 1048576 | bytes 1048576 | tf_op jit(solution)/shard_map/pallas_call | solution.py:647
  2.0 3.1 %collective-permute-start.1 = (f32[48,512]{1,0:T(8,128)S(1)}, f32[48,512]{1,0:T(8,128)S(1)}, u32[]{:S(2)}, u32[]{:S(2)}) collective-permute-start(f32[48,512]{1,0:T(8,128)S(1)} %get-tuple-element.44.refs_8_), channel_id=1, source_target_pairs={{0,1},{1,0},{2,3},{3,2},{4,5},{5,4},{6,7},{7,6},{8,9},{9,8},{10,11... | collective-permute-start | bytes 294920 | tf_op jit(solution)/shard_map/ppermute | solution.py:570
  5.0 0.0 collective-permute-start
  5.0 2.6 %collective-permute-start.2 = (f32[64,512]{1,0:T(8,128)S(1)}, f32[64,512]{1,0:T(8,128)S(1)}, u32[]{:S(2)}, u32[]{:S(2)}) collective-permute-start(f32[64,512]{1,0:T(8,128)S(1)} %get-tuple-element.64), channel_id=1, source_target_pairs={{0,28},{1,29},{2,30},{3,31},{4,8},{5,9},{6,10},{7,11},{8,4},{9,5},... | collective-permute-start | bytes 393224 | tf_op jit(solution)/shard_map/ppermute | solution.py:581
  7.6 0.0 collective-permute-start.4
  7.6 1.4 %shard_map.150 = (bf16[512,256]{1,0:T(8,128)(2,1)S(1)}, f32[512,512]{1,0:T(8,128)S(1)}, f32[64,64]{1,0:T(8,128)S(1)}, f32[64,64]{1,0:T(8,128)S(1)}, f32[1,64]{1,0:T(1,128)S(1)}, /*index=5*/f32[1,64]{1,0:T(1,128)S(1)}) custom-call(s32[2,512]{1,0:T(2,128)S(1)} %get-tuple-element.41.refs_0_, f32[7,2,8]{2,1,0:T(2,128)S(1)} %get-tuple-element.42.refs_1_, ...), custom_call_target="tpu_custom_call" | custom-call | flops 1966080 | bytes 262144 | tf_op jit(solution)/shard_map/pallas_call | solution.py:657
  9.0 0.0 collective-permute-done.1.refs_1_
  9.0 0.0 collective-permute-done.refs_0_
  9.1 2.3 %collective-permute-start.3 = (f32[24,512]{1,0:T(8,128)S(1)}, f32[24,512]{1,0:T(8,128)S(1)}, u32[]{:S(2)}, u32[]{:S(2)}) collective-permute-start(f32[24,512]{1,0:T(8,128)S(1)} %get-tuple-element.53.refs_7_), channel_id=1, source_target_pairs={{0,1},{1,0},{2,3},{3,2},{4,8},{5,9},{6,10},{7,11},{8,4},{9,5},{10,... | collective-permute-start | bytes 147464 | tf_op jit(solution)/shard_map/ppermute | solution.py:581
  11.3 0.0 collective-permute-start.5
  11.3 1.0 %shard_map.152 = (bf16[1024,512]{1,0:T(8,128)(2,1)S(1)}, f32[14,8,512]{2,1,0:T(8,128)S(1)}, f32[64,1024]{1,0:T(8,128)S(1)}, bf16[256,256]{1,0:T(8,128)(2,1)S(1)}...) custom-call(f32[512,512]{1,0:T(8,128)S(1)} %get-tuple-element.45.ref, ...), custom_call_target="tpu_custom_call" | custom-call | flops 2097152 | bytes 1048576 | tf_op jit(solution)/shard_map/pallas_call | solution.py:674
  12.3 0.0 collective-permute-done.2.refs_1_.refs_3_
  12.3 0.0 copy-start.1
  12.4 0.6 shard_map.153.refs_12_.refs_6_
  13.0 0.4 collective-permute-done.3.refs_4_
  13.4 0.0 collective-permute-done.5.refs_6_
  13.4 1.3 %shard_map.154 = f32[512,128]{1,0:T(8,128)S(1)} custom-call(f32[128,512]{1,0:T(8,128)S(1)} %get-tuple-element.61.refs_0_, f32[48,512]{1,0:T(8,128)S(1)} %get-tuple-element.62.refs_1_.refs_4_, f32[48,512]{1,0:T(8,128)S(1)} %get-tuple-element.63.refs_2_.refs_5_, f32[64,512]{1,0:T(8,128)S(1)} %collective-permute-done.2.refs_1_.refs_3_, ...), custom_call_target="tpu_custom_call" | custom-call | flops 402653184 | bytes 2359296 | tf_op jit(solution)/shard_map/pallas_call | solution.py:723
  14.7 14.7 %all_to_all.44 = f32[32,16,128]{2,1,0:T(8,128)S(1)} all-to-all(f32[32,16,128]{2,1,0:T(8,128)S(1)} %bitcast.21), channel_id=1, replica_groups=mesh['py'=8,'pz'=4] {'py','pz'}, dimensions={0} | all-to-all | bytes 524288 | tf_op jit(solution)/shard_map/all_to_all | solution.py:727
  29.4 1.4 %shard_map.155 = f32[768,128]{1,0:T(8,128)S(1)} custom-call(f32[64,1024]{1,0:T(8,128)S(1)} %get-tuple-element.54.refs_3_.refs_0_, bf16[256,256]{1,0:T(8,128)(2,1)S(1)} %get-tuple-element.55.refs_1_, bf16[256,256]{1,0:T(8,128)(2,1)S(1)} %get-tuple-element.56.refs_2_, bf16[64,192]{1,0:T(8,128)(2,1)S(1)} %get-tuple-element.57.refs_3_, ...), custom_call_target="tpu_custom_call" | custom-call | flops 402653184 | bytes 524288 | tf_op jit(solution)/shard_map/pallas_call | solution.py:684
  30.8 0.0 copy-start
  30.8 14.4 %all_to_all.45 = f32[32,24,128]{2,1,0:T(8,128)S(1)} all-to-all(f32[32,24,128]{2,1,0:T(8,128)S(1)} %bitcast.19), channel_id=1, replica_groups=mesh['py'=8,'pz'=4] {'py','pz'}, dimensions={0} | all-to-all | bytes 786432 | tf_op jit(solution)/shard_map/all_to_all | solution.py:729
  45.1 1.3 %shard_map.156 = (f32[128,512]{1,0:T(8,128)S(1)}, f32[128,512]{1,0:T(8,128)S(1)}, f32[24,512]{1,0:T(8,128)S(1)}, f32[24,512]{1,0:T(8,128)S(1)}, f32[48,512]{1,0:T(8,128)S(1)}, /*index=5*/f32[48,512]{1,0:T(8,128)S(1)}) custom-call(f32[768,128]{1,0:T(8,128)S(1)} %bitcast.18, bf16[1024,512]{1,0:T(8,128)(2,1)S(1)} %get-tuple-element.69.refs_11_.refs_1_.vectors_ref, ...), custom_call_target="tpu_custom_call" | custom-call | flops 201326592 | bytes 2097152 | tf_op jit(solution)/shard_map/pallas_call | solution.py:737
  46.4 2.1 %collective-permute-start.6 = (f32[48,512]{1,0:T(8,128)S(1)}, f32[48,512]{1,0:T(8,128)S(1)}, u32[]{:S(2)}, u32[]{:S(2)}) collective-permute-start(f32[48,512]{1,0:T(8,128)S(1)} %get-tuple-element.73), channel_id=1, source_target_pairs={{0,28},{1,29},{2,30},{3,31},{4,8},{5,9},{6,10},{7,11},{8,4},{9,5},... | collective-permute-start | bytes 294920 | tf_op jit(solution)/shard_map/ppermute | solution.py:581
  48.5 0.0 collective-permute-start.7
  48.5 0.8 %shard_map.157.applied_ref = f32[128,512]{1,0:T(8,128)S(1)} custom-call(f32[128,512]{1,0:T(8,128)S(1)} %get-tuple-element.70.refs_0_, f32[24,512]{1,0:T(8,128)S(1)} %get-tuple-element.71.refs_1_, f32[24,512]{1,0:T(8,128)S(1)} %get-tuple-element.72.refs_2_, bf16[512,256]{1,0:T(8,128)(2,1)S(1)} %get-tuple-element.52.refs_2_.refs_7_.refs_3_, ...), custom_call_target="tpu_custom_call" | custom-call | flops 402653184 | bytes 2359296 | tf_op jit(solution)/shard_map/pallas_call | solution.py:716
  49.3 2.1 %collective-permute-done.6.yodd_ref = f32[48,512]{1,0:T(8,128)S(1)} collective-permute-done((f32[48,512]{1,0:T(8,128)S(1)}, f32[48,512]{1,0:T(8,128)S(1)}, u32[]{:S(2)}, u32[]{:S(2)}) %collective-permute-start.6) | collective-permute-done | bytes 98336 | tf_op jit(solution)/shard_map/ppermute | solution.py:581
  51.4 0.0 collective-permute-done.7.yeven_ref
  51.4 0.6 shard_map.158
  52.0 14.0 %all_to_all.46 = f32[32,16,128]{2,1,0:T(8,128)S(1)} all-to-all(f32[32,16,128]{2,1,0:T(8,128)S(1)} %bitcast.27), channel_id=1, replica_groups=mesh['py'=8,'pz'=4] {'py','pz'}, dimensions={0} | all-to-all | bytes 524288 | tf_op jit(solution)/shard_map/all_to_all | solution.py:727
  66.0 1.3 %shard_map.159 = f32[512,128]{1,0:T(8,128)S(1)} custom-call(f32[64,1024]{1,0:T(8,128)S(1)} %get-tuple-element.54.refs_3_.refs_0_, bf16[256,256]{1,0:T(8,128)(2,1)S(1)} %get-tuple-element.55.refs_1_, bf16[256,256]{1,0:T(8,128)(2,1)S(1)} %get-tuple-element.56.refs_2_, bf16[64,192]{1,0:T(8,128)(2,1)S(1)} %get-tuple-element.57.refs_3_, ...), custom_call_target="tpu_custom_call" | custom-call | flops 402653184 | bytes 524288 | tf_op jit(solution)/shard_map/pallas_call | solution.py:684
  67.3 12.7 %all_to_all.47 = f32[32,16,128]{2,1,0:T(8,128)S(1)} all-to-all(f32[32,16,128]{2,1,0:T(8,128)S(1)} %bitcast.29), channel_id=1, replica_groups=mesh['py'=8,'pz'=4] {'py','pz'}, dimensions={0} | all-to-all | bytes 524288 | tf_op jit(solution)/shard_map/all_to_all | solution.py:729
  80.0 1.1 %shard_map.160 = (f32[128,512]{1,0:T(8,128)}, f32[128,512]{1,0:T(8,128)}) custom-call(f32[512,128]{1,0:T(8,128)S(1)} %bitcast.20, bf16[1024,512]{1,0:T(8,128)(2,1)S(1)} %get-tuple-element.69.refs_11_.refs_1_.vectors_ref, f32[128,512]{1,0:T(8,128)S(1)} %get-tuple-element.76.field_ref, f32[128,512]{1,0:T(8,128)S(1)} %get-tuple-element.77.residual_ref), custom_call_target="tpu_custom_call" | custom-call | flops 201326592 | bytes 2097152 | tf_op jit(solution)/shard_map/pallas_call | solution.py:732
  (4 shorter events, 0.1 us)
Async XLA Ops:
  2.0 7.1 %collective-permute-start.1 = (f32[48,512]{1,0:T(8,128)S(1)}, f32[48,512]{1,0:T(8,128)S(1)}, u32[]{:S(2)}, u32[]{:S(2)}) collective-permute-start(f32[48,512]{1,0:T(8,128)S(1)} %get-tuple-element.44.refs_8_), channel_id=1, source_target_pairs={{0,1},{1,0},{2,3},{3,2},{4,5},{5,4},{6,7},{7,6},{8,9},{9,8},{10,11... | collective-permute-start | bytes 294920 | tf_op jit(solution)/shard_map/ppermute | solution.py:570
  5.0 4.0 %collective-permute-start = (f32[48,512]{1,0:T(8,128)S(1)}, f32[48,512]{1,0:T(8,128)S(1)}, u32[]{:S(2)}, u32[]{:S(2)}) collective-permute-start(f32[48,512]{1,0:T(8,128)S(1)} %get-tuple-element.51), channel_id=1, source_target_pairs={{0,4},{1,2},{2,1},{3,7},{4,0},{5,6},{6,5},{7,3},{8,12},{9,10},{10,... | collective-permute-start | bytes 294920 | tf_op jit(solution)/shard_map/ppermute | solution.py:591
  5.0 7.3 %collective-permute-start.2 = (f32[64,512]{1,0:T(8,128)S(1)}, f32[64,512]{1,0:T(8,128)S(1)}, u32[]{:S(2)}, u32[]{:S(2)}) collective-permute-start(f32[64,512]{1,0:T(8,128)S(1)} %get-tuple-element.64), channel_id=1, source_target_pairs={{0,28},{1,29},{2,30},{3,31},{4,8},{5,9},{6,10},{7,11},{8,4},{9,5},... | collective-permute-start | bytes 393224 | tf_op jit(solution)/shard_map/ppermute | solution.py:581
  7.6 4.7 %collective-permute-start.4 = (f32[64,512]{1,0:T(8,128)S(1)}, f32[64,512]{1,0:T(8,128)S(1)}, u32[]{:S(2)}, u32[]{:S(2)}) collective-permute-start(f32[64,512]{1,0:T(8,128)S(1)} %get-tuple-element.65), channel_id=1, source_target_pairs={{0,4},{4,0},{8,12},{12,8},{16,20},{20,16},{24,28},{28,24},{1,5},{5... | collective-permute-start | bytes 393224 | tf_op jit(solution)/shard_map/ppermute | solution.py:570
  9.1 4.3 %collective-permute-start.3 = (f32[24,512]{1,0:T(8,128)S(1)}, f32[24,512]{1,0:T(8,128)S(1)}, u32[]{:S(2)}, u32[]{:S(2)}) collective-permute-start(f32[24,512]{1,0:T(8,128)S(1)} %get-tuple-element.53.refs_7_), channel_id=1, source_target_pairs={{0,1},{1,0},{2,3},{3,2},{4,8},{5,9},{6,10},{7,11},{8,4},{9,5},{10,... | collective-permute-start | bytes 147464 | tf_op jit(solution)/shard_map/ppermute | solution.py:581
  11.3 2.1 %collective-permute-start.5 = (f32[24,512]{1,0:T(8,128)S(1)}, f32[24,512]{1,0:T(8,128)S(1)}, u32[]{:S(2)}, u32[]{:S(2)}) collective-permute-start(f32[24,512]{1,0:T(8,128)S(1)} %get-tuple-element.66), channel_id=1, source_target_pairs={{0,4},{4,0},{8,12},{12,8},{16,20},{20,16},{24,28},{28,24},{1,5},{5... | collective-permute-start | bytes 147464 | tf_op jit(solution)/shard_map/ppermute | solution.py:570
  12.3 1.1 %copy-start.1 = (f32[8,16,512]{2,1,0:T(8,128)S(1)}, f32[8,16,512]{2,1,0:T(8,128)}, u32[]{:S(2)}) copy-start(f32[8,16,512]{2,1,0:T(8,128)} %param.15) | copy-start | bytes 786436
  30.8 14.4 %copy-start = (f32[8,16,512]{2,1,0:T(8,128)S(1)}, f32[8,16,512]{2,1,0:T(8,128)}, u32[]{:S(2)}) copy-start(f32[8,16,512]{2,1,0:T(8,128)} %param.14) | copy-start | bytes 786436
  46.4 5.0 %collective-permute-start.6 = (f32[48,512]{1,0:T(8,128)S(1)}, f32[48,512]{1,0:T(8,128)S(1)}, u32[]{:S(2)}, u32[]{:S(2)}) collective-permute-start(f32[48,512]{1,0:T(8,128)S(1)} %get-tuple-element.73), channel_id=1, source_target_pairs={{0,28},{1,29},{2,30},{3,31},{4,8},{5,9},{6,10},{7,11},{8,4},{9,5},... | collective-permute-start | bytes 294920 | tf_op jit(solution)/shard_map/ppermute | solution.py:581
  48.5 2.9 %collective-permute-start.7 = (f32[48,512]{1,0:T(8,128)S(1)}, f32[48,512]{1,0:T(8,128)S(1)}, u32[]{:S(2)}, u32[]{:S(2)}) collective-permute-start(f32[48,512]{1,0:T(8,128)S(1)} %get-tuple-element.74), channel_id=1, source_target_pairs={{0,4},{4,0},{8,12},{12,8},{16,20},{20,16},{24,28},{28,24},{1,5},{5... | collective-permute-start | bytes 294920 | tf_op jit(solution)/shard_map/ppermute | solution.py:570
